TPU v7x, 32 devices: a whole 2x2x4 slice. The times are simulated.
32 devices in a mesh: groups: 2 (over y), expert: 16 (over z, x, core), tensor: 1.
Axes of the slice: x: 2, y: 2, z: 4, core: 2. Of those that a mesh axis runs over, the one named last changes fastest.
Arguments:
- hidden: bfloat16 [2048, 8, 1024], P(('groups', 'expert'), None, 'tensor'), parts along dimension 0, may hold values from -6 to 6
- expert_ids: int32 [2048, 8], P(('groups', 'expert')), parts along dimension 0, may hold values from 0 to 15, all different within a row; in each aligned block of 64 rows (0 to 63, 64 to 127, ...) at most 64 rows name the same one
- gate_weights: float32 [2048, 8], P(('groups', 'expert')), parts along dimension 0, may hold values from 0.05 to 1
- down_weight: bfloat16 [16, 1024, 3584], P('expert', 'tensor'), may hold values from -0.1875 to 0.1875
Outputs:
- mixed: bfloat16 [2048, 3584], P(('groups', 'expert'), 'tensor'), parts along dimension 0
There are 2 independent parts, one for each index of `groups`. A program takes and returns all parts, laid end to end along the dimension named above; an argument that names none is the same for every part. Nothing has to cross between parts.
Inputs may be any that keep to these rules, and one draw needn't show every extreme that they name: `expert_ids`: each row names 8 different experts. Of the 64 tokens of one index of expert, at most 64 name any one expert, and in every draw some expert is named by exactly 64 tokens of some index.
All inputs are finite; a program needn't handle non-finite values.
Results may differ from a plain program's by a relative error of at most 0.0059.
Values may be sent and summed in bfloat16 or wider, within the bound.
No kernel may reach another device: no remote copies, remote signals or barrier semaphores. Data moves between devices by JAX's collectives and lax.ppermute only.
A program may use at most 64 MiB of HBM per device.

v0:
```python
import jax
import jax.numpy as jnp
from jax import lax
from jax.sharding import PartitionSpec as P


def passed_along(block, axis, distance):
    devices = range(lax.axis_size(axis))
    route = [((i - distance) % len(devices), i) for i in devices]
    return lax.ppermute(block, axis, route)


def project(arrived, weights):
    return jnp.einsum("secf,efd->secd", arrived, weights, preferred_element_type=jnp.float32)


def body(hidden, expert_ids, gate_weights, down_weight):
    token_count, choose_count, half_hidden = hidden.shape
    local_experts = down_weight.shape[0]
    owner_count = lax.axis_size("expert")
    tensor_count = lax.axis_size("tensor")
    all_experts = owner_count * local_experts
    capacity = min(token_count, max(2, 2 * token_count * choose_count // all_experts))
    flat_ids = expert_ids.reshape(-1)
    onehot = (flat_ids[:, None] == jnp.arange(all_experts, dtype=jnp.int32)[None, :]).astype(
        jnp.int32
    )
    running = jnp.cumsum(onehot, axis=0)
    ranks = jnp.sum(onehot * running, axis=1) - 1
    slots = flat_ids * capacity + ranks
    copy_rows = hidden.reshape(token_count * choose_count, half_hidden)
    outgoing = (
        jnp.zeros((all_experts * capacity, half_hidden), hidden.dtype).at[slots].set(copy_rows)
    )
    outgoing = outgoing.reshape(owner_count, local_experts, capacity, half_hidden)
    width_total = down_weight.shape[2]
    width_half = width_total // tensor_count
    position = lax.axis_index("tensor")
    other = 1 - position
    arrived = lax.all_to_all(outgoing, "expert", split_axis=0, concat_axis=0, tiled=True)
    if tensor_count == 1:
        summed = project(arrived, down_weight).astype(jnp.bfloat16)
    else:
        partial_rows = project(arrived, down_weight).astype(jnp.bfloat16)
        outbound = lax.dynamic_slice_in_dim(partial_rows, other * width_half, width_half, 3)
        mine = lax.dynamic_slice_in_dim(partial_rows, position * width_half, width_half, 3)
        inbound = passed_along(outbound, "tensor", 1)
        summed = (mine.astype(jnp.float32) + inbound.astype(jnp.float32)).astype(jnp.bfloat16)
    returned = lax.all_to_all(summed, "expert", split_axis=0, concat_axis=0, tiled=True)
    flat_back = returned.reshape(all_experts * capacity, returned.shape[3])
    picked = (
        flat_back[slots].astype(jnp.float32).reshape(token_count, choose_count, returned.shape[3])
    )
    combined = jnp.sum(picked * gate_weights[:, :, None], axis=1)
    return combined.astype(jnp.bfloat16)


def solution(mesh):
    placed = (
        P(("groups", "expert"), None, "tensor"),
        P(("groups", "expert"), None),
        P(("groups", "expert"), None),
        P("expert", "tensor", None),
    )
    return jax.shard_map(
        body,
        mesh=mesh,
        in_specs=placed,
        out_specs=P(("groups", "expert"), "tensor"),
        check_vma=False,
    )
```

profile of v0, /device:TPU:11, one launch (start us, length us, event | category | flops | bytes accessed | tf_op | source)
XLA Modules:
  0.0 256.1 jit_solution(12781084938769049418)
XLA Ops:
  0.0 0.0 copy-start
  0.0 0.9 copy.12
  0.9 0.1 eq.29
  1.0 0.1 eq.25
  1.0 0.7 broadcast_multiply_fusion
  1.7 1.1 reduce-window.6
  2.9 0.2 slice_reduce_fusion
  3.1 0.1 fusion.10
  3.3 0.1 copy.11
  3.3 0.1 mul.29
  3.5 0.0 copy-done
  3.5 3.2 %scatter_custom_fusion = bf16[1024,1024]{1,0:T(8,128)(2,1)S(1)} fusion(s32[512]{0:T(512)S(1)} %bitcast.43, bf16[64,8,1024]{2,1,0:T(8,128)(2,1)S(1)} %copy-done, bf16[]{:T(256)} %constant.6.clone.1), kind=kCustom, calls=%fused_computation.8 | custom fusion | bytes 3145730 | tf_op jit(solution)/shard_map/scatter | solution.py:33
  6.7 53.7 %all_to_all.10 = bf16[16,1,64,1024]{3,2,1,0:T(8,128)(2,1)S(1)} all-to-all(bf16[16,1,64,1024]{3,2,1,0:T(8,128)(2,1)S(1)} %bitcast.42), channel_id=1, replica_groups=mesh['groups'=2,'expert'=16,'tensor'=1] {'expert'}, dimensions={0} | all-to-all | bytes 4194304 | tf_op jit(solution)/shard_map/all_to_all | solution.py:40
  60.4 12.8 %fusion.2 = bf16[16,1,64,3584]{3,2,1,0:T(8,128)(2,1)} fusion(bf16[1,1024,3584]{2,1,0:T(8,128)(2,1)} %param.7, bf16[16,1,64,1024]{3,2,1,0:T(8,128)(2,1)S(1)} %all_to_all.10), kind=kOutput, calls=%fused_computation.6 | convolution fusion | flops 7519862784 | bytes 16777216 | tf_op jit(solution)/shard_map/secf,efd->secd/dot_general | solution.py:14
  73.2 0.0 copy-start.1
  73.2 5.3 %all-to-all-start.1 = ((bf16[16,1,64,3584]{3,2,1,0:T(8,128)(2,1)}), bf16[16,1,64,3584]{3,2,1,0:T(8,128)(2,1)}, u32[]{:S(2)}, u32[]{:S(2)}) async-start(bf16[16,1,64,3584]{3,2,1,0:T(8,128)(2,1)} %fusion.2), calls=%async_computation.1 | async-start | bytes 14680064 | tf_op jit(solution)/shard_map/all_to_all | solution.py:49
  78.5 0.0 copy-done.1
  78.5 0.1 copy.16
  78.6 159.8 %all-to-all-done.1 = bf16[16,1,64,3584]{3,2,1,0:T(8,128)(2,1)} async-done(((bf16[16,1,64,3584]{3,2,1,0:T(8,128)(2,1)}), bf16[16,1,64,3584]{3,2,1,0:T(8,128)(2,1)}, u32[]{:S(2)}, u32[]{:S(2)}) %all-to-all-start.1) | async-done | bytes 7340064 | tf_op jit(solution)/shard_map/all_to_all | solution.py:49
  238.3 11.9 %gather_fusion = bf16[512,3584]{1,0:T(8,128)(2,1)} fusion(bf16[1024,3584]{1,0:T(8,128)(2,1)} %bitcast.12, s32[1024]{0:T(1024)S(1)} %pad_clamp_fusion), kind=kCustom, calls=%fused_computation | custom fusion | bytes 7342080 | tf_op jit(solution)/shard_map/gather | solution.py:52
  250.3 5.8 %fusion = bf16[64,3584]{1,0:T(8,128)(2,1)} fusion(bf16[512,3584]{1,0:T(8,128)(2,1)} %gather_fusion, f32[64,8]{1,0:T(8,128)S(1)} %copy.16), kind=kLoop, calls=%fused_computation.4 | loop fusion | flops 5275648 | bytes 4130816 | tf_op jit(solution)/shard_map/reduce_sum | solution.py:54
  (6 shorter events, 0.1 us)
Async XLA Ops:
  0.0 3.5 %copy-start = (bf16[64,8,1024]{2,1,0:T(8,128)(2,1)S(1)}, bf16[64,8,1024]{2,1,0:T(8,128)(2,1)}, u32[]{:S(2)}) copy-start(bf16[64,8,1024]{2,1,0:T(8,128)(2,1)} %param.4) | copy-start | bytes 3145732
  73.2 5.3 %copy-start.1 = (f32[64,8]{0,1:T(8,128)S(1)}, f32[64,8]{0,1:T(8,128)}, u32[]{:S(2)}) copy-start(f32[64,8]{0,1:T(8,128)} %param.6) | copy-start | bytes 6148
  73.2 165.1 %all-to-all-start.1 = ((bf16[16,1,64,3584]{3,2,1,0:T(8,128)(2,1)}), bf16[16,1,64,3584]{3,2,1,0:T(8,128)(2,1)}, u32[]{:S(2)}, u32[]{:S(2)}) async-start(bf16[16,1,64,3584]{3,2,1,0:T(8,128)(2,1)} %fusion.2), calls=%async_computation.1 | async-start | bytes 14680064 | tf_op jit(solution)/shard_map/all_to_all | solution.py:49
where the time goes:
time: 256 us
  waiting for transfers between devices  160 us (62%)
  blocking collectives  53.7 us (21%)
  local copies, waits for them, and re-layouts  16.7 us (7%)
  matrix products  12.8 us (5%)
  other arithmetic  7.82 us (3%)
  starting transfers between devices  5.26 us (2%)
    all_to_all x1, waiting for transfers between devices, body(): lax.all_to_all(summed, 'expert', split_axis=0, concat_axis=0, tiled=True)  160 us
    all_to_all x1, blocking collectives, body(): lax.all_to_all(outgoing, 'expert', split_axis=0, concat_axis=0, tiled=True)  53.7 us
    dot_general x1, matrix products, project(): jnp.einsum('secf,efd->secd', arrived, weights, preferred_element_type=jnp...  12.8 us
    gather x1, local copies, waits for them, and re-layouts, body(): flat_back[slots].astype(jnp.float32)  11.9 us
    reduce_sum x1, other arithmetic, body(): combined = jnp.sum(picked * gate_weights[:, :, None], axis=1)  5.82 us
    all_to_all x1, starting transfers between devices, body(): lax.all_to_all(summed, 'expert', split_axis=0, concat_axis=0, tiled=True)  5.26 us
  transfers between devices with their start and end apart: 1, of which 1 were waited for; matrix products, arithmetic and copies ran while one was open for 0% of the time, Pallas kernels for 0%

commit v1 on v0

--- a/solution.py
+++ b/solution.py
@@ -14,7 +14,7 @@
     return jnp.einsum("secf,efd->secd", arrived, weights, preferred_element_type=jnp.float32)
 
 
-def body(hidden, expert_ids, gate_weights, down_weight):
+def slotted_body(hidden, expert_ids, gate_weights, down_weight):
     token_count, choose_count, half_hidden = hidden.shape
     local_experts = down_weight.shape[0]
     owner_count = lax.axis_size("expert")
@@ -55,6 +55,34 @@
     return combined.astype(jnp.bfloat16)
 
 
+def spread_rows(hidden, expert_ids, gate_weights, all_experts):
+    token_count, choose_count, width = hidden.shape
+    chosen = expert_ids[:, :, None] == jnp.arange(all_experts, dtype=jnp.int32)
+    gates = jnp.sum(jnp.where(chosen, gate_weights[:, :, None], 0.0), axis=1).T
+    same = jnp.eye(token_count, dtype=jnp.bool_)
+    pick = (chosen.transpose(2, 0, 1)[:, :, None, :] & same[None, :, :, None]).astype(hidden.dtype)
+    rows = jnp.dot(
+        pick.reshape(all_experts * token_count, token_count * choose_count),
+        hidden.reshape(token_count * choose_count, width),
+        preferred_element_type=jnp.float32,
+    ).reshape(all_experts, token_count, width)
+    return (rows * gates[:, :, None]).astype(hidden.dtype)
+
+
+def dense_body(hidden, expert_ids, gate_weights, down_weight):
+    owner_count = lax.axis_size("expert")
+    local_experts = down_weight.shape[0]
+    token_count, _, width = hidden.shape
+    outgoing = spread_rows(hidden, expert_ids, gate_weights, owner_count * local_experts)
+    outgoing = outgoing.reshape(owner_count, local_experts, token_count, width)
+    arrived = lax.all_to_all(outgoing, "expert", split_axis=0, concat_axis=0, tiled=True)
+    mixed = jnp.einsum(
+        "setf,efd->std", arrived, down_weight, preferred_element_type=jnp.float32
+    ).astype(jnp.bfloat16)
+    mixed = mixed.reshape(owner_count * token_count, down_weight.shape[2])
+    return lax.psum_scatter(mixed, "expert", scatter_dimension=0, tiled=True)
+
+
 def solution(mesh):
     placed = (
         P(("groups", "expert"), None, "tensor"),
@@ -62,10 +90,18 @@
         P(("groups", "expert"), None),
         P("expert", "tensor", None),
     )
-    return jax.shard_map(
-        body,
-        mesh=mesh,
-        in_specs=placed,
-        out_specs=P(("groups", "expert"), "tensor"),
-        check_vma=False,
-    )
+
+    def whole(hidden, expert_ids, gate_weights, down_weight):
+        owners = mesh.shape["expert"]
+        tokens = hidden.shape[0] // (mesh.shape["groups"] * owners)
+        capacity = 2 * tokens * hidden.shape[1] // down_weight.shape[0]
+        dense = capacity >= tokens and mesh.shape["tensor"] == 1
+        return jax.shard_map(
+            dense_body if dense else slotted_body,
+            mesh=mesh,
+            in_specs=placed,
+            out_specs=P(("groups", "expert"), "tensor"),
+            check_vma=False,
+        )(hidden, expert_ids, gate_weights, down_weight)
+
+    return whole

time: 256 us -> 177 us (0.69)
  the two profiles are of different devices: /device:TPU:11 before, /device:TPU:0 now
where the time goes in v1:
time: 177 us
  waiting for transfers between devices  92.3 us (52%)
  blocking collectives  54.5 us (31%)
  matrix products  15.4 us (9%)
  between operations  13.4 us (8%)
    reduce_scatter x1, waiting for transfers between devices, dense_body(): return lax.psum_scatter(mixed, 'expert', scatter_dimension=0, tiled=True)  92.3 us
    all_to_all x1, blocking collectives, dense_body(): lax.all_to_all(outgoing, 'expert', split_axis=0, concat_axis=0, tiled=True)  54.5 us
    dot_general x1, matrix products, dense_body(): jnp.einsum('setf,efd->std', arrived, down_weight, preferred_element_type=...  9.82 us
    dot_general x1, matrix products, spread_rows(): jnp.dot(pick.reshape(all_experts * token_count, token_count * choose_coun...  5.61 us
  transfers between devices with their start and end apart: 1, of which 1 were waited for; matrix products, arithmetic and copies ran while one was open for 0% of the time, Pallas kernels for 0%

profile of v1, /device:TPU:0, one launch (start us, length us, event | category | flops | bytes accessed | tf_op | source)
XLA Modules:
  0.0 177.1 jit_solution(9472231922036286395)
XLA Ops:
  6.5 0.0 reduce-scatter.2.cloned.1.call-start
  6.5 0.7 iota_compare_fusion.1
  7.3 0.7 select_reduce_fusion
  8.0 0.0 copy-start
  8.0 5.6 %fusion.4 = bf16[16,1,64,1024]{3,2,1,0:T(8,128)(2,1)S(1)} fusion(f32[16,64]{1,0:T(8,128)S(1)} %bitcast.24, pred[64,64]{1,0:T(8,128)(4,1)S(1)} %iota_compare_fusion.2, pred[16,64,8]{1,2,0:T(8,128)(4,1)S(1)} %iota_compare_fusion.1, bf16[64,8,1024]{2,1,0:T(8,128)(2,1)} %param.4), kind=kOutput, calls=%fused_computation.6 | convolution fusion | flops 1076363264 | bytes 3162112 | tf_op jit(solution)/shard_map/dot_general | solution.py:64
  13.6 54.5 %all_to_all.5 = bf16[16,1,64,1024]{3,2,1,0:T(8,128)(2,1)S(1)} all-to-all(bf16[16,1,64,1024]{3,2,1,0:T(8,128)(2,1)S(1)} %fusion.4), channel_id=1, replica_groups=mesh['groups'=2,'expert'=16,'tensor'=1] {'expert'}, dimensions={0} | all-to-all | bytes 4194304 | tf_op jit(solution)/shard_map/all_to_all | solution.py:78
  68.1 0.0 copy-done
  68.1 9.8 %convolution_convert_fusion = bf16[16,64,3584]{2,1,0:T(8,128)(2,1)} fusion(bf16[1,1024,3584]{2,1,0:T(8,128)(2,1)S(1)} %copy-done, bf16[16,1,64,1024]{3,2,1,0:T(8,128)(2,1)S(1)} %all_to_all.5), kind=kOutput, calls=%fused_computation | convolution fusion | flops 7519862784 | bytes 16777216 | tf_op jit(solution)/shard_map/setf,efd->std/dot_general | solution.py:79
  77.9 0.0 reduce-scatter.2.cloned.1.call-update
  77.9 92.3 %reduce-scatter.2.cloned.1.call-done = bf16[64,3584]{1,0:T(8,128)(2,1)} async-done(((bf16[1024,3584]{1,0:T(8,128)(2,1)}), bf16[64,3584]{1,0:T(8,128)(2,1)}) %reduce-scatter.2.cloned.1.call-update) | async-done | bytes 458768 | tf_op jit(solution)/shard_map/reduce_scatter | solution.py:83
  (1 shorter events, 0.0 us)
Async XLA Ops:
  6.5 163.7 %reduce-scatter.2.cloned.1.call-start = ((), (), s32[]{:S(2)}) async-start(), calls=%async_computation.2 | async-start | bytes 7798784 | tf_op jit(solution)/shard_map/reduce_scatter | solution.py:83
  8.0 60.1 %copy-start = (bf16[1,1024,3584]{2,1,0:T(8,128)(2,1)S(1)}, bf16[1,1024,3584]{2,1,0:T(8,128)(2,1)}, u32[]{:S(2)}) copy-start(bf16[1,1024,3584]{2,1,0:T(8,128)(2,1)} %param.7) | copy-start | bytes 22020100
Sparse Core Ops, SparseCore 0:
  78.0 92.1 reduce-scatter.1

commit v2 on v0

--- a/solution.py
+++ b/solution.py
@@ -1,7 +1,13 @@
 import jax
 import jax.numpy as jnp
 from jax import lax
-from jax.sharding import PartitionSpec as P
+from jax.experimental import pallas as pl
+from jax.experimental.pallas import tpu as pltpu
+from jax.sharding import Mesh, PartitionSpec as P
+
+CHIPS = 8
+CHUNKS = 4
+TILE = 896
 
 
 def passed_along(block, axis, distance):
@@ -14,7 +20,7 @@
     return jnp.einsum("secf,efd->secd", arrived, weights, preferred_element_type=jnp.float32)
 
 
-def body(hidden, expert_ids, gate_weights, down_weight):
+def slotted_body(hidden, expert_ids, gate_weights, down_weight):
     token_count, choose_count, half_hidden = hidden.shape
     local_experts = down_weight.shape[0]
     owner_count = lax.axis_size("expert")
@@ -55,17 +61,129 @@
     return combined.astype(jnp.bfloat16)
 
 
+def spread_kernel(own_ref, flat_ids_ref, ids_ref, gates_ref, hidden_ref, *out_refs):
+    token_count, choose_count = ids_ref.shape
+    own = own_ref[0]
+    shape = (token_count, token_count * choose_count)
+    row = lax.broadcasted_iota(jnp.int32, shape, 0) * choose_count
+    column = lax.broadcasted_iota(jnp.int32, shape, 1)
+    same = (column >= row) & (column < row + choose_count)
+    own_row = jnp.where(same, flat_ids_ref[...], -1)
+    for relative, out_ref in enumerate(out_refs):
+        for core in range(2):
+            expert = own ^ (2 * relative + core)
+            pick = (own_row == expert).astype(jnp.float32).astype(hidden_ref.dtype)
+            gate = jnp.sum(
+                jnp.where(ids_ref[...] == expert, gates_ref[...], 0.0), axis=1, keepdims=True
+            )
+            rows = jnp.dot(pick, hidden_ref[...], preferred_element_type=jnp.float32)
+            out_ref[core] = (rows * gate).astype(out_ref.dtype)
+
+
+def spread_rows(hidden, expert_ids, gate_weights, own):
+    token_count, choose_count, width = hidden.shape
+    vmem = pl.BlockSpec(memory_space=pltpu.VMEM)
+    block = jax.ShapeDtypeStruct((2, token_count, width), hidden.dtype)
+    return pl.pallas_call(
+        spread_kernel,
+        in_specs=[pl.BlockSpec(memory_space=pltpu.SMEM)] + [vmem] * 4,
+        out_specs=[vmem] * CHIPS,
+        out_shape=[block] * CHIPS,
+        compiler_params=pltpu.CompilerParams(vmem_limit_bytes=32 << 20),
+        name="spread_rows",
+    )(
+        own.reshape(1),
+        expert_ids.reshape(1, token_count * choose_count),
+        expert_ids,
+        gate_weights,
+        hidden.reshape(token_count * choose_count, width),
+    )
+
+
+def mix_kernel(*refs):
+    rows, (near_ref, far_ref, out_ref) = refs[:-3], refs[-3:]
+    tokens = rows[0].shape[1]
+    near = jnp.concatenate([ref[0] for ref in rows], axis=0)
+    far = jnp.concatenate([ref[1] for ref in rows], axis=0)
+    total = jnp.dot(near, near_ref[...], preferred_element_type=jnp.float32)
+    total += jnp.dot(far, far_ref[...], preferred_element_type=jnp.float32)
+    out_ref[...] = total.reshape(len(rows), tokens, -1).astype(out_ref.dtype)
+
+
+def mix(rows, near, far, start, width, tile):
+    _, tokens, depth = rows[0].shape
+    whole = pl.BlockSpec((2, tokens, depth), lambda i: (0, 0, 0))
+    weight = pl.BlockSpec((depth, tile), lambda i: (0, start // tile + i))
+    return pl.pallas_call(
+        mix_kernel,
+        grid=(width // tile,),
+        in_specs=[whole] * len(rows) + [weight] * 2,
+        out_specs=pl.BlockSpec((len(rows), tokens, tile), lambda i: (0, 0, i)),
+        out_shape=jax.ShapeDtypeStruct((len(rows), tokens, width), jnp.bfloat16),
+        compiler_params=pltpu.CompilerParams(vmem_limit_bytes=32 << 20),
+        cost_estimate=pl.CostEstimate(
+            flops=4 * len(rows) * tokens * depth * width,
+            bytes_accessed=4 * depth * width + 2 * len(rows) * tokens * (2 * depth + width),
+            transcendentals=0,
+        ),
+        name="mix",
+    )(*rows, near, far)
+
+
+def swap(block, axis, distance):
+    return lax.ppermute(block, axis, [(i, i ^ distance) for i in range(lax.axis_size(axis))])
+
+
+def send_to_chip(block, relative):
+    sizes = (lax.axis_size("z"), lax.axis_size("x"))
+    return lax.ppermute(
+        block, ("z", "x"), [(i, i ^ relative) for i in range(sizes[0] * sizes[1])]
+    )
+
+
+def dense_body(hidden, expert_ids, gate_weights, down_weight):
+    width_total = down_weight.shape[2]
+    own = (lax.axis_index("z") * 2 + lax.axis_index("x")) * 2 + lax.axis_index("core")
+    near = down_weight[0]
+    far = swap(near, "core", 1)
+    outgoing = spread_rows(hidden, expert_ids, gate_weights, own)
+    arrived = [outgoing[0]] + [send_to_chip(outgoing[r], r) for r in range(1, CHIPS)]
+    chunk = width_total // CHUNKS
+    results = []
+    for start in range(0, width_total, chunk):
+        given = mix(arrived[1::2], near, far, start, chunk, TILE)
+        kept = mix(arrived[0::2], near, far, start, chunk, TILE)
+        taken = swap(given, "x", 1)
+        line = kept.astype(jnp.float32) + taken.astype(jnp.float32)
+        pair = line[0::2] + swap(line[1::2].astype(jnp.bfloat16), "z", 1).astype(jnp.float32)
+        last = pair[0] + swap(pair[1].astype(jnp.bfloat16), "z", 2).astype(jnp.float32)
+        results.append(last.astype(jnp.bfloat16))
+    return jnp.concatenate(results, axis=1)
+
+
 def solution(mesh):
-    placed = (
-        P(("groups", "expert"), None, "tensor"),
-        P(("groups", "expert"), None),
-        P(("groups", "expert"), None),
-        P("expert", "tensor", None),
-    )
-    return jax.shard_map(
-        body,
-        mesh=mesh,
-        in_specs=placed,
-        out_specs=P(("groups", "expert"), "tensor"),
-        check_vma=False,
-    )
+    groups, owners, tensors = (mesh.shape[axis] for axis in ("groups", "expert", "tensor"))
+
+    def whole(hidden, expert_ids, gate_weights, down_weight):
+        tokens = hidden.shape[0] // (groups * owners)
+        capacity = 2 * tokens * hidden.shape[1] // down_weight.shape[0]
+        one_each = owners == 2 * CHIPS and down_weight.shape[0] == owners
+        if tensors == 1 and one_each and capacity >= tokens:
+            axes = ("groups", "z", "x", "core")
+            used = Mesh(mesh.devices.reshape(groups, CHIPS // 2, 2, 2), axes)
+            run, batch = dense_body, P(axes)
+            weight, out = P(axes[1:]), P(axes)
+        else:
+            used, run, batch = mesh, slotted_body, P(("groups", "expert"))
+            weight = P("expert", "tensor", None)
+            out = P(("groups", "expert"), "tensor")
+        rows = batch if tensors == 1 else P(("groups", "expert"), None, "tensor")
+        return jax.shard_map(
+            run,
+            mesh=used,
+            in_specs=(rows, batch, batch, weight),
+            out_specs=out,
+            check_vma=False,
+        )(hidden, expert_ids, gate_weights, down_weight)
+
+    return whole

time: 256 us -> 110 us (0.43)
  the two profiles are of different devices: /device:TPU:11 before, /device:TPU:0 now
where the time goes in v2:
time: 110 us; the launch traced here: 109 us
  waiting for transfers between devices  45.5 us (41%)
  starting transfers between devices  29.1 us (26%)
  Pallas kernels  26.5 us (24%)
  local copies, waits for them, and re-layouts  6.09 us (6%)
  other arithmetic  1.65 us (2%)
    ppermute x13, waiting for transfers between devices, swap(): lax.ppermute(block, axis, [(i, i ^ distance) for i in range(lax.axis_size...  26.7 us
    pallas_call x8, Pallas kernels, mix(): pl.pallas_call(mix_kernel, grid=(width // tile,), in_specs=[whole] * len(...  23.5 us
    ppermute x7, waiting for transfers between devices, send_to_chip(): lax.ppermute(block, ('z', 'x'), [(i, i ^ relative) for i in range(sizes[0...  18.8 us
    ppermute x13, starting transfers between devices, swap(): lax.ppermute(block, axis, [(i, i ^ distance) for i in range(lax.axis_size...  17.1 us
    ppermute x7, starting transfers between devices, send_to_chip(): lax.ppermute(block, ('z', 'x'), [(i, i ^ relative) for i in range(sizes[0...  12 us
    unnamed x10, local copies, waits for them, and re-layouts  5.86 us
    pallas_call x1, Pallas kernels, spread_rows(): pl.pallas_call(spread_kernel, in_specs=[pl.BlockSpec(memory_space=pltpu.S...  3.07 us
  transfers between devices with their start and end apart: 20, of which 8 were waited for; matrix products, arithmetic and copies ran while one was open for 2% of the time, Pallas kernels for 24%

profile of v2, /device:TPU:0, one launch (start us, length us, event | category | flops | bytes accessed | tf_op | source)
XLA Modules:
  0.0 109.2 jit_solution(4576973843905729594)
XLA Ops:
  3.3 3.1 %spread_rows.1 = (bf16[2,64,1024]{2,1,0:T(8,128)(2,1)S(1)}, bf16[2,64,1024]{2,1,0:T(8,128)(2,1)S(1)}, bf16[2,64,1024]{2,1,0:T(8,128)(2,1)S(1)}, bf16[2,64,1024]{...) custom-call(s32[1]{0:T(128)} %bitcast.own_ref, ...), custom_call_target="tpu_custom_call" | custom-call | tf_op jit(solution)/shard_map/spread_rows/pallas_call | solution.py:87
  6.4 2.6 %collective-permute-start.4 = (bf16[2,64,1024]{2,1,0:T(8,128)(2,1)S(1)}, bf16[2,64,1024]{2,1,0:T(8,128)(2,1)S(1)}, u32[]{:S(2)}, u32[]{:S(2)}) collective-permute-start(bf16[2,64,1024]{2,1,0:T(8,128)(2,1)S(1)} %get-tuple-element.17), channel_id=1, source_target_pairs={{0,2},{2,0},{4,6},{6,4},{8,10},{10,8},{12,14},{14,12},{1,3},{3,1},... | collective-permute-start | bytes 786440 | tf_op jit(solution)/shard_map/ppermute | solution.py:139
  10.5 3.5 %collective-permute-start.6 = (bf16[2,64,1024]{2,1,0:T(8,128)(2,1)S(1)}, bf16[2,64,1024]{2,1,0:T(8,128)(2,1)S(1)}, u32[]{:S(2)}, u32[]{:S(2)}) collective-permute-start(bf16[2,64,1024]{2,1,0:T(8,128)(2,1)S(1)} %get-tuple-element.19), channel_id=1, source_target_pairs={{0,10},{2,8},{4,14},{6,12},{8,2},{10,0},{12,6},{14,4},{1,11},{3,9}... | collective-permute-start | bytes 786440 | tf_op jit(solution)/shard_map/ppermute | solution.py:139
  14.0 18.8 %collective-permute-done.4.refs_0_ = bf16[2,64,1024]{2,1,0:T(8,128)(2,1)S(1)} collective-permute-done((bf16[2,64,1024]{2,1,0:T(8,128)(2,1)S(1)}, bf16[2,64,1024]{2,1,0:T(8,128)(2,1)S(1)}, u32[]{:S(2)}, u32[]{:S(2)}) %collective-permute-start.4) | collective-permute-done | bytes 262176 | tf_op jit(solution)/shard_map/ppermute | solution.py:139
  32.8 4.4 %collective-permute-start.1 = (bf16[2,64,1024]{2,1,0:T(8,128)(2,1)S(1)}, bf16[2,64,1024]{2,1,0:T(8,128)(2,1)S(1)}, u32[]{:S(2)}, u32[]{:S(2)}) collective-permute-start(bf16[2,64,1024]{2,1,0:T(8,128)(2,1)S(1)} %get-tuple-element.15), channel_id=1, source_target_pairs={{0,8},{2,10},{4,12},{6,14},{8,0},{10,2},{12,4},{14,6},{1,9},{3,11}... | collective-permute-start | bytes 786440 | tf_op jit(solution)/shard_map/ppermute | solution.py:139
  37.2 3.1 %copy-done = bf16[1,1024,3584]{2,1,0:T(8,128)(2,1)S(1)} copy-done((bf16[1,1024,3584]{2,1,0:T(8,128)(2,1)S(1)}, bf16[1,1024,3584]{2,1,0:T(8,128)(2,1)}, u32[]{:S(2)}) %copy-start) | copy-done | bytes 7340056
  40.3 2.9 %mix.9 = bf16[4,64,896]{2,1,0:T(8,128)(2,1)S(1)} custom-call(bf16[2,64,1024]{2,1,0:T(8,128)(2,1)S(1)} %collective-permute-done.4.refs_0_, bf16[2,64,1024]{2,1,0:T(8,128)(2,1)S(1)} %collective-permute-done.5.refs_1_, bf16[2,64,1024]{2,1,0:T(8,128)(2,1)S(1)} %collective-permute-done.6.refs_2_, bf16[2,64,1024]{2,1,0:T(8,128)(2,1)S(1)} %collective-permute-done.7.refs_3_, ...), custom_call_target="tpu_custom_call" | custom-call | flops 939524096 | bytes 5177344 | tf_op jit(solution)/shard_map/mix/pallas_call | solution.py:117
  43.2 1.8 %collective-permute-start.8 = (bf16[4,64,896]{2,1,0:T(8,128)(2,1)S(1)}, bf16[4,64,896]{2,1,0:T(8,128)(2,1)S(1)}, u32[]{:S(2)}, u32[]{:S(2)}) collective-permute-start(bf16[4,64,896]{2,1,0:T(8,128)(2,1)S(1)} %mix.9), channel_id=1, source_target_pairs={{0,2},{2,0},{1,3},{3,1},{4,6},{6,4},{5,7},{7,5},{8,10},{10,8},{9,1... | collective-permute-start | bytes 1376264 | tf_op jit(solution)/shard_map/ppermute | solution.py:134
  45.0 2.9 %mix.11 = bf16[4,64,896]{2,1,0:T(8,128)(2,1)S(1)} custom-call(bf16[2,64,1024]{2,1,0:T(8,128)(2,1)S(1)} %collective-permute-done.4.refs_0_, bf16[2,64,1024]{2,1,0:T(8,128)(2,1)S(1)} %collective-permute-done.5.refs_1_, bf16[2,64,1024]{2,1,0:T(8,128)(2,1)S(1)} %collective-permute-done.6.refs_2_, bf16[2,64,1024]{2,1,0:T(8,128)(2,1)S(1)} %collective-permute-done.7.refs_3_, ...), custom_call_target="tpu_custom_call" | custom-call | flops 939524096 | bytes 5177344 | tf_op jit(solution)/shard_map/mix/pallas_call | solution.py:117
  48.3 3.0 %mix.13 = bf16[4,64,896]{2,1,0:T(8,128)(2,1)S(1)} custom-call(bf16[2,64,1024]{2,1,0:T(8,128)(2,1)S(1)} %collective-permute-done.4.refs_0_, bf16[2,64,1024]{2,1,0:T(8,128)(2,1)S(1)} %collective-permute-done.5.refs_1_, bf16[2,64,1024]{2,1,0:T(8,128)(2,1)S(1)} %collective-permute-done.6.refs_2_, bf16[2,64,1024]{2,1,0:T(8,128)(2,1)S(1)} %collective-permute-done.7.refs_3_, ...), custom_call_target="tpu_custom_call" | custom-call | flops 939524096 | bytes 5177344 | tf_op jit(solution)/shard_map/mix/pallas_call | solution.py:117
  51.3 3.0 %mix.15 = bf16[4,64,896]{2,1,0:T(8,128)(2,1)S(1)} custom-call(bf16[2,64,1024]{2,1,0:T(8,128)(2,1)S(1)} %collective-permute-done.4.refs_0_, bf16[2,64,1024]{2,1,0:T(8,128)(2,1)S(1)} %collective-permute-done.5.refs_1_, bf16[2,64,1024]{2,1,0:T(8,128)(2,1)S(1)} %collective-permute-done.6.refs_2_, bf16[2,64,1024]{2,1,0:T(8,128)(2,1)S(1)} %collective-permute-done.7.refs_3_, ...), custom_call_target="tpu_custom_call" | custom-call | flops 939524096 | bytes 5177344 | tf_op jit(solution)/shard_map/mix/pallas_call | solution.py:117
  54.4 1.8 %collective-permute-start.14 = (bf16[4,64,896]{2,1,0:T(8,128)(2,1)S(1)}, bf16[4,64,896]{2,1,0:T(8,128)(2,1)S(1)}, u32[]{:S(2)}, u32[]{:S(2)}) collective-permute-start(bf16[4,64,896]{2,1,0:T(8,128)(2,1)S(1)} %mix.13), channel_id=1, source_target_pairs={{0,2},{2,0},{1,3},{3,1},{4,6},{6,4},{5,7},{7,5},{8,10},{10,8},{9,1... | collective-permute-start | bytes 1376264 | tf_op jit(solution)/shard_map/ppermute | solution.py:134
  57.1 2.9 %mix.8 = bf16[4,64,896]{2,1,0:T(8,128)(2,1)S(1)} custom-call(bf16[2,64,1024]{2,1,0:T(8,128)(2,1)S(1)} %get-tuple-element.13.refs_0_, bf16[2,64,1024]{2,1,0:T(8,128)(2,1)S(1)} %collective-permute-done.refs_1_, bf16[2,64,1024]{2,1,0:T(8,128)(2,1)S(1)} %collective-permute-done.1.refs_2_, bf16[2,64,1024]{2,1,0:T(8,128)(2,1)S(1)} %collective-permute-done.2.refs_3_, ...), custom_call_target="tpu_custom_call" | custom-call | flops 939524096 | bytes 5177344 | tf_op jit(solution)/shard_map/mix/pallas_call | solution.py:117
  60.0 2.9 %mix.10 = bf16[4,64,896]{2,1,0:T(8,128)(2,1)S(1)} custom-call(bf16[2,64,1024]{2,1,0:T(8,128)(2,1)S(1)} %get-tuple-element.13.refs_0_, bf16[2,64,1024]{2,1,0:T(8,128)(2,1)S(1)} %collective-permute-done.refs_1_, bf16[2,64,1024]{2,1,0:T(8,128)(2,1)S(1)} %collective-permute-done.1.refs_2_, bf16[2,64,1024]{2,1,0:T(8,128)(2,1)S(1)} %collective-permute-done.2.refs_3_, ...), custom_call_target="tpu_custom_call" | custom-call | flops 939524096 | bytes 5177344 | tf_op jit(solution)/shard_map/mix/pallas_call | solution.py:117
  62.9 2.9 %mix.12 = bf16[4,64,896]{2,1,0:T(8,128)(2,1)S(1)} custom-call(bf16[2,64,1024]{2,1,0:T(8,128)(2,1)S(1)} %get-tuple-element.13.refs_0_, bf16[2,64,1024]{2,1,0:T(8,128)(2,1)S(1)} %collective-permute-done.refs_1_, bf16[2,64,1024]{2,1,0:T(8,128)(2,1)S(1)} %collective-permute-done.1.refs_2_, bf16[2,64,1024]{2,1,0:T(8,128)(2,1)S(1)} %collective-permute-done.2.refs_3_, ...), custom_call_target="tpu_custom_call" | custom-call | flops 939524096 | bytes 5177344 | tf_op jit(solution)/shard_map/mix/pallas_call | solution.py:117
  65.8 2.9 %mix.14 = bf16[4,64,896]{2,1,0:T(8,128)(2,1)S(1)} custom-call(bf16[2,64,1024]{2,1,0:T(8,128)(2,1)S(1)} %get-tuple-element.13.refs_0_, bf16[2,64,1024]{2,1,0:T(8,128)(2,1)S(1)} %collective-permute-done.refs_1_, bf16[2,64,1024]{2,1,0:T(8,128)(2,1)S(1)} %collective-permute-done.1.refs_2_, bf16[2,64,1024]{2,1,0:T(8,128)(2,1)S(1)} %collective-permute-done.2.refs_3_, ...), custom_call_target="tpu_custom_call" | custom-call | flops 939524096 | bytes 5177344 | tf_op jit(solution)/shard_map/mix/pallas_call | solution.py:117
  68.9 3.5 %collective-permute-start.9 = (bf16[2,64,896]{2,1,0:T(8,128)(2,1)S(1)}, bf16[2,64,896]{2,1,0:T(8,128)(2,1)S(1)}, u32[]{:S(2)}, u32[]{:S(2)}) collective-permute-start(bf16[2,64,896]{2,1,0:T(8,128)(2,1)S(1)} %slice.57), channel_id=1, source_target_pairs={{0,4},{4,0},{8,12},{12,8},{1,5},{5,1},{9,13},{13,9},{2,6},{6,2},{1... | collective-permute-start | bytes 688136 | tf_op jit(solution)/shard_map/ppermute | solution.py:134
  72.7 3.7 %collective-permute-done.14 = bf16[4,64,896]{2,1,0:T(8,128)(2,1)S(1)} collective-permute-done((bf16[4,64,896]{2,1,0:T(8,128)(2,1)S(1)}, bf16[4,64,896]{2,1,0:T(8,128)(2,1)S(1)}, u32[]{:S(2)}, u32[]{:S(2)}) %collective-permute-start.14) | collective-permute-done | bytes 458784 | tf_op jit(solution)/shard_map/ppermute | solution.py:134
  77.3 7.0 %collective-permute-done.17 = bf16[4,64,896]{2,1,0:T(8,128)(2,1)S(1)} collective-permute-done((bf16[4,64,896]{2,1,0:T(8,128)(2,1)S(1)}, bf16[4,64,896]{2,1,0:T(8,128)(2,1)S(1)}, u32[]{:S(2)}, u32[]{:S(2)}) %collective-permute-start.17) | collective-permute-done | bytes 458784 | tf_op jit(solution)/shard_map/ppermute | solution.py:134
  85.3 3.5 %collective-permute-start.10 = (bf16[64,896]{1,0:T(8,128)(2,1)S(1)}, bf16[64,896]{1,0:T(8,128)(2,1)S(1)}, u32[]{:S(2)}, u32[]{:S(2)}) collective-permute-start(bf16[64,896]{1,0:T(8,128)(2,1)S(1)} %fusion.8), channel_id=1, source_target_pairs={{0,8},{4,12},{8,0},{12,4},{1,9},{5,13},{9,1},{13,5},{2,10},{6,14},... | collective-permute-start | bytes 344072 | tf_op jit(solution)/shard_map/ppermute | solution.py:134
  89.6 2.4 %collective-permute-start.16 = (bf16[64,896]{1,0:T(8,128)(2,1)S(1)}, bf16[64,896]{1,0:T(8,128)(2,1)S(1)}, u32[]{:S(2)}, u32[]{:S(2)}) collective-permute-start(bf16[64,896]{1,0:T(8,128)(2,1)S(1)} %fusion.10), channel_id=1, source_target_pairs={{0,8},{4,12},{8,0},{12,4},{1,9},{5,13},{9,1},{13,5},{2,10},{6,14},... | collective-permute-start | bytes 344072 | tf_op jit(solution)/shard_map/ppermute | solution.py:134
  92.0 5.2 %collective-permute-done.18 = bf16[2,64,896]{2,1,0:T(8,128)(2,1)S(1)} collective-permute-done((bf16[2,64,896]{2,1,0:T(8,128)(2,1)S(1)}, bf16[2,64,896]{2,1,0:T(8,128)(2,1)S(1)}, u32[]{:S(2)}, u32[]{:S(2)}) %collective-permute-start.18) | collective-permute-done | bytes 229408 | tf_op jit(solution)/shard_map/ppermute | solution.py:134
  98.0 7.1 %collective-permute-done.13 = bf16[64,896]{1,0:T(8,128)(2,1)S(1)} collective-permute-done((bf16[64,896]{1,0:T(8,128)(2,1)S(1)}, bf16[64,896]{1,0:T(8,128)(2,1)S(1)}, u32[]{:S(2)}, u32[]{:S(2)}) %collective-permute-start.13) | collective-permute-done | bytes 114720 | tf_op jit(solution)/shard_map/ppermute | solution.py:134
  105.1 2.0 %collective-permute-done.16 = bf16[64,896]{1,0:T(8,128)(2,1)S(1)} collective-permute-done((bf16[64,896]{1,0:T(8,128)(2,1)S(1)}, bf16[64,896]{1,0:T(8,128)(2,1)S(1)}, u32[]{:S(2)}, u32[]{:S(2)}) %collective-permute-start.16) | collective-permute-done | bytes 114720 | tf_op jit(solution)/shard_map/ppermute | solution.py:134
  (58 shorter events, 12.2 us)
Async XLA Ops:
  0.0 37.2 %collective-permute-start.3 = (bf16[1024,3584]{1,0:T(8,128)(2,1)}, bf16[1024,3584]{1,0:T(8,128)(2,1)}, u32[]{:S(2)}, u32[]{:S(2)}) collective-permute-start(bf16[1024,3584]{1,0:T(8,128)(2,1)} %bitcast.35), channel_id=1, source_target_pairs={{0,1},{1,0},{2,3},{3,2},{4,5},{5,4},{6,7},{7,6},{8,9},{9,8},{10,11... | collective-permute-start | bytes 22020104 | tf_op jit(solution)/shard_map/ppermute | solution.py:134
  2.1 1.2 %copy-start.1 = (bf16[64,8,1024]{2,1,0:T(8,128)(2,1)S(1)}, bf16[64,8,1024]{2,1,0:T(8,128)(2,1)}, u32[]{:S(2)}) copy-start(bf16[64,8,1024]{2,1,0:T(8,128)(2,1)} %param.4) | copy-start | bytes 3145732
  6.4 26.4 %collective-permute-start.4 = (bf16[2,64,1024]{2,1,0:T(8,128)(2,1)S(1)}, bf16[2,64,1024]{2,1,0:T(8,128)(2,1)S(1)}, u32[]{:S(2)}, u32[]{:S(2)}) collective-permute-start(bf16[2,64,1024]{2,1,0:T(8,128)(2,1)S(1)} %get-tuple-element.17), channel_id=1, source_target_pairs={{0,2},{2,0},{4,6},{6,4},{8,10},{10,8},{12,14},{14,12},{1,3},{3,1},... | collective-permute-start | bytes 786440 | tf_op jit(solution)/shard_map/ppermute | solution.py:139
  8.9 23.8 %collective-permute-start.5 = (bf16[2,64,1024]{2,1,0:T(8,128)(2,1)S(1)}, bf16[2,64,1024]{2,1,0:T(8,128)(2,1)S(1)}, u32[]{:S(2)}, u32[]{:S(2)}) collective-permute-start(bf16[2,64,1024]{2,1,0:T(8,128)(2,1)S(1)} %get-tuple-element.18), channel_id=1, source_target_pairs={{0,6},{2,4},{4,2},{6,0},{8,14},{10,12},{12,10},{14,8},{1,7},{3,5},... | collective-permute-start | bytes 786440 | tf_op jit(solution)/shard_map/ppermute | solution.py:139
  10.5 26.7 %collective-permute-start.6 = (bf16[2,64,1024]{2,1,0:T(8,128)(2,1)S(1)}, bf16[2,64,1024]{2,1,0:T(8,128)(2,1)S(1)}, u32[]{:S(2)}, u32[]{:S(2)}) collective-permute-start(bf16[2,64,1024]{2,1,0:T(8,128)(2,1)S(1)} %get-tuple-element.19), channel_id=1, source_target_pairs={{0,10},{2,8},{4,14},{6,12},{8,2},{10,0},{12,6},{14,4},{1,11},{3,9}... | collective-permute-start | bytes 786440 | tf_op jit(solution)/shard_map/ppermute | solution.py:139
  14.0 23.2 %collective-permute-start.7 = (bf16[2,64,1024]{2,1,0:T(8,128)(2,1)S(1)}, bf16[2,64,1024]{2,1,0:T(8,128)(2,1)S(1)}, u32[]{:S(2)}, u32[]{:S(2)}) collective-permute-start(bf16[2,64,1024]{2,1,0:T(8,128)(2,1)S(1)} %get-tuple-element.20), channel_id=1, source_target_pairs={{0,14},{2,12},{4,10},{6,8},{8,6},{10,4},{12,2},{14,0},{1,15},{3,13... | collective-permute-start | bytes 786440 | tf_op jit(solution)/shard_map/ppermute | solution.py:139
  32.8 21.6 %collective-permute-start = (bf16[2,64,1024]{2,1,0:T(8,128)(2,1)S(1)}, bf16[2,64,1024]{2,1,0:T(8,128)(2,1)S(1)}, u32[]{:S(2)}, u32[]{:S(2)}) collective-permute-start(bf16[2,64,1024]{2,1,0:T(8,128)(2,1)S(1)} %get-tuple-element.14), channel_id=1, source_target_pairs={{0,4},{2,6},{4,0},{6,2},{8,12},{10,14},{12,8},{14,10},{1,5},{3,7},... | collective-permute-start | bytes 786440 | tf_op jit(solution)/shard_map/ppermute | solution.py:139
  32.8 23.4 %collective-permute-start.1 = (bf16[2,64,1024]{2,1,0:T(8,128)(2,1)S(1)}, bf16[2,64,1024]{2,1,0:T(8,128)(2,1)S(1)}, u32[]{:S(2)}, u32[]{:S(2)}) collective-permute-start(bf16[2,64,1024]{2,1,0:T(8,128)(2,1)S(1)} %get-tuple-element.15), channel_id=1, source_target_pairs={{0,8},{2,10},{4,12},{6,14},{8,0},{10,2},{12,4},{14,6},{1,9},{3,11}... | collective-permute-start | bytes 786440 | tf_op jit(solution)/shard_map/ppermute | solution.py:139
  37.2 19.9 %collective-permute-start.2 = (bf16[2,64,1024]{2,1,0:T(8,128)(2,1)S(1)}, bf16[2,64,1024]{2,1,0:T(8,128)(2,1)S(1)}, u32[]{:S(2)}, u32[]{:S(2)}) collective-permute-start(bf16[2,64,1024]{2,1,0:T(8,128)(2,1)S(1)} %get-tuple-element.16), channel_id=1, source_target_pairs={{0,12},{2,14},{4,8},{6,10},{8,4},{10,6},{12,0},{14,2},{1,13},{3,15... | collective-permute-start | bytes 786440 | tf_op jit(solution)/shard_map/ppermute | solution.py:139
  37.2 3.1 %copy-start = (bf16[1,1024,3584]{2,1,0:T(8,128)(2,1)S(1)}, bf16[1,1024,3584]{2,1,0:T(8,128)(2,1)}, u32[]{:S(2)}) copy-start(bf16[1,1024,3584]{2,1,0:T(8,128)(2,1)} %param.7) | copy-start | bytes 22020100
  43.2 25.5 %collective-permute-start.8 = (bf16[4,64,896]{2,1,0:T(8,128)(2,1)S(1)}, bf16[4,64,896]{2,1,0:T(8,128)(2,1)S(1)}, u32[]{:S(2)}, u32[]{:S(2)}) collective-permute-start(bf16[4,64,896]{2,1,0:T(8,128)(2,1)S(1)} %mix.9), channel_id=1, source_target_pairs={{0,2},{2,0},{1,3},{3,1},{4,6},{6,4},{5,7},{7,5},{8,10},{10,8},{9,1... | collective-permute-start | bytes 1376264 | tf_op jit(solution)/shard_map/ppermute | solution.py:134
  47.9 24.6 %collective-permute-start.11 = (bf16[4,64,896]{2,1,0:T(8,128)(2,1)S(1)}, bf16[4,64,896]{2,1,0:T(8,128)(2,1)S(1)}, u32[]{:S(2)}, u32[]{:S(2)}) collective-permute-start(bf16[4,64,896]{2,1,0:T(8,128)(2,1)S(1)} %mix.11), channel_id=1, source_target_pairs={{0,2},{2,0},{1,3},{3,1},{4,6},{6,4},{5,7},{7,5},{8,10},{10,8},{9,1... | collective-permute-start | bytes 1376264 | tf_op jit(solution)/shard_map/ppermute | solution.py:134
  48.3 8.8 %slice-start = ((s8[7340032]{0:T(1024)(128)(4,1)}), s8[4194304]{0:T(1024)(128)(4,1)S(1)}, s32[]{:S(2)}) async-start(s8[7340032]{0:T(1024)(128)(4,1)} %bitcast.40), calls=%async_computation | async-start | bytes 8388608
  51.3 5.8 %slice-start.1 = ((s8[7340032]{0:T(1024)(128)(4,1)}), s8[3145728]{0:T(1024)(128)(4,1)S(1)}, s32[]{:S(2)}) async-start(s8[7340032]{0:T(1024)(128)(4,1)} %bitcast.40), calls=%async_computation.1 | async-start | bytes 6291456
  54.4 22.0 %collective-permute-start.14 = (bf16[4,64,896]{2,1,0:T(8,128)(2,1)S(1)}, bf16[4,64,896]{2,1,0:T(8,128)(2,1)S(1)}, u32[]{:S(2)}, u32[]{:S(2)}) collective-permute-start(bf16[4,64,896]{2,1,0:T(8,128)(2,1)S(1)} %mix.13), channel_id=1, source_target_pairs={{0,2},{2,0},{1,3},{3,1},{4,6},{6,4},{5,7},{7,5},{8,10},{10,8},{9,1... | collective-permute-start | bytes 1376264 | tf_op jit(solution)/shard_map/ppermute | solution.py:134
  56.2 28.2 %collective-permute-start.17 = (bf16[4,64,896]{2,1,0:T(8,128)(2,1)S(1)}, bf16[4,64,896]{2,1,0:T(8,128)(2,1)S(1)}, u32[]{:S(2)}, u32[]{:S(2)}) collective-permute-start(bf16[4,64,896]{2,1,0:T(8,128)(2,1)S(1)} %mix.15), channel_id=1, source_target_pairs={{0,2},{2,0},{1,3},{3,1},{4,6},{6,4},{5,7},{7,5},{8,10},{10,8},{9,1... | collective-permute-start | bytes 1376264 | tf_op jit(solution)/shard_map/ppermute | solution.py:134
  68.9 16.3 %collective-permute-start.9 = (bf16[2,64,896]{2,1,0:T(8,128)(2,1)S(1)}, bf16[2,64,896]{2,1,0:T(8,128)(2,1)S(1)}, u32[]{:S(2)}, u32[]{:S(2)}) collective-permute-start(bf16[2,64,896]{2,1,0:T(8,128)(2,1)S(1)} %slice.57), channel_id=1, source_target_pairs={{0,4},{4,0},{8,12},{12,8},{1,5},{5,1},{9,13},{13,9},{2,6},{6,2},{1... | collective-permute-start | bytes 688136 | tf_op jit(solution)/shard_map/ppermute | solution.py:134
  72.6 16.2 %collective-permute-start.12 = (bf16[2,64,896]{2,1,0:T(8,128)(2,1)S(1)}, bf16[2,64,896]{2,1,0:T(8,128)(2,1)S(1)}, u32[]{:S(2)}, u32[]{:S(2)}) collective-permute-start(bf16[2,64,896]{2,1,0:T(8,128)(2,1)S(1)} %slice.61), channel_id=1, source_target_pairs={{0,4},{4,0},{8,12},{12,8},{1,5},{5,1},{9,13},{13,9},{2,6},{6,2},{1... | collective-permute-start | bytes 688136 | tf_op jit(solution)/shard_map/ppermute | solution.py:134
  76.6 13.0 %collective-permute-start.15 = (bf16[2,64,896]{2,1,0:T(8,128)(2,1)S(1)}, bf16[2,64,896]{2,1,0:T(8,128)(2,1)S(1)}, u32[]{:S(2)}, u32[]{:S(2)}) collective-permute-start(bf16[2,64,896]{2,1,0:T(8,128)(2,1)S(1)} %slice.65), channel_id=1, source_target_pairs={{0,4},{4,0},{8,12},{12,8},{1,5},{5,1},{9,13},{13,9},{2,6},{6,2},{1... | collective-permute-start | bytes 688136 | tf_op jit(solution)/shard_map/ppermute | solution.py:134
  84.5 12.7 %collective-permute-start.18 = (bf16[2,64,896]{2,1,0:T(8,128)(2,1)S(1)}, bf16[2,64,896]{2,1,0:T(8,128)(2,1)S(1)}, u32[]{:S(2)}, u32[]{:S(2)}) collective-permute-start(bf16[2,64,896]{2,1,0:T(8,128)(2,1)S(1)} %slice.69), channel_id=1, source_target_pairs={{0,4},{4,0},{8,12},{12,8},{1,5},{5,1},{9,13},{13,9},{2,6},{6,2},{1... | collective-permute-start | bytes 688136 | tf_op jit(solution)/shard_map/ppermute | solution.py:134
  85.3 12.7 %collective-permute-start.10 = (bf16[64,896]{1,0:T(8,128)(2,1)S(1)}, bf16[64,896]{1,0:T(8,128)(2,1)S(1)}, u32[]{:S(2)}, u32[]{:S(2)}) collective-permute-start(bf16[64,896]{1,0:T(8,128)(2,1)S(1)} %fusion.8), channel_id=1, source_target_pairs={{0,8},{4,12},{8,0},{12,4},{1,9},{5,13},{9,1},{13,5},{2,10},{6,14},... | collective-permute-start | bytes 344072 | tf_op jit(solution)/shard_map/ppermute | solution.py:134
  88.9 16.2 %collective-permute-start.13 = (bf16[64,896]{1,0:T(8,128)(2,1)S(1)}, bf16[64,896]{1,0:T(8,128)(2,1)S(1)}, u32[]{:S(2)}, u32[]{:S(2)}) collective-permute-start(bf16[64,896]{1,0:T(8,128)(2,1)S(1)} %fusion.9), channel_id=1, source_target_pairs={{0,8},{4,12},{8,0},{12,4},{1,9},{5,13},{9,1},{13,5},{2,10},{6,14},... | collective-permute-start | bytes 344072 | tf_op jit(solution)/shard_map/ppermute | solution.py:134
  89.6 17.5 %collective-permute-start.16 = (bf16[64,896]{1,0:T(8,128)(2,1)S(1)}, bf16[64,896]{1,0:T(8,128)(2,1)S(1)}, u32[]{:S(2)}, u32[]{:S(2)}) collective-permute-start(bf16[64,896]{1,0:T(8,128)(2,1)S(1)} %fusion.10), channel_id=1, source_target_pairs={{0,8},{4,12},{8,0},{12,4},{1,9},{5,13},{9,1},{13,5},{2,10},{6,14},... | collective-permute-start | bytes 344072 | tf_op jit(solution)/shard_map/ppermute | solution.py:134
  97.3 11.1 %collective-permute-start.19 = (bf16[64,896]{1,0:T(8,128)(2,1)S(1)}, bf16[64,896]{1,0:T(8,128)(2,1)S(1)}, u32[]{:S(2)}, u32[]{:S(2)}) collective-permute-start(bf16[64,896]{1,0:T(8,128)(2,1)S(1)} %fusion.11), channel_id=1, source_target_pairs={{0,8},{4,12},{8,0},{12,4},{1,9},{5,13},{9,1},{13,5},{2,10},{6,14},... | collective-permute-start | bytes 344072 | tf_op jit(solution)/shard_map/ppermute | solution.py:134

commit v3 on v2

--- a/solution.py
+++ b/solution.py
@@ -1,3 +1,5 @@
+import functools
+
 import jax
 import jax.numpy as jnp
 from jax import lax
@@ -7,7 +9,6 @@
 
 CHIPS = 8
 CHUNKS = 4
-TILE = 896
 
 
 def passed_along(block, axis, distance):
@@ -61,69 +62,82 @@
     return combined.astype(jnp.bfloat16)
 
 
-def spread_kernel(own_ref, flat_ids_ref, ids_ref, gates_ref, hidden_ref, *out_refs):
-    token_count, choose_count = ids_ref.shape
+def spread_kernel(relatives, own_ref, ids_ref, gates_ref, hidden_ref, *refs):
+    out_refs = refs[-len(relatives) :]
     own = own_ref[0]
+    choose_count, token_count = ids_ref.shape
     shape = (token_count, token_count * choose_count)
     row = lax.broadcasted_iota(jnp.int32, shape, 0) * choose_count
     column = lax.broadcasted_iota(jnp.int32, shape, 1)
     same = (column >= row) & (column < row + choose_count)
-    own_row = jnp.where(same, flat_ids_ref[...], -1)
-    for relative, out_ref in enumerate(out_refs):
-        for core in range(2):
-            expert = own ^ (2 * relative + core)
-            pick = (own_row == expert).astype(jnp.float32).astype(hidden_ref.dtype)
-            gate = jnp.sum(
-                jnp.where(ids_ref[...] == expert, gates_ref[...], 0.0), axis=1, keepdims=True
-            )
-            rows = jnp.dot(pick, hidden_ref[...], preferred_element_type=jnp.float32)
-            out_ref[core] = (rows * gate).astype(out_ref.dtype)
-
-
-def spread_rows(hidden, expert_ids, gate_weights, own):
+    across = (choose_count, token_count * choose_count)
+    choice = lax.rem(lax.broadcasted_iota(jnp.int32, across, 1), choose_count)
+    repeat = (choice == lax.broadcasted_iota(jnp.int32, across, 0)).astype(jnp.float32)
+    ids, gate_weights = ids_ref[...].T, gates_ref[...].T
+    spread_ids = jnp.dot(ids.astype(jnp.float32), repeat, preferred_element_type=jnp.float32)
+    own_row = jnp.where(same, (spread_ids + 0.5).astype(jnp.int32), -1)
+    for at in range(0, len(relatives), 2):
+        picks, gates = [], []
+        for relative in relatives[at : at + 2]:
+            for core in range(2):
+                expert = own ^ (2 * relative + core)
+                picks.append((own_row == expert).astype(jnp.float32).astype(hidden_ref.dtype))
+                gates.append(
+                    jnp.sum(jnp.where(ids == expert, gate_weights, 0.0), axis=1, keepdims=True)
+                )
+        rows = jnp.dot(
+            jnp.concatenate(picks, axis=0), hidden_ref[...], preferred_element_type=jnp.float32
+        )
+        scaled = (rows * jnp.concatenate(gates, axis=0)).astype(hidden_ref.dtype)
+        for place in range(len(picks) // 2):
+            block = scaled[2 * place * token_count : 2 * (place + 1) * token_count]
+            out_refs[at + place][...] = block.reshape(2, token_count, -1)
+
+
+def spread_rows(hidden, expert_ids, gate_weights, own, relatives, held=None):
     token_count, choose_count, width = hidden.shape
     vmem = pl.BlockSpec(memory_space=pltpu.VMEM)
     block = jax.ShapeDtypeStruct((2, token_count, width), hidden.dtype)
+    more = [] if held is None else [held]
     return pl.pallas_call(
-        spread_kernel,
-        in_specs=[pl.BlockSpec(memory_space=pltpu.SMEM)] + [vmem] * 4,
-        out_specs=[vmem] * CHIPS,
-        out_shape=[block] * CHIPS,
-        compiler_params=pltpu.CompilerParams(vmem_limit_bytes=32 << 20),
+        functools.partial(spread_kernel, relatives),
+        in_specs=[pl.BlockSpec(memory_space=pltpu.SMEM)] + [vmem] * (3 + len(more)),
+        out_specs=[vmem] * len(relatives),
+        out_shape=[block] * len(relatives),
+        compiler_params=pltpu.CompilerParams(vmem_limit_bytes=24 << 20),
         name="spread_rows",
     )(
         own.reshape(1),
-        expert_ids.reshape(1, token_count * choose_count),
-        expert_ids,
-        gate_weights,
+        expert_ids.T,
+        gate_weights.T,
         hidden.reshape(token_count * choose_count, width),
-    )
-
-
-def mix_kernel(*refs):
+        *more,
+    )
+
+
+def mix_kernel(start, *refs):
     rows, (near_ref, far_ref, out_ref) = refs[:-3], refs[-3:]
-    tokens = rows[0].shape[1]
+    tokens, width = rows[0].shape[1], out_ref.shape[2]
+    columns = pl.ds(start, width)
     near = jnp.concatenate([ref[0] for ref in rows], axis=0)
     far = jnp.concatenate([ref[1] for ref in rows], axis=0)
-    total = jnp.dot(near, near_ref[...], preferred_element_type=jnp.float32)
-    total += jnp.dot(far, far_ref[...], preferred_element_type=jnp.float32)
+    total = jnp.dot(near, near_ref[:, columns], preferred_element_type=jnp.float32)
+    total += jnp.dot(far, far_ref[:, columns], preferred_element_type=jnp.float32)
     out_ref[...] = total.reshape(len(rows), tokens, -1).astype(out_ref.dtype)
 
 
-def mix(rows, near, far, start, width, tile):
+def mix(rows, near, far, start, width):
     _, tokens, depth = rows[0].shape
-    whole = pl.BlockSpec((2, tokens, depth), lambda i: (0, 0, 0))
-    weight = pl.BlockSpec((depth, tile), lambda i: (0, start // tile + i))
+    vmem = pl.BlockSpec(memory_space=pltpu.VMEM)
     return pl.pallas_call(
-        mix_kernel,
-        grid=(width // tile,),
-        in_specs=[whole] * len(rows) + [weight] * 2,
-        out_specs=pl.BlockSpec((len(rows), tokens, tile), lambda i: (0, 0, i)),
+        functools.partial(mix_kernel, start),
+        in_specs=[vmem] * (len(rows) + 2),
+        out_specs=vmem,
         out_shape=jax.ShapeDtypeStruct((len(rows), tokens, width), jnp.bfloat16),
-        compiler_params=pltpu.CompilerParams(vmem_limit_bytes=32 << 20),
+        compiler_params=pltpu.CompilerParams(vmem_limit_bytes=24 << 20),
         cost_estimate=pl.CostEstimate(
             flops=4 * len(rows) * tokens * depth * width,
-            bytes_accessed=4 * depth * width + 2 * len(rows) * tokens * (2 * depth + width),
+            bytes_accessed=2 * len(rows) * tokens * (2 * depth + width),
             transcendentals=0,
         ),
         name="mix",
@@ -146,13 +160,19 @@
     own = (lax.axis_index("z") * 2 + lax.axis_index("x")) * 2 + lax.axis_index("core")
     near = down_weight[0]
     far = swap(near, "core", 1)
-    outgoing = spread_rows(hidden, expert_ids, gate_weights, own)
-    arrived = [outgoing[0]] + [send_to_chip(outgoing[r], r) for r in range(1, CHIPS)]
+    odd, even = (7, 5, 3, 1), (6, 4, 2, 0)
+    arrived = [None] * CHIPS
+    blocks = spread_rows(hidden, expert_ids, gate_weights, own, odd)
+    for relative, block in zip(odd, blocks):
+        arrived[relative] = send_to_chip(block, relative)
+    blocks = spread_rows(hidden, expert_ids, gate_weights, own, even, near)
+    for relative, block in zip(even, blocks):
+        arrived[relative] = send_to_chip(block, relative) if relative else block
     chunk = width_total // CHUNKS
     results = []
     for start in range(0, width_total, chunk):
-        given = mix(arrived[1::2], near, far, start, chunk, TILE)
-        kept = mix(arrived[0::2], near, far, start, chunk, TILE)
+        given = mix(arrived[1::2], near, far, start, chunk)
+        kept = mix(arrived[0::2], near, far, start, chunk)
         taken = swap(given, "x", 1)
         line = kept.astype(jnp.float32) + taken.astype(jnp.float32)
         pair = line[0::2] + swap(line[1::2].astype(jnp.bfloat16), "z", 1).astype(jnp.float32)

time: 110 us -> 113 us (1.027)
  Pallas kernels: 26.5 us -> 36.5 us
  waiting for transfers between devices: 45.5 us -> 38.4 us
    pallas_call x9 -> x10, Pallas kernels: 26.5 us -> 36.5 us  [the longest x8 34.7 us: mix(): pl.pallas_call(functools.partial(mix_kernel, start), in_specs=[vmem] * (l...]
    ppermute x7, waiting for transfers between devices: 18.8 us -> 14.8 us  [send_to_chip(): lax.ppermute(block, ('z', 'x'), [(i, i ^ relative) for i in range(sizes[0...]
    ppermute x13, waiting for transfers between devices: 26.7 us -> 23.6 us  [swap(): lax.ppermute(block, axis, [(i, i ^ distance) for i in range(lax.axis_size...]
  transfers between devices with their start and end apart: 20 -> 20, of which waited for: 8 -> 9; matrix products, arithmetic and copies ran while one was open for 2% -> 1% of each run, Pallas kernels for 24% -> 33%
where the time goes in v3:
time: 113 us; the launch traced here: 112 us
  waiting for transfers between devices  38.4 us (34%)
  Pallas kernels  36.5 us (32%)
  starting transfers between devices  29.5 us (26%)
  local copies, waits for them, and re-layouts  5.83 us (5%)
  other arithmetic  1.66 us (1%)
    pallas_call x8, Pallas kernels, mix(): pl.pallas_call(functools.partial(mix_kernel, start), in_specs=[vmem] * (l...  34.7 us
    ppermute x13, waiting for transfers between devices, swap(): lax.ppermute(block, axis, [(i, i ^ distance) for i in range(lax.axis_size...  23.6 us
    ppermute x13, starting transfers between devices, swap(): lax.ppermute(block, axis, [(i, i ^ distance) for i in range(lax.axis_size...  17.4 us
    ppermute x7, waiting for transfers between devices, send_to_chip(): lax.ppermute(block, ('z', 'x'), [(i, i ^ relative) for i in range(sizes[0...  14.8 us
    ppermute x7, starting transfers between devices, send_to_chip(): lax.ppermute(block, ('z', 'x'), [(i, i ^ relative) for i in range(sizes[0...  12 us
    unnamed x10, local copies, waits for them, and re-layouts  5.68 us
  transfers between devices with their start and end apart: 20, of which 9 were waited for; matrix products, arithmetic and copies ran while one was open for 1% of the time, Pallas kernels for 33%

profile of v3, /device:TPU:0, one launch (start us, length us, event | category | flops | bytes accessed | tf_op | source)
XLA Modules:
  0.0 112.1 jit_solution(13723374500216862194)
XLA Ops:
  4.0 2.5 %collective-permute-start.4 = (bf16[2,64,1024]{2,1,0:T(8,128)(2,1)S(1)}, bf16[2,64,1024]{2,1,0:T(8,128)(2,1)S(1)}, u32[]{:S(2)}, u32[]{:S(2)}) collective-permute-start(bf16[2,64,1024]{2,1,0:T(8,128)(2,1)S(1)} %get-tuple-element.17), channel_id=1, source_target_pairs={{0,2},{2,0},{4,6},{6,4},{8,10},{10,8},{12,14},{14,12},{1,3},{3,1},... | collective-permute-start | bytes 786440 | tf_op jit(solution)/shard_map/ppermute | solution.py:153
  8.1 3.5 %collective-permute-start.6 = (bf16[2,64,1024]{2,1,0:T(8,128)(2,1)S(1)}, bf16[2,64,1024]{2,1,0:T(8,128)(2,1)S(1)}, u32[]{:S(2)}, u32[]{:S(2)}) collective-permute-start(bf16[2,64,1024]{2,1,0:T(8,128)(2,1)S(1)} %get-tuple-element.19), channel_id=1, source_target_pairs={{0,10},{2,8},{4,14},{6,12},{8,2},{10,0},{12,6},{14,4},{1,11},{3,9}... | collective-permute-start | bytes 786440 | tf_op jit(solution)/shard_map/ppermute | solution.py:153
  11.6 3.1 %copy-done = bf16[1,1024,3584]{2,1,0:T(8,128)(2,1)S(1)} copy-done((bf16[1,1024,3584]{2,1,0:T(8,128)(2,1)S(1)}, bf16[1,1024,3584]{2,1,0:T(8,128)(2,1)}, u32[]{:S(2)}) %copy-start) | copy-done | bytes 7340056
  15.6 14.8 %collective-permute-done.4.refs_0_ = bf16[2,64,1024]{2,1,0:T(8,128)(2,1)S(1)} collective-permute-done((bf16[2,64,1024]{2,1,0:T(8,128)(2,1)S(1)}, bf16[2,64,1024]{2,1,0:T(8,128)(2,1)S(1)}, u32[]{:S(2)}, u32[]{:S(2)}) %collective-permute-start.4) | collective-permute-done | bytes 262176 | tf_op jit(solution)/shard_map/ppermute | solution.py:153
  30.3 4.4 %collective-permute-start.1 = (bf16[2,64,1024]{2,1,0:T(8,128)(2,1)S(1)}, bf16[2,64,1024]{2,1,0:T(8,128)(2,1)S(1)}, u32[]{:S(2)}, u32[]{:S(2)}) collective-permute-start(bf16[2,64,1024]{2,1,0:T(8,128)(2,1)S(1)} %get-tuple-element.15), channel_id=1, source_target_pairs={{0,8},{2,10},{4,12},{6,14},{8,0},{10,2},{12,4},{14,6},{1,9},{3,11}... | collective-permute-start | bytes 786440 | tf_op jit(solution)/shard_map/ppermute | solution.py:153
  34.8 4.3 %mix.9 = bf16[4,64,896]{2,1,0:T(8,128)(2,1)S(1)} custom-call(bf16[2,64,1024]{2,1,0:T(8,128)(2,1)S(1)} %collective-permute-done.4.refs_0_, bf16[2,64,1024]{2,1,0:T(8,128)(2,1)S(1)} %collective-permute-done.5.refs_1_, bf16[2,64,1024]{2,1,0:T(8,128)(2,1)S(1)} %collective-permute-done.6.refs_2_, bf16[2,64,1024]{2,1,0:T(8,128)(2,1)S(1)} %collective-permute-done.7.refs_3_, ...), custom_call_target="tpu_custom_call" | custom-call | flops 939524096 | bytes 1507328 | tf_op jit(solution)/shard_map/mix/pallas_call | solution.py:132
  40.9 4.3 %mix.11 = bf16[4,64,896]{2,1,0:T(8,128)(2,1)S(1)} custom-call(bf16[2,64,1024]{2,1,0:T(8,128)(2,1)S(1)} %collective-permute-done.4.refs_0_, bf16[2,64,1024]{2,1,0:T(8,128)(2,1)S(1)} %collective-permute-done.5.refs_1_, bf16[2,64,1024]{2,1,0:T(8,128)(2,1)S(1)} %collective-permute-done.6.refs_2_, bf16[2,64,1024]{2,1,0:T(8,128)(2,1)S(1)} %collective-permute-done.7.refs_3_, ...), custom_call_target="tpu_custom_call" | custom-call | flops 939524096 | bytes 1507328 | tf_op jit(solution)/shard_map/mix/pallas_call | solution.py:132
  45.6 4.3 %mix.13 = bf16[4,64,896]{2,1,0:T(8,128)(2,1)S(1)} custom-call(bf16[2,64,1024]{2,1,0:T(8,128)(2,1)S(1)} %collective-permute-done.4.refs_0_, bf16[2,64,1024]{2,1,0:T(8,128)(2,1)S(1)} %collective-permute-done.5.refs_1_, bf16[2,64,1024]{2,1,0:T(8,128)(2,1)S(1)} %collective-permute-done.6.refs_2_, bf16[2,64,1024]{2,1,0:T(8,128)(2,1)S(1)} %collective-permute-done.7.refs_3_, ...), custom_call_target="tpu_custom_call" | custom-call | flops 939524096 | bytes 1507328 | tf_op jit(solution)/shard_map/mix/pallas_call | solution.py:132
  50.0 4.3 %mix.15 = bf16[4,64,896]{2,1,0:T(8,128)(2,1)S(1)} custom-call(bf16[2,64,1024]{2,1,0:T(8,128)(2,1)S(1)} %collective-permute-done.4.refs_0_, bf16[2,64,1024]{2,1,0:T(8,128)(2,1)S(1)} %collective-permute-done.5.refs_1_, bf16[2,64,1024]{2,1,0:T(8,128)(2,1)S(1)} %collective-permute-done.6.refs_2_, bf16[2,64,1024]{2,1,0:T(8,128)(2,1)S(1)} %collective-permute-done.7.refs_3_, ...), custom_call_target="tpu_custom_call" | custom-call | flops 939524096 | bytes 1507328 | tf_op jit(solution)/shard_map/mix/pallas_call | solution.py:132
  56.4 4.3 %mix.8 = bf16[4,64,896]{2,1,0:T(8,128)(2,1)S(1)} custom-call(bf16[2,64,1024]{2,1,0:T(8,128)(2,1)S(1)} %get-tuple-element.13.refs_0_, bf16[2,64,1024]{2,1,0:T(8,128)(2,1)S(1)} %collective-permute-done.refs_1_, bf16[2,64,1024]{2,1,0:T(8,128)(2,1)S(1)} %collective-permute-done.1.refs_2_, bf16[2,64,1024]{2,1,0:T(8,128)(2,1)S(1)} %collective-permute-done.2.refs_3_, ...), custom_call_target="tpu_custom_call" | custom-call | flops 939524096 | bytes 1507328 | tf_op jit(solution)/shard_map/mix/pallas_call | solution.py:132
  60.8 4.3 %mix.10 = bf16[4,64,896]{2,1,0:T(8,128)(2,1)S(1)} custom-call(bf16[2,64,1024]{2,1,0:T(8,128)(2,1)S(1)} %get-tuple-element.13.refs_0_, bf16[2,64,1024]{2,1,0:T(8,128)(2,1)S(1)} %collective-permute-done.refs_1_, bf16[2,64,1024]{2,1,0:T(8,128)(2,1)S(1)} %collective-permute-done.1.refs_2_, bf16[2,64,1024]{2,1,0:T(8,128)(2,1)S(1)} %collective-permute-done.2.refs_3_, ...), custom_call_target="tpu_custom_call" | custom-call | flops 939524096 | bytes 1507328 | tf_op jit(solution)/shard_map/mix/pallas_call | solution.py:132
  65.1 4.3 %mix.12 = bf16[4,64,896]{2,1,0:T(8,128)(2,1)S(1)} custom-call(bf16[2,64,1024]{2,1,0:T(8,128)(2,1)S(1)} %get-tuple-element.13.refs_0_, bf16[2,64,1024]{2,1,0:T(8,128)(2,1)S(1)} %collective-permute-done.refs_1_, bf16[2,64,1024]{2,1,0:T(8,128)(2,1)S(1)} %collective-permute-done.1.refs_2_, bf16[2,64,1024]{2,1,0:T(8,128)(2,1)S(1)} %collective-permute-done.2.refs_3_, ...), custom_call_target="tpu_custom_call" | custom-call | flops 939524096 | bytes 1507328 | tf_op jit(solution)/shard_map/mix/pallas_call | solution.py:132
  69.4 4.3 %mix.14 = bf16[4,64,896]{2,1,0:T(8,128)(2,1)S(1)} custom-call(bf16[2,64,1024]{2,1,0:T(8,128)(2,1)S(1)} %get-tuple-element.13.refs_0_, bf16[2,64,1024]{2,1,0:T(8,128)(2,1)S(1)} %collective-permute-done.refs_1_, bf16[2,64,1024]{2,1,0:T(8,128)(2,1)S(1)} %collective-permute-done.1.refs_2_, bf16[2,64,1024]{2,1,0:T(8,128)(2,1)S(1)} %collective-permute-done.2.refs_3_, ...), custom_call_target="tpu_custom_call" | custom-call | flops 939524096 | bytes 1507328 | tf_op jit(solution)/shard_map/mix/pallas_call | solution.py:132
  74.0 1.8 %collective-permute-start.9 = (bf16[2,64,896]{2,1,0:T(8,128)(2,1)S(1)}, bf16[2,64,896]{2,1,0:T(8,128)(2,1)S(1)}, u32[]{:S(2)}, u32[]{:S(2)}) collective-permute-start(bf16[2,64,896]{2,1,0:T(8,128)(2,1)S(1)} %slice.57), channel_id=1, source_target_pairs={{0,4},{4,0},{8,12},{12,8},{1,5},{5,1},{9,13},{13,9},{2,6},{6,2},{1... | collective-permute-start | bytes 688136 | tf_op jit(solution)/shard_map/ppermute | solution.py:148
  76.5 1.8 %collective-permute-start.15 = (bf16[2,64,896]{2,1,0:T(8,128)(2,1)S(1)}, bf16[2,64,896]{2,1,0:T(8,128)(2,1)S(1)}, u32[]{:S(2)}, u32[]{:S(2)}) collective-permute-start(bf16[2,64,896]{2,1,0:T(8,128)(2,1)S(1)} %slice.65), channel_id=1, source_target_pairs={{0,4},{4,0},{8,12},{12,8},{1,5},{5,1},{9,13},{13,9},{2,6},{6,2},{1... | collective-permute-start | bytes 688136 | tf_op jit(solution)/shard_map/ppermute | solution.py:148
  78.3 2.0 %collective-permute-done.17 = bf16[4,64,896]{2,1,0:T(8,128)(2,1)S(1)} collective-permute-done((bf16[4,64,896]{2,1,0:T(8,128)(2,1)S(1)}, bf16[4,64,896]{2,1,0:T(8,128)(2,1)S(1)}, u32[]{:S(2)}, u32[]{:S(2)}) %collective-permute-start.17) | collective-permute-done | bytes 458784 | tf_op jit(solution)/shard_map/ppermute | solution.py:148
  82.7 3.1 %collective-permute-start.10 = (bf16[64,896]{1,0:T(8,128)(2,1)S(1)}, bf16[64,896]{1,0:T(8,128)(2,1)S(1)}, u32[]{:S(2)}, u32[]{:S(2)}) collective-permute-start(bf16[64,896]{1,0:T(8,128)(2,1)S(1)} %fusion.8), channel_id=1, source_target_pairs={{0,8},{4,12},{8,0},{12,4},{1,9},{5,13},{9,1},{13,5},{2,10},{6,14},... | collective-permute-start | bytes 344072 | tf_op jit(solution)/shard_map/ppermute | solution.py:148
  85.7 5.5 %collective-permute-done.12 = bf16[2,64,896]{2,1,0:T(8,128)(2,1)S(1)} collective-permute-done((bf16[2,64,896]{2,1,0:T(8,128)(2,1)S(1)}, bf16[2,64,896]{2,1,0:T(8,128)(2,1)S(1)}, u32[]{:S(2)}, u32[]{:S(2)}) %collective-permute-start.12) | collective-permute-done | bytes 229408 | tf_op jit(solution)/shard_map/ppermute | solution.py:148
  91.3 2.0 %collective-permute-start.13 = (bf16[64,896]{1,0:T(8,128)(2,1)S(1)}, bf16[64,896]{1,0:T(8,128)(2,1)S(1)}, u32[]{:S(2)}, u32[]{:S(2)}) collective-permute-start(bf16[64,896]{1,0:T(8,128)(2,1)S(1)} %fusion.9), channel_id=1, source_target_pairs={{0,8},{4,12},{8,0},{12,4},{1,9},{5,13},{9,1},{13,5},{2,10},{6,14},... | collective-permute-start | bytes 344072 | tf_op jit(solution)/shard_map/ppermute | solution.py:148
  93.2 3.5 %collective-permute-done.15 = bf16[2,64,896]{2,1,0:T(8,128)(2,1)S(1)} collective-permute-done((bf16[2,64,896]{2,1,0:T(8,128)(2,1)S(1)}, bf16[2,64,896]{2,1,0:T(8,128)(2,1)S(1)}, u32[]{:S(2)}, u32[]{:S(2)}) %collective-permute-start.15) | collective-permute-done | bytes 229408 | tf_op jit(solution)/shard_map/ppermute | solution.py:148
  96.8 2.3 %collective-permute-start.16 = (bf16[64,896]{1,0:T(8,128)(2,1)S(1)}, bf16[64,896]{1,0:T(8,128)(2,1)S(1)}, u32[]{:S(2)}, u32[]{:S(2)}) collective-permute-start(bf16[64,896]{1,0:T(8,128)(2,1)S(1)} %fusion.10), channel_id=1, source_target_pairs={{0,8},{4,12},{8,0},{12,4},{1,9},{5,13},{9,1},{13,5},{2,10},{6,14},... | collective-permute-start | bytes 344072 | tf_op jit(solution)/shard_map/ppermute | solution.py:148
  99.1 1.8 %collective-permute-done.18 = bf16[2,64,896]{2,1,0:T(8,128)(2,1)S(1)} collective-permute-done((bf16[2,64,896]{2,1,0:T(8,128)(2,1)S(1)}, bf16[2,64,896]{2,1,0:T(8,128)(2,1)S(1)}, u32[]{:S(2)}, u32[]{:S(2)}) %collective-permute-start.18) | collective-permute-done | bytes 229408 | tf_op jit(solution)/shard_map/ppermute | solution.py:148
  101.8 6.0 %collective-permute-done.13 = bf16[64,896]{1,0:T(8,128)(2,1)S(1)} collective-permute-done((bf16[64,896]{1,0:T(8,128)(2,1)S(1)}, bf16[64,896]{1,0:T(8,128)(2,1)S(1)}, u32[]{:S(2)}, u32[]{:S(2)}) %collective-permute-start.13) | collective-permute-done | bytes 114720 | tf_op jit(solution)/shard_map/ppermute | solution.py:148
  107.7 2.3 %collective-permute-done.16 = bf16[64,896]{1,0:T(8,128)(2,1)S(1)} collective-permute-done((bf16[64,896]{1,0:T(8,128)(2,1)S(1)}, bf16[64,896]{1,0:T(8,128)(2,1)S(1)}, u32[]{:S(2)}, u32[]{:S(2)}) %collective-permute-start.16) | collective-permute-done | bytes 114720 | tf_op jit(solution)/shard_map/ppermute | solution.py:148
  (57 shorter events, 17.0 us)
Async XLA Ops:
  0.0 34.8 %collective-permute-start.3 = (bf16[1024,3584]{1,0:T(8,128)(2,1)}, bf16[1024,3584]{1,0:T(8,128)(2,1)}, u32[]{:S(2)}, u32[]{:S(2)}) collective-permute-start(bf16[1024,3584]{1,0:T(8,128)(2,1)} %bitcast.37), channel_id=1, source_target_pairs={{0,1},{1,0},{2,3},{3,2},{4,5},{5,4},{6,7},{7,6},{8,9},{9,8},{10,11... | collective-permute-start | bytes 22020104 | tf_op jit(solution)/shard_map/ppermute | solution.py:148
  0.5 1.2 %copy-start.2 = (bf16[64,8,1024]{2,1,0:T(8,128)(2,1)S(1)}, bf16[64,8,1024]{2,1,0:T(8,128)(2,1)}, u32[]{:S(2)}) copy-start(bf16[64,8,1024]{2,1,0:T(8,128)(2,1)} %param.4) | copy-start | bytes 3145732
  1.7 0.7 copy-start.3
  4.0 26.4 %collective-permute-start.4 = (bf16[2,64,1024]{2,1,0:T(8,128)(2,1)S(1)}, bf16[2,64,1024]{2,1,0:T(8,128)(2,1)S(1)}, u32[]{:S(2)}, u32[]{:S(2)}) collective-permute-start(bf16[2,64,1024]{2,1,0:T(8,128)(2,1)S(1)} %get-tuple-element.17), channel_id=1, source_target_pairs={{0,2},{2,0},{4,6},{6,4},{8,10},{10,8},{12,14},{14,12},{1,3},{3,1},... | collective-permute-start | bytes 786440 | tf_op jit(solution)/shard_map/ppermute | solution.py:153
  6.5 23.8 %collective-permute-start.5 = (bf16[2,64,1024]{2,1,0:T(8,128)(2,1)S(1)}, bf16[2,64,1024]{2,1,0:T(8,128)(2,1)S(1)}, u32[]{:S(2)}, u32[]{:S(2)}) collective-permute-start(bf16[2,64,1024]{2,1,0:T(8,128)(2,1)S(1)} %get-tuple-element.18), channel_id=1, source_target_pairs={{0,6},{2,4},{4,2},{6,0},{8,14},{10,12},{12,10},{14,8},{1,7},{3,5},... | collective-permute-start | bytes 786440 | tf_op jit(solution)/shard_map/ppermute | solution.py:153
  8.1 26.7 %collective-permute-start.6 = (bf16[2,64,1024]{2,1,0:T(8,128)(2,1)S(1)}, bf16[2,64,1024]{2,1,0:T(8,128)(2,1)S(1)}, u32[]{:S(2)}, u32[]{:S(2)}) collective-permute-start(bf16[2,64,1024]{2,1,0:T(8,128)(2,1)S(1)} %get-tuple-element.19), channel_id=1, source_target_pairs={{0,10},{2,8},{4,14},{6,12},{8,2},{10,0},{12,6},{14,4},{1,11},{3,9}... | collective-permute-start | bytes 786440 | tf_op jit(solution)/shard_map/ppermute | solution.py:153
  11.6 23.2 %collective-permute-start.7 = (bf16[2,64,1024]{2,1,0:T(8,128)(2,1)S(1)}, bf16[2,64,1024]{2,1,0:T(8,128)(2,1)S(1)}, u32[]{:S(2)}, u32[]{:S(2)}) collective-permute-start(bf16[2,64,1024]{2,1,0:T(8,128)(2,1)S(1)} %get-tuple-element.20), channel_id=1, source_target_pairs={{0,14},{2,12},{4,10},{6,8},{8,6},{10,4},{12,2},{14,0},{1,15},{3,13... | collective-permute-start | bytes 786440 | tf_op jit(solution)/shard_map/ppermute | solution.py:153
  11.6 3.1 %copy-start = (bf16[1,1024,3584]{2,1,0:T(8,128)(2,1)S(1)}, bf16[1,1024,3584]{2,1,0:T(8,128)(2,1)}, u32[]{:S(2)}) copy-start(bf16[1,1024,3584]{2,1,0:T(8,128)(2,1)} %param.7) | copy-start | bytes 22020100
  14.7 20.1 %copy-start.1 = (bf16[1,1024,3584]{2,1,0:T(8,128)(2,1)S(1)}, bf16[1,1024,3584]{2,1,0:T(8,128)(2,1)}, u32[]{:S(2)}) copy-start(bf16[1,1024,3584]{2,1,0:T(8,128)(2,1)} %param.7) | copy-start | bytes 22020100
  30.3 24.0 %collective-permute-start = (bf16[2,64,1024]{2,1,0:T(8,128)(2,1)S(1)}, bf16[2,64,1024]{2,1,0:T(8,128)(2,1)S(1)}, u32[]{:S(2)}, u32[]{:S(2)}) collective-permute-start(bf16[2,64,1024]{2,1,0:T(8,128)(2,1)S(1)} %get-tuple-element.14), channel_id=1, source_target_pairs={{0,4},{2,6},{4,0},{6,2},{8,12},{10,14},{12,8},{14,10},{1,5},{3,7},... | collective-permute-start | bytes 786440 | tf_op jit(solution)/shard_map/ppermute | solution.py:153
  30.3 25.7 %collective-permute-start.1 = (bf16[2,64,1024]{2,1,0:T(8,128)(2,1)S(1)}, bf16[2,64,1024]{2,1,0:T(8,128)(2,1)S(1)}, u32[]{:S(2)}, u32[]{:S(2)}) collective-permute-start(bf16[2,64,1024]{2,1,0:T(8,128)(2,1)S(1)} %get-tuple-element.15), channel_id=1, source_target_pairs={{0,8},{2,10},{4,12},{6,14},{8,0},{10,2},{12,4},{14,6},{1,9},{3,11}... | collective-permute-start | bytes 786440 | tf_op jit(solution)/shard_map/ppermute | solution.py:153
  34.8 21.7 %collective-permute-start.2 = (bf16[2,64,1024]{2,1,0:T(8,128)(2,1)S(1)}, bf16[2,64,1024]{2,1,0:T(8,128)(2,1)S(1)}, u32[]{:S(2)}, u32[]{:S(2)}) collective-permute-start(bf16[2,64,1024]{2,1,0:T(8,128)(2,1)S(1)} %get-tuple-element.16), channel_id=1, source_target_pairs={{0,12},{2,14},{4,8},{6,10},{8,4},{10,6},{12,0},{14,2},{1,13},{3,15... | collective-permute-start | bytes 786440 | tf_op jit(solution)/shard_map/ppermute | solution.py:153
  39.1 34.7 %collective-permute-start.8 = (bf16[4,64,896]{2,1,0:T(8,128)(2,1)S(1)}, bf16[4,64,896]{2,1,0:T(8,128)(2,1)S(1)}, u32[]{:S(2)}, u32[]{:S(2)}) collective-permute-start(bf16[4,64,896]{2,1,0:T(8,128)(2,1)S(1)} %mix.9), channel_id=1, source_target_pairs={{0,2},{2,0},{1,3},{3,1},{4,6},{6,4},{5,7},{7,5},{8,10},{10,8},{9,1... | collective-permute-start | bytes 1376264 | tf_op jit(solution)/shard_map/ppermute | solution.py:148
  45.2 30.5 %collective-permute-start.11 = (bf16[4,64,896]{2,1,0:T(8,128)(2,1)S(1)}, bf16[4,64,896]{2,1,0:T(8,128)(2,1)S(1)}, u32[]{:S(2)}, u32[]{:S(2)}) collective-permute-start(bf16[4,64,896]{2,1,0:T(8,128)(2,1)S(1)} %mix.11), channel_id=1, source_target_pairs={{0,2},{2,0},{1,3},{3,1},{4,6},{6,4},{5,7},{7,5},{8,10},{10,8},{9,1... | collective-permute-start | bytes 1376264 | tf_op jit(solution)/shard_map/ppermute | solution.py:148
  54.3 22.0 %collective-permute-start.14 = (bf16[4,64,896]{2,1,0:T(8,128)(2,1)S(1)}, bf16[4,64,896]{2,1,0:T(8,128)(2,1)S(1)}, u32[]{:S(2)}, u32[]{:S(2)}) collective-permute-start(bf16[4,64,896]{2,1,0:T(8,128)(2,1)S(1)} %mix.13), channel_id=1, source_target_pairs={{0,2},{2,0},{1,3},{3,1},{4,6},{6,4},{5,7},{7,5},{8,10},{10,8},{9,1... | collective-permute-start | bytes 1376264 | tf_op jit(solution)/shard_map/ppermute | solution.py:148
  56.1 24.2 %collective-permute-start.17 = (bf16[4,64,896]{2,1,0:T(8,128)(2,1)S(1)}, bf16[4,64,896]{2,1,0:T(8,128)(2,1)S(1)}, u32[]{:S(2)}, u32[]{:S(2)}) collective-permute-start(bf16[4,64,896]{2,1,0:T(8,128)(2,1)S(1)} %mix.15), channel_id=1, source_target_pairs={{0,2},{2,0},{1,3},{3,1},{4,6},{6,4},{5,7},{7,5},{8,10},{10,8},{9,1... | collective-permute-start | bytes 1376264 | tf_op jit(solution)/shard_map/ppermute | solution.py:148
  74.0 8.6 %collective-permute-start.9 = (bf16[2,64,896]{2,1,0:T(8,128)(2,1)S(1)}, bf16[2,64,896]{2,1,0:T(8,128)(2,1)S(1)}, u32[]{:S(2)}, u32[]{:S(2)}) collective-permute-start(bf16[2,64,896]{2,1,0:T(8,128)(2,1)S(1)} %slice.57), channel_id=1, source_target_pairs={{0,4},{4,0},{8,12},{12,8},{1,5},{5,1},{9,13},{13,9},{2,6},{6,2},{1... | collective-permute-start | bytes 688136 | tf_op jit(solution)/shard_map/ppermute | solution.py:148
  75.9 15.2 %collective-permute-start.12 = (bf16[2,64,896]{2,1,0:T(8,128)(2,1)S(1)}, bf16[2,64,896]{2,1,0:T(8,128)(2,1)S(1)}, u32[]{:S(2)}, u32[]{:S(2)}) collective-permute-start(bf16[2,64,896]{2,1,0:T(8,128)(2,1)S(1)} %slice.61), channel_id=1, source_target_pairs={{0,4},{4,0},{8,12},{12,8},{1,5},{5,1},{9,13},{13,9},{2,6},{6,2},{1... | collective-permute-start | bytes 688136 | tf_op jit(solution)/shard_map/ppermute | solution.py:148
  76.5 20.2 %collective-permute-start.15 = (bf16[2,64,896]{2,1,0:T(8,128)(2,1)S(1)}, bf16[2,64,896]{2,1,0:T(8,128)(2,1)S(1)}, u32[]{:S(2)}, u32[]{:S(2)}) collective-permute-start(bf16[2,64,896]{2,1,0:T(8,128)(2,1)S(1)} %slice.65), channel_id=1, source_target_pairs={{0,4},{4,0},{8,12},{12,8},{1,5},{5,1},{9,13},{13,9},{2,6},{6,2},{1... | collective-permute-start | bytes 688136 | tf_op jit(solution)/shard_map/ppermute | solution.py:148
  80.5 20.4 %collective-permute-start.18 = (bf16[2,64,896]{2,1,0:T(8,128)(2,1)S(1)}, bf16[2,64,896]{2,1,0:T(8,128)(2,1)S(1)}, u32[]{:S(2)}, u32[]{:S(2)}) collective-permute-start(bf16[2,64,896]{2,1,0:T(8,128)(2,1)S(1)} %slice.69), channel_id=1, source_target_pairs={{0,4},{4,0},{8,12},{12,8},{1,5},{5,1},{9,13},{13,9},{2,6},{6,2},{1... | collective-permute-start | bytes 688136 | tf_op jit(solution)/shard_map/ppermute | solution.py:148
  82.7 19.1 %collective-permute-start.10 = (bf16[64,896]{1,0:T(8,128)(2,1)S(1)}, bf16[64,896]{1,0:T(8,128)(2,1)S(1)}, u32[]{:S(2)}, u32[]{:S(2)}) collective-permute-start(bf16[64,896]{1,0:T(8,128)(2,1)S(1)} %fusion.8), channel_id=1, source_target_pairs={{0,8},{4,12},{8,0},{12,4},{1,9},{5,13},{9,1},{13,5},{2,10},{6,14},... | collective-permute-start | bytes 344072 | tf_op jit(solution)/shard_map/ppermute | solution.py:148
  91.3 16.5 %collective-permute-start.13 = (bf16[64,896]{1,0:T(8,128)(2,1)S(1)}, bf16[64,896]{1,0:T(8,128)(2,1)S(1)}, u32[]{:S(2)}, u32[]{:S(2)}) collective-permute-start(bf16[64,896]{1,0:T(8,128)(2,1)S(1)} %fusion.9), channel_id=1, source_target_pairs={{0,8},{4,12},{8,0},{12,4},{1,9},{5,13},{9,1},{13,5},{2,10},{6,14},... | collective-permute-start | bytes 344072 | tf_op jit(solution)/shard_map/ppermute | solution.py:148
  96.8 13.2 %collective-permute-start.16 = (bf16[64,896]{1,0:T(8,128)(2,1)S(1)}, bf16[64,896]{1,0:T(8,128)(2,1)S(1)}, u32[]{:S(2)}, u32[]{:S(2)}) collective-permute-start(bf16[64,896]{1,0:T(8,128)(2,1)S(1)} %fusion.10), channel_id=1, source_target_pairs={{0,8},{4,12},{8,0},{12,4},{1,9},{5,13},{9,1},{13,5},{2,10},{6,14},... | collective-permute-start | bytes 344072 | tf_op jit(solution)/shard_map/ppermute | solution.py:148
  101.0 10.3 %collective-permute-start.19 = (bf16[64,896]{1,0:T(8,128)(2,1)S(1)}, bf16[64,896]{1,0:T(8,128)(2,1)S(1)}, u32[]{:S(2)}, u32[]{:S(2)}) collective-permute-start(bf16[64,896]{1,0:T(8,128)(2,1)S(1)} %fusion.11), channel_id=1, source_target_pairs={{0,8},{4,12},{8,0},{12,4},{1,9},{5,13},{9,1},{13,5},{2,10},{6,14},... | collective-permute-start | bytes 344072 | tf_op jit(solution)/shard_map/ppermute | solution.py:148
  (1 other events, 0.7 us)

commit v4 on v3

--- a/solution.py
+++ b/solution.py
@@ -8,7 +8,8 @@
 from jax.sharding import Mesh, PartitionSpec as P
 
 CHIPS = 8
-CHUNKS = 4
+TILE = 256
+COLUMNS = ((0, 1024), (1024, 1024), (2048, 1024), (3072, 512))
 
 
 def passed_along(block, axis, distance):
@@ -115,29 +116,30 @@
     )
 
 
-def mix_kernel(start, *refs):
+def mix_kernel(*refs):
     rows, (near_ref, far_ref, out_ref) = refs[:-3], refs[-3:]
-    tokens, width = rows[0].shape[1], out_ref.shape[2]
-    columns = pl.ds(start, width)
+    tokens = rows[0].shape[1]
     near = jnp.concatenate([ref[0] for ref in rows], axis=0)
     far = jnp.concatenate([ref[1] for ref in rows], axis=0)
-    total = jnp.dot(near, near_ref[:, columns], preferred_element_type=jnp.float32)
-    total += jnp.dot(far, far_ref[:, columns], preferred_element_type=jnp.float32)
+    total = jnp.dot(near, near_ref[...], preferred_element_type=jnp.float32)
+    total += jnp.dot(far, far_ref[...], preferred_element_type=jnp.float32)
     out_ref[...] = total.reshape(len(rows), tokens, -1).astype(out_ref.dtype)
 
 
 def mix(rows, near, far, start, width):
     _, tokens, depth = rows[0].shape
-    vmem = pl.BlockSpec(memory_space=pltpu.VMEM)
+    whole = pl.BlockSpec((2, tokens, depth), lambda i: (0, 0, 0))
+    weight = pl.BlockSpec((depth, TILE), lambda i: (0, start // TILE + i))
     return pl.pallas_call(
-        functools.partial(mix_kernel, start),
-        in_specs=[vmem] * (len(rows) + 2),
-        out_specs=vmem,
+        mix_kernel,
+        grid=(width // TILE,),
+        in_specs=[whole] * len(rows) + [weight] * 2,
+        out_specs=pl.BlockSpec((len(rows), tokens, TILE), lambda i: (0, 0, i)),
         out_shape=jax.ShapeDtypeStruct((len(rows), tokens, width), jnp.bfloat16),
         compiler_params=pltpu.CompilerParams(vmem_limit_bytes=24 << 20),
         cost_estimate=pl.CostEstimate(
             flops=4 * len(rows) * tokens * depth * width,
-            bytes_accessed=2 * len(rows) * tokens * (2 * depth + width),
+            bytes_accessed=4 * depth * width + 2 * len(rows) * tokens * (2 * depth + width),
             transcendentals=0,
         ),
         name="mix",
@@ -156,7 +158,6 @@
 
 
 def dense_body(hidden, expert_ids, gate_weights, down_weight):
-    width_total = down_weight.shape[2]
     own = (lax.axis_index("z") * 2 + lax.axis_index("x")) * 2 + lax.axis_index("core")
     near = down_weight[0]
     far = swap(near, "core", 1)
@@ -167,15 +168,18 @@
         arrived[relative] = send_to_chip(block, relative)
     blocks = spread_rows(hidden, expert_ids, gate_weights, own, even, near)
     for relative, block in zip(even, blocks):
+        block, arrived[relative + 1] = lax.optimization_barrier((block, arrived[relative + 1]))
         arrived[relative] = send_to_chip(block, relative) if relative else block
-    chunk = width_total // CHUNKS
+    given = [mix(arrived[1::2], near, far, *columns) for columns in COLUMNS]
+    taken = [swap(block, "x", 1) for block in given]
     results = []
-    for start in range(0, width_total, chunk):
-        given = mix(arrived[1::2], near, far, start, chunk)
-        kept = mix(arrived[0::2], near, far, start, chunk)
-        taken = swap(given, "x", 1)
-        line = kept.astype(jnp.float32) + taken.astype(jnp.float32)
-        pair = line[0::2] + swap(line[1::2].astype(jnp.bfloat16), "z", 1).astype(jnp.float32)
+    for at, columns in enumerate(COLUMNS):
+        kept = mix(arrived[0::2], near, far, *columns)
+        line = kept.astype(jnp.float32) + taken[at].astype(jnp.float32)
+        half = swap(line[1::2].astype(jnp.bfloat16), "z", 1)
+        if at + 1 < len(COLUMNS):
+            half, taken[at + 1] = lax.optimization_barrier((half, taken[at + 1]))
+        pair = line[0::2] + half.astype(jnp.float32)
         last = pair[0] + swap(pair[1].astype(jnp.bfloat16), "z", 2).astype(jnp.float32)
         results.append(last.astype(jnp.bfloat16))
     return jnp.concatenate(results, axis=1)

time: 113 us -> 116 us (1.027)
  waiting for transfers between devices: 38.4 us -> 49.5 us
  Pallas kernels: 36.5 us -> 27.6 us
  starting transfers between devices: 29.5 us -> 30.8 us
    ppermute x7, waiting for transfers between devices: 14.8 us -> 26.9 us  [send_to_chip(): lax.ppermute(block, ('z', 'x'), [(i, i ^ relative) for i in range(sizes[0...]
    pallas_call x8, Pallas kernels: 34.7 us -> 25.8 us  [mix(): pl.pallas_call(mix_kernel, grid=(width // TILE,), in_specs=[whole] * len(...]
    ppermute x7, starting transfers between devices: 12 us -> 14.1 us  [send_to_chip(): lax.ppermute(block, ('z', 'x'), [(i, i ^ relative) for i in range(sizes[0...]
  transfers between devices with their start and end apart: 20 -> 20, of which waited for: 9 -> 8; matrix products, arithmetic and copies ran while one was open for 1% -> 1% of each run, Pallas kernels for 33% -> 21%
where the time goes in v4:
time: 116 us
  waiting for transfers between devices  49.5 us (43%)
  starting transfers between devices  30.8 us (27%)
  Pallas kernels  27.6 us (24%)
  local copies, waits for them, and re-layouts  5.81 us (5%)
  other arithmetic  1.83 us (2%)
    ppermute x7, waiting for transfers between devices, send_to_chip(): lax.ppermute(block, ('z', 'x'), [(i, i ^ relative) for i in range(sizes[0...  26.9 us
    pallas_call x8, Pallas kernels, mix(): pl.pallas_call(mix_kernel, grid=(width // TILE,), in_specs=[whole] * len(...  25.8 us
    ppermute x13, waiting for transfers between devices, swap(): lax.ppermute(block, axis, [(i, i ^ distance) for i in range(lax.axis_size...  22.6 us
    ppermute x13, starting transfers between devices, swap(): lax.ppermute(block, axis, [(i, i ^ distance) for i in range(lax.axis_size...  16.8 us
    ppermute x7, starting transfers between devices, send_to_chip(): lax.ppermute(block, ('z', 'x'), [(i, i ^ relative) for i in range(sizes[0...  14.1 us
    unnamed x10, local copies, waits for them, and re-layouts  5.68 us
  transfers between devices with their start and end apart: 20, of which 8 were waited for; matrix products, arithmetic and copies ran while one was open for 1% of the time, Pallas kernels for 21%

profile of v4, /device:TPU:0, one launch (start us, length us, event | category | flops | bytes accessed | tf_op | source)
XLA Modules:
  0.0 115.9 jit_solution(1850580524366543388)
XLA Ops:
  4.0 2.5 %collective-permute-start = (bf16[2,64,1024]{2,1,0:T(8,128)(2,1)S(1)}, bf16[2,64,1024]{2,1,0:T(8,128)(2,1)S(1)}, u32[]{:S(2)}, u32[]{:S(2)}) collective-permute-start(bf16[2,64,1024]{2,1,0:T(8,128)(2,1)S(1)} %get-tuple-element.28), channel_id=1, source_target_pairs={{0,2},{2,0},{4,6},{6,4},{8,10},{10,8},{12,14},{14,12},{1,3},{3,1},... | collective-permute-start | bytes 786440 | tf_op jit(solution)/shard_map/ppermute | solution.py:155
  8.1 3.5 %collective-permute-start.3 = (bf16[2,64,1024]{2,1,0:T(8,128)(2,1)S(1)}, bf16[2,64,1024]{2,1,0:T(8,128)(2,1)S(1)}, u32[]{:S(2)}, u32[]{:S(2)}) collective-permute-start(bf16[2,64,1024]{2,1,0:T(8,128)(2,1)S(1)} %get-tuple-element.34), channel_id=1, source_target_pairs={{0,10},{2,8},{4,14},{6,12},{8,2},{10,0},{12,6},{14,4},{1,11},{3,9}... | collective-permute-start | bytes 786440 | tf_op jit(solution)/shard_map/ppermute | solution.py:155
  11.6 3.1 %copy-done = bf16[1,1024,3584]{2,1,0:T(8,128)(2,1)S(1)} copy-done((bf16[1,1024,3584]{2,1,0:T(8,128)(2,1)S(1)}, bf16[1,1024,3584]{2,1,0:T(8,128)(2,1)}, u32[]{:S(2)}) %copy-start) | copy-done | bytes 7340056
  15.6 14.8 %collective-permute-done.refs_0_ = bf16[2,64,1024]{2,1,0:T(8,128)(2,1)S(1)} collective-permute-done((bf16[2,64,1024]{2,1,0:T(8,128)(2,1)S(1)}, bf16[2,64,1024]{2,1,0:T(8,128)(2,1)S(1)}, u32[]{:S(2)}, u32[]{:S(2)}) %collective-permute-start) | collective-permute-done | bytes 262176 | tf_op jit(solution)/shard_map/ppermute | solution.py:155
  30.4 3.6 %mix.9 = bf16[4,64,1024]{2,1,0:T(8,128)(2,1)S(1)} custom-call(bf16[2,64,1024]{2,1,0:T(8,128)(2,1)S(1)} %collective-permute-done.refs_0_, bf16[2,64,1024]{2,1,0:T(8,128)(2,1)S(1)} %collective-permute-done.1.refs_1_, bf16[2,64,1024]{2,1,0:T(8,128)(2,1)S(1)} %collective-permute-done.3.refs_2_, bf16[2,64,1024]{2,1,0:T(8,128)(2,1)S(1)} %collective-permute-done.5.refs_3_, ...), custom_call_target="tpu_custom_call" | custom-call | flops 1073741824 | bytes 5767168 | tf_op jit(solution)/shard_map/mix/pallas_call | solution.py:133
  34.0 1.8 %collective-permute-start.8 = (bf16[4,64,1024]{2,1,0:T(8,128)(2,1)S(1)}, bf16[4,64,1024]{2,1,0:T(8,128)(2,1)S(1)}, u32[]{:S(2)}, u32[]{:S(2)}) collective-permute-start(bf16[4,64,1024]{2,1,0:T(8,128)(2,1)S(1)} %mix.9), channel_id=1, source_target_pairs={{0,2},{2,0},{1,3},{3,1},{4,6},{6,4},{5,7},{7,5},{8,10},{10,8},{9,1... | collective-permute-start | bytes 1572872 | tf_op jit(solution)/shard_map/ppermute | solution.py:150
  35.8 3.6 %collective-permute-start.6 = (bf16[2,64,1024]{2,1,0:T(8,128)(2,1)S(1)}, bf16[2,64,1024]{2,1,0:T(8,128)(2,1)S(1)}, u32[]{:S(2)}, u32[]{:S(2)}) collective-permute-start(bf16[2,64,1024]{2,1,0:T(8,128)(2,1)S(1)} %get-tuple-element.38), channel_id=1, source_target_pairs={{0,12},{2,14},{4,8},{6,10},{8,4},{10,6},{12,0},{14,2},{1,13},{3,15... | collective-permute-start | bytes 786440 | tf_op jit(solution)/shard_map/ppermute | solution.py:155
  39.4 2.7 %collective-permute-start.4 = (bf16[2,64,1024]{2,1,0:T(8,128)(2,1)S(1)}, bf16[2,64,1024]{2,1,0:T(8,128)(2,1)S(1)}, u32[]{:S(2)}, u32[]{:S(2)}) collective-permute-start(bf16[2,64,1024]{2,1,0:T(8,128)(2,1)S(1)} %get-tuple-element.35), channel_id=1, source_target_pairs={{0,8},{2,10},{4,12},{6,14},{8,0},{10,2},{12,4},{14,6},{1,9},{3,11}... | collective-permute-start | bytes 786440 | tf_op jit(solution)/shard_map/ppermute | solution.py:155
  42.3 2.0 %mix.14 = bf16[4,64,512]{2,1,0:T(8,128)(2,1)S(1)} custom-call(bf16[2,64,1024]{2,1,0:T(8,128)(2,1)S(1)} %collective-permute-done.refs_0_, bf16[2,64,1024]{2,1,0:T(8,128)(2,1)S(1)} %collective-permute-done.1.refs_1_, bf16[2,64,1024]{2,1,0:T(8,128)(2,1)S(1)} %collective-permute-done.3.refs_2_, bf16[2,64,1024]{2,1,0:T(8,128)(2,1)S(1)} %collective-permute-done.5.refs_3_, ...), custom_call_target="tpu_custom_call" | custom-call | flops 536870912 | bytes 3407872 | tf_op jit(solution)/shard_map/mix/pallas_call | solution.py:133
  44.9 3.6 %mix.10 = bf16[4,64,1024]{2,1,0:T(8,128)(2,1)S(1)} custom-call(bf16[2,64,1024]{2,1,0:T(8,128)(2,1)S(1)} %collective-permute-done.refs_0_, bf16[2,64,1024]{2,1,0:T(8,128)(2,1)S(1)} %collective-permute-done.1.refs_1_, bf16[2,64,1024]{2,1,0:T(8,128)(2,1)S(1)} %collective-permute-done.3.refs_2_, bf16[2,64,1024]{2,1,0:T(8,128)(2,1)S(1)} %collective-permute-done.5.refs_3_, ...), custom_call_target="tpu_custom_call" | custom-call | flops 1073741824 | bytes 5767168 | tf_op jit(solution)/shard_map/mix/pallas_call | solution.py:133
  50.1 12.1 %collective-permute-done.4.refs_2_ = bf16[2,64,1024]{2,1,0:T(8,128)(2,1)S(1)} collective-permute-done((bf16[2,64,1024]{2,1,0:T(8,128)(2,1)S(1)}, bf16[2,64,1024]{2,1,0:T(8,128)(2,1)S(1)}, u32[]{:S(2)}, u32[]{:S(2)}) %collective-permute-start.4) | collective-permute-done | bytes 262176 | tf_op jit(solution)/shard_map/ppermute | solution.py:155
  62.2 3.6 %mix.8 = bf16[4,64,1024]{2,1,0:T(8,128)(2,1)S(1)} custom-call(bf16[2,64,1024]{2,1,0:T(8,128)(2,1)S(1)} %get-tuple-element.29.refs_0_, bf16[2,64,1024]{2,1,0:T(8,128)(2,1)S(1)} %collective-permute-done.2.refs_1_, bf16[2,64,1024]{2,1,0:T(8,128)(2,1)S(1)} %collective-permute-done.4.refs_2_, bf16[2,64,1024]{2,1,0:T(8,128)(2,1)S(1)} %collective-permute-done.6.refs_3_, ...), custom_call_target="tpu_custom_call" | custom-call | flops 1073741824 | bytes 5767168 | tf_op jit(solution)/shard_map/mix/pallas_call | solution.py:133
  66.9 3.6 %mix.12 = bf16[4,64,1024]{2,1,0:T(8,128)(2,1)S(1)} custom-call(bf16[2,64,1024]{2,1,0:T(8,128)(2,1)S(1)} %collective-permute-done.refs_0_, bf16[2,64,1024]{2,1,0:T(8,128)(2,1)S(1)} %collective-permute-done.1.refs_1_, bf16[2,64,1024]{2,1,0:T(8,128)(2,1)S(1)} %collective-permute-done.3.refs_2_, bf16[2,64,1024]{2,1,0:T(8,128)(2,1)S(1)} %collective-permute-done.5.refs_3_, ...), custom_call_target="tpu_custom_call" | custom-call | flops 1073741824 | bytes 5767168 | tf_op jit(solution)/shard_map/mix/pallas_call | solution.py:133
  71.1 2.0 %mix.15 = bf16[4,64,512]{2,1,0:T(8,128)(2,1)S(1)} custom-call(bf16[2,64,1024]{2,1,0:T(8,128)(2,1)S(1)} %get-tuple-element.29.refs_0_, bf16[2,64,1024]{2,1,0:T(8,128)(2,1)S(1)} %collective-permute-done.2.refs_1_, bf16[2,64,1024]{2,1,0:T(8,128)(2,1)S(1)} %collective-permute-done.4.refs_2_, bf16[2,64,1024]{2,1,0:T(8,128)(2,1)S(1)} %collective-permute-done.6.refs_3_, ...), custom_call_target="tpu_custom_call" | custom-call | flops 536870912 | bytes 3407872 | tf_op jit(solution)/shard_map/mix/pallas_call | solution.py:133
  73.1 3.7 %mix.13 = bf16[4,64,1024]{2,1,0:T(8,128)(2,1)S(1)} custom-call(bf16[2,64,1024]{2,1,0:T(8,128)(2,1)S(1)} %get-tuple-element.29.refs_0_, bf16[2,64,1024]{2,1,0:T(8,128)(2,1)S(1)} %collective-permute-done.2.refs_1_, bf16[2,64,1024]{2,1,0:T(8,128)(2,1)S(1)} %collective-permute-done.4.refs_2_, bf16[2,64,1024]{2,1,0:T(8,128)(2,1)S(1)} %collective-permute-done.6.refs_3_, ...), custom_call_target="tpu_custom_call" | custom-call | flops 1073741824 | bytes 5767168 | tf_op jit(solution)/shard_map/mix/pallas_call | solution.py:133
  76.8 3.7 %mix.11 = bf16[4,64,1024]{2,1,0:T(8,128)(2,1)S(1)} custom-call(bf16[2,64,1024]{2,1,0:T(8,128)(2,1)S(1)} %get-tuple-element.29.refs_0_, bf16[2,64,1024]{2,1,0:T(8,128)(2,1)S(1)} %collective-permute-done.2.refs_1_, bf16[2,64,1024]{2,1,0:T(8,128)(2,1)S(1)} %collective-permute-done.4.refs_2_, bf16[2,64,1024]{2,1,0:T(8,128)(2,1)S(1)} %collective-permute-done.6.refs_3_, ...), custom_call_target="tpu_custom_call" | custom-call | flops 1073741824 | bytes 5767168 | tf_op jit(solution)/shard_map/mix/pallas_call | solution.py:133
  82.2 2.2 %collective-permute-start.11 = (bf16[64,1024]{1,0:T(8,128)(2,1)S(1)}, bf16[64,1024]{1,0:T(8,128)(2,1)S(1)}, u32[]{:S(2)}, u32[]{:S(2)}) collective-permute-start(bf16[64,1024]{1,0:T(8,128)(2,1)S(1)} %fusion.6), channel_id=1, source_target_pairs={{0,8},{4,12},{8,0},{12,4},{1,9},{5,13},{9,1},{13,5},{2,10},{6,14},... | collective-permute-start | bytes 393224 | tf_op jit(solution)/shard_map/ppermute | solution.py:150
  84.3 6.9 %collective-permute-done.12 = bf16[2,64,1024]{2,1,0:T(8,128)(2,1)S(1)} collective-permute-done((bf16[2,64,1024]{2,1,0:T(8,128)(2,1)S(1)}, bf16[2,64,1024]{2,1,0:T(8,128)(2,1)S(1)}, u32[]{:S(2)}, u32[]{:S(2)}) %collective-permute-start.12) | collective-permute-done | bytes 262176 | tf_op jit(solution)/shard_map/ppermute | solution.py:150
  91.3 2.0 %collective-permute-start.14 = (bf16[64,1024]{1,0:T(8,128)(2,1)S(1)}, bf16[64,1024]{1,0:T(8,128)(2,1)S(1)}, u32[]{:S(2)}, u32[]{:S(2)}) collective-permute-start(bf16[64,1024]{1,0:T(8,128)(2,1)S(1)} %fusion.7), channel_id=1, source_target_pairs={{0,8},{4,12},{8,0},{12,4},{1,9},{5,13},{9,1},{13,5},{2,10},{6,14},... | collective-permute-start | bytes 393224 | tf_op jit(solution)/shard_map/ppermute | solution.py:150
  95.4 4.3 %collective-permute-done.14 = bf16[64,1024]{1,0:T(8,128)(2,1)S(1)} collective-permute-done((bf16[64,1024]{1,0:T(8,128)(2,1)S(1)}, bf16[64,1024]{1,0:T(8,128)(2,1)S(1)}, u32[]{:S(2)}, u32[]{:S(2)}) %collective-permute-start.14) | collective-permute-done | bytes 131104 | tf_op jit(solution)/shard_map/ppermute | solution.py:150
  99.8 3.3 %collective-permute-done.15 = bf16[2,64,1024]{2,1,0:T(8,128)(2,1)S(1)} collective-permute-done((bf16[2,64,1024]{2,1,0:T(8,128)(2,1)S(1)}, bf16[2,64,1024]{2,1,0:T(8,128)(2,1)S(1)}, u32[]{:S(2)}, u32[]{:S(2)}) %collective-permute-start.15) | collective-permute-done | bytes 262176 | tf_op jit(solution)/shard_map/ppermute | solution.py:150
  105.6 3.4 %collective-permute-done.18 = bf16[2,64,512]{2,1,0:T(8,128)(2,1)S(1)} collective-permute-done((bf16[2,64,512]{2,1,0:T(8,128)(2,1)S(1)}, bf16[2,64,512]{2,1,0:T(8,128)(2,1)S(1)}, u32[]{:S(2)}, u32[]{:S(2)}) %collective-permute-start.18) | collective-permute-done | bytes 131104 | tf_op jit(solution)/shard_map/ppermute | solution.py:150
  110.4 2.8 %collective-permute-done.17 = bf16[64,1024]{1,0:T(8,128)(2,1)S(1)} collective-permute-done((bf16[64,1024]{1,0:T(8,128)(2,1)S(1)}, bf16[64,1024]{1,0:T(8,128)(2,1)S(1)}, u32[]{:S(2)}, u32[]{:S(2)}) %collective-permute-start.17) | collective-permute-done | bytes 131104 | tf_op jit(solution)/shard_map/ppermute | solution.py:150
  113.2 1.8 %collective-permute-done.19 = bf16[64,512]{1,0:T(8,128)(2,1)S(1)} collective-permute-done((bf16[64,512]{1,0:T(8,128)(2,1)S(1)}, bf16[64,512]{1,0:T(8,128)(2,1)S(1)}, u32[]{:S(2)}, u32[]{:S(2)}) %collective-permute-start.19) | collective-permute-done | bytes 65568 | tf_op jit(solution)/shard_map/ppermute | solution.py:150
  (57 shorter events, 18.8 us)
Async XLA Ops:
  0.0 30.4 %collective-permute-start.7 = (bf16[1024,3584]{1,0:T(8,128)(2,1)}, bf16[1024,3584]{1,0:T(8,128)(2,1)}, u32[]{:S(2)}, u32[]{:S(2)}) collective-permute-start(bf16[1024,3584]{1,0:T(8,128)(2,1)} %bitcast.37), channel_id=1, source_target_pairs={{0,1},{1,0},{2,3},{3,2},{4,5},{5,4},{6,7},{7,6},{8,9},{9,8},{10,11... | collective-permute-start | bytes 22020104 | tf_op jit(solution)/shard_map/ppermute | solution.py:150
  0.5 1.2 %copy-start.2 = (bf16[64,8,1024]{2,1,0:T(8,128)(2,1)S(1)}, bf16[64,8,1024]{2,1,0:T(8,128)(2,1)}, u32[]{:S(2)}) copy-start(bf16[64,8,1024]{2,1,0:T(8,128)(2,1)} %param.4) | copy-start | bytes 3145732
  1.7 0.7 copy-start.3
  4.0 26.4 %collective-permute-start = (bf16[2,64,1024]{2,1,0:T(8,128)(2,1)S(1)}, bf16[2,64,1024]{2,1,0:T(8,128)(2,1)S(1)}, u32[]{:S(2)}, u32[]{:S(2)}) collective-permute-start(bf16[2,64,1024]{2,1,0:T(8,128)(2,1)S(1)} %get-tuple-element.28), channel_id=1, source_target_pairs={{0,2},{2,0},{4,6},{6,4},{8,10},{10,8},{12,14},{14,12},{1,3},{3,1},... | collective-permute-start | bytes 786440 | tf_op jit(solution)/shard_map/ppermute | solution.py:155
  6.5 23.8 %collective-permute-start.1 = (bf16[2,64,1024]{2,1,0:T(8,128)(2,1)S(1)}, bf16[2,64,1024]{2,1,0:T(8,128)(2,1)S(1)}, u32[]{:S(2)}, u32[]{:S(2)}) collective-permute-start(bf16[2,64,1024]{2,1,0:T(8,128)(2,1)S(1)} %get-tuple-element.31), channel_id=1, source_target_pairs={{0,6},{2,4},{4,2},{6,0},{8,14},{10,12},{12,10},{14,8},{1,7},{3,5},... | collective-permute-start | bytes 786440 | tf_op jit(solution)/shard_map/ppermute | solution.py:155
  8.1 22.3 %collective-permute-start.3 = (bf16[2,64,1024]{2,1,0:T(8,128)(2,1)S(1)}, bf16[2,64,1024]{2,1,0:T(8,128)(2,1)S(1)}, u32[]{:S(2)}, u32[]{:S(2)}) collective-permute-start(bf16[2,64,1024]{2,1,0:T(8,128)(2,1)S(1)} %get-tuple-element.34), channel_id=1, source_target_pairs={{0,10},{2,8},{4,14},{6,12},{8,2},{10,0},{12,6},{14,4},{1,11},{3,9}... | collective-permute-start | bytes 786440 | tf_op jit(solution)/shard_map/ppermute | solution.py:155
  11.6 18.8 %collective-permute-start.5 = (bf16[2,64,1024]{2,1,0:T(8,128)(2,1)S(1)}, bf16[2,64,1024]{2,1,0:T(8,128)(2,1)S(1)}, u32[]{:S(2)}, u32[]{:S(2)}) collective-permute-start(bf16[2,64,1024]{2,1,0:T(8,128)(2,1)S(1)} %get-tuple-element.37), channel_id=1, source_target_pairs={{0,14},{2,12},{4,10},{6,8},{8,6},{10,4},{12,2},{14,0},{1,15},{3,13... | collective-permute-start | bytes 786440 | tf_op jit(solution)/shard_map/ppermute | solution.py:155
  11.6 3.1 %copy-start = (bf16[1,1024,3584]{2,1,0:T(8,128)(2,1)S(1)}, bf16[1,1024,3584]{2,1,0:T(8,128)(2,1)}, u32[]{:S(2)}) copy-start(bf16[1,1024,3584]{2,1,0:T(8,128)(2,1)} %param.7) | copy-start | bytes 22020100
  14.7 15.7 %copy-start.1 = (bf16[1,1024,3584]{2,1,0:T(8,128)(2,1)S(1)}, bf16[1,1024,3584]{2,1,0:T(8,128)(2,1)}, u32[]{:S(2)}) copy-start(bf16[1,1024,3584]{2,1,0:T(8,128)(2,1)} %param.7) | copy-start | bytes 22020100
  34.0 31.8 %collective-permute-start.8 = (bf16[4,64,1024]{2,1,0:T(8,128)(2,1)S(1)}, bf16[4,64,1024]{2,1,0:T(8,128)(2,1)S(1)}, u32[]{:S(2)}, u32[]{:S(2)}) collective-permute-start(bf16[4,64,1024]{2,1,0:T(8,128)(2,1)S(1)} %mix.9), channel_id=1, source_target_pairs={{0,2},{2,0},{1,3},{3,1},{4,6},{6,4},{5,7},{7,5},{8,10},{10,8},{9,1... | collective-permute-start | bytes 1572872 | tf_op jit(solution)/shard_map/ppermute | solution.py:150
  35.8 12.7 %collective-permute-start.6 = (bf16[2,64,1024]{2,1,0:T(8,128)(2,1)S(1)}, bf16[2,64,1024]{2,1,0:T(8,128)(2,1)S(1)}, u32[]{:S(2)}, u32[]{:S(2)}) collective-permute-start(bf16[2,64,1024]{2,1,0:T(8,128)(2,1)S(1)} %get-tuple-element.38), channel_id=1, source_target_pairs={{0,12},{2,14},{4,8},{6,10},{8,4},{10,6},{12,0},{14,2},{1,13},{3,15... | collective-permute-start | bytes 786440 | tf_op jit(solution)/shard_map/ppermute | solution.py:155
  39.4 22.8 %collective-permute-start.4 = (bf16[2,64,1024]{2,1,0:T(8,128)(2,1)S(1)}, bf16[2,64,1024]{2,1,0:T(8,128)(2,1)S(1)}, u32[]{:S(2)}, u32[]{:S(2)}) collective-permute-start(bf16[2,64,1024]{2,1,0:T(8,128)(2,1)S(1)} %get-tuple-element.35), channel_id=1, source_target_pairs={{0,8},{2,10},{4,12},{6,14},{8,0},{10,2},{12,4},{14,6},{1,9},{3,11}... | collective-permute-start | bytes 786440 | tf_op jit(solution)/shard_map/ppermute | solution.py:155
  42.1 20.1 %collective-permute-start.2 = (bf16[2,64,1024]{2,1,0:T(8,128)(2,1)S(1)}, bf16[2,64,1024]{2,1,0:T(8,128)(2,1)S(1)}, u32[]{:S(2)}, u32[]{:S(2)}) collective-permute-start(bf16[2,64,1024]{2,1,0:T(8,128)(2,1)S(1)} %get-tuple-element.32), channel_id=1, source_target_pairs={{0,4},{2,6},{4,0},{6,2},{8,12},{10,14},{12,8},{14,10},{1,5},{3,7},... | collective-permute-start | bytes 786440 | tf_op jit(solution)/shard_map/ppermute | solution.py:155
  44.3 55.5 %collective-permute-start.16 = (bf16[4,64,512]{2,1,0:T(8,128)(2,1)S(1)}, bf16[4,64,512]{2,1,0:T(8,128)(2,1)S(1)}, u32[]{:S(2)}, u32[]{:S(2)}) collective-permute-start(bf16[4,64,512]{2,1,0:T(8,128)(2,1)S(1)} %mix.14), channel_id=1, source_target_pairs={{0,2},{2,0},{1,3},{3,1},{4,6},{6,4},{5,7},{7,5},{8,10},{10,8},{9,1... | collective-permute-start | bytes 786440 | tf_op jit(solution)/shard_map/ppermute | solution.py:150
  48.5 31.9 %collective-permute-start.10 = (bf16[4,64,1024]{2,1,0:T(8,128)(2,1)S(1)}, bf16[4,64,1024]{2,1,0:T(8,128)(2,1)S(1)}, u32[]{:S(2)}, u32[]{:S(2)}) collective-permute-start(bf16[4,64,1024]{2,1,0:T(8,128)(2,1)S(1)} %mix.10), channel_id=1, source_target_pairs={{0,2},{2,0},{1,3},{3,1},{4,6},{6,4},{5,7},{7,5},{8,10},{10,8},{9,1... | collective-permute-start | bytes 1572872 | tf_op jit(solution)/shard_map/ppermute | solution.py:150
  66.1 14.4 %collective-permute-start.9 = (bf16[2,64,1024]{2,1,0:T(8,128)(2,1)S(1)}, bf16[2,64,1024]{2,1,0:T(8,128)(2,1)S(1)}, u32[]{:S(2)}, u32[]{:S(2)}) collective-permute-start(bf16[2,64,1024]{2,1,0:T(8,128)(2,1)S(1)} %slice.57), channel_id=1, source_target_pairs={{0,4},{4,0},{8,12},{12,8},{1,5},{5,1},{9,13},{13,9},{2,6},{6,2},{1... | collective-permute-start | bytes 786440 | tf_op jit(solution)/shard_map/ppermute | solution.py:150
  70.5 13.8 %collective-permute-start.13 = (bf16[4,64,1024]{2,1,0:T(8,128)(2,1)S(1)}, bf16[4,64,1024]{2,1,0:T(8,128)(2,1)S(1)}, u32[]{:S(2)}, u32[]{:S(2)}) collective-permute-start(bf16[4,64,1024]{2,1,0:T(8,128)(2,1)S(1)} %mix.12), channel_id=1, source_target_pairs={{0,2},{2,0},{1,3},{3,1},{4,6},{6,4},{5,7},{7,5},{8,10},{10,8},{9,1... | collective-permute-start | bytes 1572872 | tf_op jit(solution)/shard_map/ppermute | solution.py:150
  80.7 10.5 %collective-permute-start.12 = (bf16[2,64,1024]{2,1,0:T(8,128)(2,1)S(1)}, bf16[2,64,1024]{2,1,0:T(8,128)(2,1)S(1)}, u32[]{:S(2)}, u32[]{:S(2)}) collective-permute-start(bf16[2,64,1024]{2,1,0:T(8,128)(2,1)S(1)} %slice.61), channel_id=1, source_target_pairs={{0,4},{4,0},{8,12},{12,8},{1,5},{5,1},{9,13},{13,9},{2,6},{6,2},{1... | collective-permute-start | bytes 786440 | tf_op jit(solution)/shard_map/ppermute | solution.py:150
  82.2 13.2 %collective-permute-start.11 = (bf16[64,1024]{1,0:T(8,128)(2,1)S(1)}, bf16[64,1024]{1,0:T(8,128)(2,1)S(1)}, u32[]{:S(2)}, u32[]{:S(2)}) collective-permute-start(bf16[64,1024]{1,0:T(8,128)(2,1)S(1)} %fusion.6), channel_id=1, source_target_pairs={{0,8},{4,12},{8,0},{12,4},{1,9},{5,13},{9,1},{13,5},{2,10},{6,14},... | collective-permute-start | bytes 393224 | tf_op jit(solution)/shard_map/ppermute | solution.py:150
  91.3 8.4 %collective-permute-start.14 = (bf16[64,1024]{1,0:T(8,128)(2,1)S(1)}, bf16[64,1024]{1,0:T(8,128)(2,1)S(1)}, u32[]{:S(2)}, u32[]{:S(2)}) collective-permute-start(bf16[64,1024]{1,0:T(8,128)(2,1)S(1)} %fusion.7), channel_id=1, source_target_pairs={{0,8},{4,12},{8,0},{12,4},{1,9},{5,13},{9,1},{13,5},{2,10},{6,14},... | collective-permute-start | bytes 393224 | tf_op jit(solution)/shard_map/ppermute | solution.py:150
  93.6 9.5 %collective-permute-start.15 = (bf16[2,64,1024]{2,1,0:T(8,128)(2,1)S(1)}, bf16[2,64,1024]{2,1,0:T(8,128)(2,1)S(1)}, u32[]{:S(2)}, u32[]{:S(2)}) collective-permute-start(bf16[2,64,1024]{2,1,0:T(8,128)(2,1)S(1)} %slice.65), channel_id=1, source_target_pairs={{0,4},{4,0},{8,12},{12,8},{1,5},{5,1},{9,13},{13,9},{2,6},{6,2},{1... | collective-permute-start | bytes 786440 | tf_op jit(solution)/shard_map/ppermute | solution.py:150
  103.2 5.9 %collective-permute-start.18 = (bf16[2,64,512]{2,1,0:T(8,128)(2,1)S(1)}, bf16[2,64,512]{2,1,0:T(8,128)(2,1)S(1)}, u32[]{:S(2)}, u32[]{:S(2)}) collective-permute-start(bf16[2,64,512]{2,1,0:T(8,128)(2,1)S(1)} %slice.69), channel_id=1, source_target_pairs={{0,4},{4,0},{8,12},{12,8},{1,5},{5,1},{9,13},{13,9},{2,6},{6,2},{1... | collective-permute-start | bytes 393224 | tf_op jit(solution)/shard_map/ppermute | solution.py:150
  103.9 9.3 %collective-permute-start.17 = (bf16[64,1024]{1,0:T(8,128)(2,1)S(1)}, bf16[64,1024]{1,0:T(8,128)(2,1)S(1)}, u32[]{:S(2)}, u32[]{:S(2)}) collective-permute-start(bf16[64,1024]{1,0:T(8,128)(2,1)S(1)} %fusion.8), channel_id=1, source_target_pairs={{0,8},{4,12},{8,0},{12,4},{1,9},{5,13},{9,1},{13,5},{2,10},{6,14},... | collective-permute-start | bytes 393224 | tf_op jit(solution)/shard_map/ppermute | solution.py:150
  109.1 5.9 %collective-permute-start.19 = (bf16[64,512]{1,0:T(8,128)(2,1)S(1)}, bf16[64,512]{1,0:T(8,128)(2,1)S(1)}, u32[]{:S(2)}, u32[]{:S(2)}) collective-permute-start(bf16[64,512]{1,0:T(8,128)(2,1)S(1)} %fusion.11), channel_id=1, source_target_pairs={{0,8},{4,12},{8,0},{12,4},{1,9},{5,13},{9,1},{13,5},{2,10},{6,14},... | collective-permute-start | bytes 196616 | tf_op jit(solution)/shard_map/ppermute | solution.py:150
  (1 other events, 0.7 us)

commit v5 on v4

--- a/solution.py
+++ b/solution.py
@@ -8,7 +8,7 @@
 from jax.sharding import Mesh, PartitionSpec as P
 
 CHIPS = 8
-TILE = 256
+TILE = 512
 COLUMNS = ((0, 1024), (1024, 1024), (2048, 1024), (3072, 512))
 
 
@@ -117,12 +117,16 @@
 
 
 def mix_kernel(*refs):
-    rows, (near_ref, far_ref, out_ref) = refs[:-3], refs[-3:]
+    rows, (near_ref, far_ref, out_ref, joined_ref) = refs[:-4], refs[-4:]
     tokens = rows[0].shape[1]
-    near = jnp.concatenate([ref[0] for ref in rows], axis=0)
-    far = jnp.concatenate([ref[1] for ref in rows], axis=0)
-    total = jnp.dot(near, near_ref[...], preferred_element_type=jnp.float32)
-    total += jnp.dot(far, far_ref[...], preferred_element_type=jnp.float32)
+
+    @pl.when(pl.program_id(0) == 0)
+    def _():
+        for place, ref in enumerate(rows):
+            joined_ref[:, place * tokens : (place + 1) * tokens] = ref[...]
+
+    total = jnp.dot(joined_ref[0], near_ref[...], preferred_element_type=jnp.float32)
+    total += jnp.dot(joined_ref[1], far_ref[...], preferred_element_type=jnp.float32)
     out_ref[...] = total.reshape(len(rows), tokens, -1).astype(out_ref.dtype)
 
 
@@ -136,6 +140,7 @@
         in_specs=[whole] * len(rows) + [weight] * 2,
         out_specs=pl.BlockSpec((len(rows), tokens, TILE), lambda i: (0, 0, i)),
         out_shape=jax.ShapeDtypeStruct((len(rows), tokens, width), jnp.bfloat16),
+        scratch_shapes=[pltpu.VMEM((2, len(rows) * tokens, depth), jnp.bfloat16)],
         compiler_params=pltpu.CompilerParams(vmem_limit_bytes=24 << 20),
         cost_estimate=pl.CostEstimate(
             flops=4 * len(rows) * tokens * depth * width,
@@ -155,6 +160,10 @@
     return lax.ppermute(
         block, ("z", "x"), [(i, i ^ relative) for i in range(sizes[0] * sizes[1])]
     )
+
+
+def after(value, earlier):
+    return lax.optimization_barrier((value, earlier))[0]
 
 
 def dense_body(hidden, expert_ids, gate_weights, down_weight):
@@ -168,20 +177,42 @@
         arrived[relative] = send_to_chip(block, relative)
     blocks = spread_rows(hidden, expert_ids, gate_weights, own, even, near)
     for relative, block in zip(even, blocks):
-        block, arrived[relative + 1] = lax.optimization_barrier((block, arrived[relative + 1]))
         arrived[relative] = send_to_chip(block, relative) if relative else block
-    given = [mix(arrived[1::2], near, far, *columns) for columns in COLUMNS]
-    taken = [swap(block, "x", 1) for block in given]
-    results = []
-    for at, columns in enumerate(COLUMNS):
-        kept = mix(arrived[0::2], near, far, *columns)
-        line = kept.astype(jnp.float32) + taken[at].astype(jnp.float32)
-        half = swap(line[1::2].astype(jnp.bfloat16), "z", 1)
-        if at + 1 < len(COLUMNS):
-            half, taken[at + 1] = lax.optimization_barrier((half, taken[at + 1]))
-        pair = line[0::2] + half.astype(jnp.float32)
-        last = pair[0] + swap(pair[1].astype(jnp.bfloat16), "z", 2).astype(jnp.float32)
-        results.append(last.astype(jnp.bfloat16))
+    across, last = [], blocks[-1]
+    for columns in COLUMNS:
+        arrived[1] = after(arrived[1], last)
+        last = mix(arrived[1::2], near, far, *columns)
+        across.append(swap(last, "x", 1))
+    kept, lines, pairs, results = [], [], [], []
+
+    def mix_even(parts):
+        start, width = COLUMNS[parts[0]][0], sum(COLUMNS[i][1] for i in parts)
+        arrived[0] = after(arrived[0], last)
+        block = mix(arrived[0::2], near, far, start, width)
+        for i in parts:
+            low = COLUMNS[i][0] - start
+            kept.append(block[:, :, low : low + COLUMNS[i][1]])
+        return block
+
+    def add_x(i, last):
+        line = after(kept[i], last).astype(jnp.float32) + across[i].astype(jnp.float32)
+        lines.append((line[0::2], swap(line[1::2].astype(jnp.bfloat16), "z", 1)))
+        return line
+
+    def add_z(i, last):
+        pair = after(lines[i][0], last) + lines[i][1].astype(jnp.float32)
+        pairs.append((pair[0], swap(pair[1].astype(jnp.bfloat16), "z", 2)))
+        return pair
+
+    last = mix_even((0, 1))
+    last = add_x(0, last)
+    last = mix_even((2, 3))
+    for i in range(1, len(COLUMNS)):
+        last = add_x(i, last)
+        last = add_z(i - 1, last)
+    add_z(len(COLUMNS) - 1, last)
+    for mine, theirs in pairs:
+        results.append((mine + theirs.astype(jnp.float32)).astype(jnp.bfloat16))
     return jnp.concatenate(results, axis=1)
 
 

time: 116 us -> 114 us (0.983)
  Pallas kernels: 27.6 us -> 21.4 us
  starting transfers between devices: 30.8 us -> 32.6 us
  waiting for transfers between devices: 49.5 us -> 51.2 us
    ppermute x13, waiting for transfers between devices: 22.6 us -> 32.4 us  [swap(): lax.ppermute(block, axis, [(i, i ^ distance) for i in range(lax.axis_size...]
    ppermute x7, waiting for transfers between devices: 26.9 us -> 18.8 us  [send_to_chip(): lax.ppermute(block, ('z', 'x'), [(i, i ^ relative) for i in range(sizes[0...]
    pallas_call x8 -> x6, Pallas kernels: 25.8 us -> 19.6 us  [mix(): pl.pallas_call(mix_kernel, grid=(width // TILE,), in_specs=[whole] * len(...]
    ppermute x13, starting transfers between devices: 16.8 us -> 20.6 us  [swap(): lax.ppermute(block, axis, [(i, i ^ distance) for i in range(lax.axis_size...]
    ppermute x7, starting transfers between devices: 14.1 us -> 12 us  [send_to_chip(): lax.ppermute(block, ('z', 'x'), [(i, i ^ relative) for i in range(sizes[0...]
  transfers between devices with their start and end apart: 20 -> 20, of which waited for: 8 -> 8; matrix products, arithmetic and copies ran while one was open for 1% -> 1% of each run, Pallas kernels for 21% -> 19%
where the time goes in v5:
time: 114 us; the launch traced here: 113 us
  waiting for transfers between devices  51.2 us (45%)
  starting transfers between devices  32.6 us (29%)
  Pallas kernels  21.4 us (19%)
  local copies, waits for them, and re-layouts  6.1 us (5%)
  other arithmetic  1.81 us (2%)
    ppermute x13, waiting for transfers between devices, swap(): lax.ppermute(block, axis, [(i, i ^ distance) for i in range(lax.axis_size...  32.4 us
    ppermute x13, starting transfers between devices, swap(): lax.ppermute(block, axis, [(i, i ^ distance) for i in range(lax.axis_size...  20.6 us
    pallas_call x6, Pallas kernels, mix(): pl.pallas_call(mix_kernel, grid=(width // TILE,), in_specs=[whole] * len(...  19.6 us
    ppermute x7, waiting for transfers between devices, send_to_chip(): lax.ppermute(block, ('z', 'x'), [(i, i ^ relative) for i in range(sizes[0...  18.8 us
    ppermute x7, starting transfers between devices, send_to_chip(): lax.ppermute(block, ('z', 'x'), [(i, i ^ relative) for i in range(sizes[0...  12 us
    unnamed x10, local copies, waits for them, and re-layouts  5.68 us
  transfers between devices with their start and end apart: 20, of which 8 were waited for; matrix products, arithmetic and copies ran while one was open for 1% of the time, Pallas kernels for 19%

profile of v5, /device:TPU:0, one launch (start us, length us, event | category | flops | bytes accessed | tf_op | source)
XLA Modules:
  0.0 113.5 jit_solution(11865217519873670795)
XLA Ops:
  4.0 2.5 %collective-permute-start = (bf16[2,64,1024]{2,1,0:T(8,128)(2,1)S(1)}, bf16[2,64,1024]{2,1,0:T(8,128)(2,1)S(1)}, u32[]{:S(2)}, u32[]{:S(2)}) collective-permute-start(bf16[2,64,1024]{2,1,0:T(8,128)(2,1)S(1)} %get-tuple-element.28), channel_id=1, source_target_pairs={{0,2},{2,0},{4,6},{6,4},{8,10},{10,8},{12,14},{14,12},{1,3},{3,1},... | collective-permute-start | bytes 786440 | tf_op jit(solution)/shard_map/ppermute | solution.py:160
  6.5 1.5 %collective-permute-start.1 = (bf16[2,64,1024]{2,1,0:T(8,128)(2,1)S(1)}, bf16[2,64,1024]{2,1,0:T(8,128)(2,1)S(1)}, u32[]{:S(2)}, u32[]{:S(2)}) collective-permute-start(bf16[2,64,1024]{2,1,0:T(8,128)(2,1)S(1)} %get-tuple-element.30), channel_id=1, source_target_pairs={{0,6},{2,4},{4,2},{6,0},{8,14},{10,12},{12,10},{14,8},{1,7},{3,5},... | collective-permute-start | bytes 786440 | tf_op jit(solution)/shard_map/ppermute | solution.py:160
  8.1 3.5 %collective-permute-start.2 = (bf16[2,64,1024]{2,1,0:T(8,128)(2,1)S(1)}, bf16[2,64,1024]{2,1,0:T(8,128)(2,1)S(1)}, u32[]{:S(2)}, u32[]{:S(2)}) collective-permute-start(bf16[2,64,1024]{2,1,0:T(8,128)(2,1)S(1)} %get-tuple-element.31), channel_id=1, source_target_pairs={{0,10},{2,8},{4,14},{6,12},{8,2},{10,0},{12,6},{14,4},{1,11},{3,9}... | collective-permute-start | bytes 786440 | tf_op jit(solution)/shard_map/ppermute | solution.py:160
  11.6 3.1 %copy-done = bf16[1,1024,3584]{2,1,0:T(8,128)(2,1)S(1)} copy-done((bf16[1,1024,3584]{2,1,0:T(8,128)(2,1)S(1)}, bf16[1,1024,3584]{2,1,0:T(8,128)(2,1)}, u32[]{:S(2)}) %copy-start) | copy-done | bytes 7340056
  15.6 14.8 %collective-permute-done.refs_0_ = bf16[2,64,1024]{2,1,0:T(8,128)(2,1)S(1)} collective-permute-done((bf16[2,64,1024]{2,1,0:T(8,128)(2,1)S(1)}, bf16[2,64,1024]{2,1,0:T(8,128)(2,1)S(1)}, u32[]{:S(2)}, u32[]{:S(2)}) %collective-permute-start) | collective-permute-done | bytes 262176 | tf_op jit(solution)/shard_map/ppermute | solution.py:160
  30.3 4.4 %collective-permute-start.6 = (bf16[2,64,1024]{2,1,0:T(8,128)(2,1)S(1)}, bf16[2,64,1024]{2,1,0:T(8,128)(2,1)S(1)}, u32[]{:S(2)}, u32[]{:S(2)}) collective-permute-start(bf16[2,64,1024]{2,1,0:T(8,128)(2,1)S(1)} %get-tuple-element.38), channel_id=1, source_target_pairs={{0,8},{2,10},{4,12},{6,14},{8,0},{10,2},{12,4},{14,6},{1,9},{3,11}... | collective-permute-start | bytes 786440 | tf_op jit(solution)/shard_map/ppermute | solution.py:160
  34.8 2.8 %mix.6 = bf16[4,64,1024]{2,1,0:T(8,128)(2,1)S(1)} custom-call(bf16[2,64,1024]{2,1,0:T(8,128)(2,1)S(1)} %collective-permute-done.refs_0_, bf16[2,64,1024]{2,1,0:T(8,128)(2,1)S(1)} %collective-permute-done.1.refs_1_, bf16[2,64,1024]{2,1,0:T(8,128)(2,1)S(1)} %collective-permute-done.2.refs_2_, bf16[2,64,1024]{2,1,0:T(8,128)(2,1)S(1)} %collective-permute-done.3.refs_3_, ...), custom_call_target="tpu_custom_call" | custom-call | flops 1073741824 | bytes 5767168 | tf_op jit(solution)/shard_map/mix/pallas_call | solution.py:137
  37.6 1.8 %collective-permute-start.8 = (bf16[4,64,1024]{2,1,0:T(8,128)(2,1)S(1)}, bf16[4,64,1024]{2,1,0:T(8,128)(2,1)S(1)}, u32[]{:S(2)}, u32[]{:S(2)}) collective-permute-start(bf16[4,64,1024]{2,1,0:T(8,128)(2,1)S(1)} %mix.6), channel_id=1, source_target_pairs={{0,2},{2,0},{1,3},{3,1},{4,6},{6,4},{5,7},{7,5},{8,10},{10,8},{9,1... | collective-permute-start | bytes 1572872 | tf_op jit(solution)/shard_map/ppermute | solution.py:155
  39.4 2.8 %mix.7 = bf16[4,64,1024]{2,1,0:T(8,128)(2,1)S(1)} custom-call(bf16[2,64,1024]{2,1,0:T(8,128)(2,1)S(1)} %collective-permute-done.refs_0_, bf16[2,64,1024]{2,1,0:T(8,128)(2,1)S(1)} %collective-permute-done.1.refs_1_, bf16[2,64,1024]{2,1,0:T(8,128)(2,1)S(1)} %collective-permute-done.2.refs_2_, bf16[2,64,1024]{2,1,0:T(8,128)(2,1)S(1)} %collective-permute-done.3.refs_3_, ...), custom_call_target="tpu_custom_call" | custom-call | flops 1073741824 | bytes 5767168 | tf_op jit(solution)/shard_map/mix/pallas_call | solution.py:137
  42.2 2.8 %mix.8 = bf16[4,64,1024]{2,1,0:T(8,128)(2,1)S(1)} custom-call(bf16[2,64,1024]{2,1,0:T(8,128)(2,1)S(1)} %collective-permute-done.refs_0_, bf16[2,64,1024]{2,1,0:T(8,128)(2,1)S(1)} %collective-permute-done.1.refs_1_, bf16[2,64,1024]{2,1,0:T(8,128)(2,1)S(1)} %collective-permute-done.2.refs_2_, bf16[2,64,1024]{2,1,0:T(8,128)(2,1)S(1)} %collective-permute-done.3.refs_3_, ...), custom_call_target="tpu_custom_call" | custom-call | flops 1073741824 | bytes 5767168 | tf_op jit(solution)/shard_map/mix/pallas_call | solution.py:137
  45.1 2.0 %mix.9 = bf16[4,64,512]{2,1,0:T(8,128)(2,1)S(1)} custom-call(bf16[2,64,1024]{2,1,0:T(8,128)(2,1)S(1)} %collective-permute-done.refs_0_, bf16[2,64,1024]{2,1,0:T(8,128)(2,1)S(1)} %collective-permute-done.1.refs_1_, bf16[2,64,1024]{2,1,0:T(8,128)(2,1)S(1)} %collective-permute-done.2.refs_2_, bf16[2,64,1024]{2,1,0:T(8,128)(2,1)S(1)} %collective-permute-done.3.refs_3_, ...), custom_call_target="tpu_custom_call" | custom-call | flops 536870912 | bytes 3407872 | tf_op jit(solution)/shard_map/mix/pallas_call | solution.py:137
  47.5 1.7 %collective-permute-start.12 = (bf16[4,64,1024]{2,1,0:T(8,128)(2,1)S(1)}, bf16[4,64,1024]{2,1,0:T(8,128)(2,1)S(1)}, u32[]{:S(2)}, u32[]{:S(2)}) collective-permute-start(bf16[4,64,1024]{2,1,0:T(8,128)(2,1)S(1)} %mix.8), channel_id=1, source_target_pairs={{0,2},{2,0},{1,3},{3,1},{4,6},{6,4},{5,7},{7,5},{8,10},{10,8},{9,1... | collective-permute-start | bytes 1572872 | tf_op jit(solution)/shard_map/ppermute | solution.py:155
  49.2 4.0 %collective-permute-done.6.refs_2_ = bf16[2,64,1024]{2,1,0:T(8,128)(2,1)S(1)} collective-permute-done((bf16[2,64,1024]{2,1,0:T(8,128)(2,1)S(1)}, bf16[2,64,1024]{2,1,0:T(8,128)(2,1)S(1)}, u32[]{:S(2)}, u32[]{:S(2)}) %collective-permute-start.6) | collective-permute-done | bytes 262176 | tf_op jit(solution)/shard_map/ppermute | solution.py:160
  54.7 5.0 %mix.10 = bf16[4,64,2048]{2,1,0:T(8,128)(2,1)S(1)} custom-call(bf16[2,64,1024]{2,1,0:T(8,128)(2,1)S(1)} %get-tuple-element.41.refs_0_, bf16[2,64,1024]{2,1,0:T(8,128)(2,1)S(1)} %collective-permute-done.5.refs_1_, bf16[2,64,1024]{2,1,0:T(8,128)(2,1)S(1)} %collective-permute-done.6.refs_2_, bf16[2,64,1024]{2,1,0:T(8,128)(2,1)S(1)} %collective-permute-done.7.refs_3_, ...), custom_call_target="tpu_custom_call" | custom-call | flops 2147483648 | bytes 10485760 | tf_op jit(solution)/shard_map/mix/pallas_call | solution.py:137
  60.0 4.1 %mix.11 = bf16[4,64,1536]{2,1,0:T(8,128)(2,1)S(1)} custom-call(bf16[2,64,1024]{2,1,0:T(8,128)(2,1)S(1)} %get-tuple-element.41.refs_0_, bf16[2,64,1024]{2,1,0:T(8,128)(2,1)S(1)} %collective-permute-done.5.refs_1_, bf16[2,64,1024]{2,1,0:T(8,128)(2,1)S(1)} %collective-permute-done.6.refs_2_, bf16[2,64,1024]{2,1,0:T(8,128)(2,1)S(1)} %collective-permute-done.7.refs_3_, ...), custom_call_target="tpu_custom_call" | custom-call | flops 1610612736 | bytes 8126464 | tf_op jit(solution)/shard_map/mix/pallas_call | solution.py:137
  64.1 3.5 %collective-permute-start.10 = (bf16[2,64,1024]{2,1,0:T(8,128)(2,1)S(1)}, bf16[2,64,1024]{2,1,0:T(8,128)(2,1)S(1)}, u32[]{:S(2)}, u32[]{:S(2)}) collective-permute-start(bf16[2,64,1024]{2,1,0:T(8,128)(2,1)S(1)} %slice.71), channel_id=1, source_target_pairs={{0,4},{4,0},{8,12},{12,8},{1,5},{5,1},{9,13},{13,9},{2,6},{6,2},{1... | collective-permute-start | bytes 786440 | tf_op jit(solution)/shard_map/ppermute | solution.py:155
  67.7 11.1 %collective-permute-done.9 = bf16[4,64,1024]{2,1,0:T(8,128)(2,1)S(1)} collective-permute-done((bf16[4,64,1024]{2,1,0:T(8,128)(2,1)S(1)}, bf16[4,64,1024]{2,1,0:T(8,128)(2,1)S(1)}, u32[]{:S(2)}, u32[]{:S(2)}) %collective-permute-start.9) | collective-permute-done | bytes 524320 | tf_op jit(solution)/shard_map/ppermute | solution.py:155
  80.0 3.5 %collective-permute-start.11 = (bf16[64,1024]{1,0:T(8,128)(2,1)S(1)}, bf16[64,1024]{1,0:T(8,128)(2,1)S(1)}, u32[]{:S(2)}, u32[]{:S(2)}) collective-permute-start(bf16[64,1024]{1,0:T(8,128)(2,1)S(1)} %fusion.6), channel_id=1, source_target_pairs={{0,8},{4,12},{8,0},{12,4},{1,9},{5,13},{9,1},{13,5},{2,10},{6,14},... | collective-permute-start | bytes 393224 | tf_op jit(solution)/shard_map/ppermute | solution.py:155
  83.8 4.7 %collective-permute-done.13 = bf16[2,64,1024]{2,1,0:T(8,128)(2,1)S(1)} collective-permute-done((bf16[2,64,1024]{2,1,0:T(8,128)(2,1)S(1)}, bf16[2,64,1024]{2,1,0:T(8,128)(2,1)S(1)}, u32[]{:S(2)}, u32[]{:S(2)}) %collective-permute-start.13) | collective-permute-done | bytes 262176 | tf_op jit(solution)/shard_map/ppermute | solution.py:155
  90.1 2.5 %collective-permute-start.18 = (bf16[2,64,512]{2,1,0:T(8,128)(2,1)S(1)}, bf16[2,64,512]{2,1,0:T(8,128)(2,1)S(1)}, u32[]{:S(2)}, u32[]{:S(2)}) collective-permute-start(bf16[2,64,512]{2,1,0:T(8,128)(2,1)S(1)} %slice.85), channel_id=1, source_target_pairs={{0,4},{4,0},{8,12},{12,8},{1,5},{5,1},{9,13},{13,9},{2,6},{6,2},{1... | collective-permute-start | bytes 393224 | tf_op jit(solution)/shard_map/ppermute | solution.py:155
  92.8 2.7 %collective-permute-done.14 = bf16[64,1024]{1,0:T(8,128)(2,1)S(1)} collective-permute-done((bf16[64,1024]{1,0:T(8,128)(2,1)S(1)}, bf16[64,1024]{1,0:T(8,128)(2,1)S(1)}, u32[]{:S(2)}, u32[]{:S(2)}) %collective-permute-start.14) | collective-permute-done | bytes 131104 | tf_op jit(solution)/shard_map/ppermute | solution.py:155
  95.6 6.0 %collective-permute-done.16 = bf16[2,64,1024]{2,1,0:T(8,128)(2,1)S(1)} collective-permute-done((bf16[2,64,1024]{2,1,0:T(8,128)(2,1)S(1)}, bf16[2,64,1024]{2,1,0:T(8,128)(2,1)S(1)}, u32[]{:S(2)}, u32[]{:S(2)}) %collective-permute-start.16) | collective-permute-done | bytes 262176 | tf_op jit(solution)/shard_map/ppermute | solution.py:155
  103.3 1.5 %collective-permute-start.17 = (bf16[64,1024]{1,0:T(8,128)(2,1)S(1)}, bf16[64,1024]{1,0:T(8,128)(2,1)S(1)}, u32[]{:S(2)}, u32[]{:S(2)}) collective-permute-start(bf16[64,1024]{1,0:T(8,128)(2,1)S(1)} %fusion.8), channel_id=1, source_target_pairs={{0,8},{4,12},{8,0},{12,4},{1,9},{5,13},{9,1},{13,5},{2,10},{6,14},... | collective-permute-start | bytes 393224 | tf_op jit(solution)/shard_map/ppermute | solution.py:155
  104.8 6.4 %collective-permute-done.19 = bf16[64,512]{1,0:T(8,128)(2,1)S(1)} collective-permute-done((bf16[64,512]{1,0:T(8,128)(2,1)S(1)}, bf16[64,512]{1,0:T(8,128)(2,1)S(1)}, u32[]{:S(2)}, u32[]{:S(2)}) %collective-permute-start.19) | collective-permute-done | bytes 65568 | tf_op jit(solution)/shard_map/ppermute | solution.py:155
  (62 shorter events, 14.1 us)
Async XLA Ops:
  0.0 34.8 %collective-permute-start.4 = (bf16[1024,3584]{1,0:T(8,128)(2,1)}, bf16[1024,3584]{1,0:T(8,128)(2,1)}, u32[]{:S(2)}, u32[]{:S(2)}) collective-permute-start(bf16[1024,3584]{1,0:T(8,128)(2,1)} %bitcast.37), channel_id=1, source_target_pairs={{0,1},{1,0},{2,3},{3,2},{4,5},{5,4},{6,7},{7,6},{8,9},{9,8},{10,11... | collective-permute-start | bytes 22020104 | tf_op jit(solution)/shard_map/ppermute | solution.py:155
  0.5 1.2 %copy-start.2 = (bf16[64,8,1024]{2,1,0:T(8,128)(2,1)S(1)}, bf16[64,8,1024]{2,1,0:T(8,128)(2,1)}, u32[]{:S(2)}) copy-start(bf16[64,8,1024]{2,1,0:T(8,128)(2,1)} %param.4) | copy-start | bytes 3145732
  1.7 0.7 copy-start.3
  4.0 26.4 %collective-permute-start = (bf16[2,64,1024]{2,1,0:T(8,128)(2,1)S(1)}, bf16[2,64,1024]{2,1,0:T(8,128)(2,1)S(1)}, u32[]{:S(2)}, u32[]{:S(2)}) collective-permute-start(bf16[2,64,1024]{2,1,0:T(8,128)(2,1)S(1)} %get-tuple-element.28), channel_id=1, source_target_pairs={{0,2},{2,0},{4,6},{6,4},{8,10},{10,8},{12,14},{14,12},{1,3},{3,1},... | collective-permute-start | bytes 786440 | tf_op jit(solution)/shard_map/ppermute | solution.py:160
  6.5 23.8 %collective-permute-start.1 = (bf16[2,64,1024]{2,1,0:T(8,128)(2,1)S(1)}, bf16[2,64,1024]{2,1,0:T(8,128)(2,1)S(1)}, u32[]{:S(2)}, u32[]{:S(2)}) collective-permute-start(bf16[2,64,1024]{2,1,0:T(8,128)(2,1)S(1)} %get-tuple-element.30), channel_id=1, source_target_pairs={{0,6},{2,4},{4,2},{6,0},{8,14},{10,12},{12,10},{14,8},{1,7},{3,5},... | collective-permute-start | bytes 786440 | tf_op jit(solution)/shard_map/ppermute | solution.py:160
  8.1 26.7 %collective-permute-start.2 = (bf16[2,64,1024]{2,1,0:T(8,128)(2,1)S(1)}, bf16[2,64,1024]{2,1,0:T(8,128)(2,1)S(1)}, u32[]{:S(2)}, u32[]{:S(2)}) collective-permute-start(bf16[2,64,1024]{2,1,0:T(8,128)(2,1)S(1)} %get-tuple-element.31), channel_id=1, source_target_pairs={{0,10},{2,8},{4,14},{6,12},{8,2},{10,0},{12,6},{14,4},{1,11},{3,9}... | collective-permute-start | bytes 786440 | tf_op jit(solution)/shard_map/ppermute | solution.py:160
  11.6 23.2 %collective-permute-start.3 = (bf16[2,64,1024]{2,1,0:T(8,128)(2,1)S(1)}, bf16[2,64,1024]{2,1,0:T(8,128)(2,1)S(1)}, u32[]{:S(2)}, u32[]{:S(2)}) collective-permute-start(bf16[2,64,1024]{2,1,0:T(8,128)(2,1)S(1)} %get-tuple-element.32), channel_id=1, source_target_pairs={{0,14},{2,12},{4,10},{6,8},{8,6},{10,4},{12,2},{14,0},{1,15},{3,13... | collective-permute-start | bytes 786440 | tf_op jit(solution)/shard_map/ppermute | solution.py:160
  11.6 3.1 %copy-start = (bf16[1,1024,3584]{2,1,0:T(8,128)(2,1)S(1)}, bf16[1,1024,3584]{2,1,0:T(8,128)(2,1)}, u32[]{:S(2)}) copy-start(bf16[1,1024,3584]{2,1,0:T(8,128)(2,1)} %param.7) | copy-start | bytes 22020100
  14.7 20.1 %copy-start.1 = (bf16[1,1024,3584]{2,1,0:T(8,128)(2,1)S(1)}, bf16[1,1024,3584]{2,1,0:T(8,128)(2,1)}, u32[]{:S(2)}) copy-start(bf16[1,1024,3584]{2,1,0:T(8,128)(2,1)} %param.7) | copy-start | bytes 22020100
  30.3 17.1 %collective-permute-start.5 = (bf16[2,64,1024]{2,1,0:T(8,128)(2,1)S(1)}, bf16[2,64,1024]{2,1,0:T(8,128)(2,1)S(1)}, u32[]{:S(2)}, u32[]{:S(2)}) collective-permute-start(bf16[2,64,1024]{2,1,0:T(8,128)(2,1)S(1)} %get-tuple-element.37), channel_id=1, source_target_pairs={{0,4},{2,6},{4,0},{6,2},{8,12},{10,14},{12,8},{14,10},{1,5},{3,7},... | collective-permute-start | bytes 786440 | tf_op jit(solution)/shard_map/ppermute | solution.py:160
  30.3 22.8 %collective-permute-start.6 = (bf16[2,64,1024]{2,1,0:T(8,128)(2,1)S(1)}, bf16[2,64,1024]{2,1,0:T(8,128)(2,1)S(1)}, u32[]{:S(2)}, u32[]{:S(2)}) collective-permute-start(bf16[2,64,1024]{2,1,0:T(8,128)(2,1)S(1)} %get-tuple-element.38), channel_id=1, source_target_pairs={{0,8},{2,10},{4,12},{6,14},{8,0},{10,2},{12,4},{14,6},{1,9},{3,11}... | collective-permute-start | bytes 786440 | tf_op jit(solution)/shard_map/ppermute | solution.py:160
  34.8 19.9 %collective-permute-start.7 = (bf16[2,64,1024]{2,1,0:T(8,128)(2,1)S(1)}, bf16[2,64,1024]{2,1,0:T(8,128)(2,1)S(1)}, u32[]{:S(2)}, u32[]{:S(2)}) collective-permute-start(bf16[2,64,1024]{2,1,0:T(8,128)(2,1)S(1)} %get-tuple-element.39), channel_id=1, source_target_pairs={{0,12},{2,14},{4,8},{6,10},{8,4},{10,6},{12,0},{14,2},{1,13},{3,15... | collective-permute-start | bytes 786440 | tf_op jit(solution)/shard_map/ppermute | solution.py:160
  37.6 22.1 %collective-permute-start.8 = (bf16[4,64,1024]{2,1,0:T(8,128)(2,1)S(1)}, bf16[4,64,1024]{2,1,0:T(8,128)(2,1)S(1)}, u32[]{:S(2)}, u32[]{:S(2)}) collective-permute-start(bf16[4,64,1024]{2,1,0:T(8,128)(2,1)S(1)} %mix.6), channel_id=1, source_target_pairs={{0,2},{2,0},{1,3},{3,1},{4,6},{6,4},{5,7},{7,5},{8,10},{10,8},{9,1... | collective-permute-start | bytes 1572872 | tf_op jit(solution)/shard_map/ppermute | solution.py:155
  47.1 43.0 %collective-permute-start.15 = (bf16[4,64,512]{2,1,0:T(8,128)(2,1)S(1)}, bf16[4,64,512]{2,1,0:T(8,128)(2,1)S(1)}, u32[]{:S(2)}, u32[]{:S(2)}) collective-permute-start(bf16[4,64,512]{2,1,0:T(8,128)(2,1)S(1)} %mix.9), channel_id=1, source_target_pairs={{0,2},{2,0},{1,3},{3,1},{4,6},{6,4},{5,7},{7,5},{8,10},{10,8},{9,1... | collective-permute-start | bytes 786440 | tf_op jit(solution)/shard_map/ppermute | solution.py:155
  47.5 36.0 %collective-permute-start.12 = (bf16[4,64,1024]{2,1,0:T(8,128)(2,1)S(1)}, bf16[4,64,1024]{2,1,0:T(8,128)(2,1)S(1)}, u32[]{:S(2)}, u32[]{:S(2)}) collective-permute-start(bf16[4,64,1024]{2,1,0:T(8,128)(2,1)S(1)} %mix.8), channel_id=1, source_target_pairs={{0,2},{2,0},{1,3},{3,1},{4,6},{6,4},{5,7},{7,5},{8,10},{10,8},{9,1... | collective-permute-start | bytes 1572872 | tf_op jit(solution)/shard_map/ppermute | solution.py:155
  53.2 25.6 %collective-permute-start.9 = (bf16[4,64,1024]{2,1,0:T(8,128)(2,1)S(1)}, bf16[4,64,1024]{2,1,0:T(8,128)(2,1)S(1)}, u32[]{:S(2)}, u32[]{:S(2)}) collective-permute-start(bf16[4,64,1024]{2,1,0:T(8,128)(2,1)S(1)} %mix.7), channel_id=1, source_target_pairs={{0,2},{2,0},{1,3},{3,1},{4,6},{6,4},{5,7},{7,5},{8,10},{10,8},{9,1... | collective-permute-start | bytes 1572872 | tf_op jit(solution)/shard_map/ppermute | solution.py:155
  64.1 15.8 %collective-permute-start.10 = (bf16[2,64,1024]{2,1,0:T(8,128)(2,1)S(1)}, bf16[2,64,1024]{2,1,0:T(8,128)(2,1)S(1)}, u32[]{:S(2)}, u32[]{:S(2)}) collective-permute-start(bf16[2,64,1024]{2,1,0:T(8,128)(2,1)S(1)} %slice.71), channel_id=1, source_target_pairs={{0,4},{4,0},{8,12},{12,8},{1,5},{5,1},{9,13},{13,9},{2,6},{6,2},{1... | collective-permute-start | bytes 786440 | tf_op jit(solution)/shard_map/ppermute | solution.py:155
  79.2 9.3 %collective-permute-start.13 = (bf16[2,64,1024]{2,1,0:T(8,128)(2,1)S(1)}, bf16[2,64,1024]{2,1,0:T(8,128)(2,1)S(1)}, u32[]{:S(2)}, u32[]{:S(2)}) collective-permute-start(bf16[2,64,1024]{2,1,0:T(8,128)(2,1)S(1)} %slice.76), channel_id=1, source_target_pairs={{0,4},{4,0},{8,12},{12,8},{1,5},{5,1},{9,13},{13,9},{2,6},{6,2},{1... | collective-permute-start | bytes 786440 | tf_op jit(solution)/shard_map/ppermute | solution.py:155
  80.0 12.8 %collective-permute-start.11 = (bf16[64,1024]{1,0:T(8,128)(2,1)S(1)}, bf16[64,1024]{1,0:T(8,128)(2,1)S(1)}, u32[]{:S(2)}, u32[]{:S(2)}) collective-permute-start(bf16[64,1024]{1,0:T(8,128)(2,1)S(1)} %fusion.6), channel_id=1, source_target_pairs={{0,8},{4,12},{8,0},{12,4},{1,9},{5,13},{9,1},{13,5},{2,10},{6,14},... | collective-permute-start | bytes 393224 | tf_op jit(solution)/shard_map/ppermute | solution.py:155
  88.6 6.9 %collective-permute-start.14 = (bf16[64,1024]{1,0:T(8,128)(2,1)S(1)}, bf16[64,1024]{1,0:T(8,128)(2,1)S(1)}, u32[]{:S(2)}, u32[]{:S(2)}) collective-permute-start(bf16[64,1024]{1,0:T(8,128)(2,1)S(1)} %fusion.7), channel_id=1, source_target_pairs={{0,8},{4,12},{8,0},{12,4},{1,9},{5,13},{9,1},{13,5},{2,10},{6,14},... | collective-permute-start | bytes 393224 | tf_op jit(solution)/shard_map/ppermute | solution.py:155
  90.1 11.6 %collective-permute-start.18 = (bf16[2,64,512]{2,1,0:T(8,128)(2,1)S(1)}, bf16[2,64,512]{2,1,0:T(8,128)(2,1)S(1)}, u32[]{:S(2)}, u32[]{:S(2)}) collective-permute-start(bf16[2,64,512]{2,1,0:T(8,128)(2,1)S(1)} %slice.85), channel_id=1, source_target_pairs={{0,4},{4,0},{8,12},{12,8},{1,5},{5,1},{9,13},{13,9},{2,6},{6,2},{1... | collective-permute-start | bytes 393224 | tf_op jit(solution)/shard_map/ppermute | solution.py:155
  92.7 8.9 %collective-permute-start.16 = (bf16[2,64,1024]{2,1,0:T(8,128)(2,1)S(1)}, bf16[2,64,1024]{2,1,0:T(8,128)(2,1)S(1)}, u32[]{:S(2)}, u32[]{:S(2)}) collective-permute-start(bf16[2,64,1024]{2,1,0:T(8,128)(2,1)S(1)} %slice.81), channel_id=1, source_target_pairs={{0,4},{4,0},{8,12},{12,8},{1,5},{5,1},{9,13},{13,9},{2,6},{6,2},{1... | collective-permute-start | bytes 786440 | tf_op jit(solution)/shard_map/ppermute | solution.py:155
  101.8 9.5 %collective-permute-start.19 = (bf16[64,512]{1,0:T(8,128)(2,1)S(1)}, bf16[64,512]{1,0:T(8,128)(2,1)S(1)}, u32[]{:S(2)}, u32[]{:S(2)}) collective-permute-start(bf16[64,512]{1,0:T(8,128)(2,1)S(1)} %fusion.11), channel_id=1, source_target_pairs={{0,8},{4,12},{8,0},{12,4},{1,9},{5,13},{9,1},{13,5},{2,10},{6,14},... | collective-permute-start | bytes 196616 | tf_op jit(solution)/shard_map/ppermute | solution.py:155
  103.3 9.3 %collective-permute-start.17 = (bf16[64,1024]{1,0:T(8,128)(2,1)S(1)}, bf16[64,1024]{1,0:T(8,128)(2,1)S(1)}, u32[]{:S(2)}, u32[]{:S(2)}) collective-permute-start(bf16[64,1024]{1,0:T(8,128)(2,1)S(1)} %fusion.8), channel_id=1, source_target_pairs={{0,8},{4,12},{8,0},{12,4},{1,9},{5,13},{9,1},{13,5},{2,10},{6,14},... | collective-permute-start | bytes 393224 | tf_op jit(solution)/shard_map/ppermute | solution.py:155
  (1 other events, 0.7 us)

commit v6 on v5

--- a/solution.py
+++ b/solution.py
@@ -9,7 +9,7 @@
 
 CHIPS = 8
 TILE = 512
-COLUMNS = ((0, 1024), (1024, 1024), (2048, 1024), (3072, 512))
+COLUMNS = ((0, 1024), (1024, 1536), (2560, 512), (3072, 512))
 
 
 def passed_along(block, axis, distance):
@@ -106,6 +106,7 @@
         out_specs=[vmem] * len(relatives),
         out_shape=[block] * len(relatives),
         compiler_params=pltpu.CompilerParams(vmem_limit_bytes=24 << 20),
+        cost_estimate=pl.CostEstimate(flops=0, bytes_accessed=0, transcendentals=0),
         name="spread_rows",
     )(
         own.reshape(1),
@@ -142,11 +143,7 @@
         out_shape=jax.ShapeDtypeStruct((len(rows), tokens, width), jnp.bfloat16),
         scratch_shapes=[pltpu.VMEM((2, len(rows) * tokens, depth), jnp.bfloat16)],
         compiler_params=pltpu.CompilerParams(vmem_limit_bytes=24 << 20),
-        cost_estimate=pl.CostEstimate(
-            flops=4 * len(rows) * tokens * depth * width,
-            bytes_accessed=4 * depth * width + 2 * len(rows) * tokens * (2 * depth + width),
-            transcendentals=0,
-        ),
+        cost_estimate=pl.CostEstimate(flops=4 * len(rows) * tokens * depth * width, bytes_accessed=4 * depth * width, transcendentals=0),
         name="mix",
     )(*rows, near, far)
 
@@ -204,10 +201,13 @@
         pairs.append((pair[0], swap(pair[1].astype(jnp.bfloat16), "z", 2)))
         return pair
 
-    last = mix_even((0, 1))
+    last = mix_even((0,))
     last = add_x(0, last)
+    last = mix_even((1,))
+    last = add_x(1, last)
     last = mix_even((2, 3))
-    for i in range(1, len(COLUMNS)):
+    last = add_z(0, last)
+    for i in range(2, len(COLUMNS)):
         last = add_x(i, last)
         last = add_z(i - 1, last)
     add_z(len(COLUMNS) - 1, last)

time: 114 us -> 107 us (0.939)
  waiting for transfers between devices: 51.2 us -> 43.7 us
    ppermute x13, waiting for transfers between devices: 32.4 us -> 20.3 us  [swap(): lax.ppermute(block, axis, [(i, i ^ distance) for i in range(lax.axis_size...]
    ppermute x7, waiting for transfers between devices: 18.8 us -> 23.4 us  [send_to_chip(): lax.ppermute(block, ('z', 'x'), [(i, i ^ relative) for i in range(sizes[0...]
    ppermute x13, starting transfers between devices: 20.6 us -> 17.4 us  [swap(): lax.ppermute(block, axis, [(i, i ^ distance) for i in range(lax.axis_size...]
    ppermute x7, starting transfers between devices: 12 us -> 14.9 us  [send_to_chip(): lax.ppermute(block, ('z', 'x'), [(i, i ^ relative) for i in range(sizes[0...]
    pallas_call x6 -> x7, Pallas kernels: 19.6 us -> 20.7 us  [mix(): pl.pallas_call(mix_kernel, grid=(width // TILE,), in_specs=[whole] * len(...]
  transfers between devices with their start and end apart: 20 -> 20, of which waited for: 8 -> 8; matrix products, arithmetic and copies ran while one was open for 1% -> 1% of each run, Pallas kernels for 19% -> 18%
where the time goes in v6:
time: 107 us
  waiting for transfers between devices  43.7 us (41%)
  starting transfers between devices  32.3 us (30%)
  Pallas kernels  22.5 us (21%)
  local copies, waits for them, and re-layouts  5.97 us (6%)
  other arithmetic  1.79 us (2%)
    ppermute x7, waiting for transfers between devices, send_to_chip(): lax.ppermute(block, ('z', 'x'), [(i, i ^ relative) for i in range(sizes[0...  23.4 us
    pallas_call x7, Pallas kernels, mix(): pl.pallas_call(mix_kernel, grid=(width // TILE,), in_specs=[whole] * len(...  20.7 us
    ppermute x13, waiting for transfers between devices, swap(): lax.ppermute(block, axis, [(i, i ^ distance) for i in range(lax.axis_size...  20.3 us
    ppermute x13, starting transfers between devices, swap(): lax.ppermute(block, axis, [(i, i ^ distance) for i in range(lax.axis_size...  17.4 us
    ppermute x7, starting transfers between devices, send_to_chip(): lax.ppermute(block, ('z', 'x'), [(i, i ^ relative) for i in range(sizes[0...  14.9 us
    unnamed x10, local copies, waits for them, and re-layouts  5.68 us
  transfers between devices with their start and end apart: 20, of which 8 were waited for; matrix products, arithmetic and copies ran while one was open for 1% of the time, Pallas kernels for 18%

profile of v6, /device:TPU:0, one launch (start us, length us, event | category | flops | bytes accessed | tf_op | source)
XLA Modules:
  0.0 106.5 jit_solution(8717793709435085406)
XLA Ops:
  4.0 2.5 %collective-permute-start = (bf16[2,64,1024]{2,1,0:T(8,128)(2,1)S(1)}, bf16[2,64,1024]{2,1,0:T(8,128)(2,1)S(1)}, u32[]{:S(2)}, u32[]{:S(2)}) collective-permute-start(bf16[2,64,1024]{2,1,0:T(8,128)(2,1)S(1)} %get-tuple-element.27), channel_id=1, source_target_pairs={{0,2},{2,0},{4,6},{6,4},{8,10},{10,8},{12,14},{14,12},{1,3},{3,1},... | collective-permute-start | bytes 786440 | tf_op jit(solution)/shard_map/ppermute | solution.py:157
  6.5 1.5 %collective-permute-start.1 = (bf16[2,64,1024]{2,1,0:T(8,128)(2,1)S(1)}, bf16[2,64,1024]{2,1,0:T(8,128)(2,1)S(1)}, u32[]{:S(2)}, u32[]{:S(2)}) collective-permute-start(bf16[2,64,1024]{2,1,0:T(8,128)(2,1)S(1)} %get-tuple-element.29), channel_id=1, source_target_pairs={{0,6},{2,4},{4,2},{6,0},{8,14},{10,12},{12,10},{14,8},{1,7},{3,5},... | collective-permute-start | bytes 786440 | tf_op jit(solution)/shard_map/ppermute | solution.py:157
  8.1 3.5 %collective-permute-start.2 = (bf16[2,64,1024]{2,1,0:T(8,128)(2,1)S(1)}, bf16[2,64,1024]{2,1,0:T(8,128)(2,1)S(1)}, u32[]{:S(2)}, u32[]{:S(2)}) collective-permute-start(bf16[2,64,1024]{2,1,0:T(8,128)(2,1)S(1)} %get-tuple-element.30), channel_id=1, source_target_pairs={{0,10},{2,8},{4,14},{6,12},{8,2},{10,0},{12,6},{14,4},{1,11},{3,9}... | collective-permute-start | bytes 786440 | tf_op jit(solution)/shard_map/ppermute | solution.py:157
  11.6 3.1 %copy-done = bf16[1,1024,3584]{2,1,0:T(8,128)(2,1)S(1)} copy-done((bf16[1,1024,3584]{2,1,0:T(8,128)(2,1)S(1)}, bf16[1,1024,3584]{2,1,0:T(8,128)(2,1)}, u32[]{:S(2)}) %copy-start) | copy-done | bytes 7340056
  15.6 14.8 %collective-permute-done.refs_0_ = bf16[2,64,1024]{2,1,0:T(8,128)(2,1)S(1)} collective-permute-done((bf16[2,64,1024]{2,1,0:T(8,128)(2,1)S(1)}, bf16[2,64,1024]{2,1,0:T(8,128)(2,1)S(1)}, u32[]{:S(2)}, u32[]{:S(2)}) %collective-permute-start) | collective-permute-done | bytes 262176 | tf_op jit(solution)/shard_map/ppermute | solution.py:157
  30.4 2.8 %mix.7 = bf16[4,64,1024]{2,1,0:T(8,128)(2,1)S(1)} custom-call(bf16[2,64,1024]{2,1,0:T(8,128)(2,1)S(1)} %collective-permute-done.refs_0_, bf16[2,64,1024]{2,1,0:T(8,128)(2,1)S(1)} %collective-permute-done.1.refs_1_, bf16[2,64,1024]{2,1,0:T(8,128)(2,1)S(1)} %collective-permute-done.2.refs_2_, bf16[2,64,1024]{2,1,0:T(8,128)(2,1)S(1)} %collective-permute-done.3.refs_3_, ...), custom_call_target="tpu_custom_call" | custom-call | flops 1073741824 | bytes 4194304 | tf_op jit(solution)/shard_map/mix/pallas_call | solution.py:138
  33.2 1.8 %collective-permute-start.8 = (bf16[4,64,1024]{2,1,0:T(8,128)(2,1)S(1)}, bf16[4,64,1024]{2,1,0:T(8,128)(2,1)S(1)}, u32[]{:S(2)}, u32[]{:S(2)}) collective-permute-start(bf16[4,64,1024]{2,1,0:T(8,128)(2,1)S(1)} %mix.7), channel_id=1, source_target_pairs={{0,2},{2,0},{1,3},{3,1},{4,6},{6,4},{5,7},{7,5},{8,10},{10,8},{9,1... | collective-permute-start | bytes 1572872 | tf_op jit(solution)/shard_map/ppermute | solution.py:152
  35.0 4.8 %collective-permute-start.5 = (bf16[2,64,1024]{2,1,0:T(8,128)(2,1)S(1)}, bf16[2,64,1024]{2,1,0:T(8,128)(2,1)S(1)}, u32[]{:S(2)}, u32[]{:S(2)}) collective-permute-start(bf16[2,64,1024]{2,1,0:T(8,128)(2,1)S(1)} %get-tuple-element.36), channel_id=1, source_target_pairs={{0,4},{2,6},{4,0},{6,2},{8,12},{10,14},{12,8},{14,10},{1,5},{3,7},... | collective-permute-start | bytes 786440 | tf_op jit(solution)/shard_map/ppermute | solution.py:157
  42.4 4.1 %mix.8 = bf16[4,64,1536]{2,1,0:T(8,128)(2,1)S(1)} custom-call(bf16[2,64,1024]{2,1,0:T(8,128)(2,1)S(1)} %collective-permute-done.refs_0_, bf16[2,64,1024]{2,1,0:T(8,128)(2,1)S(1)} %collective-permute-done.1.refs_1_, bf16[2,64,1024]{2,1,0:T(8,128)(2,1)S(1)} %collective-permute-done.2.refs_2_, bf16[2,64,1024]{2,1,0:T(8,128)(2,1)S(1)} %collective-permute-done.3.refs_3_, ...), custom_call_target="tpu_custom_call" | custom-call | flops 1610612736 | bytes 6291456 | tf_op jit(solution)/shard_map/mix/pallas_call | solution.py:138
  47.1 2.0 %mix.9 = bf16[4,64,512]{2,1,0:T(8,128)(2,1)S(1)} custom-call(bf16[2,64,1024]{2,1,0:T(8,128)(2,1)S(1)} %collective-permute-done.refs_0_, bf16[2,64,1024]{2,1,0:T(8,128)(2,1)S(1)} %collective-permute-done.1.refs_1_, bf16[2,64,1024]{2,1,0:T(8,128)(2,1)S(1)} %collective-permute-done.2.refs_2_, bf16[2,64,1024]{2,1,0:T(8,128)(2,1)S(1)} %collective-permute-done.3.refs_3_, ...), custom_call_target="tpu_custom_call" | custom-call | flops 536870912 | bytes 2097152 | tf_op jit(solution)/shard_map/mix/pallas_call | solution.py:138
  49.1 2.0 %mix.10 = bf16[4,64,512]{2,1,0:T(8,128)(2,1)S(1)} custom-call(bf16[2,64,1024]{2,1,0:T(8,128)(2,1)S(1)} %collective-permute-done.refs_0_, bf16[2,64,1024]{2,1,0:T(8,128)(2,1)S(1)} %collective-permute-done.1.refs_1_, bf16[2,64,1024]{2,1,0:T(8,128)(2,1)S(1)} %collective-permute-done.2.refs_2_, bf16[2,64,1024]{2,1,0:T(8,128)(2,1)S(1)} %collective-permute-done.3.refs_3_, ...), custom_call_target="tpu_custom_call" | custom-call | flops 536870912 | bytes 2097152 | tf_op jit(solution)/shard_map/mix/pallas_call | solution.py:138
  51.1 1.6 %collective-permute-start.15 = (bf16[4,64,512]{2,1,0:T(8,128)(2,1)S(1)}, bf16[4,64,512]{2,1,0:T(8,128)(2,1)S(1)}, u32[]{:S(2)}, u32[]{:S(2)}) collective-permute-start(bf16[4,64,512]{2,1,0:T(8,128)(2,1)S(1)} %mix.10), channel_id=1, source_target_pairs={{0,2},{2,0},{1,3},{3,1},{4,6},{6,4},{5,7},{7,5},{8,10},{10,8},{9,1... | collective-permute-start | bytes 786440 | tf_op jit(solution)/shard_map/ppermute | solution.py:152
  52.6 8.6 %collective-permute-done.6.refs_2_ = bf16[2,64,1024]{2,1,0:T(8,128)(2,1)S(1)} collective-permute-done((bf16[2,64,1024]{2,1,0:T(8,128)(2,1)S(1)}, bf16[2,64,1024]{2,1,0:T(8,128)(2,1)S(1)}, u32[]{:S(2)}, u32[]{:S(2)}) %collective-permute-start.6) | collective-permute-done | bytes 262176 | tf_op jit(solution)/shard_map/ppermute | solution.py:157
  61.8 2.8 %mix.11 = bf16[4,64,1024]{2,1,0:T(8,128)(2,1)S(1)} custom-call(bf16[2,64,1024]{2,1,0:T(8,128)(2,1)S(1)} %get-tuple-element.40.refs_0_, bf16[2,64,1024]{2,1,0:T(8,128)(2,1)S(1)} %collective-permute-done.5.refs_1_, bf16[2,64,1024]{2,1,0:T(8,128)(2,1)S(1)} %collective-permute-done.6.refs_2_, bf16[2,64,1024]{2,1,0:T(8,128)(2,1)S(1)} %collective-permute-done.7.refs_3_, ...), custom_call_target="tpu_custom_call" | custom-call | flops 1073741824 | bytes 4194304 | tf_op jit(solution)/shard_map/mix/pallas_call | solution.py:138
  64.9 3.3 %collective-permute-start.10 = (bf16[2,64,1024]{2,1,0:T(8,128)(2,1)S(1)}, bf16[2,64,1024]{2,1,0:T(8,128)(2,1)S(1)}, u32[]{:S(2)}, u32[]{:S(2)}) collective-permute-start(bf16[2,64,1024]{2,1,0:T(8,128)(2,1)S(1)} %slice.63), channel_id=1, source_target_pairs={{0,4},{4,0},{8,12},{12,8},{1,5},{5,1},{9,13},{13,9},{2,6},{6,2},{1... | collective-permute-start | bytes 786440 | tf_op jit(solution)/shard_map/ppermute | solution.py:152
  68.2 4.1 %mix.12 = bf16[4,64,1536]{2,1,0:T(8,128)(2,1)S(1)} custom-call(bf16[2,64,1024]{2,1,0:T(8,128)(2,1)S(1)} %get-tuple-element.40.refs_0_, bf16[2,64,1024]{2,1,0:T(8,128)(2,1)S(1)} %collective-permute-done.5.refs_1_, bf16[2,64,1024]{2,1,0:T(8,128)(2,1)S(1)} %collective-permute-done.6.refs_2_, bf16[2,64,1024]{2,1,0:T(8,128)(2,1)S(1)} %collective-permute-done.7.refs_3_, ...), custom_call_target="tpu_custom_call" | custom-call | flops 1610612736 | bytes 6291456 | tf_op jit(solution)/shard_map/mix/pallas_call | solution.py:138
  72.6 2.8 %mix.13 = bf16[4,64,1024]{2,1,0:T(8,128)(2,1)S(1)} custom-call(bf16[2,64,1024]{2,1,0:T(8,128)(2,1)S(1)} %get-tuple-element.40.refs_0_, bf16[2,64,1024]{2,1,0:T(8,128)(2,1)S(1)} %collective-permute-done.5.refs_1_, bf16[2,64,1024]{2,1,0:T(8,128)(2,1)S(1)} %collective-permute-done.6.refs_2_, bf16[2,64,1024]{2,1,0:T(8,128)(2,1)S(1)} %collective-permute-done.7.refs_3_, ...), custom_call_target="tpu_custom_call" | custom-call | flops 1073741824 | bytes 4194304 | tf_op jit(solution)/shard_map/mix/pallas_call | solution.py:138
  76.8 2.0 %collective-permute-start.13 = (bf16[2,64,1536]{2,1,0:T(8,128)(2,1)S(1)}, bf16[2,64,1536]{2,1,0:T(8,128)(2,1)S(1)}, u32[]{:S(2)}, u32[]{:S(2)}) collective-permute-start(bf16[2,64,1536]{2,1,0:T(8,128)(2,1)S(1)} %slice.68), channel_id=1, source_target_pairs={{0,4},{4,0},{8,12},{12,8},{1,5},{5,1},{9,13},{13,9},{2,6},{6,2},{1... | collective-permute-start | bytes 1179656 | tf_op jit(solution)/shard_map/ppermute | solution.py:152
  79.6 3.3 %collective-permute-done.11 = bf16[64,1024]{1,0:T(8,128)(2,1)S(1)} collective-permute-done((bf16[64,1024]{1,0:T(8,128)(2,1)S(1)}, bf16[64,1024]{1,0:T(8,128)(2,1)S(1)}, u32[]{:S(2)}, u32[]{:S(2)}) %collective-permute-start.11) | collective-permute-done | bytes 131104 | tf_op jit(solution)/shard_map/ppermute | solution.py:152
  83.0 6.6 %collective-permute-done.13 = bf16[2,64,1536]{2,1,0:T(8,128)(2,1)S(1)} collective-permute-done((bf16[2,64,1536]{2,1,0:T(8,128)(2,1)S(1)}, bf16[2,64,1536]{2,1,0:T(8,128)(2,1)S(1)}, u32[]{:S(2)}, u32[]{:S(2)}) %collective-permute-start.13) | collective-permute-done | bytes 393248 | tf_op jit(solution)/shard_map/ppermute | solution.py:152
  91.4 2.7 %collective-permute-start.14 = (bf16[64,1536]{1,0:T(8,128)(2,1)S(1)}, bf16[64,1536]{1,0:T(8,128)(2,1)S(1)}, u32[]{:S(2)}, u32[]{:S(2)}) collective-permute-start(bf16[64,1536]{1,0:T(8,128)(2,1)S(1)} %fusion.4), channel_id=1, source_target_pairs={{0,8},{4,12},{8,0},{12,4},{1,9},{5,13},{9,1},{13,5},{2,10},{6,14},... | collective-permute-start | bytes 589832 | tf_op jit(solution)/shard_map/ppermute | solution.py:152
  94.5 5.9 %collective-permute-done.17 = bf16[64,512]{1,0:T(8,128)(2,1)S(1)} collective-permute-done((bf16[64,512]{1,0:T(8,128)(2,1)S(1)}, bf16[64,512]{1,0:T(8,128)(2,1)S(1)}, u32[]{:S(2)}, u32[]{:S(2)}) %collective-permute-start.17) | collective-permute-done | bytes 65568 | tf_op jit(solution)/shard_map/ppermute | solution.py:152
  100.5 1.9 %collective-permute-start.19 = (bf16[64,512]{1,0:T(8,128)(2,1)S(1)}, bf16[64,512]{1,0:T(8,128)(2,1)S(1)}, u32[]{:S(2)}, u32[]{:S(2)}) collective-permute-start(bf16[64,512]{1,0:T(8,128)(2,1)S(1)} %fusion.11), channel_id=1, source_target_pairs={{0,8},{4,12},{8,0},{12,4},{1,9},{5,13},{9,1},{13,5},{2,10},{6,14},... | collective-permute-start | bytes 196616 | tf_op jit(solution)/shard_map/ppermute | solution.py:152
  102.4 2.2 %collective-permute-done.14 = bf16[64,1536]{1,0:T(8,128)(2,1)S(1)} collective-permute-done((bf16[64,1536]{1,0:T(8,128)(2,1)S(1)}, bf16[64,1536]{1,0:T(8,128)(2,1)S(1)}, u32[]{:S(2)}, u32[]{:S(2)}) %collective-permute-start.14) | collective-permute-done | bytes 196640 | tf_op jit(solution)/shard_map/ppermute | solution.py:152
  (61 shorter events, 15.4 us)
Async XLA Ops:
  0.0 30.4 %collective-permute-start.4 = (bf16[1024,3584]{1,0:T(8,128)(2,1)}, bf16[1024,3584]{1,0:T(8,128)(2,1)}, u32[]{:S(2)}, u32[]{:S(2)}) collective-permute-start(bf16[1024,3584]{1,0:T(8,128)(2,1)} %bitcast.37), channel_id=1, source_target_pairs={{0,1},{1,0},{2,3},{3,2},{4,5},{5,4},{6,7},{7,6},{8,9},{9,8},{10,11... | collective-permute-start | bytes 22020104 | tf_op jit(solution)/shard_map/ppermute | solution.py:152
  0.5 1.2 %copy-start.2 = (bf16[64,8,1024]{2,1,0:T(8,128)(2,1)S(1)}, bf16[64,8,1024]{2,1,0:T(8,128)(2,1)}, u32[]{:S(2)}) copy-start(bf16[64,8,1024]{2,1,0:T(8,128)(2,1)} %param.4) | copy-start | bytes 3145732
  1.7 0.7 copy-start.3
  4.0 26.4 %collective-permute-start = (bf16[2,64,1024]{2,1,0:T(8,128)(2,1)S(1)}, bf16[2,64,1024]{2,1,0:T(8,128)(2,1)S(1)}, u32[]{:S(2)}, u32[]{:S(2)}) collective-permute-start(bf16[2,64,1024]{2,1,0:T(8,128)(2,1)S(1)} %get-tuple-element.27), channel_id=1, source_target_pairs={{0,2},{2,0},{4,6},{6,4},{8,10},{10,8},{12,14},{14,12},{1,3},{3,1},... | collective-permute-start | bytes 786440 | tf_op jit(solution)/shard_map/ppermute | solution.py:157
  6.5 23.8 %collective-permute-start.1 = (bf16[2,64,1024]{2,1,0:T(8,128)(2,1)S(1)}, bf16[2,64,1024]{2,1,0:T(8,128)(2,1)S(1)}, u32[]{:S(2)}, u32[]{:S(2)}) collective-permute-start(bf16[2,64,1024]{2,1,0:T(8,128)(2,1)S(1)} %get-tuple-element.29), channel_id=1, source_target_pairs={{0,6},{2,4},{4,2},{6,0},{8,14},{10,12},{12,10},{14,8},{1,7},{3,5},... | collective-permute-start | bytes 786440 | tf_op jit(solution)/shard_map/ppermute | solution.py:157
  8.1 22.3 %collective-permute-start.2 = (bf16[2,64,1024]{2,1,0:T(8,128)(2,1)S(1)}, bf16[2,64,1024]{2,1,0:T(8,128)(2,1)S(1)}, u32[]{:S(2)}, u32[]{:S(2)}) collective-permute-start(bf16[2,64,1024]{2,1,0:T(8,128)(2,1)S(1)} %get-tuple-element.30), channel_id=1, source_target_pairs={{0,10},{2,8},{4,14},{6,12},{8,2},{10,0},{12,6},{14,4},{1,11},{3,9}... | collective-permute-start | bytes 786440 | tf_op jit(solution)/shard_map/ppermute | solution.py:157
  11.6 18.8 %collective-permute-start.3 = (bf16[2,64,1024]{2,1,0:T(8,128)(2,1)S(1)}, bf16[2,64,1024]{2,1,0:T(8,128)(2,1)S(1)}, u32[]{:S(2)}, u32[]{:S(2)}) collective-permute-start(bf16[2,64,1024]{2,1,0:T(8,128)(2,1)S(1)} %get-tuple-element.31), channel_id=1, source_target_pairs={{0,14},{2,12},{4,10},{6,8},{8,6},{10,4},{12,2},{14,0},{1,15},{3,13... | collective-permute-start | bytes 786440 | tf_op jit(solution)/shard_map/ppermute | solution.py:157
  11.6 3.1 %copy-start = (bf16[1,1024,3584]{2,1,0:T(8,128)(2,1)S(1)}, bf16[1,1024,3584]{2,1,0:T(8,128)(2,1)}, u32[]{:S(2)}) copy-start(bf16[1,1024,3584]{2,1,0:T(8,128)(2,1)} %param.7) | copy-start | bytes 22020100
  14.7 15.7 %copy-start.1 = (bf16[1,1024,3584]{2,1,0:T(8,128)(2,1)S(1)}, bf16[1,1024,3584]{2,1,0:T(8,128)(2,1)}, u32[]{:S(2)}) copy-start(bf16[1,1024,3584]{2,1,0:T(8,128)(2,1)} %param.7) | copy-start | bytes 22020100
  33.2 31.4 %collective-permute-start.8 = (bf16[4,64,1024]{2,1,0:T(8,128)(2,1)S(1)}, bf16[4,64,1024]{2,1,0:T(8,128)(2,1)S(1)}, u32[]{:S(2)}, u32[]{:S(2)}) collective-permute-start(bf16[4,64,1024]{2,1,0:T(8,128)(2,1)S(1)} %mix.7), channel_id=1, source_target_pairs={{0,2},{2,0},{1,3},{3,1},{4,6},{6,4},{5,7},{7,5},{8,10},{10,8},{9,1... | collective-permute-start | bytes 1572872 | tf_op jit(solution)/shard_map/ppermute | solution.py:152
  35.0 16.0 %collective-permute-start.5 = (bf16[2,64,1024]{2,1,0:T(8,128)(2,1)S(1)}, bf16[2,64,1024]{2,1,0:T(8,128)(2,1)S(1)}, u32[]{:S(2)}, u32[]{:S(2)}) collective-permute-start(bf16[2,64,1024]{2,1,0:T(8,128)(2,1)S(1)} %get-tuple-element.36), channel_id=1, source_target_pairs={{0,4},{2,6},{4,0},{6,2},{8,12},{10,14},{12,8},{14,10},{1,5},{3,7},... | collective-permute-start | bytes 786440 | tf_op jit(solution)/shard_map/ppermute | solution.py:157
  39.9 21.4 %collective-permute-start.6 = (bf16[2,64,1024]{2,1,0:T(8,128)(2,1)S(1)}, bf16[2,64,1024]{2,1,0:T(8,128)(2,1)S(1)}, u32[]{:S(2)}, u32[]{:S(2)}) collective-permute-start(bf16[2,64,1024]{2,1,0:T(8,128)(2,1)S(1)} %get-tuple-element.37), channel_id=1, source_target_pairs={{0,8},{2,10},{4,12},{6,14},{8,0},{10,2},{12,4},{14,6},{1,9},{3,11}... | collective-permute-start | bytes 786440 | tf_op jit(solution)/shard_map/ppermute | solution.py:157
  40.9 20.9 %collective-permute-start.7 = (bf16[2,64,1024]{2,1,0:T(8,128)(2,1)S(1)}, bf16[2,64,1024]{2,1,0:T(8,128)(2,1)S(1)}, u32[]{:S(2)}, u32[]{:S(2)}) collective-permute-start(bf16[2,64,1024]{2,1,0:T(8,128)(2,1)S(1)} %get-tuple-element.38), channel_id=1, source_target_pairs={{0,12},{2,14},{4,8},{6,10},{8,4},{10,6},{12,0},{14,2},{1,13},{3,15... | collective-permute-start | bytes 786440 | tf_op jit(solution)/shard_map/ppermute | solution.py:157
  46.5 25.9 %collective-permute-start.9 = (bf16[4,64,1536]{2,1,0:T(8,128)(2,1)S(1)}, bf16[4,64,1536]{2,1,0:T(8,128)(2,1)S(1)}, u32[]{:S(2)}, u32[]{:S(2)}) collective-permute-start(bf16[4,64,1536]{2,1,0:T(8,128)(2,1)S(1)} %mix.8), channel_id=1, source_target_pairs={{0,2},{2,0},{1,3},{3,1},{4,6},{6,4},{5,7},{7,5},{8,10},{10,8},{9,1... | collective-permute-start | bytes 2359304 | tf_op jit(solution)/shard_map/ppermute | solution.py:152
  51.1 38.6 %collective-permute-start.15 = (bf16[4,64,512]{2,1,0:T(8,128)(2,1)S(1)}, bf16[4,64,512]{2,1,0:T(8,128)(2,1)S(1)}, u32[]{:S(2)}, u32[]{:S(2)}) collective-permute-start(bf16[4,64,512]{2,1,0:T(8,128)(2,1)S(1)} %mix.10), channel_id=1, source_target_pairs={{0,2},{2,0},{1,3},{3,1},{4,6},{6,4},{5,7},{7,5},{8,10},{10,8},{9,1... | collective-permute-start | bytes 786440 | tf_op jit(solution)/shard_map/ppermute | solution.py:152
  61.2 17.6 %collective-permute-start.12 = (bf16[4,64,512]{2,1,0:T(8,128)(2,1)S(1)}, bf16[4,64,512]{2,1,0:T(8,128)(2,1)S(1)}, u32[]{:S(2)}, u32[]{:S(2)}) collective-permute-start(bf16[4,64,512]{2,1,0:T(8,128)(2,1)S(1)} %mix.9), channel_id=1, source_target_pairs={{0,2},{2,0},{1,3},{3,1},{4,6},{6,4},{5,7},{7,5},{8,10},{10,8},{9,1... | collective-permute-start | bytes 786440 | tf_op jit(solution)/shard_map/ppermute | solution.py:152
  64.9 10.6 %collective-permute-start.10 = (bf16[2,64,1024]{2,1,0:T(8,128)(2,1)S(1)}, bf16[2,64,1024]{2,1,0:T(8,128)(2,1)S(1)}, u32[]{:S(2)}, u32[]{:S(2)}) collective-permute-start(bf16[2,64,1024]{2,1,0:T(8,128)(2,1)S(1)} %slice.63), channel_id=1, source_target_pairs={{0,4},{4,0},{8,12},{12,8},{1,5},{5,1},{9,13},{13,9},{2,6},{6,2},{1... | collective-permute-start | bytes 786440 | tf_op jit(solution)/shard_map/ppermute | solution.py:152
  75.7 7.3 %collective-permute-start.11 = (bf16[64,1024]{1,0:T(8,128)(2,1)S(1)}, bf16[64,1024]{1,0:T(8,128)(2,1)S(1)}, u32[]{:S(2)}, u32[]{:S(2)}) collective-permute-start(bf16[64,1024]{1,0:T(8,128)(2,1)S(1)} %fusion.5), channel_id=1, source_target_pairs={{0,8},{4,12},{8,0},{12,4},{1,9},{5,13},{9,1},{13,5},{2,10},{6,14},... | collective-permute-start | bytes 393224 | tf_op jit(solution)/shard_map/ppermute | solution.py:152
  76.8 12.8 %collective-permute-start.13 = (bf16[2,64,1536]{2,1,0:T(8,128)(2,1)S(1)}, bf16[2,64,1536]{2,1,0:T(8,128)(2,1)S(1)}, u32[]{:S(2)}, u32[]{:S(2)}) collective-permute-start(bf16[2,64,1536]{2,1,0:T(8,128)(2,1)S(1)} %slice.68), channel_id=1, source_target_pairs={{0,4},{4,0},{8,12},{12,8},{1,5},{5,1},{9,13},{13,9},{2,6},{6,2},{1... | collective-permute-start | bytes 1179656 | tf_op jit(solution)/shard_map/ppermute | solution.py:152
  79.0 12.0 %collective-permute-start.16 = (bf16[2,64,512]{2,1,0:T(8,128)(2,1)S(1)}, bf16[2,64,512]{2,1,0:T(8,128)(2,1)S(1)}, u32[]{:S(2)}, u32[]{:S(2)}) collective-permute-start(bf16[2,64,512]{2,1,0:T(8,128)(2,1)S(1)} %slice.73), channel_id=1, source_target_pairs={{0,4},{4,0},{8,12},{12,8},{1,5},{5,1},{9,13},{13,9},{2,6},{6,2},{1... | collective-permute-start | bytes 393224 | tf_op jit(solution)/shard_map/ppermute | solution.py:152
  91.0 9.4 %collective-permute-start.17 = (bf16[64,512]{1,0:T(8,128)(2,1)S(1)}, bf16[64,512]{1,0:T(8,128)(2,1)S(1)}, u32[]{:S(2)}, u32[]{:S(2)}) collective-permute-start(bf16[64,512]{1,0:T(8,128)(2,1)S(1)} %fusion.10), channel_id=1, source_target_pairs={{0,8},{4,12},{8,0},{12,4},{1,9},{5,13},{9,1},{13,5},{2,10},{6,14},... | collective-permute-start | bytes 196616 | tf_op jit(solution)/shard_map/ppermute | solution.py:152
  91.4 13.2 %collective-permute-start.14 = (bf16[64,1536]{1,0:T(8,128)(2,1)S(1)}, bf16[64,1536]{1,0:T(8,128)(2,1)S(1)}, u32[]{:S(2)}, u32[]{:S(2)}) collective-permute-start(bf16[64,1536]{1,0:T(8,128)(2,1)S(1)} %fusion.4), channel_id=1, source_target_pairs={{0,8},{4,12},{8,0},{12,4},{1,9},{5,13},{9,1},{13,5},{2,10},{6,14},... | collective-permute-start | bytes 589832 | tf_op jit(solution)/shard_map/ppermute | solution.py:152
  94.1 6.3 %collective-permute-start.18 = (bf16[2,64,512]{2,1,0:T(8,128)(2,1)S(1)}, bf16[2,64,512]{2,1,0:T(8,128)(2,1)S(1)}, u32[]{:S(2)}, u32[]{:S(2)}) collective-permute-start(bf16[2,64,512]{2,1,0:T(8,128)(2,1)S(1)} %slice.77), channel_id=1, source_target_pairs={{0,4},{4,0},{8,12},{12,8},{1,5},{5,1},{9,13},{13,9},{2,6},{6,2},{1... | collective-permute-start | bytes 393224 | tf_op jit(solution)/shard_map/ppermute | solution.py:152
  100.5 5.2 %collective-permute-start.19 = (bf16[64,512]{1,0:T(8,128)(2,1)S(1)}, bf16[64,512]{1,0:T(8,128)(2,1)S(1)}, u32[]{:S(2)}, u32[]{:S(2)}) collective-permute-start(bf16[64,512]{1,0:T(8,128)(2,1)S(1)} %fusion.11), channel_id=1, source_target_pairs={{0,8},{4,12},{8,0},{12,4},{1,9},{5,13},{9,1},{13,5},{2,10},{6,14},... | collective-permute-start | bytes 196616 | tf_op jit(solution)/shard_map/ppermute | solution.py:152
  (1 other events, 0.7 us)

commit v7 on v6

--- a/solution.py
+++ b/solution.py
@@ -10,6 +10,7 @@
 CHIPS = 8
 TILE = 512
 COLUMNS = ((0, 1024), (1024, 1536), (2560, 512), (3072, 512))
+LIGHT, HEAVY = 0.01, 4.0
 
 
 def passed_along(block, axis, distance):
@@ -131,7 +132,7 @@
     out_ref[...] = total.reshape(len(rows), tokens, -1).astype(out_ref.dtype)
 
 
-def mix(rows, near, far, start, width):
+def mix(rows, near, far, start, width, weight_of_cost):
     _, tokens, depth = rows[0].shape
     whole = pl.BlockSpec((2, tokens, depth), lambda i: (0, 0, 0))
     weight = pl.BlockSpec((depth, TILE), lambda i: (0, start // TILE + i))
@@ -143,7 +144,11 @@
         out_shape=jax.ShapeDtypeStruct((len(rows), tokens, width), jnp.bfloat16),
         scratch_shapes=[pltpu.VMEM((2, len(rows) * tokens, depth), jnp.bfloat16)],
         compiler_params=pltpu.CompilerParams(vmem_limit_bytes=24 << 20),
-        cost_estimate=pl.CostEstimate(flops=4 * len(rows) * tokens * depth * width, bytes_accessed=4 * depth * width, transcendentals=0),
+        cost_estimate=pl.CostEstimate(
+            flops=int(weight_of_cost * 4 * len(rows) * tokens * depth * width),
+            bytes_accessed=int(weight_of_cost * 4 * depth * width),
+            transcendentals=0,
+        ),
         name="mix",
     )(*rows, near, far)
 
@@ -175,37 +180,42 @@
     blocks = spread_rows(hidden, expert_ids, gate_weights, own, even, near)
     for relative, block in zip(even, blocks):
         arrived[relative] = send_to_chip(block, relative) if relative else block
-    across, last = [], blocks[-1]
-    for columns in COLUMNS:
-        arrived[1] = after(arrived[1], last)
-        last = mix(arrived[1::2], near, far, *columns)
-        across.append(swap(last, "x", 1))
-    kept, lines, pairs, results = [], [], [], []
-
-    def mix_even(parts):
+    across, kept, lines, pairs, results = [], [], [], [], []
+
+    def mix_odd(i, earlier):
+        arrived[7] = after(arrived[7], earlier)
+        block = mix([arrived[r] for r in odd], near, far, *COLUMNS[i], LIGHT)
+        across.append(swap(block, "x", 1))
+        return block
+
+    def mix_even(parts, earlier, weight):
         start, width = COLUMNS[parts[0]][0], sum(COLUMNS[i][1] for i in parts)
-        arrived[0] = after(arrived[0], last)
-        block = mix(arrived[0::2], near, far, start, width)
+        arrived[0] = after(arrived[0], earlier)
+        block = mix([arrived[r] for r in even], near, far, start, width, weight)
         for i in parts:
             low = COLUMNS[i][0] - start
             kept.append(block[:, :, low : low + COLUMNS[i][1]])
         return block
 
-    def add_x(i, last):
-        line = after(kept[i], last).astype(jnp.float32) + across[i].astype(jnp.float32)
-        lines.append((line[0::2], swap(line[1::2].astype(jnp.bfloat16), "z", 1)))
+    def add_x(i, earlier):
+        line = after(kept[i], earlier).astype(jnp.float32) + across[i].astype(jnp.float32)
+        lines.append((line[1::2], swap(line[0::2].astype(jnp.bfloat16), "z", 1)))
         return line
 
-    def add_z(i, last):
-        pair = after(lines[i][0], last) + lines[i][1].astype(jnp.float32)
-        pairs.append((pair[0], swap(pair[1].astype(jnp.bfloat16), "z", 2)))
+    def add_z(i, earlier):
+        pair = after(lines[i][0], earlier) + lines[i][1].astype(jnp.float32)
+        pairs.append((pair[1], swap(pair[0].astype(jnp.bfloat16), "z", 2)))
         return pair
 
-    last = mix_even((0,))
+    last = mix_odd(0, blocks[-1])
+    last = mix_odd(1, last)
+    last = mix_even((0,), last, HEAVY)
     last = add_x(0, last)
-    last = mix_even((1,))
+    last = mix_odd(2, last)
+    last = mix_even((1,), last, LIGHT)
     last = add_x(1, last)
-    last = mix_even((2, 3))
+    last = mix_odd(3, last)
+    last = mix_even((2, 3), last, LIGHT)
     last = add_z(0, last)
     for i in range(2, len(COLUMNS)):
         last = add_x(i, last)

time: 107 us -> 119 us (1.11)
  waiting for transfers between devices: 43.7 us -> 52.9 us
  starting transfers between devices: 32.3 us -> 35.1 us
    ppermute x13, waiting for transfers between devices: 20.3 us -> 31.5 us  [swap(): lax.ppermute(block, axis, [(i, i ^ distance) for i in range(lax.axis_size...]
    ppermute x7, starting transfers between devices: 14.9 us -> 17.4 us  [send_to_chip(): lax.ppermute(block, ('z', 'x'), [(i, i ^ relative) for i in range(sizes[0...]
    ppermute x7, waiting for transfers between devices: 23.4 us -> 21.4 us  [send_to_chip(): lax.ppermute(block, ('z', 'x'), [(i, i ^ relative) for i in range(sizes[0...]
  transfers between devices with their start and end apart: 20 -> 20, of which waited for: 8 -> 10; matrix products, arithmetic and copies ran while one was open for 1% -> 1% of each run, Pallas kernels for 18% -> 19%
where the time goes in v7:
time: 119 us
  waiting for transfers between devices  52.9 us (44%)
  starting transfers between devices  35.1 us (29%)
  Pallas kernels  22.5 us (19%)
  local copies, waits for them, and re-layouts  5.98 us (5%)
  other arithmetic  1.78 us (1%)
    ppermute x13, waiting for transfers between devices, swap(): lax.ppermute(block, axis, [(i, i ^ distance) for i in range(lax.axis_size...  31.5 us
    ppermute x7, waiting for transfers between devices, send_to_chip(): lax.ppermute(block, ('z', 'x'), [(i, i ^ relative) for i in range(sizes[0...  21.4 us
    pallas_call x7, Pallas kernels, mix(): pl.pallas_call(mix_kernel, grid=(width // TILE,), in_specs=[whole] * len(...  20.7 us
    ppermute x13, starting transfers between devices, swap(): lax.ppermute(block, axis, [(i, i ^ distance) for i in range(lax.axis_size...  17.7 us
    ppermute x7, starting transfers between devices, send_to_chip(): lax.ppermute(block, ('z', 'x'), [(i, i ^ relative) for i in range(sizes[0...  17.4 us
    unnamed x10, local copies, waits for them, and re-layouts  5.68 us
  transfers between devices with their start and end apart: 20, of which 10 were waited for; matrix products, arithmetic and copies ran while one was open for 1% of the time, Pallas kernels for 19%

profile of v7, /device:TPU:0, one launch (start us, length us, event | category | flops | bytes accessed | tf_op | source)
XLA Modules:
  0.0 118.6 jit_solution(10244478423269674695)
XLA Ops:
  4.0 5.6 %collective-permute-start.3 = (bf16[2,64,1024]{2,1,0:T(8,128)(2,1)S(1)}, bf16[2,64,1024]{2,1,0:T(8,128)(2,1)S(1)}, u32[]{:S(2)}, u32[]{:S(2)}) collective-permute-start(bf16[2,64,1024]{2,1,0:T(8,128)(2,1)S(1)} %get-tuple-element.30), channel_id=1, source_target_pairs={{0,14},{2,12},{4,10},{6,8},{8,6},{10,4},{12,2},{14,0},{1,15},{3,13... | collective-permute-start | bytes 786440 | tf_op jit(solution)/shard_map/ppermute | solution.py:162
  11.7 3.1 %copy-done = bf16[1,1024,3584]{2,1,0:T(8,128)(2,1)S(1)} copy-done((bf16[1,1024,3584]{2,1,0:T(8,128)(2,1)S(1)}, bf16[1,1024,3584]{2,1,0:T(8,128)(2,1)}, u32[]{:S(2)}) %copy-start) | copy-done | bytes 7340056
  17.0 3.7 %collective-permute-start = (bf16[2,64,1024]{2,1,0:T(8,128)(2,1)S(1)}, bf16[2,64,1024]{2,1,0:T(8,128)(2,1)S(1)}, u32[]{:S(2)}, u32[]{:S(2)}) collective-permute-start(bf16[2,64,1024]{2,1,0:T(8,128)(2,1)S(1)} %get-tuple-element.26), channel_id=1, source_target_pairs={{0,12},{2,14},{4,8},{6,10},{8,4},{10,6},{12,0},{14,2},{1,13},{3,15... | collective-permute-start | bytes 786440 | tf_op jit(solution)/shard_map/ppermute | solution.py:162
  20.7 20.1 %collective-permute-done.4.refs_1_ = bf16[2,64,1024]{2,1,0:T(8,128)(2,1)S(1)} collective-permute-done((bf16[2,64,1024]{2,1,0:T(8,128)(2,1)S(1)}, bf16[2,64,1024]{2,1,0:T(8,128)(2,1)S(1)}, u32[]{:S(2)}, u32[]{:S(2)}) %collective-permute-start.4) | collective-permute-done | bytes 262176 | tf_op jit(solution)/shard_map/ppermute | solution.py:162
  40.8 6.0 %collective-permute-start.2 = (bf16[2,64,1024]{2,1,0:T(8,128)(2,1)S(1)}, bf16[2,64,1024]{2,1,0:T(8,128)(2,1)S(1)}, u32[]{:S(2)}, u32[]{:S(2)}) collective-permute-start(bf16[2,64,1024]{2,1,0:T(8,128)(2,1)S(1)} %get-tuple-element.28), channel_id=1, source_target_pairs={{0,4},{2,6},{4,0},{6,2},{8,12},{10,14},{12,8},{14,10},{1,5},{3,7},... | collective-permute-start | bytes 786440 | tf_op jit(solution)/shard_map/ppermute | solution.py:162
  46.8 2.8 %mix.7 = bf16[4,64,1024]{2,1,0:T(8,128)(2,1)S(1)} custom-call(bf16[2,64,1024]{2,1,0:T(8,128)(2,1)S(1)} %collective-permute-done.3.refs_0_, bf16[2,64,1024]{2,1,0:T(8,128)(2,1)S(1)} %collective-permute-done.4.refs_1_, bf16[2,64,1024]{2,1,0:T(8,128)(2,1)S(1)} %collective-permute-done.5.refs_2_, bf16[2,64,1024]{2,1,0:T(8,128)(2,1)S(1)} %collective-permute-done.6.refs_3_, ...), custom_call_target="tpu_custom_call" | custom-call | flops 10737418 | bytes 41943 | tf_op jit(solution)/shard_map/mix/pallas_call | solution.py:139
  49.6 5.4 %collective-permute-start.8 = (bf16[4,64,1024]{2,1,0:T(8,128)(2,1)S(1)}, bf16[4,64,1024]{2,1,0:T(8,128)(2,1)S(1)}, u32[]{:S(2)}, u32[]{:S(2)}) collective-permute-start(bf16[4,64,1024]{2,1,0:T(8,128)(2,1)S(1)} %mix.7), channel_id=1, source_target_pairs={{0,2},{2,0},{1,3},{3,1},{4,6},{6,4},{5,7},{7,5},{8,10},{10,8},{9,1... | collective-permute-start | bytes 1572872 | tf_op jit(solution)/shard_map/ppermute | solution.py:157
  55.0 4.1 %mix.8 = bf16[4,64,1536]{2,1,0:T(8,128)(2,1)S(1)} custom-call(bf16[2,64,1024]{2,1,0:T(8,128)(2,1)S(1)} %collective-permute-done.3.refs_0_, bf16[2,64,1024]{2,1,0:T(8,128)(2,1)S(1)} %collective-permute-done.4.refs_1_, bf16[2,64,1024]{2,1,0:T(8,128)(2,1)S(1)} %collective-permute-done.5.refs_2_, bf16[2,64,1024]{2,1,0:T(8,128)(2,1)S(1)} %collective-permute-done.6.refs_3_, ...), custom_call_target="tpu_custom_call" | custom-call | flops 16106127 | bytes 62914 | tf_op jit(solution)/shard_map/mix/pallas_call | solution.py:139
  59.3 2.8 %mix.9 = bf16[4,64,1024]{2,1,0:T(8,128)(2,1)S(1)} custom-call(bf16[2,64,1024]{2,1,0:T(8,128)(2,1)S(1)} %collective-permute-done.refs_0_, bf16[2,64,1024]{2,1,0:T(8,128)(2,1)S(1)} %collective-permute-done.1.refs_1_, bf16[2,64,1024]{2,1,0:T(8,128)(2,1)S(1)} %collective-permute-done.2.refs_2_, bf16[2,64,1024]{2,1,0:T(8,128)(2,1)S(1)} %get-tuple-element.40.refs_3_, ...), custom_call_target="tpu_custom_call" | custom-call | flops 4294967296 | bytes 16777216 | tf_op jit(solution)/shard_map/mix/pallas_call | solution.py:139
  62.1 5.8 %collective-permute-done.8 = bf16[4,64,1024]{2,1,0:T(8,128)(2,1)S(1)} collective-permute-done((bf16[4,64,1024]{2,1,0:T(8,128)(2,1)S(1)}, bf16[4,64,1024]{2,1,0:T(8,128)(2,1)S(1)}, u32[]{:S(2)}, u32[]{:S(2)}) %collective-permute-start.8) | collective-permute-done | bytes 524320 | tf_op jit(solution)/shard_map/ppermute | solution.py:157
  68.1 2.0 %mix.10 = bf16[4,64,512]{2,1,0:T(8,128)(2,1)S(1)} custom-call(bf16[2,64,1024]{2,1,0:T(8,128)(2,1)S(1)} %collective-permute-done.3.refs_0_, bf16[2,64,1024]{2,1,0:T(8,128)(2,1)S(1)} %collective-permute-done.4.refs_1_, bf16[2,64,1024]{2,1,0:T(8,128)(2,1)S(1)} %collective-permute-done.5.refs_2_, bf16[2,64,1024]{2,1,0:T(8,128)(2,1)S(1)} %collective-permute-done.6.refs_3_, ...), custom_call_target="tpu_custom_call" | custom-call | flops 5368709 | bytes 20971 | tf_op jit(solution)/shard_map/mix/pallas_call | solution.py:139
  70.1 2.1 %collective-permute-start.12 = (bf16[4,64,512]{2,1,0:T(8,128)(2,1)S(1)}, bf16[4,64,512]{2,1,0:T(8,128)(2,1)S(1)}, u32[]{:S(2)}, u32[]{:S(2)}) collective-permute-start(bf16[4,64,512]{2,1,0:T(8,128)(2,1)S(1)} %mix.10), channel_id=1, source_target_pairs={{0,2},{2,0},{1,3},{3,1},{4,6},{6,4},{5,7},{7,5},{8,10},{10,8},{9,1... | collective-permute-start | bytes 786440 | tf_op jit(solution)/shard_map/ppermute | solution.py:157
  72.3 4.1 %mix.11 = bf16[4,64,1536]{2,1,0:T(8,128)(2,1)S(1)} custom-call(bf16[2,64,1024]{2,1,0:T(8,128)(2,1)S(1)} %collective-permute-done.refs_0_, bf16[2,64,1024]{2,1,0:T(8,128)(2,1)S(1)} %collective-permute-done.1.refs_1_, bf16[2,64,1024]{2,1,0:T(8,128)(2,1)S(1)} %collective-permute-done.2.refs_2_, bf16[2,64,1024]{2,1,0:T(8,128)(2,1)S(1)} %get-tuple-element.40.refs_3_, ...), custom_call_target="tpu_custom_call" | custom-call | flops 16106127 | bytes 62914 | tf_op jit(solution)/shard_map/mix/pallas_call | solution.py:139
  76.5 7.3 %collective-permute-done.9 = bf16[4,64,1536]{2,1,0:T(8,128)(2,1)S(1)} collective-permute-done((bf16[4,64,1536]{2,1,0:T(8,128)(2,1)S(1)}, bf16[4,64,1536]{2,1,0:T(8,128)(2,1)S(1)}, u32[]{:S(2)}, u32[]{:S(2)}) %collective-permute-start.9) | collective-permute-done | bytes 786464 | tf_op jit(solution)/shard_map/ppermute | solution.py:157
  84.0 2.0 %mix.12 = bf16[4,64,512]{2,1,0:T(8,128)(2,1)S(1)} custom-call(bf16[2,64,1024]{2,1,0:T(8,128)(2,1)S(1)} %collective-permute-done.3.refs_0_, bf16[2,64,1024]{2,1,0:T(8,128)(2,1)S(1)} %collective-permute-done.4.refs_1_, bf16[2,64,1024]{2,1,0:T(8,128)(2,1)S(1)} %collective-permute-done.5.refs_2_, bf16[2,64,1024]{2,1,0:T(8,128)(2,1)S(1)} %collective-permute-done.6.refs_3_, ...), custom_call_target="tpu_custom_call" | custom-call | flops 5368709 | bytes 20971 | tf_op jit(solution)/shard_map/mix/pallas_call | solution.py:139
  87.7 2.8 %mix.13 = bf16[4,64,1024]{2,1,0:T(8,128)(2,1)S(1)} custom-call(bf16[2,64,1024]{2,1,0:T(8,128)(2,1)S(1)} %collective-permute-done.refs_0_, bf16[2,64,1024]{2,1,0:T(8,128)(2,1)S(1)} %collective-permute-done.1.refs_1_, bf16[2,64,1024]{2,1,0:T(8,128)(2,1)S(1)} %collective-permute-done.2.refs_2_, bf16[2,64,1024]{2,1,0:T(8,128)(2,1)S(1)} %get-tuple-element.40.refs_3_, ...), custom_call_target="tpu_custom_call" | custom-call | flops 10737418 | bytes 41943 | tf_op jit(solution)/shard_map/mix/pallas_call | solution.py:139
  91.5 1.8 %collective-permute-start.16 = (bf16[2,64,512]{2,1,0:T(8,128)(2,1)S(1)}, bf16[2,64,512]{2,1,0:T(8,128)(2,1)S(1)}, u32[]{:S(2)}, u32[]{:S(2)}) collective-permute-start(bf16[2,64,512]{2,1,0:T(8,128)(2,1)S(1)} %slice.73), channel_id=1, source_target_pairs={{0,4},{4,0},{8,12},{12,8},{1,5},{5,1},{9,13},{13,9},{2,6},{6,2},{1... | collective-permute-start | bytes 393224 | tf_op jit(solution)/shard_map/ppermute | solution.py:157
  93.3 6.1 %collective-permute-done.11 = bf16[64,1024]{1,0:T(8,128)(2,1)S(1)} collective-permute-done((bf16[64,1024]{1,0:T(8,128)(2,1)S(1)}, bf16[64,1024]{1,0:T(8,128)(2,1)S(1)}, u32[]{:S(2)}, u32[]{:S(2)}) %collective-permute-start.11) | collective-permute-done | bytes 131104 | tf_op jit(solution)/shard_map/ppermute | solution.py:157
  99.5 3.4 %collective-permute-done.13 = bf16[2,64,1536]{2,1,0:T(8,128)(2,1)S(1)} collective-permute-done((bf16[2,64,1536]{2,1,0:T(8,128)(2,1)S(1)}, bf16[2,64,1536]{2,1,0:T(8,128)(2,1)S(1)}, u32[]{:S(2)}, u32[]{:S(2)}) %collective-permute-start.13) | collective-permute-done | bytes 393248 | tf_op jit(solution)/shard_map/ppermute | solution.py:157
  104.5 2.9 %collective-permute-start.14 = (bf16[64,1536]{1,0:T(8,128)(2,1)S(1)}, bf16[64,1536]{1,0:T(8,128)(2,1)S(1)}, u32[]{:S(2)}, u32[]{:S(2)}) collective-permute-start(bf16[64,1536]{1,0:T(8,128)(2,1)S(1)} %fusion.4), channel_id=1, source_target_pairs={{0,8},{4,12},{8,0},{12,4},{1,9},{5,13},{9,1},{13,5},{2,10},{6,14},... | collective-permute-start | bytes 589832 | tf_op jit(solution)/shard_map/ppermute | solution.py:157
  107.6 2.2 %collective-permute-done.17 = bf16[64,512]{1,0:T(8,128)(2,1)S(1)} collective-permute-done((bf16[64,512]{1,0:T(8,128)(2,1)S(1)}, bf16[64,512]{1,0:T(8,128)(2,1)S(1)}, u32[]{:S(2)}, u32[]{:S(2)}) %collective-permute-start.17) | collective-permute-done | bytes 65568 | tf_op jit(solution)/shard_map/ppermute | solution.py:157
  109.8 2.7 %collective-permute-done.18 = bf16[2,64,512]{2,1,0:T(8,128)(2,1)S(1)} collective-permute-done((bf16[2,64,512]{2,1,0:T(8,128)(2,1)S(1)}, bf16[2,64,512]{2,1,0:T(8,128)(2,1)S(1)}, u32[]{:S(2)}, u32[]{:S(2)}) %collective-permute-start.18) | collective-permute-done | bytes 131104 | tf_op jit(solution)/shard_map/ppermute | solution.py:157
  112.5 2.3 %collective-permute-start.19 = (bf16[64,512]{1,0:T(8,128)(2,1)S(1)}, bf16[64,512]{1,0:T(8,128)(2,1)S(1)}, u32[]{:S(2)}, u32[]{:S(2)}) collective-permute-start(bf16[64,512]{1,0:T(8,128)(2,1)S(1)} %fusion.11), channel_id=1, source_target_pairs={{0,8},{4,12},{8,0},{12,4},{1,9},{5,13},{9,1},{13,5},{2,10},{6,14},... | collective-permute-start | bytes 196616 | tf_op jit(solution)/shard_map/ppermute | solution.py:157
  114.9 2.9 %collective-permute-done.19 = bf16[64,512]{1,0:T(8,128)(2,1)S(1)} collective-permute-done((bf16[64,512]{1,0:T(8,128)(2,1)S(1)}, bf16[64,512]{1,0:T(8,128)(2,1)S(1)}, u32[]{:S(2)}, u32[]{:S(2)}) %collective-permute-start.19) | collective-permute-done | bytes 65568 | tf_op jit(solution)/shard_map/ppermute | solution.py:157
  (61 shorter events, 14.3 us)
Async XLA Ops:
  0.0 46.8 %collective-permute-start.7 = (bf16[1024,3584]{1,0:T(8,128)(2,1)}, bf16[1024,3584]{1,0:T(8,128)(2,1)}, u32[]{:S(2)}, u32[]{:S(2)}) collective-permute-start(bf16[1024,3584]{1,0:T(8,128)(2,1)} %bitcast.37), channel_id=1, source_target_pairs={{0,1},{1,0},{2,3},{3,2},{4,5},{5,4},{6,7},{7,6},{8,9},{9,8},{10,11... | collective-permute-start | bytes 22020104 | tf_op jit(solution)/shard_map/ppermute | solution.py:157
  0.5 1.2 %copy-start.2 = (bf16[64,8,1024]{2,1,0:T(8,128)(2,1)S(1)}, bf16[64,8,1024]{2,1,0:T(8,128)(2,1)}, u32[]{:S(2)}) copy-start(bf16[64,8,1024]{2,1,0:T(8,128)(2,1)} %param.4) | copy-start | bytes 3145732
  2.4 0.7 copy-start.4
  4.0 13.0 %collective-permute-start.3 = (bf16[2,64,1024]{2,1,0:T(8,128)(2,1)S(1)}, bf16[2,64,1024]{2,1,0:T(8,128)(2,1)S(1)}, u32[]{:S(2)}, u32[]{:S(2)}) collective-permute-start(bf16[2,64,1024]{2,1,0:T(8,128)(2,1)S(1)} %get-tuple-element.30), channel_id=1, source_target_pairs={{0,14},{2,12},{4,10},{6,8},{8,6},{10,4},{12,2},{14,0},{1,15},{3,13... | collective-permute-start | bytes 786440 | tf_op jit(solution)/shard_map/ppermute | solution.py:162
  9.6 31.2 %collective-permute-start.4 = (bf16[2,64,1024]{2,1,0:T(8,128)(2,1)S(1)}, bf16[2,64,1024]{2,1,0:T(8,128)(2,1)S(1)}, u32[]{:S(2)}, u32[]{:S(2)}) collective-permute-start(bf16[2,64,1024]{2,1,0:T(8,128)(2,1)S(1)} %get-tuple-element.32), channel_id=1, source_target_pairs={{0,10},{2,8},{4,14},{6,12},{8,2},{10,0},{12,6},{14,4},{1,11},{3,9}... | collective-permute-start | bytes 786440 | tf_op jit(solution)/shard_map/ppermute | solution.py:162
  9.6 31.2 %collective-permute-start.5 = (bf16[2,64,1024]{2,1,0:T(8,128)(2,1)S(1)}, bf16[2,64,1024]{2,1,0:T(8,128)(2,1)S(1)}, u32[]{:S(2)}, u32[]{:S(2)}) collective-permute-start(bf16[2,64,1024]{2,1,0:T(8,128)(2,1)S(1)} %get-tuple-element.33), channel_id=1, source_target_pairs={{0,6},{2,4},{4,2},{6,0},{8,14},{10,12},{12,10},{14,8},{1,7},{3,5},... | collective-permute-start | bytes 786440 | tf_op jit(solution)/shard_map/ppermute | solution.py:162
  11.2 35.5 %collective-permute-start.6 = (bf16[2,64,1024]{2,1,0:T(8,128)(2,1)S(1)}, bf16[2,64,1024]{2,1,0:T(8,128)(2,1)S(1)}, u32[]{:S(2)}, u32[]{:S(2)}) collective-permute-start(bf16[2,64,1024]{2,1,0:T(8,128)(2,1)S(1)} %get-tuple-element.34), channel_id=1, source_target_pairs={{0,2},{2,0},{4,6},{6,4},{8,10},{10,8},{12,14},{14,12},{1,3},{3,1},... | collective-permute-start | bytes 786440 | tf_op jit(solution)/shard_map/ppermute | solution.py:162
  11.7 3.1 %copy-start = (bf16[1,1024,3584]{2,1,0:T(8,128)(2,1)S(1)}, bf16[1,1024,3584]{2,1,0:T(8,128)(2,1)}, u32[]{:S(2)}) copy-start(bf16[1,1024,3584]{2,1,0:T(8,128)(2,1)} %param.7) | copy-start | bytes 22020100
  14.7 32.0 %copy-start.1 = (bf16[1,1024,3584]{2,1,0:T(8,128)(2,1)S(1)}, bf16[1,1024,3584]{2,1,0:T(8,128)(2,1)}, u32[]{:S(2)}) copy-start(bf16[1,1024,3584]{2,1,0:T(8,128)(2,1)} %param.7) | copy-start | bytes 22020100
  17.0 42.3 %collective-permute-start = (bf16[2,64,1024]{2,1,0:T(8,128)(2,1)S(1)}, bf16[2,64,1024]{2,1,0:T(8,128)(2,1)S(1)}, u32[]{:S(2)}, u32[]{:S(2)}) collective-permute-start(bf16[2,64,1024]{2,1,0:T(8,128)(2,1)S(1)} %get-tuple-element.26), channel_id=1, source_target_pairs={{0,12},{2,14},{4,8},{6,10},{8,4},{10,6},{12,0},{14,2},{1,13},{3,15... | collective-permute-start | bytes 786440 | tf_op jit(solution)/shard_map/ppermute | solution.py:162
  40.8 18.5 %collective-permute-start.1 = (bf16[2,64,1024]{2,1,0:T(8,128)(2,1)S(1)}, bf16[2,64,1024]{2,1,0:T(8,128)(2,1)S(1)}, u32[]{:S(2)}, u32[]{:S(2)}) collective-permute-start(bf16[2,64,1024]{2,1,0:T(8,128)(2,1)S(1)} %get-tuple-element.27), channel_id=1, source_target_pairs={{0,8},{2,10},{4,12},{6,14},{8,0},{10,2},{12,4},{14,6},{1,9},{3,11}... | collective-permute-start | bytes 786440 | tf_op jit(solution)/shard_map/ppermute | solution.py:162
  40.8 18.5 %collective-permute-start.2 = (bf16[2,64,1024]{2,1,0:T(8,128)(2,1)S(1)}, bf16[2,64,1024]{2,1,0:T(8,128)(2,1)S(1)}, u32[]{:S(2)}, u32[]{:S(2)}) collective-permute-start(bf16[2,64,1024]{2,1,0:T(8,128)(2,1)S(1)} %get-tuple-element.28), channel_id=1, source_target_pairs={{0,4},{2,6},{4,0},{6,2},{8,12},{10,14},{12,8},{14,10},{1,5},{3,7},... | collective-permute-start | bytes 786440 | tf_op jit(solution)/shard_map/ppermute | solution.py:162
  49.6 18.2 %collective-permute-start.8 = (bf16[4,64,1024]{2,1,0:T(8,128)(2,1)S(1)}, bf16[4,64,1024]{2,1,0:T(8,128)(2,1)S(1)}, u32[]{:S(2)}, u32[]{:S(2)}) collective-permute-start(bf16[4,64,1024]{2,1,0:T(8,128)(2,1)S(1)} %mix.7), channel_id=1, source_target_pairs={{0,2},{2,0},{1,3},{3,1},{4,6},{6,4},{5,7},{7,5},{8,10},{10,8},{9,1... | collective-permute-start | bytes 1572872 | tf_op jit(solution)/shard_map/ppermute | solution.py:157
  59.1 24.6 %collective-permute-start.9 = (bf16[4,64,1536]{2,1,0:T(8,128)(2,1)S(1)}, bf16[4,64,1536]{2,1,0:T(8,128)(2,1)S(1)}, u32[]{:S(2)}, u32[]{:S(2)}) collective-permute-start(bf16[4,64,1536]{2,1,0:T(8,128)(2,1)S(1)} %mix.8), channel_id=1, source_target_pairs={{0,2},{2,0},{1,3},{3,1},{4,6},{6,4},{5,7},{7,5},{8,10},{10,8},{9,1... | collective-permute-start | bytes 2359304 | tf_op jit(solution)/shard_map/ppermute | solution.py:157
  70.1 21.3 %collective-permute-start.12 = (bf16[4,64,512]{2,1,0:T(8,128)(2,1)S(1)}, bf16[4,64,512]{2,1,0:T(8,128)(2,1)S(1)}, u32[]{:S(2)}, u32[]{:S(2)}) collective-permute-start(bf16[4,64,512]{2,1,0:T(8,128)(2,1)S(1)} %mix.10), channel_id=1, source_target_pairs={{0,2},{2,0},{1,3},{3,1},{4,6},{6,4},{5,7},{7,5},{8,10},{10,8},{9,1... | collective-permute-start | bytes 786440 | tf_op jit(solution)/shard_map/ppermute | solution.py:157
  72.2 18.2 %collective-permute-start.10 = (bf16[2,64,1024]{2,1,0:T(8,128)(2,1)S(1)}, bf16[2,64,1024]{2,1,0:T(8,128)(2,1)S(1)}, u32[]{:S(2)}, u32[]{:S(2)}) collective-permute-start(bf16[2,64,1024]{2,1,0:T(8,128)(2,1)S(1)} %slice.63), channel_id=1, source_target_pairs={{0,4},{4,0},{8,12},{12,8},{1,5},{5,1},{9,13},{13,9},{2,6},{6,2},{1... | collective-permute-start | bytes 786440 | tf_op jit(solution)/shard_map/ppermute | solution.py:157
  86.0 16.9 %collective-permute-start.15 = (bf16[4,64,512]{2,1,0:T(8,128)(2,1)S(1)}, bf16[4,64,512]{2,1,0:T(8,128)(2,1)S(1)}, u32[]{:S(2)}, u32[]{:S(2)}) collective-permute-start(bf16[4,64,512]{2,1,0:T(8,128)(2,1)S(1)} %mix.12), channel_id=1, source_target_pairs={{0,2},{2,0},{1,3},{3,1},{4,6},{6,4},{5,7},{7,5},{8,10},{10,8},{9,1... | collective-permute-start | bytes 786440 | tf_op jit(solution)/shard_map/ppermute | solution.py:157
  90.7 8.8 %collective-permute-start.11 = (bf16[64,1024]{1,0:T(8,128)(2,1)S(1)}, bf16[64,1024]{1,0:T(8,128)(2,1)S(1)}, u32[]{:S(2)}, u32[]{:S(2)}) collective-permute-start(bf16[64,1024]{1,0:T(8,128)(2,1)S(1)} %fusion.5), channel_id=1, source_target_pairs={{0,8},{4,12},{8,0},{12,4},{1,9},{5,13},{9,1},{13,5},{2,10},{6,14},... | collective-permute-start | bytes 393224 | tf_op jit(solution)/shard_map/ppermute | solution.py:157
  91.0 11.8 %collective-permute-start.13 = (bf16[2,64,1536]{2,1,0:T(8,128)(2,1)S(1)}, bf16[2,64,1536]{2,1,0:T(8,128)(2,1)S(1)}, u32[]{:S(2)}, u32[]{:S(2)}) collective-permute-start(bf16[2,64,1536]{2,1,0:T(8,128)(2,1)S(1)} %slice.68), channel_id=1, source_target_pairs={{0,4},{4,0},{8,12},{12,8},{1,5},{5,1},{9,13},{13,9},{2,6},{6,2},{1... | collective-permute-start | bytes 1179656 | tf_op jit(solution)/shard_map/ppermute | solution.py:157
  91.5 12.7 %collective-permute-start.16 = (bf16[2,64,512]{2,1,0:T(8,128)(2,1)S(1)}, bf16[2,64,512]{2,1,0:T(8,128)(2,1)S(1)}, u32[]{:S(2)}, u32[]{:S(2)}) collective-permute-start(bf16[2,64,512]{2,1,0:T(8,128)(2,1)S(1)} %slice.73), channel_id=1, source_target_pairs={{0,4},{4,0},{8,12},{12,8},{1,5},{5,1},{9,13},{13,9},{2,6},{6,2},{1... | collective-permute-start | bytes 393224 | tf_op jit(solution)/shard_map/ppermute | solution.py:157
  104.3 5.5 %collective-permute-start.17 = (bf16[64,512]{1,0:T(8,128)(2,1)S(1)}, bf16[64,512]{1,0:T(8,128)(2,1)S(1)}, u32[]{:S(2)}, u32[]{:S(2)}) collective-permute-start(bf16[64,512]{1,0:T(8,128)(2,1)S(1)} %fusion.10), channel_id=1, source_target_pairs={{0,8},{4,12},{8,0},{12,4},{1,9},{5,13},{9,1},{13,5},{2,10},{6,14},... | collective-permute-start | bytes 196616 | tf_op jit(solution)/shard_map/ppermute | solution.py:157
  104.5 10.3 %collective-permute-start.14 = (bf16[64,1536]{1,0:T(8,128)(2,1)S(1)}, bf16[64,1536]{1,0:T(8,128)(2,1)S(1)}, u32[]{:S(2)}, u32[]{:S(2)}) collective-permute-start(bf16[64,1536]{1,0:T(8,128)(2,1)S(1)} %fusion.4), channel_id=1, source_target_pairs={{0,8},{4,12},{8,0},{12,4},{1,9},{5,13},{9,1},{13,5},{2,10},{6,14},... | collective-permute-start | bytes 589832 | tf_op jit(solution)/shard_map/ppermute | solution.py:157
  107.4 5.0 %collective-permute-start.18 = (bf16[2,64,512]{2,1,0:T(8,128)(2,1)S(1)}, bf16[2,64,512]{2,1,0:T(8,128)(2,1)S(1)}, u32[]{:S(2)}, u32[]{:S(2)}) collective-permute-start(bf16[2,64,512]{2,1,0:T(8,128)(2,1)S(1)} %slice.77), channel_id=1, source_target_pairs={{0,4},{4,0},{8,12},{12,8},{1,5},{5,1},{9,13},{13,9},{2,6},{6,2},{1... | collective-permute-start | bytes 393224 | tf_op jit(solution)/shard_map/ppermute | solution.py:157
  112.5 5.2 %collective-permute-start.19 = (bf16[64,512]{1,0:T(8,128)(2,1)S(1)}, bf16[64,512]{1,0:T(8,128)(2,1)S(1)}, u32[]{:S(2)}, u32[]{:S(2)}) collective-permute-start(bf16[64,512]{1,0:T(8,128)(2,1)S(1)} %fusion.11), channel_id=1, source_target_pairs={{0,8},{4,12},{8,0},{12,4},{1,9},{5,13},{9,1},{13,5},{2,10},{6,14},... | collective-permute-start | bytes 196616 | tf_op jit(solution)/shard_map/ppermute | solution.py:157
  (1 other events, 0.7 us)

commit v8 on v7

--- a/solution.py
+++ b/solution.py
@@ -9,7 +9,7 @@
 
 CHIPS = 8
 TILE = 512
-COLUMNS = ((0, 1024), (1024, 1536), (2560, 512), (3072, 512))
+COLUMNS = ((0, 1024), (1024, 1536), (2560, 1024))
 LIGHT, HEAVY = 0.01, 4.0
 
 
@@ -178,6 +178,7 @@
     for relative, block in zip(odd, blocks):
         arrived[relative] = send_to_chip(block, relative)
     blocks = spread_rows(hidden, expert_ids, gate_weights, own, even, near)
+    blocks = after(blocks, [arrived[r] for r in odd])
     for relative, block in zip(even, blocks):
         arrived[relative] = send_to_chip(block, relative) if relative else block
     across, kept, lines, pairs, results = [], [], [], [], []
@@ -214,9 +215,8 @@
     last = mix_odd(2, last)
     last = mix_even((1,), last, LIGHT)
     last = add_x(1, last)
-    last = mix_odd(3, last)
-    last = mix_even((2, 3), last, LIGHT)
     last = add_z(0, last)
+    last = mix_even((2,), last, LIGHT)
     for i in range(2, len(COLUMNS)):
         last = add_x(i, last)
         last = add_z(i - 1, last)

time: 119 us -> 108 us (0.908)
  starting transfers between devices: 35.1 us -> 22.8 us
  waiting for transfers between devices: 52.9 us -> 55.2 us
    ppermute x7, waiting for transfers between devices: 21.4 us -> 30.9 us  [send_to_chip(): lax.ppermute(block, ('z', 'x'), [(i, i ^ relative) for i in range(sizes[0...]
    ppermute x13 -> x10, starting transfers between devices: 17.7 us -> 10.1 us  [swap(): lax.ppermute(block, axis, [(i, i ^ distance) for i in range(lax.axis_size...]
    ppermute x13 -> x10, waiting for transfers between devices: 31.5 us -> 24.3 us  [swap(): lax.ppermute(block, axis, [(i, i ^ distance) for i in range(lax.axis_size...]
    ppermute x7, starting transfers between devices: 17.4 us -> 12.7 us  [send_to_chip(): lax.ppermute(block, ('z', 'x'), [(i, i ^ relative) for i in range(sizes[0...]
    pallas_call x7 -> x6, Pallas kernels: 20.7 us -> 19.6 us  [mix(): pl.pallas_call(mix_kernel, grid=(width // TILE,), in_specs=[whole] * len(...]
  transfers between devices with their start and end apart: 20 -> 17, of which waited for: 10 -> 9; matrix products, arithmetic and copies ran while one was open for 1% -> 1% of each run, Pallas kernels for 19% -> 20%
where the time goes in v8:
time: 108 us; the launch traced here: 107 us
  waiting for transfers between devices  55.2 us (51%)
  starting transfers between devices  22.8 us (21%)
  Pallas kernels  21.4 us (20%)
  local copies, waits for them, and re-layouts  5.93 us (5%)
  other arithmetic  1.8 us (2%)
    ppermute x7, waiting for transfers between devices, send_to_chip(): lax.ppermute(block, ('z', 'x'), [(i, i ^ relative) for i in range(sizes[0...  30.9 us
    ppermute x10, waiting for transfers between devices, swap(): lax.ppermute(block, axis, [(i, i ^ distance) for i in range(lax.axis_size...  24.3 us
    pallas_call x6, Pallas kernels, mix(): pl.pallas_call(mix_kernel, grid=(width // TILE,), in_specs=[whole] * len(...  19.6 us
    ppermute x7, starting transfers between devices, send_to_chip(): lax.ppermute(block, ('z', 'x'), [(i, i ^ relative) for i in range(sizes[0...  12.7 us
    ppermute x10, starting transfers between devices, swap(): lax.ppermute(block, axis, [(i, i ^ distance) for i in range(lax.axis_size...  10.1 us
    unnamed x10, local copies, waits for them, and re-layouts  5.68 us
  transfers between devices with their start and end apart: 17, of which 9 were waited for; matrix products, arithmetic and copies ran while one was open for 1% of the time, Pallas kernels for 20%

profile of v8, /device:TPU:0, one launch (start us, length us, event | category | flops | bytes accessed | tf_op | source)
XLA Modules:
  0.0 107.3 jit_solution(8741459084281690025)
XLA Ops:
  0.5 1.2 %copy-done.2 = bf16[64,8,1024]{2,1,0:T(8,128)(2,1)S(1)} copy-done((bf16[64,8,1024]{2,1,0:T(8,128)(2,1)S(1)}, bf16[64,8,1024]{2,1,0:T(8,128)(2,1)}, u32[]{:S(2)}) %copy-start.2) | copy-done | bytes 1048600
  4.0 5.6 %collective-permute-start = (bf16[2,64,1024]{2,1,0:T(8,128)(2,1)S(1)}, bf16[2,64,1024]{2,1,0:T(8,128)(2,1)S(1)}, u32[]{:S(2)}, u32[]{:S(2)}) collective-permute-start(bf16[2,64,1024]{2,1,0:T(8,128)(2,1)S(1)} %get-tuple-element.30), channel_id=1, source_target_pairs={{0,14},{2,12},{4,10},{6,8},{8,6},{10,4},{12,2},{14,0},{1,15},{3,13... | collective-permute-start | bytes 786440 | tf_op jit(solution)/shard_map/ppermute | solution.py:162
  9.6 1.7 %collective-permute-start.2 = (bf16[2,64,1024]{2,1,0:T(8,128)(2,1)S(1)}, bf16[2,64,1024]{2,1,0:T(8,128)(2,1)S(1)}, u32[]{:S(2)}, u32[]{:S(2)}) collective-permute-start(bf16[2,64,1024]{2,1,0:T(8,128)(2,1)S(1)} %get-tuple-element.32), channel_id=1, source_target_pairs={{0,6},{2,4},{4,2},{6,0},{8,14},{10,12},{12,10},{14,8},{1,7},{3,5},... | collective-permute-start | bytes 786440 | tf_op jit(solution)/shard_map/ppermute | solution.py:162
  11.7 3.1 %copy-done = bf16[1,1024,3584]{2,1,0:T(8,128)(2,1)S(1)} copy-done((bf16[1,1024,3584]{2,1,0:T(8,128)(2,1)S(1)}, bf16[1,1024,3584]{2,1,0:T(8,128)(2,1)}, u32[]{:S(2)}) %copy-start) | copy-done | bytes 7340056
  15.6 1.3 %collective-permute-done.refs_0_ = bf16[2,64,1024]{2,1,0:T(8,128)(2,1)S(1)} collective-permute-done((bf16[2,64,1024]{2,1,0:T(8,128)(2,1)S(1)}, bf16[2,64,1024]{2,1,0:T(8,128)(2,1)S(1)}, u32[]{:S(2)}, u32[]{:S(2)}) %collective-permute-start) | collective-permute-done | bytes 262176 | tf_op jit(solution)/shard_map/ppermute | solution.py:162
  17.0 17.8 %collective-permute-done.1.refs_1_ = bf16[2,64,1024]{2,1,0:T(8,128)(2,1)S(1)} collective-permute-done((bf16[2,64,1024]{2,1,0:T(8,128)(2,1)S(1)}, bf16[2,64,1024]{2,1,0:T(8,128)(2,1)S(1)}, u32[]{:S(2)}, u32[]{:S(2)}) %collective-permute-start.1) | collective-permute-done | bytes 262176 | tf_op jit(solution)/shard_map/ppermute | solution.py:162
  34.8 4.4 %collective-permute-start.4 = (bf16[2,64,1024]{2,1,0:T(8,128)(2,1)S(1)}, bf16[2,64,1024]{2,1,0:T(8,128)(2,1)S(1)}, u32[]{:S(2)}, u32[]{:S(2)}) collective-permute-start(bf16[2,64,1024]{2,1,0:T(8,128)(2,1)S(1)} %get-tuple-element.34), channel_id=1, source_target_pairs={{0,12},{2,14},{4,8},{6,10},{8,4},{10,6},{12,0},{14,2},{1,13},{3,15... | collective-permute-start | bytes 786440 | tf_op jit(solution)/shard_map/ppermute | solution.py:162
  39.8 2.8 %mix.6 = bf16[4,64,1024]{2,1,0:T(8,128)(2,1)S(1)} custom-call(bf16[2,64,1024]{2,1,0:T(8,128)(2,1)S(1)} %collective-permute-done.refs_0_, bf16[2,64,1024]{2,1,0:T(8,128)(2,1)S(1)} %collective-permute-done.1.refs_1_, bf16[2,64,1024]{2,1,0:T(8,128)(2,1)S(1)} %collective-permute-done.2.refs_2_, bf16[2,64,1024]{2,1,0:T(8,128)(2,1)S(1)} %collective-permute-done.3.refs_3_, ...), custom_call_target="tpu_custom_call" | custom-call | flops 10737418 | bytes 41943 | tf_op jit(solution)/shard_map/mix/pallas_call | solution.py:139
  42.6 1.6 %collective-permute-start.8 = (bf16[4,64,1024]{2,1,0:T(8,128)(2,1)S(1)}, bf16[4,64,1024]{2,1,0:T(8,128)(2,1)S(1)}, u32[]{:S(2)}, u32[]{:S(2)}) collective-permute-start(bf16[4,64,1024]{2,1,0:T(8,128)(2,1)S(1)} %mix.6), channel_id=1, source_target_pairs={{0,2},{2,0},{1,3},{3,1},{4,6},{6,4},{5,7},{7,5},{8,10},{10,8},{9,1... | collective-permute-start | bytes 1572872 | tf_op jit(solution)/shard_map/ppermute | solution.py:157
  44.3 4.1 %mix.7 = bf16[4,64,1536]{2,1,0:T(8,128)(2,1)S(1)} custom-call(bf16[2,64,1024]{2,1,0:T(8,128)(2,1)S(1)} %collective-permute-done.refs_0_, bf16[2,64,1024]{2,1,0:T(8,128)(2,1)S(1)} %collective-permute-done.1.refs_1_, bf16[2,64,1024]{2,1,0:T(8,128)(2,1)S(1)} %collective-permute-done.2.refs_2_, bf16[2,64,1024]{2,1,0:T(8,128)(2,1)S(1)} %collective-permute-done.3.refs_3_, ...), custom_call_target="tpu_custom_call" | custom-call | flops 16106127 | bytes 62914 | tf_op jit(solution)/shard_map/mix/pallas_call | solution.py:139
  48.9 11.8 %collective-permute-done.5.refs_1_ = bf16[2,64,1024]{2,1,0:T(8,128)(2,1)S(1)} collective-permute-done((bf16[2,64,1024]{2,1,0:T(8,128)(2,1)S(1)}, bf16[2,64,1024]{2,1,0:T(8,128)(2,1)S(1)}, u32[]{:S(2)}, u32[]{:S(2)}) %collective-permute-start.5) | collective-permute-done | bytes 262176 | tf_op jit(solution)/shard_map/ppermute | solution.py:162
  60.7 2.8 %mix.8 = bf16[4,64,1024]{2,1,0:T(8,128)(2,1)S(1)} custom-call(bf16[2,64,1024]{2,1,0:T(8,128)(2,1)S(1)} %collective-permute-done.4.refs_0_, bf16[2,64,1024]{2,1,0:T(8,128)(2,1)S(1)} %collective-permute-done.5.refs_1_, bf16[2,64,1024]{2,1,0:T(8,128)(2,1)S(1)} %collective-permute-done.6.refs_2_, bf16[2,64,1024]{2,1,0:T(8,128)(2,1)S(1)} %get-tuple-element.44.refs_3_, ...), custom_call_target="tpu_custom_call" | custom-call | flops 4294967296 | bytes 16777216 | tf_op jit(solution)/shard_map/mix/pallas_call | solution.py:139
  63.8 2.8 %mix.9 = bf16[4,64,1024]{2,1,0:T(8,128)(2,1)S(1)} custom-call(bf16[2,64,1024]{2,1,0:T(8,128)(2,1)S(1)} %collective-permute-done.refs_0_, bf16[2,64,1024]{2,1,0:T(8,128)(2,1)S(1)} %collective-permute-done.1.refs_1_, bf16[2,64,1024]{2,1,0:T(8,128)(2,1)S(1)} %collective-permute-done.2.refs_2_, bf16[2,64,1024]{2,1,0:T(8,128)(2,1)S(1)} %collective-permute-done.3.refs_3_, ...), custom_call_target="tpu_custom_call" | custom-call | flops 10737418 | bytes 41943 | tf_op jit(solution)/shard_map/mix/pallas_call | solution.py:139
  67.3 4.1 %mix.10 = bf16[4,64,1536]{2,1,0:T(8,128)(2,1)S(1)} custom-call(bf16[2,64,1024]{2,1,0:T(8,128)(2,1)S(1)} %collective-permute-done.4.refs_0_, bf16[2,64,1024]{2,1,0:T(8,128)(2,1)S(1)} %collective-permute-done.5.refs_1_, bf16[2,64,1024]{2,1,0:T(8,128)(2,1)S(1)} %collective-permute-done.6.refs_2_, bf16[2,64,1024]{2,1,0:T(8,128)(2,1)S(1)} %get-tuple-element.44.refs_3_, ...), custom_call_target="tpu_custom_call" | custom-call | flops 16106127 | bytes 62914 | tf_op jit(solution)/shard_map/mix/pallas_call | solution.py:139
  71.4 3.0 %collective-permute-done.9 = bf16[4,64,1536]{2,1,0:T(8,128)(2,1)S(1)} collective-permute-done((bf16[4,64,1536]{2,1,0:T(8,128)(2,1)S(1)}, bf16[4,64,1536]{2,1,0:T(8,128)(2,1)S(1)}, u32[]{:S(2)}, u32[]{:S(2)}) %collective-permute-start.9) | collective-permute-done | bytes 786464 | tf_op jit(solution)/shard_map/ppermute | solution.py:157
  74.8 2.4 %collective-permute-start.11 = (bf16[64,1024]{1,0:T(8,128)(2,1)S(1)}, bf16[64,1024]{1,0:T(8,128)(2,1)S(1)}, u32[]{:S(2)}, u32[]{:S(2)}) collective-permute-start(bf16[64,1024]{1,0:T(8,128)(2,1)S(1)} %fusion.7), channel_id=1, source_target_pairs={{0,8},{4,12},{8,0},{12,4},{1,9},{5,13},{9,1},{13,5},{2,10},{6,14},... | collective-permute-start | bytes 393224 | tf_op jit(solution)/shard_map/ppermute | solution.py:157
  77.3 2.8 %mix.11 = bf16[4,64,1024]{2,1,0:T(8,128)(2,1)S(1)} custom-call(bf16[2,64,1024]{2,1,0:T(8,128)(2,1)S(1)} %collective-permute-done.4.refs_0_, bf16[2,64,1024]{2,1,0:T(8,128)(2,1)S(1)} %collective-permute-done.5.refs_1_, bf16[2,64,1024]{2,1,0:T(8,128)(2,1)S(1)} %collective-permute-done.6.refs_2_, bf16[2,64,1024]{2,1,0:T(8,128)(2,1)S(1)} %get-tuple-element.44.refs_3_, ...), custom_call_target="tpu_custom_call" | custom-call | flops 10737418 | bytes 41943 | tf_op jit(solution)/shard_map/mix/pallas_call | solution.py:139
  80.1 2.1 %collective-permute-start.13 = (bf16[2,64,1536]{2,1,0:T(8,128)(2,1)S(1)}, bf16[2,64,1536]{2,1,0:T(8,128)(2,1)S(1)}, u32[]{:S(2)}, u32[]{:S(2)}) collective-permute-start(bf16[2,64,1536]{2,1,0:T(8,128)(2,1)S(1)} %slice.47), channel_id=1, source_target_pairs={{0,4},{4,0},{8,12},{12,8},{1,5},{5,1},{9,13},{13,9},{2,6},{6,2},{1... | collective-permute-start | bytes 1179656 | tf_op jit(solution)/shard_map/ppermute | solution.py:157
  82.2 1.6 %collective-permute-done.12 = bf16[4,64,1024]{2,1,0:T(8,128)(2,1)S(1)} collective-permute-done((bf16[4,64,1024]{2,1,0:T(8,128)(2,1)S(1)}, bf16[4,64,1024]{2,1,0:T(8,128)(2,1)S(1)}, u32[]{:S(2)}, u32[]{:S(2)}) %collective-permute-start.12) | collective-permute-done | bytes 524320 | tf_op jit(solution)/shard_map/ppermute | solution.py:157
  84.0 1.5 %collective-permute-start.15 = (bf16[2,64,1024]{2,1,0:T(8,128)(2,1)S(1)}, bf16[2,64,1024]{2,1,0:T(8,128)(2,1)S(1)}, u32[]{:S(2)}, u32[]{:S(2)}) collective-permute-start(bf16[2,64,1024]{2,1,0:T(8,128)(2,1)S(1)} %slice.51), channel_id=1, source_target_pairs={{0,4},{4,0},{8,12},{12,8},{1,5},{5,1},{9,13},{13,9},{2,6},{6,2},{1... | collective-permute-start | bytes 786440 | tf_op jit(solution)/shard_map/ppermute | solution.py:157
  85.5 8.1 %collective-permute-done.13 = bf16[2,64,1536]{2,1,0:T(8,128)(2,1)S(1)} collective-permute-done((bf16[2,64,1536]{2,1,0:T(8,128)(2,1)S(1)}, bf16[2,64,1536]{2,1,0:T(8,128)(2,1)S(1)}, u32[]{:S(2)}, u32[]{:S(2)}) %collective-permute-start.13) | collective-permute-done | bytes 393248 | tf_op jit(solution)/shard_map/ppermute | solution.py:157
  93.8 2.6 %collective-permute-done.15 = bf16[2,64,1024]{2,1,0:T(8,128)(2,1)S(1)} collective-permute-done((bf16[2,64,1024]{2,1,0:T(8,128)(2,1)S(1)}, bf16[2,64,1024]{2,1,0:T(8,128)(2,1)S(1)}, u32[]{:S(2)}, u32[]{:S(2)}) %collective-permute-start.15) | collective-permute-done | bytes 262176 | tf_op jit(solution)/shard_map/ppermute | solution.py:157
  97.5 7.6 %collective-permute-done.14 = bf16[64,1536]{1,0:T(8,128)(2,1)S(1)} collective-permute-done((bf16[64,1536]{1,0:T(8,128)(2,1)S(1)}, bf16[64,1536]{1,0:T(8,128)(2,1)S(1)}, u32[]{:S(2)}, u32[]{:S(2)}) %collective-permute-start.14) | collective-permute-done | bytes 196640 | tf_op jit(solution)/shard_map/ppermute | solution.py:157
  105.1 1.4 %collective-permute-done.16 = bf16[64,1024]{1,0:T(8,128)(2,1)S(1)} collective-permute-done((bf16[64,1024]{1,0:T(8,128)(2,1)S(1)}, bf16[64,1024]{1,0:T(8,128)(2,1)S(1)}, u32[]{:S(2)}, u32[]{:S(2)}) %collective-permute-start.16) | collective-permute-done | bytes 131104 | tf_op jit(solution)/shard_map/ppermute | solution.py:157
  (47 shorter events, 8.9 us)
Async XLA Ops:
  0.0 39.8 %collective-permute-start.7 = (bf16[1024,3584]{1,0:T(8,128)(2,1)}, bf16[1024,3584]{1,0:T(8,128)(2,1)}, u32[]{:S(2)}, u32[]{:S(2)}) collective-permute-start(bf16[1024,3584]{1,0:T(8,128)(2,1)} %bitcast.29), channel_id=1, source_target_pairs={{0,1},{1,0},{2,3},{3,2},{4,5},{5,4},{6,7},{7,6},{8,9},{9,8},{10,11... | collective-permute-start | bytes 22020104 | tf_op jit(solution)/shard_map/ppermute | solution.py:157
  0.5 1.2 %copy-start.2 = (bf16[64,8,1024]{2,1,0:T(8,128)(2,1)S(1)}, bf16[64,8,1024]{2,1,0:T(8,128)(2,1)}, u32[]{:S(2)}) copy-start(bf16[64,8,1024]{2,1,0:T(8,128)(2,1)} %param.4) | copy-start | bytes 3145732
  1.7 0.7 copy-start.3
  2.4 0.7 copy-start.4
  4.0 13.0 %collective-permute-start = (bf16[2,64,1024]{2,1,0:T(8,128)(2,1)S(1)}, bf16[2,64,1024]{2,1,0:T(8,128)(2,1)S(1)}, u32[]{:S(2)}, u32[]{:S(2)}) collective-permute-start(bf16[2,64,1024]{2,1,0:T(8,128)(2,1)S(1)} %get-tuple-element.30), channel_id=1, source_target_pairs={{0,14},{2,12},{4,10},{6,8},{8,6},{10,4},{12,2},{14,0},{1,15},{3,13... | collective-permute-start | bytes 786440 | tf_op jit(solution)/shard_map/ppermute | solution.py:162
  9.6 25.2 %collective-permute-start.1 = (bf16[2,64,1024]{2,1,0:T(8,128)(2,1)S(1)}, bf16[2,64,1024]{2,1,0:T(8,128)(2,1)S(1)}, u32[]{:S(2)}, u32[]{:S(2)}) collective-permute-start(bf16[2,64,1024]{2,1,0:T(8,128)(2,1)S(1)} %get-tuple-element.31), channel_id=1, source_target_pairs={{0,10},{2,8},{4,14},{6,12},{8,2},{10,0},{12,6},{14,4},{1,11},{3,9}... | collective-permute-start | bytes 786440 | tf_op jit(solution)/shard_map/ppermute | solution.py:162
  9.6 25.2 %collective-permute-start.2 = (bf16[2,64,1024]{2,1,0:T(8,128)(2,1)S(1)}, bf16[2,64,1024]{2,1,0:T(8,128)(2,1)S(1)}, u32[]{:S(2)}, u32[]{:S(2)}) collective-permute-start(bf16[2,64,1024]{2,1,0:T(8,128)(2,1)S(1)} %get-tuple-element.32), channel_id=1, source_target_pairs={{0,6},{2,4},{4,2},{6,0},{8,14},{10,12},{12,10},{14,8},{1,7},{3,5},... | collective-permute-start | bytes 786440 | tf_op jit(solution)/shard_map/ppermute | solution.py:162
  11.2 23.5 %collective-permute-start.3 = (bf16[2,64,1024]{2,1,0:T(8,128)(2,1)S(1)}, bf16[2,64,1024]{2,1,0:T(8,128)(2,1)S(1)}, u32[]{:S(2)}, u32[]{:S(2)}) collective-permute-start(bf16[2,64,1024]{2,1,0:T(8,128)(2,1)S(1)} %get-tuple-element.33), channel_id=1, source_target_pairs={{0,2},{2,0},{4,6},{6,4},{8,10},{10,8},{12,14},{14,12},{1,3},{3,1},... | collective-permute-start | bytes 786440 | tf_op jit(solution)/shard_map/ppermute | solution.py:162
  11.7 3.1 %copy-start = (bf16[1,1024,3584]{2,1,0:T(8,128)(2,1)S(1)}, bf16[1,1024,3584]{2,1,0:T(8,128)(2,1)}, u32[]{:S(2)}) copy-start(bf16[1,1024,3584]{2,1,0:T(8,128)(2,1)} %param.7) | copy-start | bytes 22020100
  14.7 25.1 %copy-start.1 = (bf16[1,1024,3584]{2,1,0:T(8,128)(2,1)S(1)}, bf16[1,1024,3584]{2,1,0:T(8,128)(2,1)}, u32[]{:S(2)}) copy-start(bf16[1,1024,3584]{2,1,0:T(8,128)(2,1)} %param.7) | copy-start | bytes 22020100
  34.8 14.1 %collective-permute-start.4 = (bf16[2,64,1024]{2,1,0:T(8,128)(2,1)S(1)}, bf16[2,64,1024]{2,1,0:T(8,128)(2,1)S(1)}, u32[]{:S(2)}, u32[]{:S(2)}) collective-permute-start(bf16[2,64,1024]{2,1,0:T(8,128)(2,1)S(1)} %get-tuple-element.34), channel_id=1, source_target_pairs={{0,12},{2,14},{4,8},{6,10},{8,4},{10,6},{12,0},{14,2},{1,13},{3,15... | collective-permute-start | bytes 786440 | tf_op jit(solution)/shard_map/ppermute | solution.py:162
  39.2 21.5 %collective-permute-start.5 = (bf16[2,64,1024]{2,1,0:T(8,128)(2,1)S(1)}, bf16[2,64,1024]{2,1,0:T(8,128)(2,1)S(1)}, u32[]{:S(2)}, u32[]{:S(2)}) collective-permute-start(bf16[2,64,1024]{2,1,0:T(8,128)(2,1)S(1)} %get-tuple-element.35), channel_id=1, source_target_pairs={{0,8},{2,10},{4,12},{6,14},{8,0},{10,2},{12,4},{14,6},{1,9},{3,11}... | collective-permute-start | bytes 786440 | tf_op jit(solution)/shard_map/ppermute | solution.py:162
  39.2 21.5 %collective-permute-start.6 = (bf16[2,64,1024]{2,1,0:T(8,128)(2,1)S(1)}, bf16[2,64,1024]{2,1,0:T(8,128)(2,1)S(1)}, u32[]{:S(2)}, u32[]{:S(2)}) collective-permute-start(bf16[2,64,1024]{2,1,0:T(8,128)(2,1)S(1)} %get-tuple-element.36), channel_id=1, source_target_pairs={{0,4},{2,6},{4,0},{6,2},{8,12},{10,14},{12,8},{14,10},{1,5},{3,7},... | collective-permute-start | bytes 786440 | tf_op jit(solution)/shard_map/ppermute | solution.py:162
  42.6 20.9 %collective-permute-start.8 = (bf16[4,64,1024]{2,1,0:T(8,128)(2,1)S(1)}, bf16[4,64,1024]{2,1,0:T(8,128)(2,1)S(1)}, u32[]{:S(2)}, u32[]{:S(2)}) collective-permute-start(bf16[4,64,1024]{2,1,0:T(8,128)(2,1)S(1)} %mix.6), channel_id=1, source_target_pairs={{0,2},{2,0},{1,3},{3,1},{4,6},{6,4},{5,7},{7,5},{8,10},{10,8},{9,1... | collective-permute-start | bytes 1572872 | tf_op jit(solution)/shard_map/ppermute | solution.py:157
  48.4 26.0 %collective-permute-start.9 = (bf16[4,64,1536]{2,1,0:T(8,128)(2,1)S(1)}, bf16[4,64,1536]{2,1,0:T(8,128)(2,1)S(1)}, u32[]{:S(2)}, u32[]{:S(2)}) collective-permute-start(bf16[4,64,1536]{2,1,0:T(8,128)(2,1)S(1)} %mix.7), channel_id=1, source_target_pairs={{0,2},{2,0},{1,3},{3,1},{4,6},{6,4},{5,7},{7,5},{8,10},{10,8},{9,1... | collective-permute-start | bytes 2359304 | tf_op jit(solution)/shard_map/ppermute | solution.py:157
  66.6 17.1 %collective-permute-start.12 = (bf16[4,64,1024]{2,1,0:T(8,128)(2,1)S(1)}, bf16[4,64,1024]{2,1,0:T(8,128)(2,1)S(1)}, u32[]{:S(2)}, u32[]{:S(2)}) collective-permute-start(bf16[4,64,1024]{2,1,0:T(8,128)(2,1)S(1)} %mix.9), channel_id=1, source_target_pairs={{0,2},{2,0},{1,3},{3,1},{4,6},{6,4},{5,7},{7,5},{8,10},{10,8},{9,1... | collective-permute-start | bytes 1572872 | tf_op jit(solution)/shard_map/ppermute | solution.py:157
  67.2 7.5 %collective-permute-start.10 = (bf16[2,64,1024]{2,1,0:T(8,128)(2,1)S(1)}, bf16[2,64,1024]{2,1,0:T(8,128)(2,1)S(1)}, u32[]{:S(2)}, u32[]{:S(2)}) collective-permute-start(bf16[2,64,1024]{2,1,0:T(8,128)(2,1)S(1)} %slice.43), channel_id=1, source_target_pairs={{0,4},{4,0},{8,12},{12,8},{1,5},{5,1},{9,13},{13,9},{2,6},{6,2},{1... | collective-permute-start | bytes 786440 | tf_op jit(solution)/shard_map/ppermute | solution.py:157
  74.8 7.4 %collective-permute-start.11 = (bf16[64,1024]{1,0:T(8,128)(2,1)S(1)}, bf16[64,1024]{1,0:T(8,128)(2,1)S(1)}, u32[]{:S(2)}, u32[]{:S(2)}) collective-permute-start(bf16[64,1024]{1,0:T(8,128)(2,1)S(1)} %fusion.7), channel_id=1, source_target_pairs={{0,8},{4,12},{8,0},{12,4},{1,9},{5,13},{9,1},{13,5},{2,10},{6,14},... | collective-permute-start | bytes 393224 | tf_op jit(solution)/shard_map/ppermute | solution.py:157
  80.1 13.5 %collective-permute-start.13 = (bf16[2,64,1536]{2,1,0:T(8,128)(2,1)S(1)}, bf16[2,64,1536]{2,1,0:T(8,128)(2,1)S(1)}, u32[]{:S(2)}, u32[]{:S(2)}) collective-permute-start(bf16[2,64,1536]{2,1,0:T(8,128)(2,1)S(1)} %slice.47), channel_id=1, source_target_pairs={{0,4},{4,0},{8,12},{12,8},{1,5},{5,1},{9,13},{13,9},{2,6},{6,2},{1... | collective-permute-start | bytes 1179656 | tf_op jit(solution)/shard_map/ppermute | solution.py:157
  84.0 12.4 %collective-permute-start.15 = (bf16[2,64,1024]{2,1,0:T(8,128)(2,1)S(1)}, bf16[2,64,1024]{2,1,0:T(8,128)(2,1)S(1)}, u32[]{:S(2)}, u32[]{:S(2)}) collective-permute-start(bf16[2,64,1024]{2,1,0:T(8,128)(2,1)S(1)} %slice.51), channel_id=1, source_target_pairs={{0,4},{4,0},{8,12},{12,8},{1,5},{5,1},{9,13},{13,9},{2,6},{6,2},{1... | collective-permute-start | bytes 786440 | tf_op jit(solution)/shard_map/ppermute | solution.py:157
  93.7 11.3 %collective-permute-start.14 = (bf16[64,1536]{1,0:T(8,128)(2,1)S(1)}, bf16[64,1536]{1,0:T(8,128)(2,1)S(1)}, u32[]{:S(2)}, u32[]{:S(2)}) collective-permute-start(bf16[64,1536]{1,0:T(8,128)(2,1)S(1)} %fusion.6), channel_id=1, source_target_pairs={{0,8},{4,12},{8,0},{12,4},{1,9},{5,13},{9,1},{13,5},{2,10},{6,14},... | collective-permute-start | bytes 589832 | tf_op jit(solution)/shard_map/ppermute | solution.py:157
  96.5 10.0 %collective-permute-start.16 = (bf16[64,1024]{1,0:T(8,128)(2,1)S(1)}, bf16[64,1024]{1,0:T(8,128)(2,1)S(1)}, u32[]{:S(2)}, u32[]{:S(2)}) collective-permute-start(bf16[64,1024]{1,0:T(8,128)(2,1)S(1)} %fusion.8), channel_id=1, source_target_pairs={{0,8},{4,12},{8,0},{12,4},{1,9},{5,13},{9,1},{13,5},{2,10},{6,14},... | collective-permute-start | bytes 393224 | tf_op jit(solution)/shard_map/ppermute | solution.py:157

commit v9 on v8

--- a/solution.py
+++ b/solution.py
@@ -9,8 +9,8 @@
 
 CHIPS = 8
 TILE = 512
-COLUMNS = ((0, 1024), (1024, 1536), (2560, 1024))
-LIGHT, HEAVY = 0.01, 4.0
+COLUMNS = ((0, 1536), (1536, 1536), (3072, 512))
+LIGHT = 0.01
 
 
 def passed_along(block, axis, distance):
@@ -181,12 +181,12 @@
     blocks = after(blocks, [arrived[r] for r in odd])
     for relative, block in zip(even, blocks):
         arrived[relative] = send_to_chip(block, relative) if relative else block
-    across, kept, lines, pairs, results = [], [], [], [], []
+    given, kept, lines, pairs, results = [], [], [], [], []
 
     def mix_odd(i, earlier):
         arrived[7] = after(arrived[7], earlier)
         block = mix([arrived[r] for r in odd], near, far, *COLUMNS[i], LIGHT)
-        across.append(swap(block, "x", 1))
+        given.append(block)
         return block
 
     def mix_even(parts, earlier, weight):
@@ -208,19 +208,19 @@
         pairs.append((pair[1], swap(pair[0].astype(jnp.bfloat16), "z", 2)))
         return pair
 
-    last = mix_odd(0, blocks[-1])
-    last = mix_odd(1, last)
-    last = mix_even((0,), last, HEAVY)
+    last = blocks[-1]
+    for i in range(len(COLUMNS)):
+        last = mix_odd(i, last)
+    across = [swap(block, "x", 1) for block in given]
+    last = mix_even((0,), last, LIGHT)
     last = add_x(0, last)
-    last = mix_odd(2, last)
     last = mix_even((1,), last, LIGHT)
+    last = mix_even((2,), last, LIGHT)
     last = add_x(1, last)
     last = add_z(0, last)
-    last = mix_even((2,), last, LIGHT)
-    for i in range(2, len(COLUMNS)):
-        last = add_x(i, last)
-        last = add_z(i - 1, last)
-    add_z(len(COLUMNS) - 1, last)
+    last = add_x(2, last)
+    last = add_z(1, last)
+    add_z(2, last)
     for mine, theirs in pairs:
         results.append((mine + theirs.astype(jnp.float32)).astype(jnp.bfloat16))
     return jnp.concatenate(results, axis=1)

time: 108 us -> 106 us (0.981)
  starting transfers between devices: 22.8 us -> 20.6 us
    ppermute x10, starting transfers between devices: 10.1 us -> 7.78 us  [swap(): lax.ppermute(block, axis, [(i, i ^ distance) for i in range(lax.axis_size...]
  transfers between devices with their start and end apart: 17 -> 17, of which waited for: 9 -> 9; matrix products, arithmetic and copies ran while one was open for 1% -> 1% of each run, Pallas kernels for 20% -> 17%
where the time goes in v9:
time: 106 us
  waiting for transfers between devices  54.9 us (52%)
  Pallas kernels  22.2 us (21%)
  starting transfers between devices  20.6 us (19%)
  local copies, waits for them, and re-layouts  5.93 us (6%)
  other arithmetic  1.76 us (2%)
    ppermute x7, waiting for transfers between devices, send_to_chip(): lax.ppermute(block, ('z', 'x'), [(i, i ^ relative) for i in range(sizes[0...  30.5 us
    ppermute x10, waiting for transfers between devices, swap(): lax.ppermute(block, axis, [(i, i ^ distance) for i in range(lax.axis_size...  24.4 us
    pallas_call x6, Pallas kernels, mix(): pl.pallas_call(mix_kernel, grid=(width // TILE,), in_specs=[whole] * len(...  20.4 us
    ppermute x7, starting transfers between devices, send_to_chip(): lax.ppermute(block, ('z', 'x'), [(i, i ^ relative) for i in range(sizes[0...  12.8 us
    ppermute x10, starting transfers between devices, swap(): lax.ppermute(block, axis, [(i, i ^ distance) for i in range(lax.axis_size...  7.78 us
    unnamed x10, local copies, waits for them, and re-layouts  5.68 us
  transfers between devices with their start and end apart: 17, of which 9 were waited for; matrix products, arithmetic and copies ran while one was open for 1% of the time, Pallas kernels for 17%

profile of v9, /device:TPU:0, one launch (start us, length us, event | category | flops | bytes accessed | tf_op | source)
XLA Modules:
  0.0 105.7 jit_solution(14847293736307063426)
XLA Ops:
  0.5 1.2 %copy-done.2 = bf16[64,8,1024]{2,1,0:T(8,128)(2,1)S(1)} copy-done((bf16[64,8,1024]{2,1,0:T(8,128)(2,1)S(1)}, bf16[64,8,1024]{2,1,0:T(8,128)(2,1)}, u32[]{:S(2)}) %copy-start.2) | copy-done | bytes 1048600
  3.1 0.9 spread_rows.3
  4.0 5.6 %collective-permute-start = (bf16[2,64,1024]{2,1,0:T(8,128)(2,1)S(1)}, bf16[2,64,1024]{2,1,0:T(8,128)(2,1)S(1)}, u32[]{:S(2)}, u32[]{:S(2)}) collective-permute-start(bf16[2,64,1024]{2,1,0:T(8,128)(2,1)S(1)} %get-tuple-element.32), channel_id=1, source_target_pairs={{0,14},{2,12},{4,10},{6,8},{8,6},{10,4},{12,2},{14,0},{1,15},{3,13... | collective-permute-start | bytes 786440 | tf_op jit(solution)/shard_map/ppermute | solution.py:162
  9.6 1.7 %collective-permute-start.2 = (bf16[2,64,1024]{2,1,0:T(8,128)(2,1)S(1)}, bf16[2,64,1024]{2,1,0:T(8,128)(2,1)S(1)}, u32[]{:S(2)}, u32[]{:S(2)}) collective-permute-start(bf16[2,64,1024]{2,1,0:T(8,128)(2,1)S(1)} %get-tuple-element.34), channel_id=1, source_target_pairs={{0,6},{2,4},{4,2},{6,0},{8,14},{10,12},{12,10},{14,8},{1,7},{3,5},... | collective-permute-start | bytes 786440 | tf_op jit(solution)/shard_map/ppermute | solution.py:162
  11.7 3.1 %copy-done = bf16[1,1024,3584]{2,1,0:T(8,128)(2,1)S(1)} copy-done((bf16[1,1024,3584]{2,1,0:T(8,128)(2,1)S(1)}, bf16[1,1024,3584]{2,1,0:T(8,128)(2,1)}, u32[]{:S(2)}) %copy-start) | copy-done | bytes 7340056
  14.7 0.9 spread_rows.2
  15.6 1.3 %collective-permute-done.refs_0_ = bf16[2,64,1024]{2,1,0:T(8,128)(2,1)S(1)} collective-permute-done((bf16[2,64,1024]{2,1,0:T(8,128)(2,1)S(1)}, bf16[2,64,1024]{2,1,0:T(8,128)(2,1)S(1)}, u32[]{:S(2)}, u32[]{:S(2)}) %collective-permute-start) | collective-permute-done | bytes 262176 | tf_op jit(solution)/shard_map/ppermute | solution.py:162
  17.0 17.8 %collective-permute-done.1.refs_1_ = bf16[2,64,1024]{2,1,0:T(8,128)(2,1)S(1)} collective-permute-done((bf16[2,64,1024]{2,1,0:T(8,128)(2,1)S(1)}, bf16[2,64,1024]{2,1,0:T(8,128)(2,1)S(1)}, u32[]{:S(2)}, u32[]{:S(2)}) %collective-permute-start.1) | collective-permute-done | bytes 262176 | tf_op jit(solution)/shard_map/ppermute | solution.py:162
  34.8 4.1 %mix.6 = bf16[4,64,1536]{2,1,0:T(8,128)(2,1)S(1)} custom-call(bf16[2,64,1024]{2,1,0:T(8,128)(2,1)S(1)} %collective-permute-done.refs_0_, bf16[2,64,1024]{2,1,0:T(8,128)(2,1)S(1)} %collective-permute-done.1.refs_1_, bf16[2,64,1024]{2,1,0:T(8,128)(2,1)S(1)} %collective-permute-done.2.refs_2_, bf16[2,64,1024]{2,1,0:T(8,128)(2,1)S(1)} %collective-permute-done.3.refs_3_, ...), custom_call_target="tpu_custom_call" | custom-call | flops 16106127 | bytes 62914 | tf_op jit(solution)/shard_map/mix/pallas_call | solution.py:139
  38.9 1.5 %collective-permute-start.8 = (bf16[4,64,1536]{2,1,0:T(8,128)(2,1)S(1)}, bf16[4,64,1536]{2,1,0:T(8,128)(2,1)S(1)}, u32[]{:S(2)}, u32[]{:S(2)}) collective-permute-start(bf16[4,64,1536]{2,1,0:T(8,128)(2,1)S(1)} %mix.6), channel_id=1, source_target_pairs={{0,2},{2,0},{1,3},{3,1},{4,6},{6,4},{5,7},{7,5},{8,10},{10,8},{9,1... | collective-permute-start | bytes 2359304 | tf_op jit(solution)/shard_map/ppermute | solution.py:157
  40.4 4.5 %collective-permute-start.4 = (bf16[2,64,1024]{2,1,0:T(8,128)(2,1)S(1)}, bf16[2,64,1024]{2,1,0:T(8,128)(2,1)S(1)}, u32[]{:S(2)}, u32[]{:S(2)}) collective-permute-start(bf16[2,64,1024]{2,1,0:T(8,128)(2,1)S(1)} %get-tuple-element.36), channel_id=1, source_target_pairs={{0,12},{2,14},{4,8},{6,10},{8,4},{10,6},{12,0},{14,2},{1,13},{3,15... | collective-permute-start | bytes 786440 | tf_op jit(solution)/shard_map/ppermute | solution.py:162
  45.5 4.1 %mix.7 = bf16[4,64,1536]{2,1,0:T(8,128)(2,1)S(1)} custom-call(bf16[2,64,1024]{2,1,0:T(8,128)(2,1)S(1)} %collective-permute-done.refs_0_, bf16[2,64,1024]{2,1,0:T(8,128)(2,1)S(1)} %collective-permute-done.1.refs_1_, bf16[2,64,1024]{2,1,0:T(8,128)(2,1)S(1)} %collective-permute-done.2.refs_2_, bf16[2,64,1024]{2,1,0:T(8,128)(2,1)S(1)} %collective-permute-done.3.refs_3_, ...), custom_call_target="tpu_custom_call" | custom-call | flops 16106127 | bytes 62914 | tf_op jit(solution)/shard_map/mix/pallas_call | solution.py:139
  50.1 2.0 %mix.8 = bf16[4,64,512]{2,1,0:T(8,128)(2,1)S(1)} custom-call(bf16[2,64,1024]{2,1,0:T(8,128)(2,1)S(1)} %collective-permute-done.refs_0_, bf16[2,64,1024]{2,1,0:T(8,128)(2,1)S(1)} %collective-permute-done.1.refs_1_, bf16[2,64,1024]{2,1,0:T(8,128)(2,1)S(1)} %collective-permute-done.2.refs_2_, bf16[2,64,1024]{2,1,0:T(8,128)(2,1)S(1)} %collective-permute-done.3.refs_3_, ...), custom_call_target="tpu_custom_call" | custom-call | flops 5368709 | bytes 20971 | tf_op jit(solution)/shard_map/mix/pallas_call | solution.py:139
  52.2 1.6 %collective-permute-start.12 = (bf16[4,64,512]{2,1,0:T(8,128)(2,1)S(1)}, bf16[4,64,512]{2,1,0:T(8,128)(2,1)S(1)}, u32[]{:S(2)}, u32[]{:S(2)}) collective-permute-start(bf16[4,64,512]{2,1,0:T(8,128)(2,1)S(1)} %mix.8), channel_id=1, source_target_pairs={{0,2},{2,0},{1,3},{3,1},{4,6},{6,4},{5,7},{7,5},{8,10},{10,8},{9,1... | collective-permute-start | bytes 786440 | tf_op jit(solution)/shard_map/ppermute | solution.py:157
  53.8 11.3 %collective-permute-done.5.refs_1_ = bf16[2,64,1024]{2,1,0:T(8,128)(2,1)S(1)} collective-permute-done((bf16[2,64,1024]{2,1,0:T(8,128)(2,1)S(1)}, bf16[2,64,1024]{2,1,0:T(8,128)(2,1)S(1)}, u32[]{:S(2)}, u32[]{:S(2)}) %collective-permute-start.5) | collective-permute-done | bytes 262176 | tf_op jit(solution)/shard_map/ppermute | solution.py:162
  65.1 4.1 %mix.9 = bf16[4,64,1536]{2,1,0:T(8,128)(2,1)S(1)} custom-call(bf16[2,64,1024]{2,1,0:T(8,128)(2,1)S(1)} %collective-permute-done.4.refs_0_, bf16[2,64,1024]{2,1,0:T(8,128)(2,1)S(1)} %collective-permute-done.5.refs_1_, bf16[2,64,1024]{2,1,0:T(8,128)(2,1)S(1)} %collective-permute-done.6.refs_2_, bf16[2,64,1024]{2,1,0:T(8,128)(2,1)S(1)} %get-tuple-element.45.refs_3_, ...), custom_call_target="tpu_custom_call" | custom-call | flops 16106127 | bytes 62914 | tf_op jit(solution)/shard_map/mix/pallas_call | solution.py:139
  69.7 4.1 %mix.10 = bf16[4,64,1536]{2,1,0:T(8,128)(2,1)S(1)} custom-call(bf16[2,64,1024]{2,1,0:T(8,128)(2,1)S(1)} %collective-permute-done.4.refs_0_, bf16[2,64,1024]{2,1,0:T(8,128)(2,1)S(1)} %collective-permute-done.5.refs_1_, bf16[2,64,1024]{2,1,0:T(8,128)(2,1)S(1)} %collective-permute-done.6.refs_2_, bf16[2,64,1024]{2,1,0:T(8,128)(2,1)S(1)} %get-tuple-element.45.refs_3_, ...), custom_call_target="tpu_custom_call" | custom-call | flops 16106127 | bytes 62914 | tf_op jit(solution)/shard_map/mix/pallas_call | solution.py:139
  73.8 2.0 %mix.11 = bf16[4,64,512]{2,1,0:T(8,128)(2,1)S(1)} custom-call(bf16[2,64,1024]{2,1,0:T(8,128)(2,1)S(1)} %collective-permute-done.4.refs_0_, bf16[2,64,1024]{2,1,0:T(8,128)(2,1)S(1)} %collective-permute-done.5.refs_1_, bf16[2,64,1024]{2,1,0:T(8,128)(2,1)S(1)} %collective-permute-done.6.refs_2_, bf16[2,64,1024]{2,1,0:T(8,128)(2,1)S(1)} %get-tuple-element.45.refs_3_, ...), custom_call_target="tpu_custom_call" | custom-call | flops 5368709 | bytes 20971 | tf_op jit(solution)/shard_map/mix/pallas_call | solution.py:139
  76.7 1.7 %collective-permute-start.13 = (bf16[2,64,1536]{2,1,0:T(8,128)(2,1)S(1)}, bf16[2,64,1536]{2,1,0:T(8,128)(2,1)S(1)}, u32[]{:S(2)}, u32[]{:S(2)}) collective-permute-start(bf16[2,64,1536]{2,1,0:T(8,128)(2,1)S(1)} %slice.47), channel_id=1, source_target_pairs={{0,4},{4,0},{8,12},{12,8},{1,5},{5,1},{9,13},{13,9},{2,6},{6,2},{1... | collective-permute-start | bytes 1179656 | tf_op jit(solution)/shard_map/ppermute | solution.py:157
  78.4 4.4 %collective-permute-done.10 = bf16[2,64,1536]{2,1,0:T(8,128)(2,1)S(1)} collective-permute-done((bf16[2,64,1536]{2,1,0:T(8,128)(2,1)S(1)}, bf16[2,64,1536]{2,1,0:T(8,128)(2,1)S(1)}, u32[]{:S(2)}, u32[]{:S(2)}) %collective-permute-start.10) | collective-permute-done | bytes 393248 | tf_op jit(solution)/shard_map/ppermute | solution.py:157
  83.2 9.9 %collective-permute-done.13 = bf16[2,64,1536]{2,1,0:T(8,128)(2,1)S(1)} collective-permute-done((bf16[2,64,1536]{2,1,0:T(8,128)(2,1)S(1)}, bf16[2,64,1536]{2,1,0:T(8,128)(2,1)S(1)}, u32[]{:S(2)}, u32[]{:S(2)}) %collective-permute-start.13) | collective-permute-done | bytes 393248 | tf_op jit(solution)/shard_map/ppermute | solution.py:157
  93.6 1.8 %collective-permute-done.15 = bf16[2,64,512]{2,1,0:T(8,128)(2,1)S(1)} collective-permute-done((bf16[2,64,512]{2,1,0:T(8,128)(2,1)S(1)}, bf16[2,64,512]{2,1,0:T(8,128)(2,1)S(1)}, u32[]{:S(2)}, u32[]{:S(2)}) %collective-permute-start.15) | collective-permute-done | bytes 131104 | tf_op jit(solution)/shard_map/ppermute | solution.py:157
  95.5 1.5 %collective-permute-start.16 = (bf16[64,512]{1,0:T(8,128)(2,1)S(1)}, bf16[64,512]{1,0:T(8,128)(2,1)S(1)}, u32[]{:S(2)}, u32[]{:S(2)}) collective-permute-start(bf16[64,512]{1,0:T(8,128)(2,1)S(1)} %fusion.8), channel_id=1, source_target_pairs={{0,8},{4,12},{8,0},{12,4},{1,9},{5,13},{9,1},{13,5},{2,10},{6,14},... | collective-permute-start | bytes 196616 | tf_op jit(solution)/shard_map/ppermute | solution.py:157
  97.0 7.9 %collective-permute-done.16 = bf16[64,512]{1,0:T(8,128)(2,1)S(1)} collective-permute-done((bf16[64,512]{1,0:T(8,128)(2,1)S(1)}, bf16[64,512]{1,0:T(8,128)(2,1)S(1)}, u32[]{:S(2)}, u32[]{:S(2)}) %collective-permute-start.16) | collective-permute-done | bytes 65568 | tf_op jit(solution)/shard_map/ppermute | solution.py:157
  (47 shorter events, 6.5 us)
Async XLA Ops:
  0.0 34.8 %collective-permute-start.7 = (bf16[1024,3584]{1,0:T(8,128)(2,1)}, bf16[1024,3584]{1,0:T(8,128)(2,1)}, u32[]{:S(2)}, u32[]{:S(2)}) collective-permute-start(bf16[1024,3584]{1,0:T(8,128)(2,1)} %bitcast.29), channel_id=1, source_target_pairs={{0,1},{1,0},{2,3},{3,2},{4,5},{5,4},{6,7},{7,6},{8,9},{9,8},{10,11... | collective-permute-start | bytes 22020104 | tf_op jit(solution)/shard_map/ppermute | solution.py:157
  0.5 1.2 %copy-start.2 = (bf16[64,8,1024]{2,1,0:T(8,128)(2,1)S(1)}, bf16[64,8,1024]{2,1,0:T(8,128)(2,1)}, u32[]{:S(2)}) copy-start(bf16[64,8,1024]{2,1,0:T(8,128)(2,1)} %param.4) | copy-start | bytes 3145732
  1.7 0.7 copy-start.3
  2.4 0.7 copy-start.4
  4.0 13.0 %collective-permute-start = (bf16[2,64,1024]{2,1,0:T(8,128)(2,1)S(1)}, bf16[2,64,1024]{2,1,0:T(8,128)(2,1)S(1)}, u32[]{:S(2)}, u32[]{:S(2)}) collective-permute-start(bf16[2,64,1024]{2,1,0:T(8,128)(2,1)S(1)} %get-tuple-element.32), channel_id=1, source_target_pairs={{0,14},{2,12},{4,10},{6,8},{8,6},{10,4},{12,2},{14,0},{1,15},{3,13... | collective-permute-start | bytes 786440 | tf_op jit(solution)/shard_map/ppermute | solution.py:162
  9.6 25.2 %collective-permute-start.1 = (bf16[2,64,1024]{2,1,0:T(8,128)(2,1)S(1)}, bf16[2,64,1024]{2,1,0:T(8,128)(2,1)S(1)}, u32[]{:S(2)}, u32[]{:S(2)}) collective-permute-start(bf16[2,64,1024]{2,1,0:T(8,128)(2,1)S(1)} %get-tuple-element.33), channel_id=1, source_target_pairs={{0,10},{2,8},{4,14},{6,12},{8,2},{10,0},{12,6},{14,4},{1,11},{3,9}... | collective-permute-start | bytes 786440 | tf_op jit(solution)/shard_map/ppermute | solution.py:162
  9.6 25.2 %collective-permute-start.2 = (bf16[2,64,1024]{2,1,0:T(8,128)(2,1)S(1)}, bf16[2,64,1024]{2,1,0:T(8,128)(2,1)S(1)}, u32[]{:S(2)}, u32[]{:S(2)}) collective-permute-start(bf16[2,64,1024]{2,1,0:T(8,128)(2,1)S(1)} %get-tuple-element.34), channel_id=1, source_target_pairs={{0,6},{2,4},{4,2},{6,0},{8,14},{10,12},{12,10},{14,8},{1,7},{3,5},... | collective-permute-start | bytes 786440 | tf_op jit(solution)/shard_map/ppermute | solution.py:162
  11.2 23.5 %collective-permute-start.3 = (bf16[2,64,1024]{2,1,0:T(8,128)(2,1)S(1)}, bf16[2,64,1024]{2,1,0:T(8,128)(2,1)S(1)}, u32[]{:S(2)}, u32[]{:S(2)}) collective-permute-start(bf16[2,64,1024]{2,1,0:T(8,128)(2,1)S(1)} %get-tuple-element.35), channel_id=1, source_target_pairs={{0,2},{2,0},{4,6},{6,4},{8,10},{10,8},{12,14},{14,12},{1,3},{3,1},... | collective-permute-start | bytes 786440 | tf_op jit(solution)/shard_map/ppermute | solution.py:162
  11.7 3.1 %copy-start = (bf16[1,1024,3584]{2,1,0:T(8,128)(2,1)S(1)}, bf16[1,1024,3584]{2,1,0:T(8,128)(2,1)}, u32[]{:S(2)}) copy-start(bf16[1,1024,3584]{2,1,0:T(8,128)(2,1)} %param.7) | copy-start | bytes 22020100
  14.7 20.0 %copy-start.1 = (bf16[1,1024,3584]{2,1,0:T(8,128)(2,1)S(1)}, bf16[1,1024,3584]{2,1,0:T(8,128)(2,1)}, u32[]{:S(2)}) copy-start(bf16[1,1024,3584]{2,1,0:T(8,128)(2,1)} %param.7) | copy-start | bytes 22020100
  38.9 30.3 %collective-permute-start.8 = (bf16[4,64,1536]{2,1,0:T(8,128)(2,1)S(1)}, bf16[4,64,1536]{2,1,0:T(8,128)(2,1)S(1)}, u32[]{:S(2)}, u32[]{:S(2)}) collective-permute-start(bf16[4,64,1536]{2,1,0:T(8,128)(2,1)S(1)} %mix.6), channel_id=1, source_target_pairs={{0,2},{2,0},{1,3},{3,1},{4,6},{6,4},{5,7},{7,5},{8,10},{10,8},{9,1... | collective-permute-start | bytes 2359304 | tf_op jit(solution)/shard_map/ppermute | solution.py:157
  40.4 11.8 %collective-permute-start.4 = (bf16[2,64,1024]{2,1,0:T(8,128)(2,1)S(1)}, bf16[2,64,1024]{2,1,0:T(8,128)(2,1)S(1)}, u32[]{:S(2)}, u32[]{:S(2)}) collective-permute-start(bf16[2,64,1024]{2,1,0:T(8,128)(2,1)S(1)} %get-tuple-element.36), channel_id=1, source_target_pairs={{0,12},{2,14},{4,8},{6,10},{8,4},{10,6},{12,0},{14,2},{1,13},{3,15... | collective-permute-start | bytes 786440 | tf_op jit(solution)/shard_map/ppermute | solution.py:162
  44.9 20.1 %collective-permute-start.5 = (bf16[2,64,1024]{2,1,0:T(8,128)(2,1)S(1)}, bf16[2,64,1024]{2,1,0:T(8,128)(2,1)S(1)}, u32[]{:S(2)}, u32[]{:S(2)}) collective-permute-start(bf16[2,64,1024]{2,1,0:T(8,128)(2,1)S(1)} %get-tuple-element.37), channel_id=1, source_target_pairs={{0,8},{2,10},{4,12},{6,14},{8,0},{10,2},{12,4},{14,6},{1,9},{3,11}... | collective-permute-start | bytes 786440 | tf_op jit(solution)/shard_map/ppermute | solution.py:162
  44.9 20.1 %collective-permute-start.6 = (bf16[2,64,1024]{2,1,0:T(8,128)(2,1)S(1)}, bf16[2,64,1024]{2,1,0:T(8,128)(2,1)S(1)}, u32[]{:S(2)}, u32[]{:S(2)}) collective-permute-start(bf16[2,64,1024]{2,1,0:T(8,128)(2,1)S(1)} %get-tuple-element.38), channel_id=1, source_target_pairs={{0,4},{2,6},{4,0},{6,2},{8,12},{10,14},{12,8},{14,10},{1,5},{3,7},... | collective-permute-start | bytes 786440 | tf_op jit(solution)/shard_map/ppermute | solution.py:162
  49.6 26.7 %collective-permute-start.9 = (bf16[4,64,1536]{2,1,0:T(8,128)(2,1)S(1)}, bf16[4,64,1536]{2,1,0:T(8,128)(2,1)S(1)}, u32[]{:S(2)}, u32[]{:S(2)}) collective-permute-start(bf16[4,64,1536]{2,1,0:T(8,128)(2,1)S(1)} %mix.7), channel_id=1, source_target_pairs={{0,2},{2,0},{1,3},{3,1},{4,6},{6,4},{5,7},{7,5},{8,10},{10,8},{9,1... | collective-permute-start | bytes 2359304 | tf_op jit(solution)/shard_map/ppermute | solution.py:157
  52.2 30.8 %collective-permute-start.12 = (bf16[4,64,512]{2,1,0:T(8,128)(2,1)S(1)}, bf16[4,64,512]{2,1,0:T(8,128)(2,1)S(1)}, u32[]{:S(2)}, u32[]{:S(2)}) collective-permute-start(bf16[4,64,512]{2,1,0:T(8,128)(2,1)S(1)} %mix.8), channel_id=1, source_target_pairs={{0,2},{2,0},{1,3},{3,1},{4,6},{6,4},{5,7},{7,5},{8,10},{10,8},{9,1... | collective-permute-start | bytes 786440 | tf_op jit(solution)/shard_map/ppermute | solution.py:157
  69.6 13.2 %collective-permute-start.10 = (bf16[2,64,1536]{2,1,0:T(8,128)(2,1)S(1)}, bf16[2,64,1536]{2,1,0:T(8,128)(2,1)S(1)}, u32[]{:S(2)}, u32[]{:S(2)}) collective-permute-start(bf16[2,64,1536]{2,1,0:T(8,128)(2,1)S(1)} %slice.43), channel_id=1, source_target_pairs={{0,4},{4,0},{8,12},{12,8},{1,5},{5,1},{9,13},{13,9},{2,6},{6,2},{1... | collective-permute-start | bytes 1179656 | tf_op jit(solution)/shard_map/ppermute | solution.py:157
  76.7 16.4 %collective-permute-start.13 = (bf16[2,64,1536]{2,1,0:T(8,128)(2,1)S(1)}, bf16[2,64,1536]{2,1,0:T(8,128)(2,1)S(1)}, u32[]{:S(2)}, u32[]{:S(2)}) collective-permute-start(bf16[2,64,1536]{2,1,0:T(8,128)(2,1)S(1)} %slice.47), channel_id=1, source_target_pairs={{0,4},{4,0},{8,12},{12,8},{1,5},{5,1},{9,13},{13,9},{2,6},{6,2},{1... | collective-permute-start | bytes 1179656 | tf_op jit(solution)/shard_map/ppermute | solution.py:157
  82.9 14.0 %collective-permute-start.11 = (bf16[64,1536]{1,0:T(8,128)(2,1)S(1)}, bf16[64,1536]{1,0:T(8,128)(2,1)S(1)}, u32[]{:S(2)}, u32[]{:S(2)}) collective-permute-start(bf16[64,1536]{1,0:T(8,128)(2,1)S(1)} %fusion.4), channel_id=1, source_target_pairs={{0,8},{4,12},{8,0},{12,4},{1,9},{5,13},{9,1},{13,5},{2,10},{6,14},... | collective-permute-start | bytes 589832 | tf_op jit(solution)/shard_map/ppermute | solution.py:157
  83.1 12.3 %collective-permute-start.15 = (bf16[2,64,512]{2,1,0:T(8,128)(2,1)S(1)}, bf16[2,64,512]{2,1,0:T(8,128)(2,1)S(1)}, u32[]{:S(2)}, u32[]{:S(2)}) collective-permute-start(bf16[2,64,512]{2,1,0:T(8,128)(2,1)S(1)} %slice.51), channel_id=1, source_target_pairs={{0,4},{4,0},{8,12},{12,8},{1,5},{5,1},{9,13},{13,9},{2,6},{6,2},{1... | collective-permute-start | bytes 393224 | tf_op jit(solution)/shard_map/ppermute | solution.py:157
  93.2 11.6 %collective-permute-start.14 = (bf16[64,1536]{1,0:T(8,128)(2,1)S(1)}, bf16[64,1536]{1,0:T(8,128)(2,1)S(1)}, u32[]{:S(2)}, u32[]{:S(2)}) collective-permute-start(bf16[64,1536]{1,0:T(8,128)(2,1)S(1)} %fusion.5), channel_id=1, source_target_pairs={{0,8},{4,12},{8,0},{12,4},{1,9},{5,13},{9,1},{13,5},{2,10},{6,14},... | collective-permute-start | bytes 589832 | tf_op jit(solution)/shard_map/ppermute | solution.py:157
  95.5 9.4 %collective-permute-start.16 = (bf16[64,512]{1,0:T(8,128)(2,1)S(1)}, bf16[64,512]{1,0:T(8,128)(2,1)S(1)}, u32[]{:S(2)}, u32[]{:S(2)}) collective-permute-start(bf16[64,512]{1,0:T(8,128)(2,1)S(1)} %fusion.8), channel_id=1, source_target_pairs={{0,8},{4,12},{8,0},{12,4},{1,9},{5,13},{9,1},{13,5},{2,10},{6,14},... | collective-permute-start | bytes 196616 | tf_op jit(solution)/shard_map/ppermute | solution.py:157

commit v10 on v9

--- a/solution.py
+++ b/solution.py
@@ -9,8 +9,8 @@
 
 CHIPS = 8
 TILE = 512
-COLUMNS = ((0, 1536), (1536, 1536), (3072, 512))
-LIGHT = 0.01
+COLUMNS = ((0, 1024), (1024, 1536), (2560, 1024))
+LIGHT, HEAVY = 0.01, 3.0
 
 
 def passed_along(block, axis, distance):
@@ -212,7 +212,7 @@
     for i in range(len(COLUMNS)):
         last = mix_odd(i, last)
     across = [swap(block, "x", 1) for block in given]
-    last = mix_even((0,), last, LIGHT)
+    last = mix_even((0,), last, HEAVY)
     last = add_x(0, last)
     last = mix_even((1,), last, LIGHT)
     last = mix_even((2,), last, LIGHT)

time: 106 us -> 109 us (1.028)
  starting transfers between devices: 20.6 us -> 25.9 us
  waiting for transfers between devices: 54.9 us -> 53.6 us
    ppermute x10, starting transfers between devices: 7.78 us -> 13.2 us  [swap(): lax.ppermute(block, axis, [(i, i ^ distance) for i in range(lax.axis_size...]
    ppermute x7, waiting for transfers between devices: 30.5 us -> 26.4 us  [send_to_chip(): lax.ppermute(block, ('z', 'x'), [(i, i ^ relative) for i in range(sizes[0...]
    ppermute x10, waiting for transfers between devices: 24.4 us -> 27.2 us  [swap(): lax.ppermute(block, axis, [(i, i ^ distance) for i in range(lax.axis_size...]
  transfers between devices with their start and end apart: 17 -> 17, of which waited for: 9 -> 9; matrix products, arithmetic and copies ran while one was open for 1% -> 1% of each run, Pallas kernels for 17% -> 20%
where the time goes in v10:
time: 109 us
  waiting for transfers between devices  53.6 us (49%)
  starting transfers between devices  25.9 us (24%)
  Pallas kernels  21.3 us (20%)
  local copies, waits for them, and re-layouts  5.93 us (5%)
  other arithmetic  1.8 us (2%)
    ppermute x10, waiting for transfers between devices, swap(): lax.ppermute(block, axis, [(i, i ^ distance) for i in range(lax.axis_size...  27.2 us
    ppermute x7, waiting for transfers between devices, send_to_chip(): lax.ppermute(block, ('z', 'x'), [(i, i ^ relative) for i in range(sizes[0...  26.4 us
    pallas_call x6, Pallas kernels, mix(): pl.pallas_call(mix_kernel, grid=(width // TILE,), in_specs=[whole] * len(...  19.5 us
    ppermute x10, starting transfers between devices, swap(): lax.ppermute(block, axis, [(i, i ^ distance) for i in range(lax.axis_size...  13.2 us
    ppermute x7, starting transfers between devices, send_to_chip(): lax.ppermute(block, ('z', 'x'), [(i, i ^ relative) for i in range(sizes[0...  12.7 us
    unnamed x10, local copies, waits for them, and re-layouts  5.68 us
  transfers between devices with their start and end apart: 17, of which 9 were waited for; matrix products, arithmetic and copies ran while one was open for 1% of the time, Pallas kernels for 20%

profile of v10, /device:TPU:0, one launch (start us, length us, event | category | flops | bytes accessed | tf_op | source)
XLA Modules:
  0.0 108.9 jit_solution(6775414290835602649)
XLA Ops:
  4.0 5.6 %collective-permute-start = (bf16[2,64,1024]{2,1,0:T(8,128)(2,1)S(1)}, bf16[2,64,1024]{2,1,0:T(8,128)(2,1)S(1)}, u32[]{:S(2)}, u32[]{:S(2)}) collective-permute-start(bf16[2,64,1024]{2,1,0:T(8,128)(2,1)S(1)} %get-tuple-element.32), channel_id=1, source_target_pairs={{0,14},{2,12},{4,10},{6,8},{8,6},{10,4},{12,2},{14,0},{1,15},{3,13... | collective-permute-start | bytes 786440 | tf_op jit(solution)/shard_map/ppermute | solution.py:162
  9.6 1.7 %collective-permute-start.2 = (bf16[2,64,1024]{2,1,0:T(8,128)(2,1)S(1)}, bf16[2,64,1024]{2,1,0:T(8,128)(2,1)S(1)}, u32[]{:S(2)}, u32[]{:S(2)}) collective-permute-start(bf16[2,64,1024]{2,1,0:T(8,128)(2,1)S(1)} %get-tuple-element.34), channel_id=1, source_target_pairs={{0,6},{2,4},{4,2},{6,0},{8,14},{10,12},{12,10},{14,8},{1,7},{3,5},... | collective-permute-start | bytes 786440 | tf_op jit(solution)/shard_map/ppermute | solution.py:162
  11.7 3.1 %copy-done = bf16[1,1024,3584]{2,1,0:T(8,128)(2,1)S(1)} copy-done((bf16[1,1024,3584]{2,1,0:T(8,128)(2,1)S(1)}, bf16[1,1024,3584]{2,1,0:T(8,128)(2,1)}, u32[]{:S(2)}) %copy-start) | copy-done | bytes 7340056
  17.0 17.8 %collective-permute-done.1.refs_1_ = bf16[2,64,1024]{2,1,0:T(8,128)(2,1)S(1)} collective-permute-done((bf16[2,64,1024]{2,1,0:T(8,128)(2,1)S(1)}, bf16[2,64,1024]{2,1,0:T(8,128)(2,1)S(1)}, u32[]{:S(2)}, u32[]{:S(2)}) %collective-permute-start.1) | collective-permute-done | bytes 262176 | tf_op jit(solution)/shard_map/ppermute | solution.py:162
  34.8 4.4 %collective-permute-start.4 = (bf16[2,64,1024]{2,1,0:T(8,128)(2,1)S(1)}, bf16[2,64,1024]{2,1,0:T(8,128)(2,1)S(1)}, u32[]{:S(2)}, u32[]{:S(2)}) collective-permute-start(bf16[2,64,1024]{2,1,0:T(8,128)(2,1)S(1)} %get-tuple-element.36), channel_id=1, source_target_pairs={{0,12},{2,14},{4,8},{6,10},{8,4},{10,6},{12,0},{14,2},{1,13},{3,15... | collective-permute-start | bytes 786440 | tf_op jit(solution)/shard_map/ppermute | solution.py:162
  39.8 2.8 %mix.6 = bf16[4,64,1024]{2,1,0:T(8,128)(2,1)S(1)} custom-call(bf16[2,64,1024]{2,1,0:T(8,128)(2,1)S(1)} %collective-permute-done.refs_0_, bf16[2,64,1024]{2,1,0:T(8,128)(2,1)S(1)} %collective-permute-done.1.refs_1_, bf16[2,64,1024]{2,1,0:T(8,128)(2,1)S(1)} %collective-permute-done.2.refs_2_, bf16[2,64,1024]{2,1,0:T(8,128)(2,1)S(1)} %collective-permute-done.3.refs_3_, ...), custom_call_target="tpu_custom_call" | custom-call | flops 10737418 | bytes 41943 | tf_op jit(solution)/shard_map/mix/pallas_call | solution.py:139
  42.6 1.6 %collective-permute-start.8 = (bf16[4,64,1024]{2,1,0:T(8,128)(2,1)S(1)}, bf16[4,64,1024]{2,1,0:T(8,128)(2,1)S(1)}, u32[]{:S(2)}, u32[]{:S(2)}) collective-permute-start(bf16[4,64,1024]{2,1,0:T(8,128)(2,1)S(1)} %mix.6), channel_id=1, source_target_pairs={{0,2},{2,0},{1,3},{3,1},{4,6},{6,4},{5,7},{7,5},{8,10},{10,8},{9,1... | collective-permute-start | bytes 1572872 | tf_op jit(solution)/shard_map/ppermute | solution.py:157
  44.3 4.1 %mix.7 = bf16[4,64,1536]{2,1,0:T(8,128)(2,1)S(1)} custom-call(bf16[2,64,1024]{2,1,0:T(8,128)(2,1)S(1)} %collective-permute-done.refs_0_, bf16[2,64,1024]{2,1,0:T(8,128)(2,1)S(1)} %collective-permute-done.1.refs_1_, bf16[2,64,1024]{2,1,0:T(8,128)(2,1)S(1)} %collective-permute-done.2.refs_2_, bf16[2,64,1024]{2,1,0:T(8,128)(2,1)S(1)} %collective-permute-done.3.refs_3_, ...), custom_call_target="tpu_custom_call" | custom-call | flops 16106127 | bytes 62914 | tf_op jit(solution)/shard_map/mix/pallas_call | solution.py:139
  48.9 2.8 %mix.8 = bf16[4,64,1024]{2,1,0:T(8,128)(2,1)S(1)} custom-call(bf16[2,64,1024]{2,1,0:T(8,128)(2,1)S(1)} %collective-permute-done.refs_0_, bf16[2,64,1024]{2,1,0:T(8,128)(2,1)S(1)} %collective-permute-done.1.refs_1_, bf16[2,64,1024]{2,1,0:T(8,128)(2,1)S(1)} %collective-permute-done.2.refs_2_, bf16[2,64,1024]{2,1,0:T(8,128)(2,1)S(1)} %collective-permute-done.3.refs_3_, ...), custom_call_target="tpu_custom_call" | custom-call | flops 10737418 | bytes 41943 | tf_op jit(solution)/shard_map/mix/pallas_call | solution.py:139
  51.8 1.6 %collective-permute-start.12 = (bf16[4,64,1024]{2,1,0:T(8,128)(2,1)S(1)}, bf16[4,64,1024]{2,1,0:T(8,128)(2,1)S(1)}, u32[]{:S(2)}, u32[]{:S(2)}) collective-permute-start(bf16[4,64,1024]{2,1,0:T(8,128)(2,1)S(1)} %mix.8), channel_id=1, source_target_pairs={{0,2},{2,0},{1,3},{3,1},{4,6},{6,4},{5,7},{7,5},{8,10},{10,8},{9,1... | collective-permute-start | bytes 1572872 | tf_op jit(solution)/shard_map/ppermute | solution.py:157
  53.4 7.3 %collective-permute-done.5.refs_1_ = bf16[2,64,1024]{2,1,0:T(8,128)(2,1)S(1)} collective-permute-done((bf16[2,64,1024]{2,1,0:T(8,128)(2,1)S(1)}, bf16[2,64,1024]{2,1,0:T(8,128)(2,1)S(1)}, u32[]{:S(2)}, u32[]{:S(2)}) %collective-permute-start.5) | collective-permute-done | bytes 262176 | tf_op jit(solution)/shard_map/ppermute | solution.py:162
  60.7 2.8 %mix.9 = bf16[4,64,1024]{2,1,0:T(8,128)(2,1)S(1)} custom-call(bf16[2,64,1024]{2,1,0:T(8,128)(2,1)S(1)} %collective-permute-done.4.refs_0_, bf16[2,64,1024]{2,1,0:T(8,128)(2,1)S(1)} %collective-permute-done.5.refs_1_, bf16[2,64,1024]{2,1,0:T(8,128)(2,1)S(1)} %collective-permute-done.6.refs_2_, bf16[2,64,1024]{2,1,0:T(8,128)(2,1)S(1)} %get-tuple-element.45.refs_3_, ...), custom_call_target="tpu_custom_call" | custom-call | flops 3221225472 | bytes 12582912 | tf_op jit(solution)/shard_map/mix/pallas_call | solution.py:139
  63.9 4.1 %mix.10 = bf16[4,64,1536]{2,1,0:T(8,128)(2,1)S(1)} custom-call(bf16[2,64,1024]{2,1,0:T(8,128)(2,1)S(1)} %collective-permute-done.4.refs_0_, bf16[2,64,1024]{2,1,0:T(8,128)(2,1)S(1)} %collective-permute-done.5.refs_1_, bf16[2,64,1024]{2,1,0:T(8,128)(2,1)S(1)} %collective-permute-done.6.refs_2_, bf16[2,64,1024]{2,1,0:T(8,128)(2,1)S(1)} %get-tuple-element.45.refs_3_, ...), custom_call_target="tpu_custom_call" | custom-call | flops 16106127 | bytes 62914 | tf_op jit(solution)/shard_map/mix/pallas_call | solution.py:139
  68.0 2.8 %mix.11 = bf16[4,64,1024]{2,1,0:T(8,128)(2,1)S(1)} custom-call(bf16[2,64,1024]{2,1,0:T(8,128)(2,1)S(1)} %collective-permute-done.4.refs_0_, bf16[2,64,1024]{2,1,0:T(8,128)(2,1)S(1)} %collective-permute-done.5.refs_1_, bf16[2,64,1024]{2,1,0:T(8,128)(2,1)S(1)} %collective-permute-done.6.refs_2_, bf16[2,64,1024]{2,1,0:T(8,128)(2,1)S(1)} %get-tuple-element.45.refs_3_, ...), custom_call_target="tpu_custom_call" | custom-call | flops 10737418 | bytes 41943 | tf_op jit(solution)/shard_map/mix/pallas_call | solution.py:139
  70.9 3.5 %collective-permute-done.9 = bf16[4,64,1536]{2,1,0:T(8,128)(2,1)S(1)} collective-permute-done((bf16[4,64,1536]{2,1,0:T(8,128)(2,1)S(1)}, bf16[4,64,1536]{2,1,0:T(8,128)(2,1)S(1)}, u32[]{:S(2)}, u32[]{:S(2)}) %collective-permute-start.9) | collective-permute-done | bytes 786464 | tf_op jit(solution)/shard_map/ppermute | solution.py:157
  74.8 2.4 %collective-permute-start.11 = (bf16[64,1024]{1,0:T(8,128)(2,1)S(1)}, bf16[64,1024]{1,0:T(8,128)(2,1)S(1)}, u32[]{:S(2)}, u32[]{:S(2)}) collective-permute-start(bf16[64,1024]{1,0:T(8,128)(2,1)S(1)} %fusion.7), channel_id=1, source_target_pairs={{0,8},{4,12},{8,0},{12,4},{1,9},{5,13},{9,1},{13,5},{2,10},{6,14},... | collective-permute-start | bytes 393224 | tf_op jit(solution)/shard_map/ppermute | solution.py:157
  77.2 2.0 %collective-permute-start.13 = (bf16[2,64,1536]{2,1,0:T(8,128)(2,1)S(1)}, bf16[2,64,1536]{2,1,0:T(8,128)(2,1)S(1)}, u32[]{:S(2)}, u32[]{:S(2)}) collective-permute-start(bf16[2,64,1536]{2,1,0:T(8,128)(2,1)S(1)} %slice.47), channel_id=1, source_target_pairs={{0,4},{4,0},{8,12},{12,8},{1,5},{5,1},{9,13},{13,9},{2,6},{6,2},{1... | collective-permute-start | bytes 1179656 | tf_op jit(solution)/shard_map/ppermute | solution.py:157
  79.2 4.6 %collective-permute-done.12 = bf16[4,64,1024]{2,1,0:T(8,128)(2,1)S(1)} collective-permute-done((bf16[4,64,1024]{2,1,0:T(8,128)(2,1)S(1)}, bf16[4,64,1024]{2,1,0:T(8,128)(2,1)S(1)}, u32[]{:S(2)}, u32[]{:S(2)}) %collective-permute-start.12) | collective-permute-done | bytes 524320 | tf_op jit(solution)/shard_map/ppermute | solution.py:157
  84.1 1.5 %collective-permute-start.15 = (bf16[2,64,1024]{2,1,0:T(8,128)(2,1)S(1)}, bf16[2,64,1024]{2,1,0:T(8,128)(2,1)S(1)}, u32[]{:S(2)}, u32[]{:S(2)}) collective-permute-start(bf16[2,64,1024]{2,1,0:T(8,128)(2,1)S(1)} %slice.51), channel_id=1, source_target_pairs={{0,4},{4,0},{8,12},{12,8},{1,5},{5,1},{9,13},{13,9},{2,6},{6,2},{1... | collective-permute-start | bytes 786440 | tf_op jit(solution)/shard_map/ppermute | solution.py:157
  85.6 1.7 %collective-permute-done.13 = bf16[2,64,1536]{2,1,0:T(8,128)(2,1)S(1)} collective-permute-done((bf16[2,64,1536]{2,1,0:T(8,128)(2,1)S(1)}, bf16[2,64,1536]{2,1,0:T(8,128)(2,1)S(1)}, u32[]{:S(2)}, u32[]{:S(2)}) %collective-permute-start.13) | collective-permute-done | bytes 393248 | tf_op jit(solution)/shard_map/ppermute | solution.py:157
  87.4 4.4 %collective-permute-done.15 = bf16[2,64,1024]{2,1,0:T(8,128)(2,1)S(1)} collective-permute-done((bf16[2,64,1024]{2,1,0:T(8,128)(2,1)S(1)}, bf16[2,64,1024]{2,1,0:T(8,128)(2,1)S(1)}, u32[]{:S(2)}, u32[]{:S(2)}) %collective-permute-start.15) | collective-permute-done | bytes 262176 | tf_op jit(solution)/shard_map/ppermute | solution.py:157
  93.2 1.7 %collective-permute-start.14 = (bf16[64,1536]{1,0:T(8,128)(2,1)S(1)}, bf16[64,1536]{1,0:T(8,128)(2,1)S(1)}, u32[]{:S(2)}, u32[]{:S(2)}) collective-permute-start(bf16[64,1536]{1,0:T(8,128)(2,1)S(1)} %fusion.6), channel_id=1, source_target_pairs={{0,8},{4,12},{8,0},{12,4},{1,9},{5,13},{9,1},{13,5},{2,10},{6,14},... | collective-permute-start | bytes 589832 | tf_op jit(solution)/shard_map/ppermute | solution.py:157
  95.0 9.6 %collective-permute-done.16 = bf16[64,1024]{1,0:T(8,128)(2,1)S(1)} collective-permute-done((bf16[64,1024]{1,0:T(8,128)(2,1)S(1)}, bf16[64,1024]{1,0:T(8,128)(2,1)S(1)}, u32[]{:S(2)}, u32[]{:S(2)}) %collective-permute-start.16) | collective-permute-done | bytes 131104 | tf_op jit(solution)/shard_map/ppermute | solution.py:157
  104.6 3.5 %collective-permute-done.14 = bf16[64,1536]{1,0:T(8,128)(2,1)S(1)} collective-permute-done((bf16[64,1536]{1,0:T(8,128)(2,1)S(1)}, bf16[64,1536]{1,0:T(8,128)(2,1)S(1)}, u32[]{:S(2)}, u32[]{:S(2)}) %collective-permute-start.14) | collective-permute-done | bytes 196640 | tf_op jit(solution)/shard_map/ppermute | solution.py:157
  (47 shorter events, 11.2 us)
Async XLA Ops:
  0.0 39.8 %collective-permute-start.7 = (bf16[1024,3584]{1,0:T(8,128)(2,1)}, bf16[1024,3584]{1,0:T(8,128)(2,1)}, u32[]{:S(2)}, u32[]{:S(2)}) collective-permute-start(bf16[1024,3584]{1,0:T(8,128)(2,1)} %bitcast.29), channel_id=1, source_target_pairs={{0,1},{1,0},{2,3},{3,2},{4,5},{5,4},{6,7},{7,6},{8,9},{9,8},{10,11... | collective-permute-start | bytes 22020104 | tf_op jit(solution)/shard_map/ppermute | solution.py:157
  0.5 1.2 %copy-start.2 = (bf16[64,8,1024]{2,1,0:T(8,128)(2,1)S(1)}, bf16[64,8,1024]{2,1,0:T(8,128)(2,1)}, u32[]{:S(2)}) copy-start(bf16[64,8,1024]{2,1,0:T(8,128)(2,1)} %param.4) | copy-start | bytes 3145732
  1.7 0.7 copy-start.3
  2.4 0.7 copy-start.4
  4.0 13.0 %collective-permute-start = (bf16[2,64,1024]{2,1,0:T(8,128)(2,1)S(1)}, bf16[2,64,1024]{2,1,0:T(8,128)(2,1)S(1)}, u32[]{:S(2)}, u32[]{:S(2)}) collective-permute-start(bf16[2,64,1024]{2,1,0:T(8,128)(2,1)S(1)} %get-tuple-element.32), channel_id=1, source_target_pairs={{0,14},{2,12},{4,10},{6,8},{8,6},{10,4},{12,2},{14,0},{1,15},{3,13... | collective-permute-start | bytes 786440 | tf_op jit(solution)/shard_map/ppermute | solution.py:162
  9.6 25.2 %collective-permute-start.1 = (bf16[2,64,1024]{2,1,0:T(8,128)(2,1)S(1)}, bf16[2,64,1024]{2,1,0:T(8,128)(2,1)S(1)}, u32[]{:S(2)}, u32[]{:S(2)}) collective-permute-start(bf16[2,64,1024]{2,1,0:T(8,128)(2,1)S(1)} %get-tuple-element.33), channel_id=1, source_target_pairs={{0,10},{2,8},{4,14},{6,12},{8,2},{10,0},{12,6},{14,4},{1,11},{3,9}... | collective-permute-start | bytes 786440 | tf_op jit(solution)/shard_map/ppermute | solution.py:162
  9.6 25.2 %collective-permute-start.2 = (bf16[2,64,1024]{2,1,0:T(8,128)(2,1)S(1)}, bf16[2,64,1024]{2,1,0:T(8,128)(2,1)S(1)}, u32[]{:S(2)}, u32[]{:S(2)}) collective-permute-start(bf16[2,64,1024]{2,1,0:T(8,128)(2,1)S(1)} %get-tuple-element.34), channel_id=1, source_target_pairs={{0,6},{2,4},{4,2},{6,0},{8,14},{10,12},{12,10},{14,8},{1,7},{3,5},... | collective-permute-start | bytes 786440 | tf_op jit(solution)/shard_map/ppermute | solution.py:162
  11.2 23.5 %collective-permute-start.3 = (bf16[2,64,1024]{2,1,0:T(8,128)(2,1)S(1)}, bf16[2,64,1024]{2,1,0:T(8,128)(2,1)S(1)}, u32[]{:S(2)}, u32[]{:S(2)}) collective-permute-start(bf16[2,64,1024]{2,1,0:T(8,128)(2,1)S(1)} %get-tuple-element.35), channel_id=1, source_target_pairs={{0,2},{2,0},{4,6},{6,4},{8,10},{10,8},{12,14},{14,12},{1,3},{3,1},... | collective-permute-start | bytes 786440 | tf_op jit(solution)/shard_map/ppermute | solution.py:162
  11.7 3.1 %copy-start = (bf16[1,1024,3584]{2,1,0:T(8,128)(2,1)S(1)}, bf16[1,1024,3584]{2,1,0:T(8,128)(2,1)}, u32[]{:S(2)}) copy-start(bf16[1,1024,3584]{2,1,0:T(8,128)(2,1)} %param.7) | copy-start | bytes 22020100
  14.7 25.1 %copy-start.1 = (bf16[1,1024,3584]{2,1,0:T(8,128)(2,1)S(1)}, bf16[1,1024,3584]{2,1,0:T(8,128)(2,1)}, u32[]{:S(2)}) copy-start(bf16[1,1024,3584]{2,1,0:T(8,128)(2,1)} %param.7) | copy-start | bytes 22020100
  34.8 17.0 %collective-permute-start.4 = (bf16[2,64,1024]{2,1,0:T(8,128)(2,1)S(1)}, bf16[2,64,1024]{2,1,0:T(8,128)(2,1)S(1)}, u32[]{:S(2)}, u32[]{:S(2)}) collective-permute-start(bf16[2,64,1024]{2,1,0:T(8,128)(2,1)S(1)} %get-tuple-element.36), channel_id=1, source_target_pairs={{0,12},{2,14},{4,8},{6,10},{8,4},{10,6},{12,0},{14,2},{1,13},{3,15... | collective-permute-start | bytes 786440 | tf_op jit(solution)/shard_map/ppermute | solution.py:162
  39.2 21.5 %collective-permute-start.5 = (bf16[2,64,1024]{2,1,0:T(8,128)(2,1)S(1)}, bf16[2,64,1024]{2,1,0:T(8,128)(2,1)S(1)}, u32[]{:S(2)}, u32[]{:S(2)}) collective-permute-start(bf16[2,64,1024]{2,1,0:T(8,128)(2,1)S(1)} %get-tuple-element.37), channel_id=1, source_target_pairs={{0,8},{2,10},{4,12},{6,14},{8,0},{10,2},{12,4},{14,6},{1,9},{3,11}... | collective-permute-start | bytes 786440 | tf_op jit(solution)/shard_map/ppermute | solution.py:162
  39.2 21.5 %collective-permute-start.6 = (bf16[2,64,1024]{2,1,0:T(8,128)(2,1)S(1)}, bf16[2,64,1024]{2,1,0:T(8,128)(2,1)S(1)}, u32[]{:S(2)}, u32[]{:S(2)}) collective-permute-start(bf16[2,64,1024]{2,1,0:T(8,128)(2,1)S(1)} %get-tuple-element.38), channel_id=1, source_target_pairs={{0,4},{2,6},{4,0},{6,2},{8,12},{10,14},{12,8},{14,10},{1,5},{3,7},... | collective-permute-start | bytes 786440 | tf_op jit(solution)/shard_map/ppermute | solution.py:162
  42.6 20.9 %collective-permute-start.8 = (bf16[4,64,1024]{2,1,0:T(8,128)(2,1)S(1)}, bf16[4,64,1024]{2,1,0:T(8,128)(2,1)S(1)}, u32[]{:S(2)}, u32[]{:S(2)}) collective-permute-start(bf16[4,64,1024]{2,1,0:T(8,128)(2,1)S(1)} %mix.6), channel_id=1, source_target_pairs={{0,2},{2,0},{1,3},{3,1},{4,6},{6,4},{5,7},{7,5},{8,10},{10,8},{9,1... | collective-permute-start | bytes 1572872 | tf_op jit(solution)/shard_map/ppermute | solution.py:157
  48.4 26.0 %collective-permute-start.9 = (bf16[4,64,1536]{2,1,0:T(8,128)(2,1)S(1)}, bf16[4,64,1536]{2,1,0:T(8,128)(2,1)S(1)}, u32[]{:S(2)}, u32[]{:S(2)}) collective-permute-start(bf16[4,64,1536]{2,1,0:T(8,128)(2,1)S(1)} %mix.7), channel_id=1, source_target_pairs={{0,2},{2,0},{1,3},{3,1},{4,6},{6,4},{5,7},{7,5},{8,10},{10,8},{9,1... | collective-permute-start | bytes 2359304 | tf_op jit(solution)/shard_map/ppermute | solution.py:157
  51.8 32.0 %collective-permute-start.12 = (bf16[4,64,1024]{2,1,0:T(8,128)(2,1)S(1)}, bf16[4,64,1024]{2,1,0:T(8,128)(2,1)S(1)}, u32[]{:S(2)}, u32[]{:S(2)}) collective-permute-start(bf16[4,64,1024]{2,1,0:T(8,128)(2,1)S(1)} %mix.8), channel_id=1, source_target_pairs={{0,2},{2,0},{1,3},{3,1},{4,6},{6,4},{5,7},{7,5},{8,10},{10,8},{9,1... | collective-permute-start | bytes 1572872 | tf_op jit(solution)/shard_map/ppermute | solution.py:157
  63.8 10.9 %collective-permute-start.10 = (bf16[2,64,1024]{2,1,0:T(8,128)(2,1)S(1)}, bf16[2,64,1024]{2,1,0:T(8,128)(2,1)S(1)}, u32[]{:S(2)}, u32[]{:S(2)}) collective-permute-start(bf16[2,64,1024]{2,1,0:T(8,128)(2,1)S(1)} %slice.43), channel_id=1, source_target_pairs={{0,4},{4,0},{8,12},{12,8},{1,5},{5,1},{9,13},{13,9},{2,6},{6,2},{1... | collective-permute-start | bytes 786440 | tf_op jit(solution)/shard_map/ppermute | solution.py:157
  74.8 10.8 %collective-permute-start.11 = (bf16[64,1024]{1,0:T(8,128)(2,1)S(1)}, bf16[64,1024]{1,0:T(8,128)(2,1)S(1)}, u32[]{:S(2)}, u32[]{:S(2)}) collective-permute-start(bf16[64,1024]{1,0:T(8,128)(2,1)S(1)} %fusion.7), channel_id=1, source_target_pairs={{0,8},{4,12},{8,0},{12,4},{1,9},{5,13},{9,1},{13,5},{2,10},{6,14},... | collective-permute-start | bytes 393224 | tf_op jit(solution)/shard_map/ppermute | solution.py:157
  77.2 10.1 %collective-permute-start.13 = (bf16[2,64,1536]{2,1,0:T(8,128)(2,1)S(1)}, bf16[2,64,1536]{2,1,0:T(8,128)(2,1)S(1)}, u32[]{:S(2)}, u32[]{:S(2)}) collective-permute-start(bf16[2,64,1536]{2,1,0:T(8,128)(2,1)S(1)} %slice.47), channel_id=1, source_target_pairs={{0,4},{4,0},{8,12},{12,8},{1,5},{5,1},{9,13},{13,9},{2,6},{6,2},{1... | collective-permute-start | bytes 1179656 | tf_op jit(solution)/shard_map/ppermute | solution.py:157
  84.1 7.7 %collective-permute-start.15 = (bf16[2,64,1024]{2,1,0:T(8,128)(2,1)S(1)}, bf16[2,64,1024]{2,1,0:T(8,128)(2,1)S(1)}, u32[]{:S(2)}, u32[]{:S(2)}) collective-permute-start(bf16[2,64,1024]{2,1,0:T(8,128)(2,1)S(1)} %slice.51), channel_id=1, source_target_pairs={{0,4},{4,0},{8,12},{12,8},{1,5},{5,1},{9,13},{13,9},{2,6},{6,2},{1... | collective-permute-start | bytes 786440 | tf_op jit(solution)/shard_map/ppermute | solution.py:157
  91.9 12.6 %collective-permute-start.16 = (bf16[64,1024]{1,0:T(8,128)(2,1)S(1)}, bf16[64,1024]{1,0:T(8,128)(2,1)S(1)}, u32[]{:S(2)}, u32[]{:S(2)}) collective-permute-start(bf16[64,1024]{1,0:T(8,128)(2,1)S(1)} %fusion.8), channel_id=1, source_target_pairs={{0,8},{4,12},{8,0},{12,4},{1,9},{5,13},{9,1},{13,5},{2,10},{6,14},... | collective-permute-start | bytes 393224 | tf_op jit(solution)/shard_map/ppermute | solution.py:157
  93.2 14.8 %collective-permute-start.14 = (bf16[64,1536]{1,0:T(8,128)(2,1)S(1)}, bf16[64,1536]{1,0:T(8,128)(2,1)S(1)}, u32[]{:S(2)}, u32[]{:S(2)}) collective-permute-start(bf16[64,1536]{1,0:T(8,128)(2,1)S(1)} %fusion.6), channel_id=1, source_target_pairs={{0,8},{4,12},{8,0},{12,4},{1,9},{5,13},{9,1},{13,5},{2,10},{6,14},... | collective-permute-start | bytes 589832 | tf_op jit(solution)/shard_map/ppermute | solution.py:157

commit v11 on v9

--- a/solution.py
+++ b/solution.py
@@ -62,6 +62,19 @@
     )
     combined = jnp.sum(picked * gate_weights[:, :, None], axis=1)
     return combined.astype(jnp.bfloat16)
+
+
+def fetching_kernel(relatives, own_ref, ids_hbm, gates_hbm, hidden_hbm, *refs):
+    out_refs, fetched, sems = refs[: len(relatives)], refs[len(relatives) : -1], refs[-1]
+    copies = [
+        pltpu.make_async_copy(source, target, sems.at[i])
+        for i, (source, target) in enumerate(zip((ids_hbm, gates_hbm, hidden_hbm), fetched))
+    ]
+    for copy in copies:
+        copy.start()
+    for copy in copies:
+        copy.wait()
+    spread_kernel(relatives, own_ref, *fetched, *out_refs)
 
 
 def spread_kernel(relatives, own_ref, ids_ref, gates_ref, hidden_ref, *refs):
@@ -98,22 +111,31 @@
 
 def spread_rows(hidden, expert_ids, gate_weights, own, relatives, held=None):
     token_count, choose_count, width = hidden.shape
+    rows = token_count * choose_count
     vmem = pl.BlockSpec(memory_space=pltpu.VMEM)
     block = jax.ShapeDtypeStruct((2, token_count, width), hidden.dtype)
     more = [] if held is None else [held]
+    scratch = [] if more else [
+        pltpu.VMEM((choose_count, token_count), expert_ids.dtype),
+        pltpu.VMEM((choose_count, token_count), gate_weights.dtype),
+        pltpu.VMEM((rows, width), hidden.dtype),
+        pltpu.SemaphoreType.DMA((3,)),
+    ]
+    given = vmem if more else pl.BlockSpec(memory_space=pl.ANY)
     return pl.pallas_call(
-        functools.partial(spread_kernel, relatives),
-        in_specs=[pl.BlockSpec(memory_space=pltpu.SMEM)] + [vmem] * (3 + len(more)),
+        functools.partial(spread_kernel if more else fetching_kernel, relatives),
+        in_specs=[pl.BlockSpec(memory_space=pltpu.SMEM)] + [given] * 3 + [vmem] * len(more),
         out_specs=[vmem] * len(relatives),
         out_shape=[block] * len(relatives),
-        compiler_params=pltpu.CompilerParams(vmem_limit_bytes=24 << 20),
+        scratch_shapes=scratch,
+        compiler_params=pltpu.CompilerParams(vmem_limit_bytes=(24 if more else 56) << 20),
         cost_estimate=pl.CostEstimate(flops=0, bytes_accessed=0, transcendentals=0),
         name="spread_rows",
     )(
         own.reshape(1),
         expert_ids.T,
         gate_weights.T,
-        hidden.reshape(token_count * choose_count, width),
+        hidden.reshape(rows, width),
         *more,
     )
 
@@ -198,9 +220,10 @@
             kept.append(block[:, :, low : low + COLUMNS[i][1]])
         return block
 
-    def add_x(i, earlier):
+    def add_x(i, earlier, parts=1):
         line = after(kept[i], earlier).astype(jnp.float32) + across[i].astype(jnp.float32)
-        lines.append((line[1::2], swap(line[0::2].astype(jnp.bfloat16), "z", 1)))
+        for part in jnp.split(line, parts, axis=2):
+            lines.append((part[1::2], swap(part[0::2].astype(jnp.bfloat16), "z", 1)))
         return line
 
     def add_z(i, earlier):
@@ -216,11 +239,11 @@
     last = add_x(0, last)
     last = mix_even((1,), last, LIGHT)
     last = mix_even((2,), last, LIGHT)
-    last = add_x(1, last)
+    last = add_x(1, last, 2)
     last = add_z(0, last)
     last = add_x(2, last)
-    last = add_z(1, last)
-    add_z(2, last)
+    for i in range(1, 4):
+        last = add_z(i, last)
     for mine, theirs in pairs:
         results.append((mine + theirs.astype(jnp.float32)).astype(jnp.bfloat16))
     return jnp.concatenate(results, axis=1)

time: 106 us -> 108 us (1.019)
  starting transfers between devices: 20.6 us -> 26.1 us
  waiting for transfers between devices: 54.9 us -> 50.1 us
  Pallas kernels: 22.2 us -> 24.3 us
    ppermute x10 -> x12, starting transfers between devices: 7.78 us -> 13.3 us  [swap(): lax.ppermute(block, axis, [(i, i ^ distance) for i in range(lax.axis_size...]
    ppermute x10 -> x12, waiting for transfers between devices: 24.4 us -> 20.8 us  [swap(): lax.ppermute(block, axis, [(i, i ^ distance) for i in range(lax.axis_size...]
    pallas_call x2, Pallas kernels: 1.8 us -> 3.86 us  [spread_rows(): pl.pallas_call(functools.partial(spread_kernel if more else fetching_kern...]
    unnamed x10, local copies, waits for them, and re-layouts: 5.68 us -> 4.46 us
    ppermute x7, waiting for transfers between devices: 30.5 us -> 29.3 us  [send_to_chip(): lax.ppermute(block, ('z', 'x'), [(i, i ^ relative) for i in range(sizes[0...]
  transfers between devices with their start and end apart: 17 -> 19, of which waited for: 9 -> 11; matrix products, arithmetic and copies ran while one was open for 1% -> 1% of each run, Pallas kernels for 17% -> 19%
where the time goes in v11:
time: 108 us; the launch traced here: 107 us
  waiting for transfers between devices  50.1 us (46%)
  starting transfers between devices  26.1 us (24%)
  Pallas kernels  24.3 us (22%)
  local copies, waits for them, and re-layouts  4.94 us (5%)
  other arithmetic  1.68 us (2%)
    ppermute x7, waiting for transfers between devices, send_to_chip(): lax.ppermute(block, ('z', 'x'), [(i, i ^ relative) for i in range(sizes[0...  29.3 us
    ppermute x12, waiting for transfers between devices, swap(): lax.ppermute(block, axis, [(i, i ^ distance) for i in range(lax.axis_size...  20.8 us
    pallas_call x6, Pallas kernels, mix(): pl.pallas_call(mix_kernel, grid=(width // TILE,), in_specs=[whole] * len(...  20.4 us
    ppermute x12, starting transfers between devices, swap(): lax.ppermute(block, axis, [(i, i ^ distance) for i in range(lax.axis_size...  13.3 us
    ppermute x7, starting transfers between devices, send_to_chip(): lax.ppermute(block, ('z', 'x'), [(i, i ^ relative) for i in range(sizes[0...  12.9 us
    unnamed x10, local copies, waits for them, and re-layouts  4.46 us
    pallas_call x2, Pallas kernels, spread_rows(): pl.pallas_call(functools.partial(spread_kernel if more else fetching_kern...  3.86 us
  transfers between devices with their start and end apart: 19, of which 11 were waited for; matrix products, arithmetic and copies ran while one was open for 1% of the time, Pallas kernels for 19%

profile of v11, /device:TPU:0, one launch (start us, length us, event | category | flops | bytes accessed | tf_op | source)
XLA Modules:
  0.0 107.5 jit_solution(17777745210092340928)
XLA Ops:
  0.5 3.0 %spread_rows.3 = (bf16[2,64,1024]{2,1,0:T(8,128)(2,1)}, bf16[2,64,1024]{2,1,0:T(8,128)(2,1)}, bf16[2,64,1024]{2,1,0:T(8,128)(2,1)}, bf16[2,64,1024]{2,1,0:T(8,128)(2,1)}) custom-call(s32[1]{0:T(128)} %bitcast.own_ref, s32[8,64]{1,0:T(8,128)} %bitcast.47, f32[8,64]{1,0:T(8,128)} %bitcast.49, bf16[512,1024]{1,0:T(8,128)(2,1)} %bitcast.45), custom_call_target="tpu_custom_call" | custom-call | tf_op jit(solution)/shard_map/spread_rows/pallas_call | solution.py:125
  3.4 5.7 %collective-permute-start = (bf16[2,64,1024]{2,1,0:T(8,128)(2,1)}, bf16[2,64,1024]{2,1,0:T(8,128)(2,1)S(1)}, u32[]{:S(2)}, u32[]{:S(2)}) collective-permute-start(bf16[2,64,1024]{2,1,0:T(8,128)(2,1)} %get-tuple-element.33), channel_id=1, source_target_pairs={{0,14},{2,12},{4,10},{6,8},{8,6},{10,4},{12,2},{14,0},{1,15},{3,13... | collective-permute-start | bytes 786440 | tf_op jit(solution)/shard_map/ppermute | solution.py:184
  9.1 1.7 %collective-permute-start.2 = (bf16[2,64,1024]{2,1,0:T(8,128)(2,1)}, bf16[2,64,1024]{2,1,0:T(8,128)(2,1)S(1)}, u32[]{:S(2)}, u32[]{:S(2)}) collective-permute-start(bf16[2,64,1024]{2,1,0:T(8,128)(2,1)} %get-tuple-element.35), channel_id=1, source_target_pairs={{0,6},{2,4},{4,2},{6,0},{8,14},{10,12},{12,10},{14,8},{1,7},{3,5},... | collective-permute-start | bytes 786440 | tf_op jit(solution)/shard_map/ppermute | solution.py:184
  11.2 3.1 %copy-done = bf16[1,1024,3584]{2,1,0:T(8,128)(2,1)S(1)} copy-done((bf16[1,1024,3584]{2,1,0:T(8,128)(2,1)S(1)}, bf16[1,1024,3584]{2,1,0:T(8,128)(2,1)}, u32[]{:S(2)}) %copy-start) | copy-done | bytes 7340056
  16.7 17.7 %collective-permute-done.1.refs_1_ = bf16[2,64,1024]{2,1,0:T(8,128)(2,1)S(1)} collective-permute-done((bf16[2,64,1024]{2,1,0:T(8,128)(2,1)}, bf16[2,64,1024]{2,1,0:T(8,128)(2,1)S(1)}, u32[]{:S(2)}, u32[]{:S(2)}) %collective-permute-start.1) | collective-permute-done | bytes 262176 | tf_op jit(solution)/shard_map/ppermute | solution.py:184
  34.5 4.1 %mix.6 = bf16[4,64,1536]{2,1,0:T(8,128)(2,1)S(1)} custom-call(bf16[2,64,1024]{2,1,0:T(8,128)(2,1)S(1)} %collective-permute-done.refs_0_, bf16[2,64,1024]{2,1,0:T(8,128)(2,1)S(1)} %collective-permute-done.1.refs_1_, bf16[2,64,1024]{2,1,0:T(8,128)(2,1)S(1)} %collective-permute-done.2.refs_2_, bf16[2,64,1024]{2,1,0:T(8,128)(2,1)S(1)} %collective-permute-done.3.refs_3_, ...), custom_call_target="tpu_custom_call" | custom-call | flops 16106127 | bytes 62914 | tf_op jit(solution)/shard_map/mix/pallas_call | solution.py:161
  38.6 1.5 %collective-permute-start.8 = (bf16[4,64,1536]{2,1,0:T(8,128)(2,1)S(1)}, bf16[4,64,1536]{2,1,0:T(8,128)(2,1)S(1)}, u32[]{:S(2)}, u32[]{:S(2)}) collective-permute-start(bf16[4,64,1536]{2,1,0:T(8,128)(2,1)S(1)} %mix.6), channel_id=1, source_target_pairs={{0,2},{2,0},{1,3},{3,1},{4,6},{6,4},{5,7},{7,5},{8,10},{10,8},{9,1... | collective-permute-start | bytes 2359304 | tf_op jit(solution)/shard_map/ppermute | solution.py:179
  40.1 4.5 %collective-permute-start.4 = (bf16[2,64,1024]{2,1,0:T(8,128)(2,1)S(1)}, bf16[2,64,1024]{2,1,0:T(8,128)(2,1)S(1)}, u32[]{:S(2)}, u32[]{:S(2)}) collective-permute-start(bf16[2,64,1024]{2,1,0:T(8,128)(2,1)S(1)} %get-tuple-element.37), channel_id=1, source_target_pairs={{0,12},{2,14},{4,8},{6,10},{8,4},{10,6},{12,0},{14,2},{1,13},{3,15... | collective-permute-start | bytes 786440 | tf_op jit(solution)/shard_map/ppermute | solution.py:184
  45.2 4.1 %mix.7 = bf16[4,64,1536]{2,1,0:T(8,128)(2,1)S(1)} custom-call(bf16[2,64,1024]{2,1,0:T(8,128)(2,1)S(1)} %collective-permute-done.refs_0_, bf16[2,64,1024]{2,1,0:T(8,128)(2,1)S(1)} %collective-permute-done.1.refs_1_, bf16[2,64,1024]{2,1,0:T(8,128)(2,1)S(1)} %collective-permute-done.2.refs_2_, bf16[2,64,1024]{2,1,0:T(8,128)(2,1)S(1)} %collective-permute-done.3.refs_3_, ...), custom_call_target="tpu_custom_call" | custom-call | flops 16106127 | bytes 62914 | tf_op jit(solution)/shard_map/mix/pallas_call | solution.py:161
  49.8 2.0 %mix.8 = bf16[4,64,512]{2,1,0:T(8,128)(2,1)S(1)} custom-call(bf16[2,64,1024]{2,1,0:T(8,128)(2,1)S(1)} %collective-permute-done.refs_0_, bf16[2,64,1024]{2,1,0:T(8,128)(2,1)S(1)} %collective-permute-done.1.refs_1_, bf16[2,64,1024]{2,1,0:T(8,128)(2,1)S(1)} %collective-permute-done.2.refs_2_, bf16[2,64,1024]{2,1,0:T(8,128)(2,1)S(1)} %collective-permute-done.3.refs_3_, ...), custom_call_target="tpu_custom_call" | custom-call | flops 5368709 | bytes 20971 | tf_op jit(solution)/shard_map/mix/pallas_call | solution.py:161
  51.9 1.6 %collective-permute-start.12 = (bf16[4,64,512]{2,1,0:T(8,128)(2,1)S(1)}, bf16[4,64,512]{2,1,0:T(8,128)(2,1)S(1)}, u32[]{:S(2)}, u32[]{:S(2)}) collective-permute-start(bf16[4,64,512]{2,1,0:T(8,128)(2,1)S(1)} %mix.8), channel_id=1, source_target_pairs={{0,2},{2,0},{1,3},{3,1},{4,6},{6,4},{5,7},{7,5},{8,10},{10,8},{9,1... | collective-permute-start | bytes 786440 | tf_op jit(solution)/shard_map/ppermute | solution.py:179
  53.5 11.3 %collective-permute-done.5.refs_1_ = bf16[2,64,1024]{2,1,0:T(8,128)(2,1)S(1)} collective-permute-done((bf16[2,64,1024]{2,1,0:T(8,128)(2,1)S(1)}, bf16[2,64,1024]{2,1,0:T(8,128)(2,1)S(1)}, u32[]{:S(2)}, u32[]{:S(2)}) %collective-permute-start.5) | collective-permute-done | bytes 262176 | tf_op jit(solution)/shard_map/ppermute | solution.py:184
  64.7 4.1 %mix.9 = bf16[4,64,1536]{2,1,0:T(8,128)(2,1)S(1)} custom-call(bf16[2,64,1024]{2,1,0:T(8,128)(2,1)S(1)} %collective-permute-done.4.refs_0_, bf16[2,64,1024]{2,1,0:T(8,128)(2,1)S(1)} %collective-permute-done.5.refs_1_, bf16[2,64,1024]{2,1,0:T(8,128)(2,1)S(1)} %collective-permute-done.6.refs_2_, bf16[2,64,1024]{2,1,0:T(8,128)(2,1)S(1)} %get-tuple-element.46.refs_3_, ...), custom_call_target="tpu_custom_call" | custom-call | flops 16106127 | bytes 62914 | tf_op jit(solution)/shard_map/mix/pallas_call | solution.py:161
  69.3 4.1 %mix.10 = bf16[4,64,1536]{2,1,0:T(8,128)(2,1)S(1)} custom-call(bf16[2,64,1024]{2,1,0:T(8,128)(2,1)S(1)} %collective-permute-done.4.refs_0_, bf16[2,64,1024]{2,1,0:T(8,128)(2,1)S(1)} %collective-permute-done.5.refs_1_, bf16[2,64,1024]{2,1,0:T(8,128)(2,1)S(1)} %collective-permute-done.6.refs_2_, bf16[2,64,1024]{2,1,0:T(8,128)(2,1)S(1)} %get-tuple-element.46.refs_3_, ...), custom_call_target="tpu_custom_call" | custom-call | flops 16106127 | bytes 62914 | tf_op jit(solution)/shard_map/mix/pallas_call | solution.py:161
  73.4 2.0 %mix.11 = bf16[4,64,512]{2,1,0:T(8,128)(2,1)S(1)} custom-call(bf16[2,64,1024]{2,1,0:T(8,128)(2,1)S(1)} %collective-permute-done.4.refs_0_, bf16[2,64,1024]{2,1,0:T(8,128)(2,1)S(1)} %collective-permute-done.5.refs_1_, bf16[2,64,1024]{2,1,0:T(8,128)(2,1)S(1)} %collective-permute-done.6.refs_2_, bf16[2,64,1024]{2,1,0:T(8,128)(2,1)S(1)} %get-tuple-element.46.refs_3_, ...), custom_call_target="tpu_custom_call" | custom-call | flops 5368709 | bytes 20971 | tf_op jit(solution)/shard_map/mix/pallas_call | solution.py:161
  76.6 1.8 %collective-permute-start.13 = (bf16[2,64,768]{2,1,0:T(8,128)(2,1)S(1)}, bf16[2,64,768]{2,1,0:T(8,128)(2,1)S(1)}, u32[]{:S(2)}, u32[]{:S(2)}) collective-permute-start(bf16[2,64,768]{2,1,0:T(8,128)(2,1)S(1)} %slice.61), channel_id=1, source_target_pairs={{0,4},{4,0},{8,12},{12,8},{1,5},{5,1},{9,13},{13,9},{2,6},{6,2},{1... | collective-permute-start | bytes 589832 | tf_op jit(solution)/shard_map/ppermute | solution.py:179
  78.7 3.5 %collective-permute-done.10 = bf16[2,64,1536]{2,1,0:T(8,128)(2,1)S(1)} collective-permute-done((bf16[2,64,1536]{2,1,0:T(8,128)(2,1)S(1)}, bf16[2,64,1536]{2,1,0:T(8,128)(2,1)S(1)}, u32[]{:S(2)}, u32[]{:S(2)}) %collective-permute-start.10) | collective-permute-done | bytes 393248 | tf_op jit(solution)/shard_map/ppermute | solution.py:179
  82.5 1.5 %collective-permute-start.17 = (bf16[2,64,512]{2,1,0:T(8,128)(2,1)S(1)}, bf16[2,64,512]{2,1,0:T(8,128)(2,1)S(1)}, u32[]{:S(2)}, u32[]{:S(2)}) collective-permute-start(bf16[2,64,512]{2,1,0:T(8,128)(2,1)S(1)} %slice.69), channel_id=1, source_target_pairs={{0,4},{4,0},{8,12},{12,8},{1,5},{5,1},{9,13},{13,9},{2,6},{6,2},{1... | collective-permute-start | bytes 393224 | tf_op jit(solution)/shard_map/ppermute | solution.py:179
  84.0 2.4 %collective-permute-done.13 = bf16[2,64,768]{2,1,0:T(8,128)(2,1)S(1)} collective-permute-done((bf16[2,64,768]{2,1,0:T(8,128)(2,1)S(1)}, bf16[2,64,768]{2,1,0:T(8,128)(2,1)S(1)}, u32[]{:S(2)}, u32[]{:S(2)}) %collective-permute-start.13) | collective-permute-done | bytes 196640 | tf_op jit(solution)/shard_map/ppermute | solution.py:179
  86.5 5.0 %collective-permute-start.14 = (bf16[64,768]{1,0:T(8,128)(2,1)S(1)}, bf16[64,768]{1,0:T(8,128)(2,1)S(1)}, u32[]{:S(2)}, u32[]{:S(2)}) collective-permute-start(bf16[64,768]{1,0:T(8,128)(2,1)S(1)} %fusion.9), channel_id=1, source_target_pairs={{0,8},{4,12},{8,0},{12,4},{1,9},{5,13},{9,1},{13,5},{2,10},{6,14},... | collective-permute-start | bytes 294920 | tf_op jit(solution)/shard_map/ppermute | solution.py:179
  91.4 2.3 %collective-permute-done.15 = bf16[2,64,768]{2,1,0:T(8,128)(2,1)S(1)} collective-permute-done((bf16[2,64,768]{2,1,0:T(8,128)(2,1)S(1)}, bf16[2,64,768]{2,1,0:T(8,128)(2,1)S(1)}, u32[]{:S(2)}, u32[]{:S(2)}) %collective-permute-start.15) | collective-permute-done | bytes 196640 | tf_op jit(solution)/shard_map/ppermute | solution.py:179
  94.4 5.9 %collective-permute-done.14 = bf16[64,768]{1,0:T(8,128)(2,1)S(1)} collective-permute-done((bf16[64,768]{1,0:T(8,128)(2,1)S(1)}, bf16[64,768]{1,0:T(8,128)(2,1)S(1)}, u32[]{:S(2)}, u32[]{:S(2)}) %collective-permute-start.14) | collective-permute-done | bytes 98336 | tf_op jit(solution)/shard_map/ppermute | solution.py:179
  100.3 1.0 collective-permute-done.16
  101.6 5.1 %collective-permute-done.18 = bf16[64,512]{1,0:T(8,128)(2,1)S(1)} collective-permute-done((bf16[64,512]{1,0:T(8,128)(2,1)S(1)}, bf16[64,512]{1,0:T(8,128)(2,1)S(1)}, u32[]{:S(2)}, u32[]{:S(2)}) %collective-permute-start.18) | collective-permute-done | bytes 65568 | tf_op jit(solution)/shard_map/ppermute | solution.py:179
  (58 shorter events, 8.2 us)
Async XLA Ops:
  0.0 11.2 %copy-start.2 = (bf16[64,8,1024]{2,1,0:T(8,128)(2,1)S(1)}, bf16[64,8,1024]{2,1,0:T(8,128)(2,1)}, u32[]{:S(2)}) copy-start(bf16[64,8,1024]{2,1,0:T(8,128)(2,1)} %param.4) | copy-start | bytes 3145732
  0.0 34.5 %collective-permute-start.7 = (bf16[1024,3584]{1,0:T(8,128)(2,1)}, bf16[1024,3584]{1,0:T(8,128)(2,1)}, u32[]{:S(2)}, u32[]{:S(2)}) collective-permute-start(bf16[1024,3584]{1,0:T(8,128)(2,1)} %bitcast.37), channel_id=1, source_target_pairs={{0,1},{1,0},{2,3},{3,2},{4,5},{5,4},{6,7},{7,6},{8,9},{9,8},{10,11... | collective-permute-start | bytes 22020104 | tf_op jit(solution)/shard_map/ppermute | solution.py:179
  3.4 13.3 %collective-permute-start = (bf16[2,64,1024]{2,1,0:T(8,128)(2,1)}, bf16[2,64,1024]{2,1,0:T(8,128)(2,1)S(1)}, u32[]{:S(2)}, u32[]{:S(2)}) collective-permute-start(bf16[2,64,1024]{2,1,0:T(8,128)(2,1)} %get-tuple-element.33), channel_id=1, source_target_pairs={{0,14},{2,12},{4,10},{6,8},{8,6},{10,4},{12,2},{14,0},{1,15},{3,13... | collective-permute-start | bytes 786440 | tf_op jit(solution)/shard_map/ppermute | solution.py:184
  9.1 25.3 %collective-permute-start.1 = (bf16[2,64,1024]{2,1,0:T(8,128)(2,1)}, bf16[2,64,1024]{2,1,0:T(8,128)(2,1)S(1)}, u32[]{:S(2)}, u32[]{:S(2)}) collective-permute-start(bf16[2,64,1024]{2,1,0:T(8,128)(2,1)} %get-tuple-element.34), channel_id=1, source_target_pairs={{0,10},{2,8},{4,14},{6,12},{8,2},{10,0},{12,6},{14,4},{1,11},{3,9}... | collective-permute-start | bytes 786440 | tf_op jit(solution)/shard_map/ppermute | solution.py:184
  9.1 25.3 %collective-permute-start.2 = (bf16[2,64,1024]{2,1,0:T(8,128)(2,1)}, bf16[2,64,1024]{2,1,0:T(8,128)(2,1)S(1)}, u32[]{:S(2)}, u32[]{:S(2)}) collective-permute-start(bf16[2,64,1024]{2,1,0:T(8,128)(2,1)} %get-tuple-element.35), channel_id=1, source_target_pairs={{0,6},{2,4},{4,2},{6,0},{8,14},{10,12},{12,10},{14,8},{1,7},{3,5},... | collective-permute-start | bytes 786440 | tf_op jit(solution)/shard_map/ppermute | solution.py:184
  10.8 23.7 %collective-permute-start.3 = (bf16[2,64,1024]{2,1,0:T(8,128)(2,1)}, bf16[2,64,1024]{2,1,0:T(8,128)(2,1)S(1)}, u32[]{:S(2)}, u32[]{:S(2)}) collective-permute-start(bf16[2,64,1024]{2,1,0:T(8,128)(2,1)} %get-tuple-element.36), channel_id=1, source_target_pairs={{0,2},{2,0},{4,6},{6,4},{8,10},{10,8},{12,14},{14,12},{1,3},{3,1},... | collective-permute-start | bytes 786440 | tf_op jit(solution)/shard_map/ppermute | solution.py:184
  11.2 3.1 %copy-start = (bf16[1,1024,3584]{2,1,0:T(8,128)(2,1)S(1)}, bf16[1,1024,3584]{2,1,0:T(8,128)(2,1)}, u32[]{:S(2)}) copy-start(bf16[1,1024,3584]{2,1,0:T(8,128)(2,1)} %param.7) | copy-start | bytes 22020100
  14.3 0.7 copy-start.3
  15.0 0.7 copy-start.4
  15.7 18.8 %copy-start.1 = (bf16[1,1024,3584]{2,1,0:T(8,128)(2,1)S(1)}, bf16[1,1024,3584]{2,1,0:T(8,128)(2,1)}, u32[]{:S(2)}) copy-start(bf16[1,1024,3584]{2,1,0:T(8,128)(2,1)} %param.7) | copy-start | bytes 22020100
  38.6 30.2 %collective-permute-start.8 = (bf16[4,64,1536]{2,1,0:T(8,128)(2,1)S(1)}, bf16[4,64,1536]{2,1,0:T(8,128)(2,1)S(1)}, u32[]{:S(2)}, u32[]{:S(2)}) collective-permute-start(bf16[4,64,1536]{2,1,0:T(8,128)(2,1)S(1)} %mix.6), channel_id=1, source_target_pairs={{0,2},{2,0},{1,3},{3,1},{4,6},{6,4},{5,7},{7,5},{8,10},{10,8},{9,1... | collective-permute-start | bytes 2359304 | tf_op jit(solution)/shard_map/ppermute | solution.py:179
  40.1 11.8 %collective-permute-start.4 = (bf16[2,64,1024]{2,1,0:T(8,128)(2,1)S(1)}, bf16[2,64,1024]{2,1,0:T(8,128)(2,1)S(1)}, u32[]{:S(2)}, u32[]{:S(2)}) collective-permute-start(bf16[2,64,1024]{2,1,0:T(8,128)(2,1)S(1)} %get-tuple-element.37), channel_id=1, source_target_pairs={{0,12},{2,14},{4,8},{6,10},{8,4},{10,6},{12,0},{14,2},{1,13},{3,15... | collective-permute-start | bytes 786440 | tf_op jit(solution)/shard_map/ppermute | solution.py:184
  44.6 20.1 %collective-permute-start.5 = (bf16[2,64,1024]{2,1,0:T(8,128)(2,1)S(1)}, bf16[2,64,1024]{2,1,0:T(8,128)(2,1)S(1)}, u32[]{:S(2)}, u32[]{:S(2)}) collective-permute-start(bf16[2,64,1024]{2,1,0:T(8,128)(2,1)S(1)} %get-tuple-element.38), channel_id=1, source_target_pairs={{0,8},{2,10},{4,12},{6,14},{8,0},{10,2},{12,4},{14,6},{1,9},{3,11}... | collective-permute-start | bytes 786440 | tf_op jit(solution)/shard_map/ppermute | solution.py:184
  44.6 20.1 %collective-permute-start.6 = (bf16[2,64,1024]{2,1,0:T(8,128)(2,1)S(1)}, bf16[2,64,1024]{2,1,0:T(8,128)(2,1)S(1)}, u32[]{:S(2)}, u32[]{:S(2)}) collective-permute-start(bf16[2,64,1024]{2,1,0:T(8,128)(2,1)S(1)} %get-tuple-element.39), channel_id=1, source_target_pairs={{0,4},{2,6},{4,0},{6,2},{8,12},{10,14},{12,8},{14,10},{1,5},{3,7},... | collective-permute-start | bytes 786440 | tf_op jit(solution)/shard_map/ppermute | solution.py:184
  49.3 26.7 %collective-permute-start.9 = (bf16[4,64,1536]{2,1,0:T(8,128)(2,1)S(1)}, bf16[4,64,1536]{2,1,0:T(8,128)(2,1)S(1)}, u32[]{:S(2)}, u32[]{:S(2)}) collective-permute-start(bf16[4,64,1536]{2,1,0:T(8,128)(2,1)S(1)} %mix.7), channel_id=1, source_target_pairs={{0,2},{2,0},{1,3},{3,1},{4,6},{6,4},{5,7},{7,5},{8,10},{10,8},{9,1... | collective-permute-start | bytes 2359304 | tf_op jit(solution)/shard_map/ppermute | solution.py:179
  51.9 30.5 %collective-permute-start.12 = (bf16[4,64,512]{2,1,0:T(8,128)(2,1)S(1)}, bf16[4,64,512]{2,1,0:T(8,128)(2,1)S(1)}, u32[]{:S(2)}, u32[]{:S(2)}) collective-permute-start(bf16[4,64,512]{2,1,0:T(8,128)(2,1)S(1)} %mix.8), channel_id=1, source_target_pairs={{0,2},{2,0},{1,3},{3,1},{4,6},{6,4},{5,7},{7,5},{8,10},{10,8},{9,1... | collective-permute-start | bytes 786440 | tf_op jit(solution)/shard_map/ppermute | solution.py:179
  69.2 13.0 %collective-permute-start.10 = (bf16[2,64,1536]{2,1,0:T(8,128)(2,1)S(1)}, bf16[2,64,1536]{2,1,0:T(8,128)(2,1)S(1)}, u32[]{:S(2)}, u32[]{:S(2)}) collective-permute-start(bf16[2,64,1536]{2,1,0:T(8,128)(2,1)S(1)} %slice.57), channel_id=1, source_target_pairs={{0,4},{4,0},{8,12},{12,8},{1,5},{5,1},{9,13},{13,9},{2,6},{6,2},{1... | collective-permute-start | bytes 1179656 | tf_op jit(solution)/shard_map/ppermute | solution.py:179
  76.6 9.8 %collective-permute-start.13 = (bf16[2,64,768]{2,1,0:T(8,128)(2,1)S(1)}, bf16[2,64,768]{2,1,0:T(8,128)(2,1)S(1)}, u32[]{:S(2)}, u32[]{:S(2)}) collective-permute-start(bf16[2,64,768]{2,1,0:T(8,128)(2,1)S(1)} %slice.61), channel_id=1, source_target_pairs={{0,4},{4,0},{8,12},{12,8},{1,5},{5,1},{9,13},{13,9},{2,6},{6,2},{1... | collective-permute-start | bytes 589832 | tf_op jit(solution)/shard_map/ppermute | solution.py:179
  78.4 15.3 %collective-permute-start.15 = (bf16[2,64,768]{2,1,0:T(8,128)(2,1)S(1)}, bf16[2,64,768]{2,1,0:T(8,128)(2,1)S(1)}, u32[]{:S(2)}, u32[]{:S(2)}) collective-permute-start(bf16[2,64,768]{2,1,0:T(8,128)(2,1)S(1)} %slice.65), channel_id=1, source_target_pairs={{0,4},{4,0},{8,12},{12,8},{1,5},{5,1},{9,13},{13,9},{2,6},{6,2},{1... | collective-permute-start | bytes 589832 | tf_op jit(solution)/shard_map/ppermute | solution.py:179
  82.3 19.2 %collective-permute-start.11 = (bf16[64,1536]{1,0:T(8,128)(2,1)S(1)}, bf16[64,1536]{1,0:T(8,128)(2,1)S(1)}, u32[]{:S(2)}, u32[]{:S(2)}) collective-permute-start(bf16[64,1536]{1,0:T(8,128)(2,1)S(1)} %fusion.2), channel_id=1, source_target_pairs={{0,8},{4,12},{8,0},{12,4},{1,9},{5,13},{9,1},{13,5},{2,10},{6,14},... | collective-permute-start | bytes 589832 | tf_op jit(solution)/shard_map/ppermute | solution.py:179
  82.5 18.9 %collective-permute-start.17 = (bf16[2,64,512]{2,1,0:T(8,128)(2,1)S(1)}, bf16[2,64,512]{2,1,0:T(8,128)(2,1)S(1)}, u32[]{:S(2)}, u32[]{:S(2)}) collective-permute-start(bf16[2,64,512]{2,1,0:T(8,128)(2,1)S(1)} %slice.69), channel_id=1, source_target_pairs={{0,4},{4,0},{8,12},{12,8},{1,5},{5,1},{9,13},{13,9},{2,6},{6,2},{1... | collective-permute-start | bytes 393224 | tf_op jit(solution)/shard_map/ppermute | solution.py:179
  86.5 13.8 %collective-permute-start.14 = (bf16[64,768]{1,0:T(8,128)(2,1)S(1)}, bf16[64,768]{1,0:T(8,128)(2,1)S(1)}, u32[]{:S(2)}, u32[]{:S(2)}) collective-permute-start(bf16[64,768]{1,0:T(8,128)(2,1)S(1)} %fusion.9), channel_id=1, source_target_pairs={{0,8},{4,12},{8,0},{12,4},{1,9},{5,13},{9,1},{13,5},{2,10},{6,14},... | collective-permute-start | bytes 294920 | tf_op jit(solution)/shard_map/ppermute | solution.py:179
  93.8 7.5 %collective-permute-start.16 = (bf16[64,768]{1,0:T(8,128)(2,1)S(1)}, bf16[64,768]{1,0:T(8,128)(2,1)S(1)}, u32[]{:S(2)}, u32[]{:S(2)}) collective-permute-start(bf16[64,768]{1,0:T(8,128)(2,1)S(1)} %fusion.10), channel_id=1, source_target_pairs={{0,8},{4,12},{8,0},{12,4},{1,9},{5,13},{9,1},{13,5},{2,10},{6,14},... | collective-permute-start | bytes 294920 | tf_op jit(solution)/shard_map/ppermute | solution.py:179
  101.4 5.2 %collective-permute-start.18 = (bf16[64,512]{1,0:T(8,128)(2,1)S(1)}, bf16[64,512]{1,0:T(8,128)(2,1)S(1)}, u32[]{:S(2)}, u32[]{:S(2)}) collective-permute-start(bf16[64,512]{1,0:T(8,128)(2,1)S(1)} %fusion.11), channel_id=1, source_target_pairs={{0,8},{4,12},{8,0},{12,4},{1,9},{5,13},{9,1},{13,5},{2,10},{6,14},... | collective-permute-start | bytes 196616 | tf_op jit(solution)/shard_map/ppermute | solution.py:179

commit v12 on v11

--- a/solution.py
+++ b/solution.py
@@ -9,7 +9,7 @@
 
 CHIPS = 8
 TILE = 512
-COLUMNS = ((0, 1536), (1536, 1536), (3072, 512))
+COLUMNS = ((0, 1024), (1024, 1024), (2048, 1536))
 LIGHT = 0.01
 
 
@@ -220,10 +220,9 @@
             kept.append(block[:, :, low : low + COLUMNS[i][1]])
         return block
 
-    def add_x(i, earlier, parts=1):
+    def add_x(i, earlier):
         line = after(kept[i], earlier).astype(jnp.float32) + across[i].astype(jnp.float32)
-        for part in jnp.split(line, parts, axis=2):
-            lines.append((part[1::2], swap(part[0::2].astype(jnp.bfloat16), "z", 1)))
+        lines.append((line[1::2], swap(line[0::2].astype(jnp.bfloat16), "z", 1)))
         return line
 
     def add_z(i, earlier):
@@ -239,11 +238,11 @@
     last = add_x(0, last)
     last = mix_even((1,), last, LIGHT)
     last = mix_even((2,), last, LIGHT)
-    last = add_x(1, last, 2)
+    last = add_x(1, last)
     last = add_z(0, last)
     last = add_x(2, last)
-    for i in range(1, 4):
-        last = add_z(i, last)
+    last = add_z(1, last)
+    add_z(2, last)
     for mine, theirs in pairs:
         results.append((mine + theirs.astype(jnp.float32)).astype(jnp.bfloat16))
     return jnp.concatenate(results, axis=1)

time: 108 us -> 106 us (0.981)
  starting transfers between devices: 26.1 us -> 21.2 us
  waiting for transfers between devices: 50.1 us -> 54 us
    ppermute x12 -> x10, starting transfers between devices: 13.3 us -> 8.37 us  [swap(): lax.ppermute(block, axis, [(i, i ^ distance) for i in range(lax.axis_size...]
    ppermute x12 -> x10, waiting for transfers between devices: 20.8 us -> 25.7 us  [swap(): lax.ppermute(block, axis, [(i, i ^ distance) for i in range(lax.axis_size...]
  transfers between devices with their start and end apart: 19 -> 17, of which waited for: 11 -> 7; matrix products, arithmetic and copies ran while one was open for 1% -> 1% of each run, Pallas kernels for 19% -> 20%
where the time goes in v12:
time: 106 us; the launch traced here: 105 us
  waiting for transfers between devices  54 us (51%)
  Pallas kernels  23.4 us (22%)
  starting transfers between devices  21.2 us (20%)
  local copies, waits for them, and re-layouts  4.72 us (4%)
  other arithmetic  1.8 us (2%)
    ppermute x7, waiting for transfers between devices, send_to_chip(): lax.ppermute(block, ('z', 'x'), [(i, i ^ relative) for i in range(sizes[0...  28.3 us
    ppermute x10, waiting for transfers between devices, swap(): lax.ppermute(block, axis, [(i, i ^ distance) for i in range(lax.axis_size...  25.7 us
    pallas_call x6, Pallas kernels, mix(): pl.pallas_call(mix_kernel, grid=(width // TILE,), in_specs=[whole] * len(...  19.6 us
    ppermute x7, starting transfers between devices, send_to_chip(): lax.ppermute(block, ('z', 'x'), [(i, i ^ relative) for i in range(sizes[0...  12.9 us
    ppermute x10, starting transfers between devices, swap(): lax.ppermute(block, axis, [(i, i ^ distance) for i in range(lax.axis_size...  8.37 us
    unnamed x10, local copies, waits for them, and re-layouts  4.46 us
    pallas_call x2, Pallas kernels, spread_rows(): pl.pallas_call(functools.partial(spread_kernel if more else fetching_kern...  3.89 us
  transfers between devices with their start and end apart: 17, of which 7 were waited for; matrix products, arithmetic and copies ran while one was open for 1% of the time, Pallas kernels for 20%

profile of v12, /device:TPU:0, one launch (start us, length us, event | category | flops | bytes accessed | tf_op | source)
XLA Modules:
  0.0 105.5 jit_solution(5693276179754764782)
XLA Ops:
  0.5 3.0 %spread_rows.3 = (bf16[2,64,1024]{2,1,0:T(8,128)(2,1)}, bf16[2,64,1024]{2,1,0:T(8,128)(2,1)}, bf16[2,64,1024]{2,1,0:T(8,128)(2,1)}, bf16[2,64,1024]{2,1,0:T(8,128)(2,1)}) custom-call(s32[1]{0:T(128)} %bitcast.own_ref, s32[8,64]{1,0:T(8,128)} %bitcast.39, f32[8,64]{1,0:T(8,128)} %bitcast.41, bf16[512,1024]{1,0:T(8,128)(2,1)} %bitcast.37), custom_call_target="tpu_custom_call" | custom-call | tf_op jit(solution)/shard_map/spread_rows/pallas_call | solution.py:125
  3.5 5.7 %collective-permute-start = (bf16[2,64,1024]{2,1,0:T(8,128)(2,1)}, bf16[2,64,1024]{2,1,0:T(8,128)(2,1)S(1)}, u32[]{:S(2)}, u32[]{:S(2)}) collective-permute-start(bf16[2,64,1024]{2,1,0:T(8,128)(2,1)} %get-tuple-element.32), channel_id=1, source_target_pairs={{0,14},{2,12},{4,10},{6,8},{8,6},{10,4},{12,2},{14,0},{1,15},{3,13... | collective-permute-start | bytes 786440 | tf_op jit(solution)/shard_map/ppermute | solution.py:184
  9.1 1.7 %collective-permute-start.2 = (bf16[2,64,1024]{2,1,0:T(8,128)(2,1)}, bf16[2,64,1024]{2,1,0:T(8,128)(2,1)S(1)}, u32[]{:S(2)}, u32[]{:S(2)}) collective-permute-start(bf16[2,64,1024]{2,1,0:T(8,128)(2,1)} %get-tuple-element.34), channel_id=1, source_target_pairs={{0,6},{2,4},{4,2},{6,0},{8,14},{10,12},{12,10},{14,8},{1,7},{3,5},... | collective-permute-start | bytes 786440 | tf_op jit(solution)/shard_map/ppermute | solution.py:184
  11.3 3.1 %copy-done = bf16[1,1024,3584]{2,1,0:T(8,128)(2,1)S(1)} copy-done((bf16[1,1024,3584]{2,1,0:T(8,128)(2,1)S(1)}, bf16[1,1024,3584]{2,1,0:T(8,128)(2,1)}, u32[]{:S(2)}) %copy-start) | copy-done | bytes 7340056
  14.3 0.7 copy-done.3
  15.7 0.9 spread_rows.2
  16.8 17.7 %collective-permute-done.1.refs_1_ = bf16[2,64,1024]{2,1,0:T(8,128)(2,1)S(1)} collective-permute-done((bf16[2,64,1024]{2,1,0:T(8,128)(2,1)}, bf16[2,64,1024]{2,1,0:T(8,128)(2,1)S(1)}, u32[]{:S(2)}, u32[]{:S(2)}) %collective-permute-start.1) | collective-permute-done | bytes 262176 | tf_op jit(solution)/shard_map/ppermute | solution.py:184
  34.5 2.8 %mix.6 = bf16[4,64,1024]{2,1,0:T(8,128)(2,1)S(1)} custom-call(bf16[2,64,1024]{2,1,0:T(8,128)(2,1)S(1)} %collective-permute-done.refs_0_, bf16[2,64,1024]{2,1,0:T(8,128)(2,1)S(1)} %collective-permute-done.1.refs_1_, bf16[2,64,1024]{2,1,0:T(8,128)(2,1)S(1)} %collective-permute-done.2.refs_2_, bf16[2,64,1024]{2,1,0:T(8,128)(2,1)S(1)} %collective-permute-done.3.refs_3_, ...), custom_call_target="tpu_custom_call" | custom-call | flops 10737418 | bytes 41943 | tf_op jit(solution)/shard_map/mix/pallas_call | solution.py:161
  37.4 1.5 %collective-permute-start.8 = (bf16[4,64,1024]{2,1,0:T(8,128)(2,1)S(1)}, bf16[4,64,1024]{2,1,0:T(8,128)(2,1)S(1)}, u32[]{:S(2)}, u32[]{:S(2)}) collective-permute-start(bf16[4,64,1024]{2,1,0:T(8,128)(2,1)S(1)} %mix.6), channel_id=1, source_target_pairs={{0,2},{2,0},{1,3},{3,1},{4,6},{6,4},{5,7},{7,5},{8,10},{10,8},{9,1... | collective-permute-start | bytes 1572872 | tf_op jit(solution)/shard_map/ppermute | solution.py:179
  38.8 4.5 %collective-permute-start.4 = (bf16[2,64,1024]{2,1,0:T(8,128)(2,1)S(1)}, bf16[2,64,1024]{2,1,0:T(8,128)(2,1)S(1)}, u32[]{:S(2)}, u32[]{:S(2)}) collective-permute-start(bf16[2,64,1024]{2,1,0:T(8,128)(2,1)S(1)} %get-tuple-element.36), channel_id=1, source_target_pairs={{0,12},{2,14},{4,8},{6,10},{8,4},{10,6},{12,0},{14,2},{1,13},{3,15... | collective-permute-start | bytes 786440 | tf_op jit(solution)/shard_map/ppermute | solution.py:184
  43.9 2.8 %mix.7 = bf16[4,64,1024]{2,1,0:T(8,128)(2,1)S(1)} custom-call(bf16[2,64,1024]{2,1,0:T(8,128)(2,1)S(1)} %collective-permute-done.refs_0_, bf16[2,64,1024]{2,1,0:T(8,128)(2,1)S(1)} %collective-permute-done.1.refs_1_, bf16[2,64,1024]{2,1,0:T(8,128)(2,1)S(1)} %collective-permute-done.2.refs_2_, bf16[2,64,1024]{2,1,0:T(8,128)(2,1)S(1)} %collective-permute-done.3.refs_3_, ...), custom_call_target="tpu_custom_call" | custom-call | flops 10737418 | bytes 41943 | tf_op jit(solution)/shard_map/mix/pallas_call | solution.py:161
  47.3 4.1 %mix.8 = bf16[4,64,1536]{2,1,0:T(8,128)(2,1)S(1)} custom-call(bf16[2,64,1024]{2,1,0:T(8,128)(2,1)S(1)} %collective-permute-done.refs_0_, bf16[2,64,1024]{2,1,0:T(8,128)(2,1)S(1)} %collective-permute-done.1.refs_1_, bf16[2,64,1024]{2,1,0:T(8,128)(2,1)S(1)} %collective-permute-done.2.refs_2_, bf16[2,64,1024]{2,1,0:T(8,128)(2,1)S(1)} %collective-permute-done.3.refs_3_, ...), custom_call_target="tpu_custom_call" | custom-call | flops 16106127 | bytes 62914 | tf_op jit(solution)/shard_map/mix/pallas_call | solution.py:161
  51.4 1.7 %collective-permute-start.12 = (bf16[4,64,1536]{2,1,0:T(8,128)(2,1)S(1)}, bf16[4,64,1536]{2,1,0:T(8,128)(2,1)S(1)}, u32[]{:S(2)}, u32[]{:S(2)}) collective-permute-start(bf16[4,64,1536]{2,1,0:T(8,128)(2,1)S(1)} %mix.8), channel_id=1, source_target_pairs={{0,2},{2,0},{1,3},{3,1},{4,6},{6,4},{5,7},{7,5},{8,10},{10,8},{9,1... | collective-permute-start | bytes 2359304 | tf_op jit(solution)/shard_map/ppermute | solution.py:179
  53.0 10.4 %collective-permute-done.5.refs_1_ = bf16[2,64,1024]{2,1,0:T(8,128)(2,1)S(1)} collective-permute-done((bf16[2,64,1024]{2,1,0:T(8,128)(2,1)S(1)}, bf16[2,64,1024]{2,1,0:T(8,128)(2,1)S(1)}, u32[]{:S(2)}, u32[]{:S(2)}) %collective-permute-start.5) | collective-permute-done | bytes 262176 | tf_op jit(solution)/shard_map/ppermute | solution.py:184
  63.5 2.8 %mix.9 = bf16[4,64,1024]{2,1,0:T(8,128)(2,1)S(1)} custom-call(bf16[2,64,1024]{2,1,0:T(8,128)(2,1)S(1)} %collective-permute-done.4.refs_0_, bf16[2,64,1024]{2,1,0:T(8,128)(2,1)S(1)} %collective-permute-done.5.refs_1_, bf16[2,64,1024]{2,1,0:T(8,128)(2,1)S(1)} %collective-permute-done.6.refs_2_, bf16[2,64,1024]{2,1,0:T(8,128)(2,1)S(1)} %get-tuple-element.45.refs_3_, ...), custom_call_target="tpu_custom_call" | custom-call | flops 10737418 | bytes 41943 | tf_op jit(solution)/shard_map/mix/pallas_call | solution.py:161
  66.7 2.8 %mix.10 = bf16[4,64,1024]{2,1,0:T(8,128)(2,1)S(1)} custom-call(bf16[2,64,1024]{2,1,0:T(8,128)(2,1)S(1)} %collective-permute-done.4.refs_0_, bf16[2,64,1024]{2,1,0:T(8,128)(2,1)S(1)} %collective-permute-done.5.refs_1_, bf16[2,64,1024]{2,1,0:T(8,128)(2,1)S(1)} %collective-permute-done.6.refs_2_, bf16[2,64,1024]{2,1,0:T(8,128)(2,1)S(1)} %get-tuple-element.45.refs_3_, ...), custom_call_target="tpu_custom_call" | custom-call | flops 10737418 | bytes 41943 | tf_op jit(solution)/shard_map/mix/pallas_call | solution.py:161
  69.6 4.1 %mix.11 = bf16[4,64,1536]{2,1,0:T(8,128)(2,1)S(1)} custom-call(bf16[2,64,1024]{2,1,0:T(8,128)(2,1)S(1)} %collective-permute-done.4.refs_0_, bf16[2,64,1024]{2,1,0:T(8,128)(2,1)S(1)} %collective-permute-done.5.refs_1_, bf16[2,64,1024]{2,1,0:T(8,128)(2,1)S(1)} %collective-permute-done.6.refs_2_, bf16[2,64,1024]{2,1,0:T(8,128)(2,1)S(1)} %get-tuple-element.45.refs_3_, ...), custom_call_target="tpu_custom_call" | custom-call | flops 16106127 | bytes 62914 | tf_op jit(solution)/shard_map/mix/pallas_call | solution.py:161
  74.0 2.1 %collective-permute-start.13 = (bf16[2,64,1024]{2,1,0:T(8,128)(2,1)S(1)}, bf16[2,64,1024]{2,1,0:T(8,128)(2,1)S(1)}, u32[]{:S(2)}, u32[]{:S(2)}) collective-permute-start(bf16[2,64,1024]{2,1,0:T(8,128)(2,1)S(1)} %slice.47), channel_id=1, source_target_pairs={{0,4},{4,0},{8,12},{12,8},{1,5},{5,1},{9,13},{13,9},{2,6},{6,2},{1... | collective-permute-start | bytes 786440 | tf_op jit(solution)/shard_map/ppermute | solution.py:179
  76.2 2.8 %collective-permute-done.12 = bf16[4,64,1536]{2,1,0:T(8,128)(2,1)S(1)} collective-permute-done((bf16[4,64,1536]{2,1,0:T(8,128)(2,1)S(1)}, bf16[4,64,1536]{2,1,0:T(8,128)(2,1)S(1)}, u32[]{:S(2)}, u32[]{:S(2)}) %collective-permute-start.12) | collective-permute-done | bytes 786464 | tf_op jit(solution)/shard_map/ppermute | solution.py:179
  79.4 1.8 %collective-permute-start.15 = (bf16[2,64,1536]{2,1,0:T(8,128)(2,1)S(1)}, bf16[2,64,1536]{2,1,0:T(8,128)(2,1)S(1)}, u32[]{:S(2)}, u32[]{:S(2)}) collective-permute-start(bf16[2,64,1536]{2,1,0:T(8,128)(2,1)S(1)} %slice.51), channel_id=1, source_target_pairs={{0,4},{4,0},{8,12},{12,8},{1,5},{5,1},{9,13},{13,9},{2,6},{6,2},{1... | collective-permute-start | bytes 1179656 | tf_op jit(solution)/shard_map/ppermute | solution.py:179
  81.2 3.9 %collective-permute-done.13 = bf16[2,64,1024]{2,1,0:T(8,128)(2,1)S(1)} collective-permute-done((bf16[2,64,1024]{2,1,0:T(8,128)(2,1)S(1)}, bf16[2,64,1024]{2,1,0:T(8,128)(2,1)S(1)}, u32[]{:S(2)}, u32[]{:S(2)}) %collective-permute-start.13) | collective-permute-done | bytes 262176 | tf_op jit(solution)/shard_map/ppermute | solution.py:179
  85.4 9.2 %collective-permute-done.15 = bf16[2,64,1536]{2,1,0:T(8,128)(2,1)S(1)} collective-permute-done((bf16[2,64,1536]{2,1,0:T(8,128)(2,1)S(1)}, bf16[2,64,1536]{2,1,0:T(8,128)(2,1)S(1)}, u32[]{:S(2)}, u32[]{:S(2)}) %collective-permute-start.15) | collective-permute-done | bytes 393248 | tf_op jit(solution)/shard_map/ppermute | solution.py:179
  94.9 9.7 %collective-permute-done.16 = bf16[64,1536]{1,0:T(8,128)(2,1)S(1)} collective-permute-done((bf16[64,1536]{1,0:T(8,128)(2,1)S(1)}, bf16[64,1536]{1,0:T(8,128)(2,1)S(1)}, u32[]{:S(2)}, u32[]{:S(2)}) %collective-permute-start.16) | collective-permute-done | bytes 196640 | tf_op jit(solution)/shard_map/ppermute | solution.py:179
  104.7 0.8 pad_maximum_fusion
  (47 shorter events, 4.4 us)
Async XLA Ops:
  0.0 11.3 %copy-start.2 = (bf16[64,8,1024]{2,1,0:T(8,128)(2,1)S(1)}, bf16[64,8,1024]{2,1,0:T(8,128)(2,1)}, u32[]{:S(2)}) copy-start(bf16[64,8,1024]{2,1,0:T(8,128)(2,1)} %param.4) | copy-start | bytes 3145732
  0.0 34.5 %collective-permute-start.7 = (bf16[1024,3584]{1,0:T(8,128)(2,1)}, bf16[1024,3584]{1,0:T(8,128)(2,1)}, u32[]{:S(2)}, u32[]{:S(2)}) collective-permute-start(bf16[1024,3584]{1,0:T(8,128)(2,1)} %bitcast.29), channel_id=1, source_target_pairs={{0,1},{1,0},{2,3},{3,2},{4,5},{5,4},{6,7},{7,6},{8,9},{9,8},{10,11... | collective-permute-start | bytes 22020104 | tf_op jit(solution)/shard_map/ppermute | solution.py:179
  3.5 13.3 %collective-permute-start = (bf16[2,64,1024]{2,1,0:T(8,128)(2,1)}, bf16[2,64,1024]{2,1,0:T(8,128)(2,1)S(1)}, u32[]{:S(2)}, u32[]{:S(2)}) collective-permute-start(bf16[2,64,1024]{2,1,0:T(8,128)(2,1)} %get-tuple-element.32), channel_id=1, source_target_pairs={{0,14},{2,12},{4,10},{6,8},{8,6},{10,4},{12,2},{14,0},{1,15},{3,13... | collective-permute-start | bytes 786440 | tf_op jit(solution)/shard_map/ppermute | solution.py:184
  9.1 25.3 %collective-permute-start.1 = (bf16[2,64,1024]{2,1,0:T(8,128)(2,1)}, bf16[2,64,1024]{2,1,0:T(8,128)(2,1)S(1)}, u32[]{:S(2)}, u32[]{:S(2)}) collective-permute-start(bf16[2,64,1024]{2,1,0:T(8,128)(2,1)} %get-tuple-element.33), channel_id=1, source_target_pairs={{0,10},{2,8},{4,14},{6,12},{8,2},{10,0},{12,6},{14,4},{1,11},{3,9}... | collective-permute-start | bytes 786440 | tf_op jit(solution)/shard_map/ppermute | solution.py:184
  9.1 25.3 %collective-permute-start.2 = (bf16[2,64,1024]{2,1,0:T(8,128)(2,1)}, bf16[2,64,1024]{2,1,0:T(8,128)(2,1)S(1)}, u32[]{:S(2)}, u32[]{:S(2)}) collective-permute-start(bf16[2,64,1024]{2,1,0:T(8,128)(2,1)} %get-tuple-element.34), channel_id=1, source_target_pairs={{0,6},{2,4},{4,2},{6,0},{8,14},{10,12},{12,10},{14,8},{1,7},{3,5},... | collective-permute-start | bytes 786440 | tf_op jit(solution)/shard_map/ppermute | solution.py:184
  10.8 23.7 %collective-permute-start.3 = (bf16[2,64,1024]{2,1,0:T(8,128)(2,1)}, bf16[2,64,1024]{2,1,0:T(8,128)(2,1)S(1)}, u32[]{:S(2)}, u32[]{:S(2)}) collective-permute-start(bf16[2,64,1024]{2,1,0:T(8,128)(2,1)} %get-tuple-element.35), channel_id=1, source_target_pairs={{0,2},{2,0},{4,6},{6,4},{8,10},{10,8},{12,14},{14,12},{1,3},{3,1},... | collective-permute-start | bytes 786440 | tf_op jit(solution)/shard_map/ppermute | solution.py:184
  11.3 3.1 %copy-start = (bf16[1,1024,3584]{2,1,0:T(8,128)(2,1)S(1)}, bf16[1,1024,3584]{2,1,0:T(8,128)(2,1)}, u32[]{:S(2)}) copy-start(bf16[1,1024,3584]{2,1,0:T(8,128)(2,1)} %param.7) | copy-start | bytes 22020100
  14.3 0.7 copy-start.3
  15.0 0.7 copy-start.4
  15.7 18.8 %copy-start.1 = (bf16[1,1024,3584]{2,1,0:T(8,128)(2,1)S(1)}, bf16[1,1024,3584]{2,1,0:T(8,128)(2,1)}, u32[]{:S(2)}) copy-start(bf16[1,1024,3584]{2,1,0:T(8,128)(2,1)} %param.7) | copy-start | bytes 22020100
  37.4 29.0 %collective-permute-start.8 = (bf16[4,64,1024]{2,1,0:T(8,128)(2,1)S(1)}, bf16[4,64,1024]{2,1,0:T(8,128)(2,1)S(1)}, u32[]{:S(2)}, u32[]{:S(2)}) collective-permute-start(bf16[4,64,1024]{2,1,0:T(8,128)(2,1)S(1)} %mix.6), channel_id=1, source_target_pairs={{0,2},{2,0},{1,3},{3,1},{4,6},{6,4},{5,7},{7,5},{8,10},{10,8},{9,1... | collective-permute-start | bytes 1572872 | tf_op jit(solution)/shard_map/ppermute | solution.py:179
  38.8 12.5 %collective-permute-start.4 = (bf16[2,64,1024]{2,1,0:T(8,128)(2,1)S(1)}, bf16[2,64,1024]{2,1,0:T(8,128)(2,1)S(1)}, u32[]{:S(2)}, u32[]{:S(2)}) collective-permute-start(bf16[2,64,1024]{2,1,0:T(8,128)(2,1)S(1)} %get-tuple-element.36), channel_id=1, source_target_pairs={{0,12},{2,14},{4,8},{6,10},{8,4},{10,6},{12,0},{14,2},{1,13},{3,15... | collective-permute-start | bytes 786440 | tf_op jit(solution)/shard_map/ppermute | solution.py:184
  43.4 20.1 %collective-permute-start.5 = (bf16[2,64,1024]{2,1,0:T(8,128)(2,1)S(1)}, bf16[2,64,1024]{2,1,0:T(8,128)(2,1)S(1)}, u32[]{:S(2)}, u32[]{:S(2)}) collective-permute-start(bf16[2,64,1024]{2,1,0:T(8,128)(2,1)S(1)} %get-tuple-element.37), channel_id=1, source_target_pairs={{0,8},{2,10},{4,12},{6,14},{8,0},{10,2},{12,4},{14,6},{1,9},{3,11}... | collective-permute-start | bytes 786440 | tf_op jit(solution)/shard_map/ppermute | solution.py:184
  43.4 20.1 %collective-permute-start.6 = (bf16[2,64,1024]{2,1,0:T(8,128)(2,1)S(1)}, bf16[2,64,1024]{2,1,0:T(8,128)(2,1)S(1)}, u32[]{:S(2)}, u32[]{:S(2)}) collective-permute-start(bf16[2,64,1024]{2,1,0:T(8,128)(2,1)S(1)} %get-tuple-element.38), channel_id=1, source_target_pairs={{0,4},{2,6},{4,0},{6,2},{8,12},{10,14},{12,8},{14,10},{1,5},{3,7},... | collective-permute-start | bytes 786440 | tf_op jit(solution)/shard_map/ppermute | solution.py:184
  46.8 26.9 %collective-permute-start.9 = (bf16[4,64,1024]{2,1,0:T(8,128)(2,1)S(1)}, bf16[4,64,1024]{2,1,0:T(8,128)(2,1)S(1)}, u32[]{:S(2)}, u32[]{:S(2)}) collective-permute-start(bf16[4,64,1024]{2,1,0:T(8,128)(2,1)S(1)} %mix.7), channel_id=1, source_target_pairs={{0,2},{2,0},{1,3},{3,1},{4,6},{6,4},{5,7},{7,5},{8,10},{10,8},{9,1... | collective-permute-start | bytes 1572872 | tf_op jit(solution)/shard_map/ppermute | solution.py:179
  51.4 27.6 %collective-permute-start.12 = (bf16[4,64,1536]{2,1,0:T(8,128)(2,1)S(1)}, bf16[4,64,1536]{2,1,0:T(8,128)(2,1)S(1)}, u32[]{:S(2)}, u32[]{:S(2)}) collective-permute-start(bf16[4,64,1536]{2,1,0:T(8,128)(2,1)S(1)} %mix.8), channel_id=1, source_target_pairs={{0,2},{2,0},{1,3},{3,1},{4,6},{6,4},{5,7},{7,5},{8,10},{10,8},{9,1... | collective-permute-start | bytes 2359304 | tf_op jit(solution)/shard_map/ppermute | solution.py:179
  66.6 9.4 %collective-permute-start.10 = (bf16[2,64,1024]{2,1,0:T(8,128)(2,1)S(1)}, bf16[2,64,1024]{2,1,0:T(8,128)(2,1)S(1)}, u32[]{:S(2)}, u32[]{:S(2)}) collective-permute-start(bf16[2,64,1024]{2,1,0:T(8,128)(2,1)S(1)} %slice.43), channel_id=1, source_target_pairs={{0,4},{4,0},{8,12},{12,8},{1,5},{5,1},{9,13},{13,9},{2,6},{6,2},{1... | collective-permute-start | bytes 786440 | tf_op jit(solution)/shard_map/ppermute | solution.py:179
  74.0 11.1 %collective-permute-start.13 = (bf16[2,64,1024]{2,1,0:T(8,128)(2,1)S(1)}, bf16[2,64,1024]{2,1,0:T(8,128)(2,1)S(1)}, u32[]{:S(2)}, u32[]{:S(2)}) collective-permute-start(bf16[2,64,1024]{2,1,0:T(8,128)(2,1)S(1)} %slice.47), channel_id=1, source_target_pairs={{0,4},{4,0},{8,12},{12,8},{1,5},{5,1},{9,13},{13,9},{2,6},{6,2},{1... | collective-permute-start | bytes 786440 | tf_op jit(solution)/shard_map/ppermute | solution.py:179
  76.1 9.2 %collective-permute-start.11 = (bf16[64,1024]{1,0:T(8,128)(2,1)S(1)}, bf16[64,1024]{1,0:T(8,128)(2,1)S(1)}, u32[]{:S(2)}, u32[]{:S(2)}) collective-permute-start(bf16[64,1024]{1,0:T(8,128)(2,1)S(1)} %fusion.7), channel_id=1, source_target_pairs={{0,8},{4,12},{8,0},{12,4},{1,9},{5,13},{9,1},{13,5},{2,10},{6,14},... | collective-permute-start | bytes 393224 | tf_op jit(solution)/shard_map/ppermute | solution.py:179
  79.4 15.2 %collective-permute-start.15 = (bf16[2,64,1536]{2,1,0:T(8,128)(2,1)S(1)}, bf16[2,64,1536]{2,1,0:T(8,128)(2,1)S(1)}, u32[]{:S(2)}, u32[]{:S(2)}) collective-permute-start(bf16[2,64,1536]{2,1,0:T(8,128)(2,1)S(1)} %slice.51), channel_id=1, source_target_pairs={{0,4},{4,0},{8,12},{12,8},{1,5},{5,1},{9,13},{13,9},{2,6},{6,2},{1... | collective-permute-start | bytes 1179656 | tf_op jit(solution)/shard_map/ppermute | solution.py:179
  85.2 9.6 %collective-permute-start.14 = (bf16[64,1024]{1,0:T(8,128)(2,1)S(1)}, bf16[64,1024]{1,0:T(8,128)(2,1)S(1)}, u32[]{:S(2)}, u32[]{:S(2)}) collective-permute-start(bf16[64,1024]{1,0:T(8,128)(2,1)S(1)} %fusion.8), channel_id=1, source_target_pairs={{0,8},{4,12},{8,0},{12,4},{1,9},{5,13},{9,1},{13,5},{2,10},{6,14},... | collective-permute-start | bytes 393224 | tf_op jit(solution)/shard_map/ppermute | solution.py:179
  94.7 9.9 %collective-permute-start.16 = (bf16[64,1536]{1,0:T(8,128)(2,1)S(1)}, bf16[64,1536]{1,0:T(8,128)(2,1)S(1)}, u32[]{:S(2)}, u32[]{:S(2)}) collective-permute-start(bf16[64,1536]{1,0:T(8,128)(2,1)S(1)} %fusion.6), channel_id=1, source_target_pairs={{0,8},{4,12},{8,0},{12,4},{1,9},{5,13},{9,1},{13,5},{2,10},{6,14},... | collective-permute-start | bytes 589832 | tf_op jit(solution)/shard_map/ppermute | solution.py:179

commit v13 on v12

--- a/solution.py
+++ b/solution.py
@@ -194,7 +194,7 @@
     own = (lax.axis_index("z") * 2 + lax.axis_index("x")) * 2 + lax.axis_index("core")
     near = down_weight[0]
     far = swap(near, "core", 1)
-    odd, even = (7, 5, 3, 1), (6, 4, 2, 0)
+    odd, even = (5, 7, 1, 3), (4, 6, 0, 2)
     arrived = [None] * CHIPS
     blocks = spread_rows(hidden, expert_ids, gate_weights, own, odd)
     for relative, block in zip(odd, blocks):
@@ -222,7 +222,7 @@
 
     def add_x(i, earlier):
         line = after(kept[i], earlier).astype(jnp.float32) + across[i].astype(jnp.float32)
-        lines.append((line[1::2], swap(line[0::2].astype(jnp.bfloat16), "z", 1)))
+        lines.append((line[0::2], swap(line[1::2].astype(jnp.bfloat16), "z", 1)))
         return line
 
     def add_z(i, earlier):

time: 106 us -> 108 us (1.019)
  starting transfers between devices: 21.2 us -> 27.3 us
  waiting for transfers between devices: 54 us -> 49.7 us
    ppermute x10, starting transfers between devices: 8.37 us -> 15.5 us  [swap(): lax.ppermute(block, axis, [(i, i ^ distance) for i in range(lax.axis_size...]
    ppermute x7, waiting for transfers between devices: 28.3 us -> 25.5 us  [send_to_chip(): lax.ppermute(block, ('z', 'x'), [(i, i ^ relative) for i in range(sizes[0...]
    ppermute x10, waiting for transfers between devices: 25.7 us -> 24.2 us  [swap(): lax.ppermute(block, axis, [(i, i ^ distance) for i in range(lax.axis_size...]
    ppermute x7, starting transfers between devices: 12.9 us -> 11.8 us  [send_to_chip(): lax.ppermute(block, ('z', 'x'), [(i, i ^ relative) for i in range(sizes[0...]
  transfers between devices with their start and end apart: 17 -> 17, of which waited for: 7 -> 6; matrix products, arithmetic and copies ran while one was open for 1% -> 1% of each run, Pallas kernels for 20% -> 19%
where the time goes in v13:
time: 108 us; the launch traced here: 107 us
  waiting for transfers between devices  49.7 us (46%)
  starting transfers between devices  27.3 us (25%)
  Pallas kernels  23.4 us (22%)
  local copies, waits for them, and re-layouts  4.72 us (4%)
  other arithmetic  1.8 us (2%)
    ppermute x7, waiting for transfers between devices, send_to_chip(): lax.ppermute(block, ('z', 'x'), [(i, i ^ relative) for i in range(sizes[0...  25.5 us
    ppermute x10, waiting for transfers between devices, swap(): lax.ppermute(block, axis, [(i, i ^ distance) for i in range(lax.axis_size...  24.2 us
    pallas_call x6, Pallas kernels, mix(): pl.pallas_call(mix_kernel, grid=(width // TILE,), in_specs=[whole] * len(...  19.5 us
    ppermute x10, starting transfers between devices, swap(): lax.ppermute(block, axis, [(i, i ^ distance) for i in range(lax.axis_size...  15.5 us
    ppermute x7, starting transfers between devices, send_to_chip(): lax.ppermute(block, ('z', 'x'), [(i, i ^ relative) for i in range(sizes[0...  11.8 us
    unnamed x10, local copies, waits for them, and re-layouts  4.46 us
    pallas_call x2, Pallas kernels, spread_rows(): pl.pallas_call(functools.partial(spread_kernel if more else fetching_kern...  3.89 us
  transfers between devices with their start and end apart: 17, of which 6 were waited for; matrix products, arithmetic and copies ran while one was open for 1% of the time, Pallas kernels for 19%

profile of v13, /device:TPU:0, one launch (start us, length us, event | category | flops | bytes accessed | tf_op | source)
XLA Modules:
  0.0 107.2 jit_solution(13859955530148503922)
XLA Ops:
  0.5 3.0 %spread_rows.3 = (bf16[2,64,1024]{2,1,0:T(8,128)(2,1)}, bf16[2,64,1024]{2,1,0:T(8,128)(2,1)}, bf16[2,64,1024]{2,1,0:T(8,128)(2,1)}, bf16[2,64,1024]{2,1,0:T(8,128)(2,1)}) custom-call(s32[1]{0:T(128)} %bitcast.own_ref, s32[8,64]{1,0:T(8,128)} %bitcast.39, f32[8,64]{1,0:T(8,128)} %bitcast.41, bf16[512,1024]{1,0:T(8,128)(2,1)} %bitcast.37), custom_call_target="tpu_custom_call" | custom-call | tf_op jit(solution)/shard_map/spread_rows/pallas_call | solution.py:125
  3.5 4.7 %collective-permute-start = (bf16[2,64,1024]{2,1,0:T(8,128)(2,1)}, bf16[2,64,1024]{2,1,0:T(8,128)(2,1)S(1)}, u32[]{:S(2)}, u32[]{:S(2)}) collective-permute-start(bf16[2,64,1024]{2,1,0:T(8,128)(2,1)} %get-tuple-element.32), channel_id=1, source_target_pairs={{0,10},{2,8},{4,14},{6,12},{8,2},{10,0},{12,6},{14,4},{1,11},{3,9}... | collective-permute-start | bytes 786440 | tf_op jit(solution)/shard_map/ppermute | solution.py:184
  8.1 1.3 %collective-permute-start.1 = (bf16[2,64,1024]{2,1,0:T(8,128)(2,1)}, bf16[2,64,1024]{2,1,0:T(8,128)(2,1)S(1)}, u32[]{:S(2)}, u32[]{:S(2)}) collective-permute-start(bf16[2,64,1024]{2,1,0:T(8,128)(2,1)} %get-tuple-element.33), channel_id=1, source_target_pairs={{0,14},{2,12},{4,10},{6,8},{8,6},{10,4},{12,2},{14,0},{1,15},{3,13... | collective-permute-start | bytes 786440 | tf_op jit(solution)/shard_map/ppermute | solution.py:184
  9.5 1.5 %collective-permute-start.2 = (bf16[2,64,1024]{2,1,0:T(8,128)(2,1)}, bf16[2,64,1024]{2,1,0:T(8,128)(2,1)S(1)}, u32[]{:S(2)}, u32[]{:S(2)}) collective-permute-start(bf16[2,64,1024]{2,1,0:T(8,128)(2,1)} %get-tuple-element.34), channel_id=1, source_target_pairs={{0,2},{2,0},{4,6},{6,4},{8,10},{10,8},{12,14},{14,12},{1,3},{3,1},... | collective-permute-start | bytes 786440 | tf_op jit(solution)/shard_map/ppermute | solution.py:184
  11.2 3.1 %copy-done = bf16[1,1024,3584]{2,1,0:T(8,128)(2,1)S(1)} copy-done((bf16[1,1024,3584]{2,1,0:T(8,128)(2,1)S(1)}, bf16[1,1024,3584]{2,1,0:T(8,128)(2,1)}, u32[]{:S(2)}) %copy-start) | copy-done | bytes 7340056
  16.5 10.3 %collective-permute-done.refs_0_ = bf16[2,64,1024]{2,1,0:T(8,128)(2,1)S(1)} collective-permute-done((bf16[2,64,1024]{2,1,0:T(8,128)(2,1)}, bf16[2,64,1024]{2,1,0:T(8,128)(2,1)S(1)}, u32[]{:S(2)}, u32[]{:S(2)}) %collective-permute-start) | collective-permute-done | bytes 262176 | tf_op jit(solution)/shard_map/ppermute | solution.py:184
  26.8 6.6 %collective-permute-done.2.refs_2_ = bf16[2,64,1024]{2,1,0:T(8,128)(2,1)S(1)} collective-permute-done((bf16[2,64,1024]{2,1,0:T(8,128)(2,1)}, bf16[2,64,1024]{2,1,0:T(8,128)(2,1)S(1)}, u32[]{:S(2)}, u32[]{:S(2)}) %collective-permute-start.2) | collective-permute-done | bytes 262176 | tf_op jit(solution)/shard_map/ppermute | solution.py:184
  33.5 2.8 %mix.6 = bf16[4,64,1024]{2,1,0:T(8,128)(2,1)S(1)} custom-call(bf16[2,64,1024]{2,1,0:T(8,128)(2,1)S(1)} %collective-permute-done.refs_0_, bf16[2,64,1024]{2,1,0:T(8,128)(2,1)S(1)} %collective-permute-done.1.refs_1_, bf16[2,64,1024]{2,1,0:T(8,128)(2,1)S(1)} %collective-permute-done.2.refs_2_, bf16[2,64,1024]{2,1,0:T(8,128)(2,1)S(1)} %collective-permute-done.3.refs_3_, ...), custom_call_target="tpu_custom_call" | custom-call | flops 10737418 | bytes 41943 | tf_op jit(solution)/shard_map/mix/pallas_call | solution.py:161
  36.3 1.6 %collective-permute-start.8 = (bf16[4,64,1024]{2,1,0:T(8,128)(2,1)S(1)}, bf16[4,64,1024]{2,1,0:T(8,128)(2,1)S(1)}, u32[]{:S(2)}, u32[]{:S(2)}) collective-permute-start(bf16[4,64,1024]{2,1,0:T(8,128)(2,1)S(1)} %mix.6), channel_id=1, source_target_pairs={{0,2},{2,0},{1,3},{3,1},{4,6},{6,4},{5,7},{7,5},{8,10},{10,8},{9,1... | collective-permute-start | bytes 1572872 | tf_op jit(solution)/shard_map/ppermute | solution.py:179
  37.9 1.3 %collective-permute-start.4 = (bf16[2,64,1024]{2,1,0:T(8,128)(2,1)S(1)}, bf16[2,64,1024]{2,1,0:T(8,128)(2,1)S(1)}, u32[]{:S(2)}, u32[]{:S(2)}) collective-permute-start(bf16[2,64,1024]{2,1,0:T(8,128)(2,1)S(1)} %get-tuple-element.36), channel_id=1, source_target_pairs={{0,8},{2,10},{4,12},{6,14},{8,0},{10,2},{12,4},{14,6},{1,9},{3,11}... | collective-permute-start | bytes 786440 | tf_op jit(solution)/shard_map/ppermute | solution.py:184
  39.2 2.2 %collective-permute-start.5 = (bf16[2,64,1024]{2,1,0:T(8,128)(2,1)S(1)}, bf16[2,64,1024]{2,1,0:T(8,128)(2,1)S(1)}, u32[]{:S(2)}, u32[]{:S(2)}) collective-permute-start(bf16[2,64,1024]{2,1,0:T(8,128)(2,1)S(1)} %get-tuple-element.37), channel_id=1, source_target_pairs={{0,12},{2,14},{4,8},{6,10},{8,4},{10,6},{12,0},{14,2},{1,13},{3,15... | collective-permute-start | bytes 786440 | tf_op jit(solution)/shard_map/ppermute | solution.py:184
  42.0 2.8 %mix.7 = bf16[4,64,1024]{2,1,0:T(8,128)(2,1)S(1)} custom-call(bf16[2,64,1024]{2,1,0:T(8,128)(2,1)S(1)} %collective-permute-done.refs_0_, bf16[2,64,1024]{2,1,0:T(8,128)(2,1)S(1)} %collective-permute-done.1.refs_1_, bf16[2,64,1024]{2,1,0:T(8,128)(2,1)S(1)} %collective-permute-done.2.refs_2_, bf16[2,64,1024]{2,1,0:T(8,128)(2,1)S(1)} %collective-permute-done.3.refs_3_, ...), custom_call_target="tpu_custom_call" | custom-call | flops 10737418 | bytes 41943 | tf_op jit(solution)/shard_map/mix/pallas_call | solution.py:161
  45.4 4.1 %mix.8 = bf16[4,64,1536]{2,1,0:T(8,128)(2,1)S(1)} custom-call(bf16[2,64,1024]{2,1,0:T(8,128)(2,1)S(1)} %collective-permute-done.refs_0_, bf16[2,64,1024]{2,1,0:T(8,128)(2,1)S(1)} %collective-permute-done.1.refs_1_, bf16[2,64,1024]{2,1,0:T(8,128)(2,1)S(1)} %collective-permute-done.2.refs_2_, bf16[2,64,1024]{2,1,0:T(8,128)(2,1)S(1)} %collective-permute-done.3.refs_3_, ...), custom_call_target="tpu_custom_call" | custom-call | flops 16106127 | bytes 62914 | tf_op jit(solution)/shard_map/mix/pallas_call | solution.py:161
  49.5 8.5 %collective-permute-done.4.refs_0_ = bf16[2,64,1024]{2,1,0:T(8,128)(2,1)S(1)} collective-permute-done((bf16[2,64,1024]{2,1,0:T(8,128)(2,1)S(1)}, bf16[2,64,1024]{2,1,0:T(8,128)(2,1)S(1)}, u32[]{:S(2)}, u32[]{:S(2)}) %collective-permute-start.4) | collective-permute-done | bytes 262176 | tf_op jit(solution)/shard_map/ppermute | solution.py:184
  58.6 2.8 %mix.9 = bf16[4,64,1024]{2,1,0:T(8,128)(2,1)S(1)} custom-call(bf16[2,64,1024]{2,1,0:T(8,128)(2,1)S(1)} %collective-permute-done.4.refs_0_, bf16[2,64,1024]{2,1,0:T(8,128)(2,1)S(1)} %collective-permute-done.5.refs_1_, bf16[2,64,1024]{2,1,0:T(8,128)(2,1)S(1)} %get-tuple-element.45.refs_2_, bf16[2,64,1024]{2,1,0:T(8,128)(2,1)S(1)} %collective-permute-done.7.refs_3_, ...), custom_call_target="tpu_custom_call" | custom-call | flops 10737418 | bytes 41943 | tf_op jit(solution)/shard_map/mix/pallas_call | solution.py:161
  61.7 4.7 %collective-permute-start.10 = (bf16[2,64,1024]{2,1,0:T(8,128)(2,1)S(1)}, bf16[2,64,1024]{2,1,0:T(8,128)(2,1)S(1)}, u32[]{:S(2)}, u32[]{:S(2)}) collective-permute-start(bf16[2,64,1024]{2,1,0:T(8,128)(2,1)S(1)} %slice.43), channel_id=1, source_target_pairs={{0,4},{4,0},{8,12},{12,8},{1,5},{5,1},{9,13},{13,9},{2,6},{6,2},{1... | collective-permute-start | bytes 786440 | tf_op jit(solution)/shard_map/ppermute | solution.py:179
  66.4 2.8 %mix.10 = bf16[4,64,1024]{2,1,0:T(8,128)(2,1)S(1)} custom-call(bf16[2,64,1024]{2,1,0:T(8,128)(2,1)S(1)} %collective-permute-done.4.refs_0_, bf16[2,64,1024]{2,1,0:T(8,128)(2,1)S(1)} %collective-permute-done.5.refs_1_, bf16[2,64,1024]{2,1,0:T(8,128)(2,1)S(1)} %get-tuple-element.45.refs_2_, bf16[2,64,1024]{2,1,0:T(8,128)(2,1)S(1)} %collective-permute-done.7.refs_3_, ...), custom_call_target="tpu_custom_call" | custom-call | flops 10737418 | bytes 41943 | tf_op jit(solution)/shard_map/mix/pallas_call | solution.py:161
  69.3 4.1 %mix.11 = bf16[4,64,1536]{2,1,0:T(8,128)(2,1)S(1)} custom-call(bf16[2,64,1024]{2,1,0:T(8,128)(2,1)S(1)} %collective-permute-done.4.refs_0_, bf16[2,64,1024]{2,1,0:T(8,128)(2,1)S(1)} %collective-permute-done.5.refs_1_, bf16[2,64,1024]{2,1,0:T(8,128)(2,1)S(1)} %get-tuple-element.45.refs_2_, bf16[2,64,1024]{2,1,0:T(8,128)(2,1)S(1)} %collective-permute-done.7.refs_3_, ...), custom_call_target="tpu_custom_call" | custom-call | flops 16106127 | bytes 62914 | tf_op jit(solution)/shard_map/mix/pallas_call | solution.py:161
  73.9 3.8 %collective-permute-start.11 = (bf16[64,1024]{1,0:T(8,128)(2,1)S(1)}, bf16[64,1024]{1,0:T(8,128)(2,1)S(1)}, u32[]{:S(2)}, u32[]{:S(2)}) collective-permute-start(bf16[64,1024]{1,0:T(8,128)(2,1)S(1)} %fusion.7), channel_id=1, source_target_pairs={{0,8},{4,12},{8,0},{12,4},{1,9},{5,13},{9,1},{13,5},{2,10},{6,14},... | collective-permute-start | bytes 393224 | tf_op jit(solution)/shard_map/ppermute | solution.py:179
  79.0 6.8 %collective-permute-done.13 = bf16[2,64,1024]{2,1,0:T(8,128)(2,1)S(1)} collective-permute-done((bf16[2,64,1024]{2,1,0:T(8,128)(2,1)S(1)}, bf16[2,64,1024]{2,1,0:T(8,128)(2,1)S(1)}, u32[]{:S(2)}, u32[]{:S(2)}) %collective-permute-start.13) | collective-permute-done | bytes 262176 | tf_op jit(solution)/shard_map/ppermute | solution.py:179
  85.9 1.3 %collective-permute-start.14 = (bf16[64,1024]{1,0:T(8,128)(2,1)S(1)}, bf16[64,1024]{1,0:T(8,128)(2,1)S(1)}, u32[]{:S(2)}, u32[]{:S(2)}) collective-permute-start(bf16[64,1024]{1,0:T(8,128)(2,1)S(1)} %fusion.8), channel_id=1, source_target_pairs={{0,8},{4,12},{8,0},{12,4},{1,9},{5,13},{9,1},{13,5},{2,10},{6,14},... | collective-permute-start | bytes 393224 | tf_op jit(solution)/shard_map/ppermute | solution.py:179
  87.2 8.4 %collective-permute-done.15 = bf16[2,64,1536]{2,1,0:T(8,128)(2,1)S(1)} collective-permute-done((bf16[2,64,1536]{2,1,0:T(8,128)(2,1)S(1)}, bf16[2,64,1536]{2,1,0:T(8,128)(2,1)S(1)}, u32[]{:S(2)}, u32[]{:S(2)}) %collective-permute-start.15) | collective-permute-done | bytes 393248 | tf_op jit(solution)/shard_map/ppermute | solution.py:179
  95.7 1.5 %collective-permute-start.16 = (bf16[64,1536]{1,0:T(8,128)(2,1)S(1)}, bf16[64,1536]{1,0:T(8,128)(2,1)S(1)}, u32[]{:S(2)}, u32[]{:S(2)}) collective-permute-start(bf16[64,1536]{1,0:T(8,128)(2,1)S(1)} %fusion.6), channel_id=1, source_target_pairs={{0,8},{4,12},{8,0},{12,4},{1,9},{5,13},{9,1},{13,5},{2,10},{6,14},... | collective-permute-start | bytes 589832 | tf_op jit(solution)/shard_map/ppermute | solution.py:179
  97.3 9.1 %collective-permute-done.16 = bf16[64,1536]{1,0:T(8,128)(2,1)S(1)} collective-permute-done((bf16[64,1536]{1,0:T(8,128)(2,1)S(1)}, bf16[64,1536]{1,0:T(8,128)(2,1)S(1)}, u32[]{:S(2)}, u32[]{:S(2)}) %collective-permute-start.16) | collective-permute-done | bytes 196640 | tf_op jit(solution)/shard_map/ppermute | solution.py:179
  (47 shorter events, 7.8 us)
Async XLA Ops:
  0.0 11.2 %copy-start.2 = (bf16[64,8,1024]{2,1,0:T(8,128)(2,1)S(1)}, bf16[64,8,1024]{2,1,0:T(8,128)(2,1)}, u32[]{:S(2)}) copy-start(bf16[64,8,1024]{2,1,0:T(8,128)(2,1)} %param.4) | copy-start | bytes 3145732
  0.0 33.5 %collective-permute-start.6 = (bf16[1024,3584]{1,0:T(8,128)(2,1)}, bf16[1024,3584]{1,0:T(8,128)(2,1)}, u32[]{:S(2)}, u32[]{:S(2)}) collective-permute-start(bf16[1024,3584]{1,0:T(8,128)(2,1)} %bitcast.29), channel_id=1, source_target_pairs={{0,1},{1,0},{2,3},{3,2},{4,5},{5,4},{6,7},{7,6},{8,9},{9,8},{10,11... | collective-permute-start | bytes 22020104 | tf_op jit(solution)/shard_map/ppermute | solution.py:179
  3.5 23.4 %collective-permute-start = (bf16[2,64,1024]{2,1,0:T(8,128)(2,1)}, bf16[2,64,1024]{2,1,0:T(8,128)(2,1)S(1)}, u32[]{:S(2)}, u32[]{:S(2)}) collective-permute-start(bf16[2,64,1024]{2,1,0:T(8,128)(2,1)} %get-tuple-element.32), channel_id=1, source_target_pairs={{0,10},{2,8},{4,14},{6,12},{8,2},{10,0},{12,6},{14,4},{1,11},{3,9}... | collective-permute-start | bytes 786440 | tf_op jit(solution)/shard_map/ppermute | solution.py:184
  8.1 18.7 %collective-permute-start.1 = (bf16[2,64,1024]{2,1,0:T(8,128)(2,1)}, bf16[2,64,1024]{2,1,0:T(8,128)(2,1)S(1)}, u32[]{:S(2)}, u32[]{:S(2)}) collective-permute-start(bf16[2,64,1024]{2,1,0:T(8,128)(2,1)} %get-tuple-element.33), channel_id=1, source_target_pairs={{0,14},{2,12},{4,10},{6,8},{8,6},{10,4},{12,2},{14,0},{1,15},{3,13... | collective-permute-start | bytes 786440 | tf_op jit(solution)/shard_map/ppermute | solution.py:184
  9.5 24.0 %collective-permute-start.2 = (bf16[2,64,1024]{2,1,0:T(8,128)(2,1)}, bf16[2,64,1024]{2,1,0:T(8,128)(2,1)S(1)}, u32[]{:S(2)}, u32[]{:S(2)}) collective-permute-start(bf16[2,64,1024]{2,1,0:T(8,128)(2,1)} %get-tuple-element.34), channel_id=1, source_target_pairs={{0,2},{2,0},{4,6},{6,4},{8,10},{10,8},{12,14},{14,12},{1,3},{3,1},... | collective-permute-start | bytes 786440 | tf_op jit(solution)/shard_map/ppermute | solution.py:184
  10.9 22.5 %collective-permute-start.3 = (bf16[2,64,1024]{2,1,0:T(8,128)(2,1)}, bf16[2,64,1024]{2,1,0:T(8,128)(2,1)S(1)}, u32[]{:S(2)}, u32[]{:S(2)}) collective-permute-start(bf16[2,64,1024]{2,1,0:T(8,128)(2,1)} %get-tuple-element.35), channel_id=1, source_target_pairs={{0,6},{2,4},{4,2},{6,0},{8,14},{10,12},{12,10},{14,8},{1,7},{3,5},... | collective-permute-start | bytes 786440 | tf_op jit(solution)/shard_map/ppermute | solution.py:184
  11.2 3.1 %copy-start = (bf16[1,1024,3584]{2,1,0:T(8,128)(2,1)S(1)}, bf16[1,1024,3584]{2,1,0:T(8,128)(2,1)}, u32[]{:S(2)}) copy-start(bf16[1,1024,3584]{2,1,0:T(8,128)(2,1)} %param.7) | copy-start | bytes 22020100
  14.3 0.7 copy-start.3
  14.9 0.7 copy-start.4
  15.6 17.9 %copy-start.1 = (bf16[1,1024,3584]{2,1,0:T(8,128)(2,1)S(1)}, bf16[1,1024,3584]{2,1,0:T(8,128)(2,1)}, u32[]{:S(2)}) copy-start(bf16[1,1024,3584]{2,1,0:T(8,128)(2,1)} %param.7) | copy-start | bytes 22020100
  36.3 25.1 %collective-permute-start.8 = (bf16[4,64,1024]{2,1,0:T(8,128)(2,1)S(1)}, bf16[4,64,1024]{2,1,0:T(8,128)(2,1)S(1)}, u32[]{:S(2)}, u32[]{:S(2)}) collective-permute-start(bf16[4,64,1024]{2,1,0:T(8,128)(2,1)S(1)} %mix.6), channel_id=1, source_target_pairs={{0,2},{2,0},{1,3},{3,1},{4,6},{6,4},{5,7},{7,5},{8,10},{10,8},{9,1... | collective-permute-start | bytes 1572872 | tf_op jit(solution)/shard_map/ppermute | solution.py:179
  37.9 20.1 %collective-permute-start.4 = (bf16[2,64,1024]{2,1,0:T(8,128)(2,1)S(1)}, bf16[2,64,1024]{2,1,0:T(8,128)(2,1)S(1)}, u32[]{:S(2)}, u32[]{:S(2)}) collective-permute-start(bf16[2,64,1024]{2,1,0:T(8,128)(2,1)S(1)} %get-tuple-element.36), channel_id=1, source_target_pairs={{0,8},{2,10},{4,12},{6,14},{8,0},{10,2},{12,4},{14,6},{1,9},{3,11}... | collective-permute-start | bytes 786440 | tf_op jit(solution)/shard_map/ppermute | solution.py:184
  39.2 19.3 %collective-permute-start.5 = (bf16[2,64,1024]{2,1,0:T(8,128)(2,1)S(1)}, bf16[2,64,1024]{2,1,0:T(8,128)(2,1)S(1)}, u32[]{:S(2)}, u32[]{:S(2)}) collective-permute-start(bf16[2,64,1024]{2,1,0:T(8,128)(2,1)S(1)} %get-tuple-element.37), channel_id=1, source_target_pairs={{0,12},{2,14},{4,8},{6,10},{8,4},{10,6},{12,0},{14,2},{1,13},{3,15... | collective-permute-start | bytes 786440 | tf_op jit(solution)/shard_map/ppermute | solution.py:184
  41.4 17.2 %collective-permute-start.7 = (bf16[2,64,1024]{2,1,0:T(8,128)(2,1)S(1)}, bf16[2,64,1024]{2,1,0:T(8,128)(2,1)S(1)}, u32[]{:S(2)}, u32[]{:S(2)}) collective-permute-start(bf16[2,64,1024]{2,1,0:T(8,128)(2,1)S(1)} %get-tuple-element.39), channel_id=1, source_target_pairs={{0,4},{2,6},{4,0},{6,2},{8,12},{10,14},{12,8},{14,10},{1,5},{3,7},... | collective-permute-start | bytes 786440 | tf_op jit(solution)/shard_map/ppermute | solution.py:184
  44.8 28.6 %collective-permute-start.9 = (bf16[4,64,1024]{2,1,0:T(8,128)(2,1)S(1)}, bf16[4,64,1024]{2,1,0:T(8,128)(2,1)S(1)}, u32[]{:S(2)}, u32[]{:S(2)}) collective-permute-start(bf16[4,64,1024]{2,1,0:T(8,128)(2,1)S(1)} %mix.7), channel_id=1, source_target_pairs={{0,2},{2,0},{1,3},{3,1},{4,6},{6,4},{5,7},{7,5},{8,10},{10,8},{9,1... | collective-permute-start | bytes 1572872 | tf_op jit(solution)/shard_map/ppermute | solution.py:179
  58.0 19.7 %collective-permute-start.12 = (bf16[4,64,1536]{2,1,0:T(8,128)(2,1)S(1)}, bf16[4,64,1536]{2,1,0:T(8,128)(2,1)S(1)}, u32[]{:S(2)}, u32[]{:S(2)}) collective-permute-start(bf16[4,64,1536]{2,1,0:T(8,128)(2,1)S(1)} %mix.8), channel_id=1, source_target_pairs={{0,2},{2,0},{1,3},{3,1},{4,6},{6,4},{5,7},{7,5},{8,10},{10,8},{9,1... | collective-permute-start | bytes 2359304 | tf_op jit(solution)/shard_map/ppermute | solution.py:179
  61.7 12.1 %collective-permute-start.10 = (bf16[2,64,1024]{2,1,0:T(8,128)(2,1)S(1)}, bf16[2,64,1024]{2,1,0:T(8,128)(2,1)S(1)}, u32[]{:S(2)}, u32[]{:S(2)}) collective-permute-start(bf16[2,64,1024]{2,1,0:T(8,128)(2,1)S(1)} %slice.43), channel_id=1, source_target_pairs={{0,4},{4,0},{8,12},{12,8},{1,5},{5,1},{9,13},{13,9},{2,6},{6,2},{1... | collective-permute-start | bytes 786440 | tf_op jit(solution)/shard_map/ppermute | solution.py:179
  73.7 12.1 %collective-permute-start.13 = (bf16[2,64,1024]{2,1,0:T(8,128)(2,1)S(1)}, bf16[2,64,1024]{2,1,0:T(8,128)(2,1)S(1)}, u32[]{:S(2)}, u32[]{:S(2)}) collective-permute-start(bf16[2,64,1024]{2,1,0:T(8,128)(2,1)S(1)} %slice.47), channel_id=1, source_target_pairs={{0,4},{4,0},{8,12},{12,8},{1,5},{5,1},{9,13},{13,9},{2,6},{6,2},{1... | collective-permute-start | bytes 786440 | tf_op jit(solution)/shard_map/ppermute | solution.py:179
  73.9 13.3 %collective-permute-start.11 = (bf16[64,1024]{1,0:T(8,128)(2,1)S(1)}, bf16[64,1024]{1,0:T(8,128)(2,1)S(1)}, u32[]{:S(2)}, u32[]{:S(2)}) collective-permute-start(bf16[64,1024]{1,0:T(8,128)(2,1)S(1)} %fusion.7), channel_id=1, source_target_pairs={{0,8},{4,12},{8,0},{12,4},{1,9},{5,13},{9,1},{13,5},{2,10},{6,14},... | collective-permute-start | bytes 393224 | tf_op jit(solution)/shard_map/ppermute | solution.py:179
  78.1 17.5 %collective-permute-start.15 = (bf16[2,64,1536]{2,1,0:T(8,128)(2,1)S(1)}, bf16[2,64,1536]{2,1,0:T(8,128)(2,1)S(1)}, u32[]{:S(2)}, u32[]{:S(2)}) collective-permute-start(bf16[2,64,1536]{2,1,0:T(8,128)(2,1)S(1)} %slice.51), channel_id=1, source_target_pairs={{0,4},{4,0},{8,12},{12,8},{1,5},{5,1},{9,13},{13,9},{2,6},{6,2},{1... | collective-permute-start | bytes 1179656 | tf_op jit(solution)/shard_map/ppermute | solution.py:179
  85.9 11.3 %collective-permute-start.14 = (bf16[64,1024]{1,0:T(8,128)(2,1)S(1)}, bf16[64,1024]{1,0:T(8,128)(2,1)S(1)}, u32[]{:S(2)}, u32[]{:S(2)}) collective-permute-start(bf16[64,1024]{1,0:T(8,128)(2,1)S(1)} %fusion.8), channel_id=1, source_target_pairs={{0,8},{4,12},{8,0},{12,4},{1,9},{5,13},{9,1},{13,5},{2,10},{6,14},... | collective-permute-start | bytes 393224 | tf_op jit(solution)/shard_map/ppermute | solution.py:179
  95.7 10.6 %collective-permute-start.16 = (bf16[64,1536]{1,0:T(8,128)(2,1)S(1)}, bf16[64,1536]{1,0:T(8,128)(2,1)S(1)}, u32[]{:S(2)}, u32[]{:S(2)}) collective-permute-start(bf16[64,1536]{1,0:T(8,128)(2,1)S(1)} %fusion.6), channel_id=1, source_target_pairs={{0,8},{4,12},{8,0},{12,4},{1,9},{5,13},{9,1},{13,5},{2,10},{6,14},... | collective-permute-start | bytes 589832 | tf_op jit(solution)/shard_map/ppermute | solution.py:179

commit v14 on v12

--- a/solution.py
+++ b/solution.py
@@ -237,8 +237,8 @@
     last = mix_even((0,), last, LIGHT)
     last = add_x(0, last)
     last = mix_even((1,), last, LIGHT)
+    last = add_x(1, last)
     last = mix_even((2,), last, LIGHT)
-    last = add_x(1, last)
     last = add_z(0, last)
     last = add_x(2, last)
     last = add_z(1, last)

time: 106 us -> 106 us (level)
  no operation moved by 1% of the time
where the time goes in v14:
time: 106 us; the launch traced here: 105 us
  waiting for transfers between devices  54 us (51%)
  Pallas kernels  23.4 us (22%)
  starting transfers between devices  21.2 us (20%)
  local copies, waits for them, and re-layouts  4.71 us (4%)
  other arithmetic  1.78 us (2%)
    ppermute x7, waiting for transfers between devices, send_to_chip(): lax.ppermute(block, ('z', 'x'), [(i, i ^ relative) for i in range(sizes[0...  28.3 us
    ppermute x10, waiting for transfers between devices, swap(): lax.ppermute(block, axis, [(i, i ^ distance) for i in range(lax.axis_size...  25.7 us
    pallas_call x6, Pallas kernels, mix(): pl.pallas_call(mix_kernel, grid=(width // TILE,), in_specs=[whole] * len(...  19.6 us
    ppermute x7, starting transfers between devices, send_to_chip(): lax.ppermute(block, ('z', 'x'), [(i, i ^ relative) for i in range(sizes[0...  12.9 us
    ppermute x10, starting transfers between devices, swap(): lax.ppermute(block, axis, [(i, i ^ distance) for i in range(lax.axis_size...  8.36 us
    unnamed x10, local copies, waits for them, and re-layouts  4.46 us
    pallas_call x2, Pallas kernels, spread_rows(): pl.pallas_call(functools.partial(spread_kernel if more else fetching_kern...  3.89 us
  transfers between devices with their start and end apart: 17, of which 7 were waited for; matrix products, arithmetic and copies ran while one was open for 1% of the time, Pallas kernels for 20%

profile of v14, /device:TPU:0, one launch (start us, length us, event | category | flops | bytes accessed | tf_op | source)
XLA Modules:
  0.0 105.5 jit_solution(15906566051413752096)
XLA Ops:
  0.5 3.0 %spread_rows.3 = (bf16[2,64,1024]{2,1,0:T(8,128)(2,1)}, bf16[2,64,1024]{2,1,0:T(8,128)(2,1)}, bf16[2,64,1024]{2,1,0:T(8,128)(2,1)}, bf16[2,64,1024]{2,1,0:T(8,128)(2,1)}) custom-call(s32[1]{0:T(128)} %bitcast.own_ref, s32[8,64]{1,0:T(8,128)} %bitcast.39, f32[8,64]{1,0:T(8,128)} %bitcast.41, bf16[512,1024]{1,0:T(8,128)(2,1)} %bitcast.37), custom_call_target="tpu_custom_call" | custom-call | tf_op jit(solution)/shard_map/spread_rows/pallas_call | solution.py:125
  3.5 5.7 %collective-permute-start = (bf16[2,64,1024]{2,1,0:T(8,128)(2,1)}, bf16[2,64,1024]{2,1,0:T(8,128)(2,1)S(1)}, u32[]{:S(2)}, u32[]{:S(2)}) collective-permute-start(bf16[2,64,1024]{2,1,0:T(8,128)(2,1)} %get-tuple-element.31), channel_id=1, source_target_pairs={{0,14},{2,12},{4,10},{6,8},{8,6},{10,4},{12,2},{14,0},{1,15},{3,13... | collective-permute-start | bytes 786440 | tf_op jit(solution)/shard_map/ppermute | solution.py:184
  9.1 1.7 %collective-permute-start.2 = (bf16[2,64,1024]{2,1,0:T(8,128)(2,1)}, bf16[2,64,1024]{2,1,0:T(8,128)(2,1)S(1)}, u32[]{:S(2)}, u32[]{:S(2)}) collective-permute-start(bf16[2,64,1024]{2,1,0:T(8,128)(2,1)} %get-tuple-element.33), channel_id=1, source_target_pairs={{0,6},{2,4},{4,2},{6,0},{8,14},{10,12},{12,10},{14,8},{1,7},{3,5},... | collective-permute-start | bytes 786440 | tf_op jit(solution)/shard_map/ppermute | solution.py:184
  11.3 3.1 %copy-done = bf16[1,1024,3584]{2,1,0:T(8,128)(2,1)S(1)} copy-done((bf16[1,1024,3584]{2,1,0:T(8,128)(2,1)S(1)}, bf16[1,1024,3584]{2,1,0:T(8,128)(2,1)}, u32[]{:S(2)}) %copy-start) | copy-done | bytes 7340056
  14.3 0.7 copy-done.3
  15.7 0.9 spread_rows.2
  16.8 17.7 %collective-permute-done.1.refs_1_ = bf16[2,64,1024]{2,1,0:T(8,128)(2,1)S(1)} collective-permute-done((bf16[2,64,1024]{2,1,0:T(8,128)(2,1)}, bf16[2,64,1024]{2,1,0:T(8,128)(2,1)S(1)}, u32[]{:S(2)}, u32[]{:S(2)}) %collective-permute-start.1) | collective-permute-done | bytes 262176 | tf_op jit(solution)/shard_map/ppermute | solution.py:184
  34.5 2.8 %mix.6 = bf16[4,64,1024]{2,1,0:T(8,128)(2,1)S(1)} custom-call(bf16[2,64,1024]{2,1,0:T(8,128)(2,1)S(1)} %collective-permute-done.refs_0_, bf16[2,64,1024]{2,1,0:T(8,128)(2,1)S(1)} %collective-permute-done.1.refs_1_, bf16[2,64,1024]{2,1,0:T(8,128)(2,1)S(1)} %collective-permute-done.2.refs_2_, bf16[2,64,1024]{2,1,0:T(8,128)(2,1)S(1)} %collective-permute-done.3.refs_3_, ...), custom_call_target="tpu_custom_call" | custom-call | flops 10737418 | bytes 41943 | tf_op jit(solution)/shard_map/mix/pallas_call | solution.py:161
  37.4 1.5 %collective-permute-start.8 = (bf16[4,64,1024]{2,1,0:T(8,128)(2,1)S(1)}, bf16[4,64,1024]{2,1,0:T(8,128)(2,1)S(1)}, u32[]{:S(2)}, u32[]{:S(2)}) collective-permute-start(bf16[4,64,1024]{2,1,0:T(8,128)(2,1)S(1)} %mix.6), channel_id=1, source_target_pairs={{0,2},{2,0},{1,3},{3,1},{4,6},{6,4},{5,7},{7,5},{8,10},{10,8},{9,1... | collective-permute-start | bytes 1572872 | tf_op jit(solution)/shard_map/ppermute | solution.py:179
  38.8 4.5 %collective-permute-start.4 = (bf16[2,64,1024]{2,1,0:T(8,128)(2,1)S(1)}, bf16[2,64,1024]{2,1,0:T(8,128)(2,1)S(1)}, u32[]{:S(2)}, u32[]{:S(2)}) collective-permute-start(bf16[2,64,1024]{2,1,0:T(8,128)(2,1)S(1)} %get-tuple-element.35), channel_id=1, source_target_pairs={{0,12},{2,14},{4,8},{6,10},{8,4},{10,6},{12,0},{14,2},{1,13},{3,15... | collective-permute-start | bytes 786440 | tf_op jit(solution)/shard_map/ppermute | solution.py:184
  43.9 2.8 %mix.7 = bf16[4,64,1024]{2,1,0:T(8,128)(2,1)S(1)} custom-call(bf16[2,64,1024]{2,1,0:T(8,128)(2,1)S(1)} %collective-permute-done.refs_0_, bf16[2,64,1024]{2,1,0:T(8,128)(2,1)S(1)} %collective-permute-done.1.refs_1_, bf16[2,64,1024]{2,1,0:T(8,128)(2,1)S(1)} %collective-permute-done.2.refs_2_, bf16[2,64,1024]{2,1,0:T(8,128)(2,1)S(1)} %collective-permute-done.3.refs_3_, ...), custom_call_target="tpu_custom_call" | custom-call | flops 10737418 | bytes 41943 | tf_op jit(solution)/shard_map/mix/pallas_call | solution.py:161
  47.3 4.1 %mix.8 = bf16[4,64,1536]{2,1,0:T(8,128)(2,1)S(1)} custom-call(bf16[2,64,1024]{2,1,0:T(8,128)(2,1)S(1)} %collective-permute-done.refs_0_, bf16[2,64,1024]{2,1,0:T(8,128)(2,1)S(1)} %collective-permute-done.1.refs_1_, bf16[2,64,1024]{2,1,0:T(8,128)(2,1)S(1)} %collective-permute-done.2.refs_2_, bf16[2,64,1024]{2,1,0:T(8,128)(2,1)S(1)} %collective-permute-done.3.refs_3_, ...), custom_call_target="tpu_custom_call" | custom-call | flops 16106127 | bytes 62914 | tf_op jit(solution)/shard_map/mix/pallas_call | solution.py:161
  51.4 1.7 %collective-permute-start.12 = (bf16[4,64,1536]{2,1,0:T(8,128)(2,1)S(1)}, bf16[4,64,1536]{2,1,0:T(8,128)(2,1)S(1)}, u32[]{:S(2)}, u32[]{:S(2)}) collective-permute-start(bf16[4,64,1536]{2,1,0:T(8,128)(2,1)S(1)} %mix.8), channel_id=1, source_target_pairs={{0,2},{2,0},{1,3},{3,1},{4,6},{6,4},{5,7},{7,5},{8,10},{10,8},{9,1... | collective-permute-start | bytes 2359304 | tf_op jit(solution)/shard_map/ppermute | solution.py:179
  53.0 10.4 %collective-permute-done.5.refs_1_ = bf16[2,64,1024]{2,1,0:T(8,128)(2,1)S(1)} collective-permute-done((bf16[2,64,1024]{2,1,0:T(8,128)(2,1)S(1)}, bf16[2,64,1024]{2,1,0:T(8,128)(2,1)S(1)}, u32[]{:S(2)}, u32[]{:S(2)}) %collective-permute-start.5) | collective-permute-done | bytes 262176 | tf_op jit(solution)/shard_map/ppermute | solution.py:184
  63.5 2.8 %mix.9 = bf16[4,64,1024]{2,1,0:T(8,128)(2,1)S(1)} custom-call(bf16[2,64,1024]{2,1,0:T(8,128)(2,1)S(1)} %collective-permute-done.4.refs_0_, bf16[2,64,1024]{2,1,0:T(8,128)(2,1)S(1)} %collective-permute-done.5.refs_1_, bf16[2,64,1024]{2,1,0:T(8,128)(2,1)S(1)} %collective-permute-done.6.refs_2_, bf16[2,64,1024]{2,1,0:T(8,128)(2,1)S(1)} %get-tuple-element.44.refs_3_, ...), custom_call_target="tpu_custom_call" | custom-call | flops 10737418 | bytes 41943 | tf_op jit(solution)/shard_map/mix/pallas_call | solution.py:161
  66.7 2.8 %mix.10 = bf16[4,64,1024]{2,1,0:T(8,128)(2,1)S(1)} custom-call(bf16[2,64,1024]{2,1,0:T(8,128)(2,1)S(1)} %collective-permute-done.4.refs_0_, bf16[2,64,1024]{2,1,0:T(8,128)(2,1)S(1)} %collective-permute-done.5.refs_1_, bf16[2,64,1024]{2,1,0:T(8,128)(2,1)S(1)} %collective-permute-done.6.refs_2_, bf16[2,64,1024]{2,1,0:T(8,128)(2,1)S(1)} %get-tuple-element.44.refs_3_, ...), custom_call_target="tpu_custom_call" | custom-call | flops 10737418 | bytes 41943 | tf_op jit(solution)/shard_map/mix/pallas_call | solution.py:161
  69.8 4.1 %mix.11 = bf16[4,64,1536]{2,1,0:T(8,128)(2,1)S(1)} custom-call(bf16[2,64,1024]{2,1,0:T(8,128)(2,1)S(1)} %collective-permute-done.4.refs_0_, bf16[2,64,1024]{2,1,0:T(8,128)(2,1)S(1)} %collective-permute-done.5.refs_1_, bf16[2,64,1024]{2,1,0:T(8,128)(2,1)S(1)} %collective-permute-done.6.refs_2_, bf16[2,64,1024]{2,1,0:T(8,128)(2,1)S(1)} %get-tuple-element.44.refs_3_, ...), custom_call_target="tpu_custom_call" | custom-call | flops 16106127 | bytes 62914 | tf_op jit(solution)/shard_map/mix/pallas_call | solution.py:161
  74.0 2.1 %collective-permute-start.13 = (bf16[2,64,1024]{2,1,0:T(8,128)(2,1)S(1)}, bf16[2,64,1024]{2,1,0:T(8,128)(2,1)S(1)}, u32[]{:S(2)}, u32[]{:S(2)}) collective-permute-start(bf16[2,64,1024]{2,1,0:T(8,128)(2,1)S(1)} %slice.47), channel_id=1, source_target_pairs={{0,4},{4,0},{8,12},{12,8},{1,5},{5,1},{9,13},{13,9},{2,6},{6,2},{1... | collective-permute-start | bytes 786440 | tf_op jit(solution)/shard_map/ppermute | solution.py:179
  76.2 2.8 %collective-permute-done.12 = bf16[4,64,1536]{2,1,0:T(8,128)(2,1)S(1)} collective-permute-done((bf16[4,64,1536]{2,1,0:T(8,128)(2,1)S(1)}, bf16[4,64,1536]{2,1,0:T(8,128)(2,1)S(1)}, u32[]{:S(2)}, u32[]{:S(2)}) %collective-permute-start.12) | collective-permute-done | bytes 786464 | tf_op jit(solution)/shard_map/ppermute | solution.py:179
  79.4 1.8 %collective-permute-start.15 = (bf16[2,64,1536]{2,1,0:T(8,128)(2,1)S(1)}, bf16[2,64,1536]{2,1,0:T(8,128)(2,1)S(1)}, u32[]{:S(2)}, u32[]{:S(2)}) collective-permute-start(bf16[2,64,1536]{2,1,0:T(8,128)(2,1)S(1)} %slice.51), channel_id=1, source_target_pairs={{0,4},{4,0},{8,12},{12,8},{1,5},{5,1},{9,13},{13,9},{2,6},{6,2},{1... | collective-permute-start | bytes 1179656 | tf_op jit(solution)/shard_map/ppermute | solution.py:179
  81.2 3.9 %collective-permute-done.13 = bf16[2,64,1024]{2,1,0:T(8,128)(2,1)S(1)} collective-permute-done((bf16[2,64,1024]{2,1,0:T(8,128)(2,1)S(1)}, bf16[2,64,1024]{2,1,0:T(8,128)(2,1)S(1)}, u32[]{:S(2)}, u32[]{:S(2)}) %collective-permute-start.13) | collective-permute-done | bytes 262176 | tf_op jit(solution)/shard_map/ppermute | solution.py:179
  85.3 9.3 %collective-permute-done.15 = bf16[2,64,1536]{2,1,0:T(8,128)(2,1)S(1)} collective-permute-done((bf16[2,64,1536]{2,1,0:T(8,128)(2,1)S(1)}, bf16[2,64,1536]{2,1,0:T(8,128)(2,1)S(1)}, u32[]{:S(2)}, u32[]{:S(2)}) %collective-permute-start.15) | collective-permute-done | bytes 393248 | tf_op jit(solution)/shard_map/ppermute | solution.py:179
  94.9 9.8 %collective-permute-done.16 = bf16[64,1536]{1,0:T(8,128)(2,1)S(1)} collective-permute-done((bf16[64,1536]{1,0:T(8,128)(2,1)S(1)}, bf16[64,1536]{1,0:T(8,128)(2,1)S(1)}, u32[]{:S(2)}, u32[]{:S(2)}) %collective-permute-start.16) | collective-permute-done | bytes 196640 | tf_op jit(solution)/shard_map/ppermute | solution.py:179
  104.7 0.8 pad_maximum_fusion
  (47 shorter events, 4.4 us)
Async XLA Ops:
  0.0 11.3 %copy-start.2 = (bf16[64,8,1024]{2,1,0:T(8,128)(2,1)S(1)}, bf16[64,8,1024]{2,1,0:T(8,128)(2,1)}, u32[]{:S(2)}) copy-start(bf16[64,8,1024]{2,1,0:T(8,128)(2,1)} %param.4) | copy-start | bytes 3145732
  0.0 34.5 %collective-permute-start.7 = (bf16[1024,3584]{1,0:T(8,128)(2,1)}, bf16[1024,3584]{1,0:T(8,128)(2,1)}, u32[]{:S(2)}, u32[]{:S(2)}) collective-permute-start(bf16[1024,3584]{1,0:T(8,128)(2,1)} %bitcast.29), channel_id=1, source_target_pairs={{0,1},{1,0},{2,3},{3,2},{4,5},{5,4},{6,7},{7,6},{8,9},{9,8},{10,11... | collective-permute-start | bytes 22020104 | tf_op jit(solution)/shard_map/ppermute | solution.py:179
  3.5 13.3 %collective-permute-start = (bf16[2,64,1024]{2,1,0:T(8,128)(2,1)}, bf16[2,64,1024]{2,1,0:T(8,128)(2,1)S(1)}, u32[]{:S(2)}, u32[]{:S(2)}) collective-permute-start(bf16[2,64,1024]{2,1,0:T(8,128)(2,1)} %get-tuple-element.31), channel_id=1, source_target_pairs={{0,14},{2,12},{4,10},{6,8},{8,6},{10,4},{12,2},{14,0},{1,15},{3,13... | collective-permute-start | bytes 786440 | tf_op jit(solution)/shard_map/ppermute | solution.py:184
  9.1 25.3 %collective-permute-start.1 = (bf16[2,64,1024]{2,1,0:T(8,128)(2,1)}, bf16[2,64,1024]{2,1,0:T(8,128)(2,1)S(1)}, u32[]{:S(2)}, u32[]{:S(2)}) collective-permute-start(bf16[2,64,1024]{2,1,0:T(8,128)(2,1)} %get-tuple-element.32), channel_id=1, source_target_pairs={{0,10},{2,8},{4,14},{6,12},{8,2},{10,0},{12,6},{14,4},{1,11},{3,9}... | collective-permute-start | bytes 786440 | tf_op jit(solution)/shard_map/ppermute | solution.py:184
  9.1 25.3 %collective-permute-start.2 = (bf16[2,64,1024]{2,1,0:T(8,128)(2,1)}, bf16[2,64,1024]{2,1,0:T(8,128)(2,1)S(1)}, u32[]{:S(2)}, u32[]{:S(2)}) collective-permute-start(bf16[2,64,1024]{2,1,0:T(8,128)(2,1)} %get-tuple-element.33), channel_id=1, source_target_pairs={{0,6},{2,4},{4,2},{6,0},{8,14},{10,12},{12,10},{14,8},{1,7},{3,5},... | collective-permute-start | bytes 786440 | tf_op jit(solution)/shard_map/ppermute | solution.py:184
  10.8 23.7 %collective-permute-start.3 = (bf16[2,64,1024]{2,1,0:T(8,128)(2,1)}, bf16[2,64,1024]{2,1,0:T(8,128)(2,1)S(1)}, u32[]{:S(2)}, u32[]{:S(2)}) collective-permute-start(bf16[2,64,1024]{2,1,0:T(8,128)(2,1)} %get-tuple-element.34), channel_id=1, source_target_pairs={{0,2},{2,0},{4,6},{6,4},{8,10},{10,8},{12,14},{14,12},{1,3},{3,1},... | collective-permute-start | bytes 786440 | tf_op jit(solution)/shard_map/ppermute | solution.py:184
  11.3 3.1 %copy-start = (bf16[1,1024,3584]{2,1,0:T(8,128)(2,1)S(1)}, bf16[1,1024,3584]{2,1,0:T(8,128)(2,1)}, u32[]{:S(2)}) copy-start(bf16[1,1024,3584]{2,1,0:T(8,128)(2,1)} %param.7) | copy-start | bytes 22020100
  14.3 0.7 copy-start.3
  15.0 0.7 copy-start.4
  15.7 18.8 %copy-start.1 = (bf16[1,1024,3584]{2,1,0:T(8,128)(2,1)S(1)}, bf16[1,1024,3584]{2,1,0:T(8,128)(2,1)}, u32[]{:S(2)}) copy-start(bf16[1,1024,3584]{2,1,0:T(8,128)(2,1)} %param.7) | copy-start | bytes 22020100
  37.4 29.0 %collective-permute-start.8 = (bf16[4,64,1024]{2,1,0:T(8,128)(2,1)S(1)}, bf16[4,64,1024]{2,1,0:T(8,128)(2,1)S(1)}, u32[]{:S(2)}, u32[]{:S(2)}) collective-permute-start(bf16[4,64,1024]{2,1,0:T(8,128)(2,1)S(1)} %mix.6), channel_id=1, source_target_pairs={{0,2},{2,0},{1,3},{3,1},{4,6},{6,4},{5,7},{7,5},{8,10},{10,8},{9,1... | collective-permute-start | bytes 1572872 | tf_op jit(solution)/shard_map/ppermute | solution.py:179
  38.8 12.5 %collective-permute-start.4 = (bf16[2,64,1024]{2,1,0:T(8,128)(2,1)S(1)}, bf16[2,64,1024]{2,1,0:T(8,128)(2,1)S(1)}, u32[]{:S(2)}, u32[]{:S(2)}) collective-permute-start(bf16[2,64,1024]{2,1,0:T(8,128)(2,1)S(1)} %get-tuple-element.35), channel_id=1, source_target_pairs={{0,12},{2,14},{4,8},{6,10},{8,4},{10,6},{12,0},{14,2},{1,13},{3,15... | collective-permute-start | bytes 786440 | tf_op jit(solution)/shard_map/ppermute | solution.py:184
  43.4 20.1 %collective-permute-start.5 = (bf16[2,64,1024]{2,1,0:T(8,128)(2,1)S(1)}, bf16[2,64,1024]{2,1,0:T(8,128)(2,1)S(1)}, u32[]{:S(2)}, u32[]{:S(2)}) collective-permute-start(bf16[2,64,1024]{2,1,0:T(8,128)(2,1)S(1)} %get-tuple-element.36), channel_id=1, source_target_pairs={{0,8},{2,10},{4,12},{6,14},{8,0},{10,2},{12,4},{14,6},{1,9},{3,11}... | collective-permute-start | bytes 786440 | tf_op jit(solution)/shard_map/ppermute | solution.py:184
  43.4 20.1 %collective-permute-start.6 = (bf16[2,64,1024]{2,1,0:T(8,128)(2,1)S(1)}, bf16[2,64,1024]{2,1,0:T(8,128)(2,1)S(1)}, u32[]{:S(2)}, u32[]{:S(2)}) collective-permute-start(bf16[2,64,1024]{2,1,0:T(8,128)(2,1)S(1)} %get-tuple-element.37), channel_id=1, source_target_pairs={{0,4},{2,6},{4,0},{6,2},{8,12},{10,14},{12,8},{14,10},{1,5},{3,7},... | collective-permute-start | bytes 786440 | tf_op jit(solution)/shard_map/ppermute | solution.py:184
  46.8 22.8 %collective-permute-start.9 = (bf16[4,64,1024]{2,1,0:T(8,128)(2,1)S(1)}, bf16[4,64,1024]{2,1,0:T(8,128)(2,1)S(1)}, u32[]{:S(2)}, u32[]{:S(2)}) collective-permute-start(bf16[4,64,1024]{2,1,0:T(8,128)(2,1)S(1)} %mix.7), channel_id=1, source_target_pairs={{0,2},{2,0},{1,3},{3,1},{4,6},{6,4},{5,7},{7,5},{8,10},{10,8},{9,1... | collective-permute-start | bytes 1572872 | tf_op jit(solution)/shard_map/ppermute | solution.py:179
  51.4 27.6 %collective-permute-start.12 = (bf16[4,64,1536]{2,1,0:T(8,128)(2,1)S(1)}, bf16[4,64,1536]{2,1,0:T(8,128)(2,1)S(1)}, u32[]{:S(2)}, u32[]{:S(2)}) collective-permute-start(bf16[4,64,1536]{2,1,0:T(8,128)(2,1)S(1)} %mix.8), channel_id=1, source_target_pairs={{0,2},{2,0},{1,3},{3,1},{4,6},{6,4},{5,7},{7,5},{8,10},{10,8},{9,1... | collective-permute-start | bytes 2359304 | tf_op jit(solution)/shard_map/ppermute | solution.py:179
  66.6 9.4 %collective-permute-start.10 = (bf16[2,64,1024]{2,1,0:T(8,128)(2,1)S(1)}, bf16[2,64,1024]{2,1,0:T(8,128)(2,1)S(1)}, u32[]{:S(2)}, u32[]{:S(2)}) collective-permute-start(bf16[2,64,1024]{2,1,0:T(8,128)(2,1)S(1)} %slice.43), channel_id=1, source_target_pairs={{0,4},{4,0},{8,12},{12,8},{1,5},{5,1},{9,13},{13,9},{2,6},{6,2},{1... | collective-permute-start | bytes 786440 | tf_op jit(solution)/shard_map/ppermute | solution.py:179
  74.0 11.1 %collective-permute-start.13 = (bf16[2,64,1024]{2,1,0:T(8,128)(2,1)S(1)}, bf16[2,64,1024]{2,1,0:T(8,128)(2,1)S(1)}, u32[]{:S(2)}, u32[]{:S(2)}) collective-permute-start(bf16[2,64,1024]{2,1,0:T(8,128)(2,1)S(1)} %slice.47), channel_id=1, source_target_pairs={{0,4},{4,0},{8,12},{12,8},{1,5},{5,1},{9,13},{13,9},{2,6},{6,2},{1... | collective-permute-start | bytes 786440 | tf_op jit(solution)/shard_map/ppermute | solution.py:179
  76.1 9.1 %collective-permute-start.11 = (bf16[64,1024]{1,0:T(8,128)(2,1)S(1)}, bf16[64,1024]{1,0:T(8,128)(2,1)S(1)}, u32[]{:S(2)}, u32[]{:S(2)}) collective-permute-start(bf16[64,1024]{1,0:T(8,128)(2,1)S(1)} %fusion.7), channel_id=1, source_target_pairs={{0,8},{4,12},{8,0},{12,4},{1,9},{5,13},{9,1},{13,5},{2,10},{6,14},... | collective-permute-start | bytes 393224 | tf_op jit(solution)/shard_map/ppermute | solution.py:179
  79.4 15.2 %collective-permute-start.15 = (bf16[2,64,1536]{2,1,0:T(8,128)(2,1)S(1)}, bf16[2,64,1536]{2,1,0:T(8,128)(2,1)S(1)}, u32[]{:S(2)}, u32[]{:S(2)}) collective-permute-start(bf16[2,64,1536]{2,1,0:T(8,128)(2,1)S(1)} %slice.51), channel_id=1, source_target_pairs={{0,4},{4,0},{8,12},{12,8},{1,5},{5,1},{9,13},{13,9},{2,6},{6,2},{1... | collective-permute-start | bytes 1179656 | tf_op jit(solution)/shard_map/ppermute | solution.py:179
  85.2 9.7 %collective-permute-start.14 = (bf16[64,1024]{1,0:T(8,128)(2,1)S(1)}, bf16[64,1024]{1,0:T(8,128)(2,1)S(1)}, u32[]{:S(2)}, u32[]{:S(2)}) collective-permute-start(bf16[64,1024]{1,0:T(8,128)(2,1)S(1)} %fusion.8), channel_id=1, source_target_pairs={{0,8},{4,12},{8,0},{12,4},{1,9},{5,13},{9,1},{13,5},{2,10},{6,14},... | collective-permute-start | bytes 393224 | tf_op jit(solution)/shard_map/ppermute | solution.py:179
  94.7 9.9 %collective-permute-start.16 = (bf16[64,1536]{1,0:T(8,128)(2,1)S(1)}, bf16[64,1536]{1,0:T(8,128)(2,1)S(1)}, u32[]{:S(2)}, u32[]{:S(2)}) collective-permute-start(bf16[64,1536]{1,0:T(8,128)(2,1)S(1)} %fusion.6), channel_id=1, source_target_pairs={{0,8},{4,12},{8,0},{12,4},{1,9},{5,13},{9,1},{13,5},{2,10},{6,14},... | collective-permute-start | bytes 589832 | tf_op jit(solution)/shard_map/ppermute | solution.py:179
